TPU v7x, 32 devices: a whole 2x2x4 slice. The times are simulated.
32 devices in a mesh: seg: 8 (over y, x, core), doc: 4 (over z).
Axes of the slice: x: 2, y: 2, z: 4, core: 2. Of those that a mesh axis runs over, the one named last changes fastest.
Arguments:
- tokens: bfloat16 [4, 128, 128, 768], P('doc', 'seg'), may hold values from -6 to 6
- cotangent: bfloat16 [4, 128, 128, 768], P('doc', 'seg'), may hold values from -6 to 6
- seg_doc: int32 [4, 128], P('doc', 'seg'), may hold values from 0 to 4, as said below
- seg_pos: int32 [4, 128], P('doc', 'seg'), may hold values from 0 to 63, as said below
- master: float32 [14225408], P(('seg', 'doc'))
- momentum: float32 [14225408], P(('seg', 'doc')), may hold values from -0.6 to 0.6
- average: float32 [14225408], P(('seg', 'doc'))
Outputs:
- mixed_out: bfloat16 [4, 128, 128, 768], P('doc', 'seg')
- token_grad: bfloat16 [4, 128, 128, 768], P('doc', 'seg')
- new_master: float32 [14225408], P(('seg', 'doc'))
- new_momentum: float32 [14225408], P(('seg', 'doc'))
- new_average: float32 [14225408], P(('seg', 'doc'))
- weight_copy: bfloat16 [14225408], P(('seg', 'doc'))
Inputs may be any that keep to these rules, and one draw needn't show every extreme that they name: `seg_doc`: each group holds whole documents of 64 or 16 segments: as many of 64 as fit beside one of 16, the rest of 16, numbered from 0 upward in an order drawn from the seed; document d of a group is owned by index d of seg. One device holds at most 64 / (devices of seg) segments of one document, and every document of 64 segments has exactly that many on every device of its group. `seg_pos`: the segments of a document of length L carry the places 0 to L - 1, each once.
All inputs are finite; a program needn't handle non-finite values.
Results may differ from a plain program's by a relative error of at most 0.019.
Values may be sent and summed in bfloat16 or wider, within the bound.
No kernel may reach another device: no remote copies, remote signals or barrier semaphores. Data moves between devices by JAX's collectives and lax.ppermute only.
A program may use at most 384 MiB of HBM per device.

v0:
```python
import math

import jax
import jax.numpy as jnp
from jax import lax
from jax.sharding import PartitionSpec as P

D = 768
HEADS = 12
HEAD_DIM = 64
FF = 3072
SEG_LEN = 128
LONG_SEGS = 64


EPSILON = 1e-05
NEGATIVE = -1e30


def param_layout():
    return [
        ("w_qkv", (D, 3 * D)),
        ("b_qv", (2 * D,)),
        ("w_out", (D, D)),
        ("b_out", (D,)),
        ("gain_one", (D,)),
        ("bias_one", (D,)),
        ("w_up", (D, FF)),
        ("b_up", (FF,)),
        ("w_down", (FF, D)),
        ("b_down", (D,)),
        ("gain_two", (D,)),
        ("bias_two", (D,)),
        ("pos_table", (LONG_SEGS, D)),
        ("x_qkv", (D, 3 * D)),
        ("x_bqv", (2 * D,)),
        ("x_out", (D, D)),
        ("x_bout", (D,)),
        ("gain_three", (D,)),
        ("bias_three", (D,)),
        ("x_up", (D, FF)),
        ("x_bup", (FF,)),
        ("x_down", (FF, D)),
        ("x_bdown", (D,)),
        ("gain_four", (D,)),
        ("bias_four", (D,)),
    ]


def unpack(flat_vec):
    params = {}
    offset = 0
    for entry_name, entry_shape in param_layout():
        length = math.prod(entry_shape)
        params[entry_name] = flat_vec[offset : offset + length].reshape(entry_shape)
        offset += length
    return params


def entry_rate(entry_name):
    if entry_name in ("w_qkv", "w_out", "w_up", "x_qkv", "x_out", "x_up"):
        return 0.5 / math.sqrt(D)
    if entry_name in ("w_down", "x_down"):
        return 0.5 / math.sqrt(FF)
    if entry_name == "pos_table":
        return 1.0
    return 0.2


def entry_cross(entry_name):
    return entry_name[:2] == "x_" or entry_name in (
        "pos_table",
        "gain_three",
        "bias_three",
        "gain_four",
        "bias_four",
    )


def step_tables(flat_index, n_tokens, n_cls):
    scaling = jnp.zeros(flat_index.shape, jnp.float32)
    rating = jnp.full(flat_index.shape, 0.2, jnp.float32)
    offset = 0
    for entry_name, entry_shape in param_layout():
        length = math.prod(entry_shape)
        inside = (flat_index >= offset) & (flat_index < offset + length)
        row_count = n_cls if entry_cross(entry_name) else n_tokens
        scaling = jnp.where(inside, 1.0 / math.sqrt(row_count), scaling)
        rating = jnp.where(inside, entry_rate(entry_name), rating)
        offset += length
    return (scaling, rating)


def optimizer_step(gradient, master, momentum, average, scaling, rating):
    scaled = gradient * scaling
    moment = 0.5 * momentum + scaled
    weight = master - rating * (scaled + 0.5 * moment)
    smooth = 0.5 * average + 0.5 * weight
    return (weight, moment, smooth, weight.astype(jnp.bfloat16))


def layer_norm(values, gain_vec, shift_vec):
    center = values - jnp.mean(values, axis=-1, keepdims=True)
    spread = jnp.mean(center * center, axis=-1, keepdims=True)
    return center * lax.rsqrt(spread + EPSILON) * gain_vec + shift_vec


def full_bias(bias_pair):
    bias_pair = bias_pair.astype(jnp.float32)
    return jnp.concatenate([bias_pair[:D], jnp.zeros((D,), jnp.float32), bias_pair[D:]])


def pair_grad(grad_packed):
    summed = jnp.sum(grad_packed.astype(jnp.float32), axis=0)
    return jnp.concatenate([summed[:D], summed[2 * D :]])


def matmul(left, right):
    return jnp.dot(left, right, preferred_element_type=jnp.float32)


def exact_gelu(values):
    return jax.nn.gelu(values, approximate=False)


def head_scores(packed, n_blocks, length, key_mask):
    head_shape = (n_blocks, length, HEADS, HEAD_DIM)
    queries = packed[:, :D].reshape(head_shape)
    key_rows = packed[:, D : 2 * D].reshape(head_shape)
    values = packed[:, 2 * D :].reshape(head_shape)
    scores = jnp.einsum(
        "bqhd,bkhd->bhqk", queries, key_rows, preferred_element_type=jnp.float32
    ) * HEAD_DIM ** (-0.5)
    scores = jnp.where(key_mask[:, None, None, :], scores, NEGATIVE)
    return (scores, queries, key_rows, values)


def attend_forward(packed, n_blocks, length, key_mask):
    scores, queries, key_rows, values = head_scores(packed, n_blocks, length, key_mask)
    largest = jnp.max(scores, axis=-1, keepdims=True)
    raised = jnp.exp(scores - largest)
    summed = jnp.sum(raised, axis=-1, keepdims=True)
    weights = (raised / summed).astype(jnp.bfloat16)
    blended = jnp.einsum("bhqk,bkhd->bqhd", weights, values, preferred_element_type=jnp.float32)
    return (blended.reshape(n_blocks * length, D).astype(jnp.bfloat16), largest + jnp.log(summed))


def attend_backward(packed, log_sum, key_mask, grad_out, n_blocks, length):
    scores, queries, key_rows, values = head_scores(packed, n_blocks, length, key_mask)
    weights = jnp.exp(scores - log_sum)
    grad_heads = grad_out.reshape(n_blocks, length, HEADS, HEAD_DIM)
    grad_weights = jnp.einsum(
        "bqhd,bkhd->bhqk", grad_heads, values, preferred_element_type=jnp.float32
    )
    grad_values = jnp.einsum(
        "bhqk,bqhd->bkhd",
        weights.astype(jnp.bfloat16),
        grad_heads,
        preferred_element_type=jnp.float32,
    )
    inner = jnp.sum(grad_weights * weights, axis=-1, keepdims=True)
    grad_scores = (weights * (grad_weights - inner)).astype(jnp.bfloat16)
    grad_queries = jnp.einsum(
        "bhqk,bkhd->bqhd", grad_scores, key_rows, preferred_element_type=jnp.float32
    ) * HEAD_DIM ** (-0.5)
    grad_keys = jnp.einsum(
        "bhqk,bqhd->bkhd", grad_scores, queries, preferred_element_type=jnp.float32
    ) * HEAD_DIM ** (-0.5)
    flat_shape = (n_blocks * length, D)
    joined = jnp.concatenate(
        [
            grad_queries.reshape(flat_shape),
            grad_keys.reshape(flat_shape),
            grad_values.reshape(flat_shape),
        ],
        axis=1,
    )
    return joined.astype(jnp.bfloat16)


def local(tokens, cotangent, seg_doc, seg_pos, master, momentum, average):
    n_seg = lax.axis_size("seg")
    n_doc = lax.axis_size("doc")
    shard_len = master.shape[0]
    master_low = master.astype(jnp.bfloat16)
    flat_low = lax.all_gather(master_low, ("seg", "doc"), axis=0, tiled=True)
    params = unpack(flat_low)

    def vector(entry_name):
        return params[entry_name].astype(jnp.float32)

    seg_count = tokens.shape[1]
    inputs = tokens[0].reshape(seg_count * SEG_LEN, D)
    all_keys = jnp.ones((seg_count, SEG_LEN), jnp.bool_)
    packed = (matmul(inputs, params["w_qkv"]) + full_bias(params["b_qv"])).astype(jnp.bfloat16)
    attended, log_sum = attend_forward(packed, seg_count, SEG_LEN, all_keys)
    resid_one = inputs.astype(jnp.float32) + matmul(attended, params["w_out"]) + vector("b_out")
    hidden_one, norm_one_pull = jax.vjp(
        layer_norm, resid_one, vector("gain_one"), vector("bias_one")
    )
    hidden_low = hidden_one.astype(jnp.bfloat16)
    upward = matmul(hidden_low, params["w_up"]) + vector("b_up")
    activated, gelu_pull = jax.vjp(exact_gelu, upward)
    active_low = activated.astype(jnp.bfloat16)
    resid_two = hidden_one + matmul(active_low, params["w_down"]) + vector("b_down")
    hidden_two, norm_two_pull = jax.vjp(
        layer_norm, resid_two, vector("gain_two"), vector("bias_two")
    )
    hidden_two = hidden_two.reshape(seg_count, SEG_LEN, D)
    doc_ids = seg_doc[0]
    places = seg_pos[0]
    pos_hot = (places[:, None] == jnp.arange(LONG_SEGS)[None, :]).astype(jnp.bfloat16)
    cls_low = (hidden_two[:, 0] + matmul(pos_hot, params["pos_table"])).astype(jnp.bfloat16)
    row_ids = jnp.arange(LONG_SEGS).astype(jnp.float32)[:, None]
    doc_low = doc_ids.astype(jnp.float32).astype(jnp.bfloat16)
    place_low = places.astype(jnp.float32).astype(jnp.bfloat16)
    all_cls, all_doc, all_place = (
        lax.all_gather(cls_low, "seg", axis=0, tiled=True),
        lax.all_gather(doc_low, "seg", axis=0, tiled=True),
        lax.all_gather(place_low, "seg", axis=0, tiled=True),
    )
    owner_self = lax.axis_index("seg").astype(jnp.float32)
    placement = (all_doc.astype(jnp.float32)[None, :] == owner_self) & (
        all_place.astype(jnp.float32)[None, :] == row_ids
    )
    place_hot = placement.astype(jnp.bfloat16)
    doc_rows = matmul(place_hot, all_cls).astype(jnp.bfloat16)
    pick_target = doc_ids * LONG_SEGS + places
    pick_hot = (jnp.arange(n_seg * LONG_SEGS)[None, :] == pick_target[:, None]).astype(jnp.bfloat16)
    key_mask = (jnp.sum(placement.astype(jnp.float32), axis=1) > 0)[None, :]
    cross_packed = (matmul(doc_rows, params["x_qkv"]) + full_bias(params["x_bqv"])).astype(
        jnp.bfloat16
    )
    cross_att, cross_lse = attend_forward(cross_packed, 1, LONG_SEGS, key_mask)
    resid_three = (
        doc_rows.astype(jnp.float32) + matmul(cross_att, params["x_out"]) + vector("x_bout")
    )
    hidden_three, norm_three_pull = jax.vjp(
        layer_norm, resid_three, vector("gain_three"), vector("bias_three")
    )
    hidden_three_low = hidden_three.astype(jnp.bfloat16)
    cross_up = matmul(hidden_three_low, params["x_up"]) + vector("x_bup")
    cross_act, cross_gelu_pull = jax.vjp(exact_gelu, cross_up)
    cross_act_low = cross_act.astype(jnp.bfloat16)
    resid_four = hidden_three + matmul(cross_act_low, params["x_down"]) + vector("x_bdown")
    crossed, norm_four_pull = jax.vjp(
        layer_norm, resid_four, vector("gain_four"), vector("bias_four")
    )
    crossed_low = crossed.astype(jnp.bfloat16)
    all_crossed = lax.all_gather(crossed_low, "seg", axis=0, tiled=True)
    returned = matmul(pick_hot, all_crossed).astype(jnp.bfloat16)
    mixed_out = jnp.concatenate(
        [returned[:, None, :], hidden_two[:, 1:, :].astype(jnp.bfloat16)], axis=1
    )
    cot_rows = cotangent[0]
    all_grad = lax.all_gather(cot_rows[:, 0], "seg", axis=0, tiled=True)
    grad_doc = matmul(place_hot, all_grad)
    grad_four, grad_gain_four, grad_bias_four = norm_four_pull(grad_doc)
    grad_xdown_low = grad_four.astype(jnp.bfloat16)
    grad_xdown = matmul(cross_act_low.T, grad_xdown_low)
    grad_xbdown = jnp.sum(grad_xdown_low.astype(jnp.float32), axis=0)
    grad_xact = matmul(grad_xdown_low, params["x_down"].T)
    grad_xup_low = cross_gelu_pull(grad_xact)[0].astype(jnp.bfloat16)
    grad_xup = matmul(hidden_three_low.T, grad_xup_low)
    grad_xbup = jnp.sum(grad_xup_low.astype(jnp.float32), axis=0)
    grad_hidden_three = grad_four + matmul(grad_xup_low, params["x_up"].T)
    grad_three, grad_gain_three, grad_bias_three = norm_three_pull(grad_hidden_three)
    grad_xbranch = grad_three.astype(jnp.bfloat16)
    grad_xout = matmul(cross_att.T, grad_xbranch)
    grad_xbout = jnp.sum(grad_xbranch.astype(jnp.float32), axis=0)
    grad_xatt = matmul(grad_xbranch, params["x_out"].T).astype(jnp.bfloat16)
    grad_xpacked = attend_backward(cross_packed, cross_lse, key_mask, grad_xatt, 1, LONG_SEGS)
    grad_xqkv = matmul(doc_rows.T, grad_xpacked)
    grad_xbqv = pair_grad(grad_xpacked)
    grad_rows_low = (grad_three + matmul(grad_xpacked, params["x_qkv"].T)).astype(jnp.bfloat16)
    grad_pos = grad_rows_low.astype(jnp.float32)
    all_rows_grad = lax.all_gather(grad_rows_low, "seg", axis=0, tiled=True)
    grad_cls = matmul(pick_hot, all_rows_grad)
    grad_hidden_two = jnp.concatenate(
        [grad_cls[:, None, :], cot_rows[:, 1:, :].astype(jnp.float32)], axis=1
    )
    grad_two, grad_gain_two, grad_bias_two = norm_two_pull(grad_hidden_two.reshape(-1, D))
    grad_down_low = grad_two.astype(jnp.bfloat16)
    grad_wdown = matmul(active_low.T, grad_down_low)
    grad_bdown = jnp.sum(grad_down_low.astype(jnp.float32), axis=0)
    grad_active = matmul(grad_down_low, params["w_down"].T)
    grad_up_low = gelu_pull(grad_active)[0].astype(jnp.bfloat16)
    grad_wup = matmul(hidden_low.T, grad_up_low)
    grad_bup = jnp.sum(grad_up_low.astype(jnp.float32), axis=0)
    grad_hidden_one = grad_two + matmul(grad_up_low, params["w_up"].T)
    grad_one, grad_gain_one, grad_bias_one = norm_one_pull(grad_hidden_one)
    grad_branch = grad_one.astype(jnp.bfloat16)
    grad_wout = matmul(attended.T, grad_branch)
    grad_bout = jnp.sum(grad_branch.astype(jnp.float32), axis=0)
    grad_att = matmul(grad_branch, params["w_out"].T).astype(jnp.bfloat16)
    grad_packed = attend_backward(packed, log_sum, all_keys, grad_att, seg_count, SEG_LEN)
    grad_wqkv = matmul(inputs.T, grad_packed)
    grad_bqv = pair_grad(grad_packed)
    token_grad = (grad_one + matmul(grad_packed, params["w_qkv"].T)).astype(jnp.bfloat16)
    grad_table = {
        "w_qkv": grad_wqkv,
        "b_qv": grad_bqv,
        "w_out": grad_wout,
        "b_out": grad_bout,
        "gain_one": grad_gain_one,
        "bias_one": grad_bias_one,
        "w_up": grad_wup,
        "b_up": grad_bup,
        "w_down": grad_wdown,
        "b_down": grad_bdown,
        "gain_two": grad_gain_two,
        "bias_two": grad_bias_two,
        "pos_table": grad_pos,
        "x_qkv": grad_xqkv,
        "x_bqv": grad_xbqv,
        "x_out": grad_xout,
        "x_bout": grad_xbout,
        "gain_three": grad_gain_three,
        "bias_three": grad_bias_three,
        "x_up": grad_xup,
        "x_bup": grad_xbup,
        "x_down": grad_xdown,
        "x_bdown": grad_xbdown,
        "gain_four": grad_gain_four,
        "bias_four": grad_bias_four,
    }
    pieces = [grad_table[entry_name].reshape(-1) for entry_name, entry_shape in param_layout()]
    full_len = shard_len * n_seg * n_doc
    used_len = sum((math.prod(entry_shape) for entry_name, entry_shape in param_layout()))
    pieces.append(jnp.zeros((full_len - used_len,), jnp.float32))
    flat_grad = jnp.concatenate(pieces)
    gradient = lax.psum_scatter(flat_grad, ("seg", "doc"), scatter_dimension=0, tiled=True)
    flat_index = lax.axis_index(("seg", "doc")) * shard_len + jnp.arange(shard_len)
    n_cls = n_doc * n_seg * seg_count
    scaling, rating = step_tables(flat_index, n_cls * SEG_LEN, n_cls)
    weight, moment, smooth, copy_low = optimizer_step(
        gradient, master, momentum, average, scaling, rating
    )
    return (
        mixed_out.reshape(1, seg_count, SEG_LEN, D),
        token_grad.reshape(1, seg_count, SEG_LEN, D),
        weight,
        moment,
        smooth,
        copy_low,
    )


def solution(mesh):
    placed = (
        P("doc", "seg", None, None),
        P("doc", "seg", None, None),
        P("doc", "seg"),
        P("doc", "seg"),
        P(("seg", "doc")),
        P(("seg", "doc")),
        P(("seg", "doc")),
    )
    return jax.shard_map(
        local,
        mesh=mesh,
        in_specs=placed,
        out_specs=(
            P("doc", "seg", None, None),
            P("doc", "seg", None, None),
            P(("seg", "doc")),
            P(("seg", "doc")),
            P(("seg", "doc")),
            P(("seg", "doc")),
        ),
        check_vma=False,
    )
```

profile of v0, /device:TPU:0, one launch (start us, length us, event | category | flops | bytes accessed | tf_op | source)
XLA Modules:
  0.0 2355.6 jit_solution(334337920090643327)
XLA Ops:
  9.0 10.9 reshape.446
  21.8 15.2 all-reduce.3
  38.7 10.0 all-gather.1
  55.0 275.2 %all-gather.5.cloned.1.call-done = bf16[32,1,444544]{2,1,0:T(2,128)(2,1)} async-done(((bf16[1,1,444544]{2,1,0:T(2,128)(2,1)}), bf16[32,1,444544]{2,1,0:T(2,128)(2,1)}) %all-gather.5.cloned.1.call-update) | async-done | bytes 28450832 | tf_op jit(solution)/shard_map/all_gather | solution.py:186
  330.1 168.5 %reduce.10 = bf16[32,444544]{1,0:T(8,128)(2,1)} reduce(bf16[32,1,444544]{2,1,0:T(2,128)(2,1)} %all-gather.5.cloned.1.call-done, bf16[]{:T(256)} %constant.66), dimensions={1}, to_apply=%all-gather.2.reduce_sub_computation | reduce | bytes 56901632 | tf_op jit(solution)/shard_map/all_gather | solution.py:186
  498.7 66.0 %reshape.447 = bf16[14225408]{0:T(1024)(128)(2,1)} reshape(bf16[32,444544]{1,0:T(8,128)(2,1)} %reduce.10) | data formatting | bytes 56901632
  575.8 14.6 fusion.180
  643.5 9.8 add_convert_fusion.1
  703.7 68.9 %multiply_convert_fusion = (bf16[2048,3072]{1,0:T(8,128)(2,1)}, f32[2048,3072]{1,0:T(8,128)}, f32[2048,3072]{1,0:T(8,128)}) fusion(f32[3072]{0:T(1024)S(1)} %copy-done.93, bf16[768,3072]{1,0:T(8,128)(2,1)S(1)} %bitcast.208, f32[2048,768]{1,0:T(8,128)S(1)} %get-tuple-element.84, f32[768]{0:T(1024)S(1)} %copy-done.104, f32[768]{0:T(1024)S(1)} %copy-done.88, ...), kind=kOutput, calls=%fused_computation.4 | convolution fusion | flops 10086776832 | bytes 73959424 | tf_op jit(solution)/shard_map/dot_general | solution.py:119
  772.6 13.8 fusion.188
  856.4 10.5 all_gather.27
  885.8 15.7 fusion.193
  901.6 28.0 %convert_reduce_fusion = (f32[3072]{0:T(1024)}, bf16[2048,3072]{1,0:T(8,128)(2,1)}) fusion(f32[2048,3072]{1,0:T(8,128)} %get-tuple-element.43, bf16[2048,768]{1,0:T(8,128)(2,1)S(1)} %get-tuple-element.29, bf16[3072,768]{1,0:T(8,128)(2,1)} %reshape.402, f32[2048,3072]{1,0:T(8,128)} %get-tuple-element.85, f32[3072]{0:T(1024)S(1)} %copy-done.94), kind=kOutput, calls=%fused_computation.2 | convolution fusion | flops 9770628096 | bytes 70803456 | tf_op jit(solution)/shard_map/dot_general | solution.py:119
  929.6 18.8 multiply_reduce_fusion.2
  948.4 18.1 convolution_bitcast_fusion.2
  996.6 10.4 multiply_reduce_fusion
  1007.1 10.3 multiply_convert_fusion.1
  1039.7 9.7 convolution_bitcast_fusion
  1065.4 10.7 reshape.426
  1076.1 9.5 copy.188
  1111.9 9.5 copy.189
  1121.4 11.0 reshape.432
  1140.2 20.2 dynamic-update-slice.5
  1164.3 80.6 %dynamic-update-slice.9 = f32[14225408]{0:T(1024)} dynamic-update-slice(f32[14225408]{0:T(1024)} %constant_dynamic-update-slice_fusion.15, f32[2359296]{0:T(1024)} %bitcast.186, s32[]{} %constant.240) | dynamic-update-slice | bytes 18874372
  1246.3 80.5 %dynamic-update-slice.11 = f32[14225408]{0:T(1024)} dynamic-update-slice(f32[14225408]{0:T(1024)} %constant_dynamic-update-slice_fusion.14, f32[2359296]{0:T(1024)} %reshape.426, s32[]{} %constant.242) | dynamic-update-slice | bytes 18874372
  1339.3 20.3 dynamic-update-slice.19
  1363.5 80.6 %dynamic-update-slice.23 = f32[14225408]{0:T(1024)} dynamic-update-slice(f32[14225408]{0:T(1024)} %constant_dynamic-update-slice_fusion.6, f32[2359296]{0:T(1024)} %bitcast.185, s32[]{} %constant.254) | dynamic-update-slice | bytes 18874372
  1445.4 80.2 %dynamic-update-slice.25 = f32[14225408]{0:T(1024)} dynamic-update-slice(f32[14225408]{0:T(1024)} %constant_dynamic-update-slice_fusion.5, f32[2359296]{0:T(1024)} %reshape.432, s32[]{} %constant.256) | dynamic-update-slice | bytes 18874372
  1533.9 13.9 all_gather.25
  1551.0 14.5 add_convert_fusion.2
  1565.4 771.2 %all-reduce.6.cloned.1.call-done = f32[14225408]{0:T(1024)} async-done(((f32[14225408]{0:T(1024)}), f32[14225408]{0:T(1024)}) %all-reduce.6.cloned.1.call-update) | async-done | bytes 56901648
  2336.6 10.0 fusion.173
  (423 shorter events, 351.7 us)
Async XLA Ops:
  7.2 29.8 %copy-start.28 = (bf16[1,16,128,768]{3,2,1,0:T(8,128)(2,1)S(1)}, bf16[1,16,128,768]{3,2,1,0:T(8,128)(2,1)}, u32[]{:S(2)}) copy-start(bf16[1,16,128,768]{3,2,1,0:T(8,128)(2,1)} %param.8) | copy-start | bytes 9437188
  7.2 322.9 %all-gather.5.cloned.1.call-start = ((), (), s32[]{:S(2)}) async-start(), calls=%async_computation | async-start | bytes 58679808 | tf_op jit(solution)/shard_map/all_gather | solution.py:186
  19.9 2316.7 %all-reduce.6.cloned.1.call-start = ((), (), s32[]{:S(2)}) async-start(), calls=%async_computation.1 | async-start | bytes 113803264
  702.1 70.4 %copy-start.7 = (f32[2048,768]{1,0:T(8,128)}, f32[2048,768]{1,0:T(8,128)S(1)}, u32[]{:S(2)}) copy-start(f32[2048,768]{1,0:T(8,128)S(1)} %get-tuple-element.84) | copy-start | bytes 18874372
  702.2 70.4 %copy-start.57 = (f32[2048]{0:T(1024)}, f32[2048]{0:T(1024)S(1)}, u32[]{:S(2)}) copy-start(f32[2048]{0:T(1024)S(1)} %broadcast_multiply_fusion.1) | copy-start | bytes 24580
  703.1 69.5 %copy-start.69 = (f32[2048]{0:T(1024)}, f32[2048]{0:T(1024)S(1)}, u32[]{:S(2)}) copy-start(f32[2048]{0:T(1024)S(1)} %fusion.160) | copy-start | bytes 24580
  703.7 68.9 %copy-start.23 = (bf16[3072,768]{1,0:T(8,128)(2,1)S(1)}, bf16[3072,768]{1,0:T(8,128)(2,1)}, u32[]{:S(2)}) copy-start(bf16[3072,768]{1,0:T(8,128)(2,1)} %reshape.402) | copy-start | bytes 14155780
  703.7 68.9 %copy-start.106 = (f32[768]{0:T(1024)S(1)}, f32[768]{0:T(1024)}, u32[]{:S(2)}) copy-start(f32[768]{0:T(1024)} %get-tuple-element.52) | copy-start | bytes 9220
  789.8 25.0 %copy-start.51 = (f32[768]{0:T(1024)S(1)}, f32[768]{0:T(1024)}, u32[]{:S(2)}) copy-start(f32[768]{0:T(1024)} %get-tuple-element.48) | copy-start | bytes 9220
  789.9 25.0 %copy-start.53 = (f32[768]{0:T(1024)S(1)}, f32[768]{0:T(1024)}, u32[]{:S(2)}) copy-start(f32[768]{0:T(1024)} %get-tuple-element.47) | copy-start | bytes 9220
  836.6 33.1 %copy-start.108 = (s32[16]{0:T(128)S(1)}, s32[16]{0:T(128)}, u32[]{:S(2)}) copy-start(s32[16]{0:T(128)} %bitcast_add_fusion) | copy-start | bytes 196
  901.6 28.0 %copy-start.58 = (f32[2048]{0:T(1024)S(1)}, f32[2048]{0:T(1024)}, u32[]{:S(2)}) copy-start(f32[2048]{0:T(1024)} %copy-done.57) | copy-start | bytes 24580
  901.6 28.0 %copy-start.70 = (f32[2048]{0:T(1024)S(1)}, f32[2048]{0:T(1024)}, u32[]{:S(2)}) copy-start(f32[2048]{0:T(1024)} %copy-done.69) | copy-start | bytes 24580
  901.6 28.0 %copy-start.89 = (f32[768]{0:T(1024)S(1)}, f32[768]{0:T(1024)}, u32[]{:S(2)}) copy-start(f32[768]{0:T(1024)} %get-tuple-element.54) | copy-start | bytes 9220
  929.6 18.8 copy-start.105
  948.4 18.1 copy-start.60
  1164.3 80.6 %copy-start.92 = (f32[3072]{0:T(1024)S(1)}, f32[3072]{0:T(1024)}, u32[]{:S(2)}) copy-start(f32[3072]{0:T(1024)} %get-tuple-element.102) | copy-start | bytes 36868
  1246.3 80.5 %copy-start.75 = (f32[768]{0:T(1024)S(1)}, f32[768]{0:T(1024)}, u32[]{:S(2)}) copy-start(f32[768]{0:T(1024)} %get-tuple-element.28) | copy-start | bytes 9220
  1246.3 81.8 %copy-start.86 = (f32[768]{0:T(1024)S(1)}, f32[768]{0:T(1024)}, u32[]{:S(2)}) copy-start(f32[768]{0:T(1024)} %get-tuple-element.6) | copy-start | bytes 9220
  1246.3 83.1 %copy-start.76 = (f32[768]{0:T(1024)S(1)}, f32[768]{0:T(1024)}, u32[]{:S(2)}) copy-start(f32[768]{0:T(1024)} %fusion.121) | copy-start | bytes 9220
  1246.3 83.1 %copy-start.78 = (f32[768]{0:T(1024)S(1)}, f32[768]{0:T(1024)}, u32[]{:S(2)}) copy-start(f32[768]{0:T(1024)} %get-tuple-element.104) | copy-start | bytes 9220
  1246.3 84.4 %copy-start.46 = (f32[49152]{0:T(1024)S(1)}, f32[49152]{0:T(1024)}, u32[]{:S(2)}) copy-start(f32[49152]{0:T(1024)} %reshape.434) | copy-start | bytes 589828
  1331.4 28.2 %copy-start.85 = (f32[768]{0:T(1024)S(1)}, f32[768]{0:T(1024)}, u32[]{:S(2)}) copy-start(f32[768]{0:T(1024)} %get-tuple-element.26) | copy-start | bytes 9220
  1331.4 29.5 %copy-start.84 = (f32[768]{0:T(1024)S(1)}, f32[768]{0:T(1024)}, u32[]{:S(2)}) copy-start(f32[768]{0:T(1024)} %get-tuple-element.13) | copy-start | bytes 9220
  1331.4 30.8 %copy-start.83 = (f32[768]{0:T(1024)S(1)}, f32[768]{0:T(1024)}, u32[]{:S(2)}) copy-start(f32[768]{0:T(1024)} %get-tuple-element.16) | copy-start | bytes 9220
  1363.5 80.6 %copy-start.66 = (f32[3072]{0:T(1024)S(1)}, f32[3072]{0:T(1024)}, u32[]{:S(2)}) copy-start(f32[3072]{0:T(1024)} %get-tuple-element.24) | copy-start | bytes 36868
  1445.4 80.2 %copy-start.82 = (f32[768]{0:T(1024)S(1)}, f32[768]{0:T(1024)}, u32[]{:S(2)}) copy-start(f32[768]{0:T(1024)} %get-tuple-element.22) | copy-start | bytes 9220
  1445.4 81.5 %copy-start.81 = (f32[768]{0:T(1024)S(1)}, f32[768]{0:T(1024)}, u32[]{:S(2)}) copy-start(f32[768]{0:T(1024)} %get-tuple-element.11) | copy-start | bytes 9220
  1445.4 82.8 %copy-start.80 = (f32[768]{0:T(1024)S(1)}, f32[768]{0:T(1024)}, u32[]{:S(2)}) copy-start(f32[768]{0:T(1024)} %get-tuple-element.15) | copy-start | bytes 9220
  1530.2 20.8 copy-start.27
  1530.2 20.8 copy-start.72
  1550.9 785.6 %copy-start.21 = (f32[444544]{0:T(1024)S(1)}, f32[444544]{0:T(1024)}, u32[]{:S(2)}) copy-start(f32[444544]{0:T(1024)} %param.11) | copy-start | bytes 5334532
  (95 other events, 626.9 us)
Sparse Core Ops, SparseCore 0:
  20.0 310.0 all-gather.4
  1530.3 806.2 all-reduce.5
where the time goes:
time: 2390 us; the launch traced here: 2360 us
  waiting for transfers between devices  1050 us (44%)
  local copies, waits for them, and re-layouts  705 us (29%)
  matrix products  291 us (12%)
  other arithmetic  238 us (10%)
  blocking collectives  58.7 us (2%)
    unnamed x3, waiting for transfers between devices  771 us
    unnamed x290, local copies, waits for them, and re-layouts  522 us
    all_gather x1, waiting for transfers between devices, local(): flat_low = lax.all_gather(master_low, ('seg', 'doc'), axis=0, tiled=True)  275 us
    dot_general x29, matrix products, matmul(): return jnp.dot(left, right, preferred_element_type=jnp.float32)  245 us
    all_gather x1, other arithmetic, local(): flat_low = lax.all_gather(master_low, ('seg', 'doc'), axis=0, tiled=True)  169 us
    reshape x9, local copies, waits for them, and re-layouts, unpack(): params[entry_name] = flat_vec[offset:offset + length].reshape(entry_shape)  52.4 us
  transfers between devices with their start and end apart: 2, of which 2 were waited for; matrix products, arithmetic and copies ran while one was open for 1% of the time, Pallas kernels for 0%

commit v1 on v0

v1 whole, which is shorter than its diff:
```python
import math

import jax
import jax.numpy as jnp
import numpy as np
from jax import lax
from jax.experimental import pallas as pl
from jax.experimental.pallas import tpu as pltpu
from jax.sharding import PartitionSpec as P

D = 768
HEADS = 12
HEAD_DIM = 64
FF = 3072
SEG_LEN = 128
LONG_SEGS = 64


EPSILON = 1e-05
NEGATIVE = -1e30


def param_layout():
    return [
        ("w_qkv", (D, 3 * D)),
        ("b_qv", (2 * D,)),
        ("w_out", (D, D)),
        ("b_out", (D,)),
        ("gain_one", (D,)),
        ("bias_one", (D,)),
        ("w_up", (D, FF)),
        ("b_up", (FF,)),
        ("w_down", (FF, D)),
        ("b_down", (D,)),
        ("gain_two", (D,)),
        ("bias_two", (D,)),
        ("pos_table", (LONG_SEGS, D)),
        ("x_qkv", (D, 3 * D)),
        ("x_bqv", (2 * D,)),
        ("x_out", (D, D)),
        ("x_bout", (D,)),
        ("gain_three", (D,)),
        ("bias_three", (D,)),
        ("x_up", (D, FF)),
        ("x_bup", (FF,)),
        ("x_down", (FF, D)),
        ("x_bdown", (D,)),
        ("gain_four", (D,)),
        ("bias_four", (D,)),
    ]


def entry_rate(entry_name):
    if entry_name in ("w_qkv", "w_out", "w_up", "x_qkv", "x_out", "x_up"):
        return 0.5 / math.sqrt(D)
    if entry_name in ("w_down", "x_down"):
        return 0.5 / math.sqrt(FF)
    if entry_name == "pos_table":
        return 1.0
    return 0.2


def entry_cross(entry_name):
    return entry_name[:2] == "x_" or entry_name in (
        "pos_table",
        "gain_three",
        "bias_three",
        "gain_four",
        "bias_four",
    )


LANES = 128
BLK = 16


def ceil_to(value, step):
    return -(-value // step) * step


def item_list(total_rows):
    groups = [
        ["w_qkv"],
        ["b_qv"],
        ["w_out"],
        ["b_out", "gain_one", "bias_one"],
        ["w_up"],
        ["b_up"],
        ["w_down"],
        ["b_down", "gain_two", "bias_two"],
        ["pos_table"],
        ["x_qkv"],
        ["x_bqv"],
        ["x_out"],
        ["x_bout", "gain_three", "bias_three"],
        ["x_up"],
        ["x_bup"],
        ["x_down"],
        ["x_bdown", "gain_four", "bias_four"],
    ]
    shapes = dict(param_layout())
    items = []
    nat = 0
    blk = 0
    for names in groups:
        rows = sum(math.prod(shapes[name]) for name in names) // LANES
        items.append(dict(name=names[0], names=names, nat=nat, rows=rows, blk=blk))
        nat += rows
        blk += ceil_to(rows, BLK) // BLK
    items.append(dict(name="tail", names=[], nat=nat, rows=total_rows - nat, blk=blk))
    return items


class Geometry:
    def __init__(self, n_seg, n_doc, shard_len):
        self.n_seg, self.n_doc = n_seg, n_doc
        self.n_dev = n_seg * n_doc
        self.chunk = shard_len // LANES
        self.items = item_list(self.chunk * self.n_dev)
        self.by_name = {item["name"]: item for item in self.items}
        firsts, lasts = [], []
        for n in range(self.n_dev):
            lo, hi = n * self.chunk, (n + 1) * self.chunk
            blocks = []
            for item in self.items:
                a, b = max(lo, item["nat"]), min(hi, item["nat"] + item["rows"])
                if a < b:
                    blocks.append(item["blk"] + (a - item["nat"]) // BLK)
                    blocks.append(item["blk"] + (b - 1 - item["nat"]) // BLK)
            firsts.append(min(blocks))
            lasts.append(max(blocks))
        self.first, self.last = firsts, lasts
        most = max(b - a + 1 for a, b in zip(firsts, lasts))
        self.piece_blocks = -(-most // self.n_dev)
        self.piece = self.piece_blocks * BLK
        self.slots = self.piece_blocks * self.n_dev
        self.c_size, self.x_size = 2, 2
        self.y_size = n_seg // 4

    def block_table(self):
        table = np.zeros((self.n_dev, self.slots, 3), np.int32)
        for n in range(self.n_dev):
            lo, hi = n * self.chunk, (n + 1) * self.chunk
            for t in range(self.slots):
                b = self.first[n] + t
                if b > self.last[n]:
                    continue
                item = [it for it in self.items if it["blk"] <= b][-1]
                start = item["nat"] + (b - item["blk"]) * BLK
                a = max(start, lo)
                z = min(start + BLK, hi, item["nat"] + item["rows"])
                if a < z:
                    table[n, t] = (start - lo, a - start, z - start)
        return table

    def chunks_of(self, item):
        found = []
        n_blocks = ceil_to(item["rows"], BLK) // BLK
        for n in range(self.n_dev):
            a = max(item["blk"], self.first[n])
            b = min(item["blk"] + n_blocks, self.last[n] + 1)
            if a < b:
                found.append((n, a - item["blk"], b - item["blk"], a - self.first[n]))
        return found

    def buckets(self):
        end_attention = self.by_name["w_out"]["nat"] + self.by_name["w_out"]["rows"]
        end_segment = self.by_name["pos_table"]["nat"]
        a = (end_attention - 1) // self.chunk + 1
        b = (end_segment - 1) // self.chunk + 1
        return [range(0, a), range(a, b), range(b, self.n_dev)]

    def coords(self, device):
        seg, doc = divmod(device, self.n_doc)
        yx, c = divmod(seg, self.c_size)
        y, x = divmod(yx, self.x_size)
        return dict(y=y, x=x, c=c, z=doc)

    def device(self, y, x, c, z):
        return ((y * self.x_size + x) * self.c_size + c) * self.n_doc + z

    def size(self, axis):
        return dict(y=self.y_size, x=self.x_size, c=self.c_size, z=self.n_doc)[axis]

    def shift(self, axis, step):
        pairs = []
        for source in range(self.n_dev):
            at = self.coords(source)
            at[axis] = (at[axis] + step) % self.size(axis)
            pairs.append((source, self.device(**at)))
        return pairs
def spec_vmem():
    return pl.BlockSpec(memory_space=pltpu.VMEM)


def spec_any():
    return pl.BlockSpec(memory_space=pl.ANY)


def spec_smem():
    return pl.BlockSpec(memory_space=pltpu.SMEM)


def kernel_params(mib=56):
    return pltpu.CompilerParams(vmem_limit_bytes=mib * 1024 * 1024)


def row_mask(low, high):
    rows = lax.broadcasted_iota(jnp.int32, (BLK, LANES), 0)
    return (rows >= low) & (rows < high)


def align_rows(geo, table, padded):
    def kernel(table_ref, rows_ref, out_ref):
        def body(t, carry):
            start, low, high = table_ref[t], table_ref[geo.slots + t], table_ref[2 * geo.slots + t]
            rows = rows_ref[pl.ds(start + BLK, BLK), :]
            rows = jnp.where(row_mask(low, high), rows, 0.0)
            out_ref[pl.ds(pl.multiple_of(t * BLK, BLK), BLK), :] = rows.astype(jnp.bfloat16)
            return carry

        lax.fori_loop(0, geo.slots, body, 0, unroll=4)

    return pl.pallas_call(
        kernel,
        out_shape=jax.ShapeDtypeStruct((geo.slots * BLK, LANES), jnp.bfloat16),
        in_specs=[spec_smem(), spec_vmem()],
        out_specs=spec_vmem(),
        compiler_params=kernel_params(),
    )(table, padded)


def natural_rows(geo, table, blocks, pad_rows):
    def kernel(table_ref, blocks_ref, out_ref):
        def body(t, carry):
            start, low, high = table_ref[t], table_ref[geo.slots + t], table_ref[2 * geo.slots + t]
            rows = blocks_ref[pl.ds(pl.multiple_of(t * BLK, BLK), BLK), :].astype(jnp.float32)
            here = pl.ds(start + BLK, BLK)
            out_ref[here, :] = jnp.where(row_mask(low, high), rows, out_ref[here, :])
            return carry

        lax.fori_loop(0, geo.slots, body, 0)

    return pl.pallas_call(
        kernel,
        out_shape=jax.ShapeDtypeStruct((pad_rows, LANES), jnp.float32),
        in_specs=[spec_smem(), spec_vmem()],
        out_specs=spec_vmem(),
        compiler_params=kernel_params(),
    )(table, blocks)


class Buckets:
    def __init__(self, geo):
        self.geo = geo
        self.ranges = geo.buckets()
        self.half = [(len(r) + 1) // 2 for r in self.ranges]

    def find(self, chunk):
        for number, span in enumerate(self.ranges):
            if chunk in span:
                at = chunk - span.start
                cut = self.half[number]
                return (number, 0, at) if at < cut else (number, 1, at - cut)

    def shapes(self, number):
        geo = self.geo
        cut = self.half[number]
        rest = len(self.ranges[number]) - cut
        rows = geo.n_doc * geo.piece
        return [
            (geo.y_size, geo.x_size, cut, rows, LANES),
            (geo.x_size, geo.y_size, rest, rows, LANES),
        ]


def wrap(value, size):
    return lax.rem(value + size, size)


def copy_rows(count, step, body):
    full = count // step
    if full:
        def loop(i, carry):
            body(i * step, step)
            return carry

        lax.fori_loop(0, full, loop, 0)
    if count % step:
        body(full * step, count % step)


def unpack_matrix(geo, buckets, gathered, coords, name, depth, cols):
    item = geo.by_name[name]
    chunks = geo.chunks_of(item)
    used = sorted({buckets.find(n)[0] for n, *_ in chunks})
    operands = [array for number in used for array in gathered[number]]
    wide_cols = cols // LANES
    seg_rows = geo.n_doc * geo.piece

    def kernel(coords_ref, *refs):
        sources, (out_ref, staged, wide, sem) = refs[: len(operands)], refs[len(operands) :]
        my_y, my_x, my_c = coords_ref[0], coords_ref[1], coords_ref[2]
        for at, (n, _, _, _) in enumerate(chunks):
            number, half, place = buckets.find(n)
            for core in range(2):
                source = sources[4 * used.index(number) + 2 * half + core]
                c = my_c if core == 0 else 1 - my_c
                for ry in range(geo.y_size):
                    for rx in range(geo.x_size):
                        y = wrap(my_y - ry, geo.y_size)
                        x = wrap(my_x - rx, geo.x_size)
                        s = (y * geo.x_size + x) * 2 + c
                        index = (ry, rx, place) if half == 0 else (rx, ry, place)
                        pltpu.make_async_copy(
                            source.at[index],
                            staged.at[at, pl.ds(pl.multiple_of(s * seg_rows, BLK), seg_rows)],
                            sem,
                        ).start()
        pltpu.make_async_copy(staged, staged, sem).wait()
        done = 0
        for at, (n, b0, b1, slot) in enumerate(chunks):
            if b0 < done:
                here = pl.ds(b0 * BLK, BLK)
                extra = staged[at, pl.ds(slot * BLK, BLK), :].astype(jnp.float32)
                wide[here, :] = wide[here, :] + extra
                b0, slot = b0 + 1, slot + 1

            def widen(row, rows, at=at, b0=b0, slot=slot):
                src = pl.ds(pl.multiple_of(slot * BLK + row, BLK), rows)
                dst = pl.ds(pl.multiple_of(b0 * BLK + row, BLK), rows)
                wide[dst, :] = staged[at, src, :].astype(jnp.float32)

            copy_rows((b1 - b0) * BLK, 128, widen)
            done = b1

        def turn(kb, carry):
            rows = pl.ds(pl.multiple_of(kb * BLK, BLK), BLK)
            for cb in range(wide_cols):
                tile = wide[pl.ds(kb * BLK * wide_cols + cb, BLK, stride=wide_cols), :]
                out_ref[rows, cb * LANES : (cb + 1) * LANES] = tile.astype(jnp.bfloat16)
            return carry

        lax.fori_loop(0, depth // BLK, turn, 0)

    return pl.pallas_call(
        kernel,
        out_shape=jax.ShapeDtypeStruct((depth, cols), jnp.bfloat16),
        in_specs=[spec_smem()] + [spec_any()] * len(operands),
        out_specs=spec_vmem(),
        scratch_shapes=[
            pltpu.VMEM((len(chunks), geo.slots * BLK, LANES), jnp.bfloat16),
            pltpu.VMEM((item["rows"], LANES), jnp.float32),
            pltpu.SemaphoreType.DMA,
        ],
        compiler_params=kernel_params(),
    )(coords, *operands)


def unpack_vectors(geo, buckets, gathered, coords, names):
    blocks = []
    places = {}
    for name in names:
        item = geo.by_name[name]
        places[name] = len(blocks) * BLK
        for b in range(ceil_to(item["rows"], BLK) // BLK):
            found = []
            for n in range(geo.n_dev):
                if geo.first[n] <= item["blk"] + b <= geo.last[n]:
                    found.append((n, item["blk"] + b - geo.first[n]))
            blocks.append(found)
    used = sorted({buckets.find(n)[0] for found in blocks for n, _ in found})
    operands = [array for number in used for array in gathered[number]]
    copies = [(b, which, n, slot) for b, found in enumerate(blocks) for which, (n, slot) in enumerate(found)]

    def kernel(coords_ref, *refs):
        sources, (out_ref, staged, sem) = refs[: len(operands)], refs[len(operands) :]
        my_y, my_x, my_c = coords_ref[0], coords_ref[1], coords_ref[2]
        for at, (b, which, n, slot) in enumerate(copies):
            number, half, place = buckets.find(n)
            where = geo.coords(slot // geo.piece_blocks)
            row = where["z"] * geo.piece + slot % geo.piece_blocks * BLK
            ry, rx = wrap(my_y - where["y"], geo.y_size), wrap(my_x - where["x"], geo.x_size)
            index = (ry, rx) if half == 0 else (rx, ry)
            for core in range(2):
                source = sources[4 * used.index(number) + 2 * half + core]

                @pl.when(my_c == (where["c"] if core == 0 else 1 - where["c"]))
                def _(source=source, at=at, index=index, place=place, row=row):
                    pltpu.make_async_copy(
                        source.at[index[0], index[1], place, pl.ds(row, BLK)], staged.at[at], sem
                    ).start()

        pltpu.make_async_copy(staged, staged, sem).wait()
        for at, (b, which, n, slot) in enumerate(copies):
            rows = staged[at].astype(jnp.float32)
            here = pl.ds(b * BLK, BLK)
            out_ref[here, :] = rows if which == 0 else out_ref[here, :] + rows

    out = pl.pallas_call(
        kernel,
        out_shape=jax.ShapeDtypeStruct((len(blocks) * BLK, LANES), jnp.float32),
        in_specs=[spec_smem()] + [spec_any()] * len(operands),
        out_specs=spec_vmem(),
        scratch_shapes=[
            pltpu.VMEM((len(copies), BLK, LANES), jnp.bfloat16),
            pltpu.SemaphoreType.DMA,
        ],
        compiler_params=kernel_params(),
    )(coords, *operands)
    values = {}
    shapes = dict(param_layout())
    for name in names:
        row = places[name]
        for entry in geo.by_name[name]["names"]:
            rows = math.prod(shapes[entry]) // LANES
            values[entry] = out[row : row + rows].reshape(shapes[entry])
            row += rows
    return values


def pack_bucket(geo, buckets, number, grads, coords):
    span = buckets.ranges[number]
    shapes = dict(param_layout())
    seg_rows = geo.n_doc * geo.piece
    parts = []
    for item in geo.items:
        chunks = [entry for entry in geo.chunks_of(item) if entry[0] in span]
        if chunks and item["names"]:
            parts.append((item, chunks))
    operands, windows, scratch = [], [], []
    wide_rows = BLK
    for item, chunks in parts:
        shape = shapes[item["names"][0]]
        if len(item["names"]) == 1 and len(shape) == 2 and item["name"] != "pos_table":
            cols = shape[1] // LANES
            k0 = min(b0 for _, b0, _, _ in chunks) // cols
            k1 = -(-max(b1 for _, _, b1, _ in chunks) // cols)
            operands.append(grads[item["name"]])
            windows.append((cols, k0, k1))
            scratch.append(pltpu.VMEM(((k1 - k0) * BLK, shape[1]), jnp.bfloat16))
            wide_rows = max(wide_rows, (k1 - k0) * BLK * cols)
        else:
            rows = jnp.concatenate([grads[n].reshape(-1, LANES) for n in item["names"]])
            rows = jnp.pad(rows, ((0, ceil_to(item["rows"], BLK) - item["rows"]), (0, 0)))
            operands.append(rows.astype(jnp.bfloat16))
            windows.append(None)
            scratch.append(pltpu.VMEM(rows.shape, jnp.bfloat16))
    outs = [shape for shape in buckets.shapes(number) for _ in range(2)]

    def kernel(coords_ref, *refs):
        sources = refs[: len(parts)]
        targets = refs[len(parts) : len(parts) + 4]
        loaded = refs[len(parts) + 4 : 2 * len(parts) + 4]
        staged, wide, in_sems, out_sem = refs[2 * len(parts) + 4 :]
        my_y, my_x, my_c = coords_ref[0], coords_ref[1], coords_ref[2]
        loads = []
        for at, window in enumerate(windows):
            source = sources[at]
            if window is not None:
                source = source.at[pl.ds(window[1] * BLK, (window[2] - window[1]) * BLK)]
            loads.append(pltpu.make_async_copy(source, loaded[at], in_sems.at[at]))
            loads[-1].start()

        def clear(row, rows):
            for at in range(len(span)):
                here = pl.ds(pl.multiple_of(row, BLK), rows)
                staged[at, here, :] = jnp.zeros((rows, LANES), jnp.bfloat16)

        copy_rows(geo.slots * BLK, 128, clear)
        for at, ((item, chunks), window) in enumerate(zip(parts, windows)):
            loads[at].wait()
            values = loaded[at]
            base = 0
            if window is not None:
                cols, k0, k1 = window
                base = k0 * cols

                def turn(kb, carry, values=values, cols=cols):
                    rows = pl.ds(pl.multiple_of(kb * BLK, BLK), BLK)
                    for cb in range(cols):
                        tile = values[rows, cb * LANES : (cb + 1) * LANES].astype(jnp.float32)
                        wide[pl.ds(kb * BLK * cols + cb, BLK, stride=cols), :] = tile
                    return carry

                lax.fori_loop(0, k1 - k0, turn, 0)
            for n, b0, b1, slot in chunks:
                def narrow(row, rows, n=n, b0=b0, slot=slot, values=values, window=window, base=base):
                    src = pl.ds(pl.multiple_of((b0 - base) * BLK + row, BLK), rows)
                    dst = pl.ds(pl.multiple_of(slot * BLK + row, BLK), rows)
                    data = values[src, :] if window is None else wide[src, :].astype(jnp.bfloat16)
                    staged[n - span.start, dst, :] = data

                copy_rows((b1 - b0) * BLK, 128, narrow)
        copies = []
        for n in span:
            _, half, place = buckets.find(n)
            for core in range(2):
                c = my_c if core == 0 else 1 - my_c
                for ry in range(geo.y_size):
                    for rx in range(geo.x_size):
                        y = wrap(my_y + ry, geo.y_size)
                        x = wrap(my_x + rx, geo.x_size)
                        s = (y * geo.x_size + x) * 2 + c
                        index = (ry, rx, place) if half == 0 else (rx, ry, place)
                        pltpu.make_async_copy(
                            staged.at[n - span.start, pl.ds(pl.multiple_of(s * seg_rows, BLK), seg_rows)],
                            targets[2 * half + core].at[index],
                            out_sem,
                        ).start()
        pltpu.make_async_copy(staged, staged, out_sem).wait()

    return pl.pallas_call(
        kernel,
        out_shape=[jax.ShapeDtypeStruct(shape, jnp.bfloat16) for shape in outs],
        in_specs=[spec_smem()] + [spec_any()] * len(operands),
        out_specs=[spec_any()] * 4,
        scratch_shapes=scratch
        + [
            pltpu.VMEM((len(span), geo.slots * BLK, LANES), jnp.bfloat16),
            pltpu.VMEM((wide_rows, LANES), jnp.float32),
            pltpu.SemaphoreType.DMA((len(parts),)),
            pltpu.SemaphoreType.DMA,
        ],
        compiler_params=kernel_params(),
    )(coords, *operands)


AXES = ("seg", "doc")


def send(geo, value, axis, step):
    return lax.ppermute(value, AXES, geo.shift(axis, step))


def gather_axis(geo, value, axis):
    parts = [value] + [send(geo, value, axis, r) for r in range(1, geo.size(axis))]
    return jnp.stack(parts)


def gather_bucket(geo, pieces, my_z, cut):
    nd = geo.n_doc
    parts = [pieces] + [send(geo, pieces, "z", r) for r in range(1, nd)]
    parts = parts[::-1]
    line = jnp.stack(parts + parts[: nd - 1], axis=1)
    line = lax.dynamic_slice_in_dim(line, nd - 1 - my_z, nd, axis=1)
    line = line.reshape(pieces.shape[0], nd * geo.piece, LANES)
    result = []
    for part, order in ((line[:cut], ("x", "y")), (line[cut:], ("y", "x"))):
        for axis in order:
            part = gather_axis(geo, part, axis)
        result += [part, send(geo, part, "c", 1)]
    return result


def plus(*terms):
    return sum(term.astype(jnp.float32) for term in terms)


def reduce_axis(geo, value, axis):
    parts = [value[0]] + [send(geo, value[r], axis, r) for r in range(1, geo.size(axis))]
    return plus(*parts).astype(jnp.bfloat16)


def reduce_bucket(geo, arrays, my_z):
    nd = geo.n_doc
    lines = []
    for half, order in ((0, ("y", "x")), (1, ("x", "y"))):
        keep, give = arrays[2 * half], arrays[2 * half + 1]
        part = plus(keep, send(geo, give, "c", 1)).astype(jnp.bfloat16)
        for axis in order:
            part = reduce_axis(geo, part, axis)
        lines.append(part)
    line = jnp.concatenate(lines)
    line = line.reshape(line.shape[0], nd, geo.piece, LANES)

    def to(r):
        return lax.dynamic_index_in_dim(line, lax.rem(my_z + r, nd), axis=1, keepdims=False)

    return plus(to(0), *[send(geo, to(r), "z", r) for r in range(1, nd)]).astype(jnp.bfloat16)
def optimizer_step(gradient, master, momentum, average, scaling, rating):
    scaled = gradient * scaling
    moment = 0.5 * momentum + scaled
    weight = master - rating * (scaled + 0.5 * moment)
    smooth = 0.5 * average + 0.5 * weight
    return (weight, moment, smooth, weight.astype(jnp.bfloat16))


def row_rates(geo, n_tokens, n_cls):
    total = geo.chunk * geo.n_dev
    scaling = np.zeros((total,), np.float32)
    rating = np.full((total,), 0.2, np.float32)
    row = 0
    for entry_name, entry_shape in param_layout():
        rows = math.prod(entry_shape) // LANES
        count = n_cls if entry_cross(entry_name) else n_tokens
        scaling[row : row + rows] = 1.0 / math.sqrt(count)
        rating[row : row + rows] = entry_rate(entry_name)
        row += rows
    return scaling.reshape(geo.n_dev, geo.chunk), rating.reshape(geo.n_dev, geo.chunk)


def norm_forward(values, gain_vec, shift_vec):
    center = values - jnp.mean(values, axis=-1, keepdims=True)
    rate = lax.rsqrt(jnp.mean(center * center, axis=-1, keepdims=True) + EPSILON)
    normal = center * rate
    return normal * gain_vec + shift_vec, normal, rate


def norm_backward(grad, normal, rate, gain_vec):
    scaled = grad * gain_vec
    return rate * (
        scaled
        - jnp.mean(scaled, axis=-1, keepdims=True)
        - normal * jnp.mean(scaled * normal, axis=-1, keepdims=True)
    )


def full_bias(bias_pair):
    return jnp.concatenate([bias_pair[:D], jnp.zeros((D,), jnp.float32), bias_pair[D:]])


def column_sum(rows):
    return jnp.sum(rows.astype(jnp.float32), axis=0)


def pair_grad(grad_packed):
    summed = column_sum(grad_packed)
    return jnp.concatenate([summed[:D], summed[2 * D :]])


def matmul(left, right):
    return jnp.dot(left, right, preferred_element_type=jnp.float32)


def exact_gelu(values):
    return jax.nn.gelu(values, approximate=False)


def head_scores(packed, n_blocks, length, mask):
    head_shape = (n_blocks, length, HEADS, HEAD_DIM)
    queries = packed[:, :D].reshape(head_shape)
    key_rows = packed[:, D : 2 * D].reshape(head_shape)
    values = packed[:, 2 * D :].reshape(head_shape)
    scores = jnp.einsum(
        "bqhd,bkhd->bhqk", queries, key_rows, preferred_element_type=jnp.float32
    ) * HEAD_DIM ** (-0.5)
    if mask is not None:
        scores = jnp.where(mask[None, None], scores, NEGATIVE)
    return (scores, queries, key_rows, values)


def attend_forward(packed, n_blocks, length, mask):
    scores, queries, key_rows, values = head_scores(packed, n_blocks, length, mask)
    largest = jnp.max(scores, axis=-1, keepdims=True)
    raised = jnp.exp(scores - largest)
    summed = jnp.sum(raised, axis=-1, keepdims=True)
    weights = (raised / summed).astype(jnp.bfloat16)
    blended = jnp.einsum("bhqk,bkhd->bqhd", weights, values, preferred_element_type=jnp.float32)
    return (blended.reshape(n_blocks * length, D).astype(jnp.bfloat16), largest + jnp.log(summed))


def attend_backward(packed, log_sum, mask, grad_out, n_blocks, length):
    scores, queries, key_rows, values = head_scores(packed, n_blocks, length, mask)
    weights = jnp.exp(scores - log_sum)
    grad_heads = grad_out.reshape(n_blocks, length, HEADS, HEAD_DIM)
    grad_weights = jnp.einsum(
        "bqhd,bkhd->bhqk", grad_heads, values, preferred_element_type=jnp.float32
    )
    grad_values = jnp.einsum(
        "bhqk,bqhd->bkhd",
        weights.astype(jnp.bfloat16),
        grad_heads,
        preferred_element_type=jnp.float32,
    )
    inner = jnp.sum(grad_weights * weights, axis=-1, keepdims=True)
    grad_scores = (weights * (grad_weights - inner)).astype(jnp.bfloat16)
    grad_queries = jnp.einsum(
        "bhqk,bkhd->bqhd", grad_scores, key_rows, preferred_element_type=jnp.float32
    ) * HEAD_DIM ** (-0.5)
    grad_keys = jnp.einsum(
        "bhqk,bqhd->bkhd", grad_scores, queries, preferred_element_type=jnp.float32
    ) * HEAD_DIM ** (-0.5)
    flat_shape = (n_blocks * length, D)
    joined = jnp.concatenate(
        [
            grad_queries.reshape(flat_shape),
            grad_keys.reshape(flat_shape),
            grad_values.reshape(flat_shape),
        ],
        axis=1,
    )
    return joined.astype(jnp.bfloat16)


def low(values):
    return values.astype(jnp.bfloat16)


def local(tokens, cotangent, seg_doc, seg_pos, master, momentum, average):
    n_seg = lax.axis_size("seg")
    n_doc = lax.axis_size("doc")
    geo = Geometry(n_seg, n_doc, master.shape[0])
    buckets = Buckets(geo)
    my_seg, my_doc = lax.axis_index("seg"), lax.axis_index("doc")
    me = my_seg * n_doc + my_doc
    coords = jnp.stack(
        [my_seg // 4, my_seg // 2 % 2, my_seg % 2, my_doc]
    ).astype(jnp.int32)
    table = lax.dynamic_index_in_dim(
        jnp.asarray(geo.block_table().transpose(0, 2, 1).reshape(geo.n_dev, -1)), me, 0, False
    )
    pad_rows = ceil_to(geo.chunk + 2 * BLK, 8)
    padded = jnp.pad(
        master.reshape(geo.chunk, LANES), ((BLK, pad_rows - geo.chunk - BLK), (0, 0))
    )
    aligned = align_rows(geo, table, padded)
    pieces = lax.all_to_all(
        aligned.reshape(geo.n_dev, geo.piece, LANES), AXES, 0, 0, tiled=True
    )
    gathered = [
        gather_bucket(geo, pieces[span.start : span.stop], my_doc, cut)
        for span, cut in zip(buckets.ranges, buckets.half)
    ]

    def matrix(name):
        depth, cols = dict(param_layout())[name]
        return unpack_matrix(geo, buckets, gathered, coords, name, depth, cols)

    vec = unpack_vectors(geo, buckets, gathered, coords, ["b_qv", "b_out", "b_up", "b_down"])

    seg_count = tokens.shape[1]
    cot_rows = cotangent[0]
    tagged = jnp.concatenate(
        [cot_rows[:, 0], jnp.broadcast_to(low(seg_doc[0].astype(jnp.float32))[:, None], (seg_count, LANES))],
        axis=1,
    )
    all_tagged = lax.all_gather(tagged, "seg", axis=0, tiled=True)
    all_grad, all_doc = all_tagged[:, :D], all_tagged[:, D].astype(jnp.float32)
    same_doc = all_doc[:, None] == all_doc[None, :]

    inputs = tokens[0].reshape(seg_count * SEG_LEN, D)
    w_qkv, w_out = matrix("w_qkv"), matrix("w_out")
    packed = low(matmul(inputs, w_qkv) + full_bias(vec["b_qv"]))
    attended, log_sum = attend_forward(packed, seg_count, SEG_LEN, None)
    resid_one = inputs.astype(jnp.float32) + matmul(attended, w_out) + vec["b_out"]
    hidden_one, normal_one, rate_one = norm_forward(resid_one, vec["gain_one"], vec["bias_one"])
    hidden_low = low(hidden_one)
    w_up, w_down = matrix("w_up"), matrix("w_down")
    upward = matmul(hidden_low, w_up) + vec["b_up"]
    activated, gelu_pull = jax.vjp(exact_gelu, upward)
    active_low = low(activated)
    resid_two = hidden_one + matmul(active_low, w_down) + vec["b_down"]
    hidden_two, normal_two, rate_two = norm_forward(resid_two, vec["gain_two"], vec["bias_two"])
    hidden_two = hidden_two.reshape(seg_count, SEG_LEN, D)

    xvec = unpack_vectors(
        geo, buckets, gathered, coords, ["pos_table", "x_bqv", "x_bout", "x_bup", "x_bdown"]
    )
    vec.update(xvec)
    x_qkv, x_out, x_up, x_down = matrix("x_qkv"), matrix("x_out"), matrix("x_up"), matrix("x_down")
    places = seg_pos[0]
    pos_hot = (places[:, None] == jnp.arange(LONG_SEGS)[None, :]).astype(jnp.bfloat16)
    cls_low = low(hidden_two[:, 0] + matmul(pos_hot, low(vec["pos_table"])))
    rows = lax.all_gather(cls_low, "seg", axis=0, tiled=True)
    n_rows = rows.shape[0]

    def own(values):
        return lax.dynamic_slice_in_dim(values, my_seg * seg_count, seg_count, axis=0)

    x_packed = low(matmul(rows, x_qkv) + full_bias(vec["x_bqv"]))
    x_att, x_lse = attend_forward(x_packed, 1, n_rows, same_doc)
    resid_three = rows.astype(jnp.float32) + matmul(x_att, x_out) + vec["x_bout"]
    hidden_three, normal_three, rate_three = norm_forward(
        resid_three, vec["gain_three"], vec["bias_three"]
    )
    hidden_three_low = low(hidden_three)
    x_upward = matmul(hidden_three_low, x_up) + vec["x_bup"]
    x_act, x_gelu_pull = jax.vjp(exact_gelu, x_upward)
    x_act_low = low(x_act)
    resid_four = hidden_three + matmul(x_act_low, x_down) + vec["x_bdown"]
    crossed, normal_four, rate_four = norm_forward(resid_four, vec["gain_four"], vec["bias_four"])
    mixed_out = jnp.concatenate(
        [own(low(crossed))[:, None, :], low(hidden_two[:, 1:, :])], axis=1
    )

    grads = {}
    grad_z = all_grad.astype(jnp.float32)
    grads["gain_four"] = column_sum(own(grad_z * normal_four))
    grads["bias_four"] = column_sum(own(grad_z))
    grad_four = norm_backward(grad_z, normal_four, rate_four, vec["gain_four"])
    grad_xm = low(grad_four)
    grads["x_down"] = low(matmul(own(x_act_low).T, own(grad_xm)))
    grads["x_bdown"] = column_sum(own(grad_xm))
    grad_xu = low(x_gelu_pull(matmul(grad_xm, x_down.T))[0])
    grads["x_up"] = low(matmul(own(hidden_three_low).T, own(grad_xu)))
    grads["x_bup"] = column_sum(own(grad_xu))
    grad_h3 = grad_four + matmul(grad_xu, x_up.T)
    grads["gain_three"] = column_sum(own(grad_h3 * normal_three))
    grads["bias_three"] = column_sum(own(grad_h3))
    grad_three = norm_backward(grad_h3, normal_three, rate_three, vec["gain_three"])
    grad_xa_out = low(grad_three)
    grads["x_out"] = low(matmul(own(x_att).T, own(grad_xa_out)))
    grads["x_bout"] = column_sum(own(grad_xa_out))
    grad_xa = low(matmul(grad_xa_out, x_out.T))
    grad_xpacked = attend_backward(x_packed, x_lse, same_doc, grad_xa, 1, n_rows)
    grads["x_qkv"] = low(matmul(own(rows).T, own(grad_xpacked)))
    grads["x_bqv"] = pair_grad(own(grad_xpacked))
    grad_rows = own(low(grad_three + matmul(grad_xpacked, x_qkv.T)))
    grads["pos_table"] = matmul(pos_hot.T, grad_rows)
    zero_vec = {"b_down": D, "gain_two": D, "bias_two": D}

    grad_h2 = jnp.concatenate(
        [grad_rows[:, None, :].astype(jnp.float32), cot_rows[:, 1:, :].astype(jnp.float32)], axis=1
    ).reshape(-1, D)
    grads["gain_two"] = column_sum(grad_h2 * normal_two)
    grads["bias_two"] = column_sum(grad_h2)
    grad_two = norm_backward(grad_h2, normal_two, rate_two, vec["gain_two"])
    grad_m = low(grad_two)
    grads["w_down"] = low(matmul(active_low.T, grad_m))
    grads["b_down"] = column_sum(grad_m)

    cross_arrays = pack_bucket(geo, buckets, 2, grads, coords)
    cross_pieces = reduce_bucket(geo, cross_arrays, my_doc)

    grad_u = low(gelu_pull(matmul(grad_m, w_down.T))[0])
    grads["w_up"] = low(matmul(hidden_low.T, grad_u))
    grads["b_up"] = column_sum(grad_u)
    feed_arrays = pack_bucket(geo, buckets, 1, grads, coords)
    feed_pieces = reduce_bucket(geo, feed_arrays, my_doc)
    grad_h1 = grad_two + matmul(grad_u, w_up.T)
    grads["gain_one"] = column_sum(grad_h1 * normal_one)
    grads["bias_one"] = column_sum(grad_h1)
    grad_one = norm_backward(grad_h1, normal_one, rate_one, vec["gain_one"])
    grad_branch = low(grad_one)
    grads["w_out"] = low(matmul(attended.T, grad_branch))
    grads["b_out"] = column_sum(grad_branch)
    grad_att = low(matmul(grad_branch, w_out.T))
    grad_packed = attend_backward(packed, log_sum, None, grad_att, seg_count, SEG_LEN)
    grads["w_qkv"] = low(matmul(inputs.T, grad_packed))
    grads["b_qv"] = pair_grad(grad_packed)
    token_grad = low(grad_one + matmul(grad_packed, w_qkv.T))
    att_arrays = pack_bucket(geo, buckets, 0, grads, coords)
    att_pieces = reduce_bucket(geo, att_arrays, my_doc)

    all_pieces = jnp.concatenate([att_pieces, feed_pieces, cross_pieces])
    owned = lax.all_to_all(all_pieces, AXES, 0, 0, tiled=True)
    natural = natural_rows(geo, table, owned.reshape(-1, LANES), pad_rows)
    gradient = natural[BLK : BLK + geo.chunk].reshape(-1)
    n_cls = n_doc * n_seg * seg_count
    scaling, rating = (
        jnp.broadcast_to(
            lax.dynamic_index_in_dim(jnp.asarray(rates), me, 0, False)[:, None], (geo.chunk, LANES)
        ).reshape(-1)
        for rates in row_rates(geo, n_cls * SEG_LEN, n_cls)
    )
    weight, moment, smooth, copy_low = optimizer_step(
        gradient, master, momentum, average, scaling, rating
    )
    return (
        mixed_out.reshape(1, seg_count, SEG_LEN, D),
        token_grad.reshape(1, seg_count, SEG_LEN, D),
        weight,
        moment,
        smooth,
        copy_low,
    )


def solution(mesh):
    layer = P("doc", "seg", None, None)
    ids = P("doc", "seg")
    flat = P(("seg", "doc"))
    return jax.shard_map(
        local,
        mesh=mesh,
        in_specs=(layer, layer, ids, ids, flat, flat, flat),
        out_specs=(layer, layer, flat, flat, flat, flat),
        check_vma=False,
    )
```

time: 2390 us -> 1010 us (0.42); the launches traced: 2360 us -> 1000 us
  waiting for transfers between devices: 1050 us -> 328 us
  local copies, waits for them, and re-layouts: 705 us -> 75 us
  other arithmetic: 238 us -> 87.2 us
  Pallas kernels: 0 us -> 103 us
  starting transfers between devices: 0.08 us -> 68.3 us
    unnamed x3 -> x0, waiting for transfers between devices: 771 us -> none
    unnamed x290 -> x220, local copies, waits for them, and re-layouts: 522 us -> 28.9 us
    ppermute x0 -> x54, waiting for transfers between devices: none -> 319 us  [send(): return lax.ppermute(value, AXES, geo.shift(axis, step))]
    all_gather x1 -> x0, waiting for transfers between devices: 275 us -> none  [local(): flat_low = lax.all_gather(master_low, ('seg', 'doc'), axis=0, tiled=True)]
    all_gather x1 -> x0, other arithmetic: 169 us -> none  [local(): flat_low = lax.all_gather(master_low, ('seg', 'doc'), axis=0, tiled=True)]
    pallas_call x0 -> x15, Pallas kernels: none -> 103 us  [the longest x8 56.4 us: unpack_matrix(): pl.pallas_call(kernel, out_shape=jax.ShapeDtypeStruct((depth, cols), jnp....]
    reshape x19 -> x0, local copies, waits for them, and re-layouts: 101 us -> none  [the longest x9 52.4 us: unpack(): params[entry_name] = flat_vec[offset:offset + length].reshape(entry_shape)]
    ppermute x0 -> x54, starting transfers between devices: none -> 65.6 us  [send(): return lax.ppermute(value, AXES, geo.shift(axis, step))]
  transfers between devices with their start and end apart: 2 -> 55, of which waited for: 2 -> 25; matrix products, arithmetic and copies ran while one was open for 1% -> 8% of each run, Pallas kernels for 0% -> 6%
where the time goes in v1:
time: 1010 us; the launch traced here: 1000 us
  waiting for transfers between devices  328 us (32%)
  matrix products  291 us (29%)
  Pallas kernels  103 us (10%)
  other arithmetic  87.2 us (9%)
  local copies, waits for them, and re-layouts  75 us (7%)
  starting transfers between devices  68.3 us (7%)
  blocking collectives  48.7 us (5%)
    ppermute x54, waiting for transfers between devices, send(): return lax.ppermute(value, AXES, geo.shift(axis, step))  319 us
    dot_general x26, matrix products, matmul(): return jnp.dot(left, right, preferred_element_type=jnp.float32)  251 us
    ppermute x54, starting transfers between devices, send(): return lax.ppermute(value, AXES, geo.shift(axis, step))  65.6 us
    pallas_call x8, Pallas kernels, unpack_matrix(): pl.pallas_call(kernel, out_shape=jax.ShapeDtypeStruct((depth, cols), jnp....  56.4 us
    pallas_call x3, Pallas kernels, pack_bucket(): pl.pallas_call(kernel, out_shape=[jax.ShapeDtypeStruct(shape, jnp.bfloat1...  34.3 us
    all_to_all x1, blocking collectives, local(): lax.all_to_all(aligned.reshape(geo.n_dev, geo.piece, LANES), AXES, 0, 0,...  29.6 us
    unnamed x220, local copies, waits for them, and re-layouts  28.9 us
    reduce_sum x11, other arithmetic, column_sum(): return jnp.sum(rows.astype(jnp.float32), axis=0)  22.4 us
  transfers between devices with their start and end apart: 55, of which 25 were waited for; matrix products, arithmetic and copies ran while one was open for 8% of the time, Pallas kernels for 6%

profile of v1, /device:TPU:0, one launch (start us, length us, event | category | flops | bytes accessed | tf_op | source)
XLA Modules:
  0.0 1004.5 jit_solution(15204879430612349074)
XLA Ops:
  8.2 29.6 %all_to_all.10 = bf16[32,112,128]{2,1,0:T(8,128)(2,1)S(1)} all-to-all(bf16[32,112,128]{2,1,0:T(8,128)(2,1)} %bitcast.496), channel_id=1, replica_groups=mesh['seg'=8,'doc'=4] {'seg','doc'}, dimensions={0} | all-to-all | bytes 1835008 | tf_op jit(solution)/shard_map/all_to_all | solution.py:718
  50.2 20.4 %collective-permute-done.1 = bf16[6,112,128]{2,1,0:T(8,128)(2,1)S(1)} collective-permute-done((bf16[6,112,128]{2,1,0:T(8,128)(2,1)S(1)}, bf16[6,112,128]{2,1,0:T(8,128)(2,1)S(1)}, u32[]{:S(2)}, u32[]{:S(2)}) %collective-permute-start.1) | collective-permute-done | bytes 172064 | tf_op jit(solution)/shard_map/ppermute | solution.py:533
  74.6 16.5 %collective-permute-done.9 = bf16[10,112,128]{2,1,0:T(8,128)(2,1)S(1)} collective-permute-done((bf16[10,112,128]{2,1,0:T(8,128)(2,1)S(1)}, bf16[10,112,128]{2,1,0:T(8,128)(2,1)S(1)}, u32[]{:S(2)}, u32[]{:S(2)}) %collective-permute-start.9) | collective-permute-done | bytes 286752 | tf_op jit(solution)/shard_map/ppermute | solution.py:533
  98.0 22.7 %collective-permute-done.19 = bf16[16,112,128]{2,1,0:T(8,128)(2,1)S(1)} collective-permute-done((bf16[16,112,128]{2,1,0:T(8,128)(2,1)S(1)}, bf16[16,112,128]{2,1,0:T(8,128)(2,1)S(1)}, u32[]{:S(2)}, u32[]{:S(2)}) %collective-permute-start.19) | collective-permute-done | bytes 458784 | tf_op jit(solution)/shard_map/ppermute | solution.py:533
  123.9 19.8 %collective-permute-done.24 = bf16[8,448,128]{2,1,0:T(8,128)(2,1)S(1)} collective-permute-done((bf16[8,448,128]{2,1,0:T(8,128)(2,1)S(1)}, bf16[8,448,128]{2,1,0:T(8,128)(2,1)S(1)}, u32[]{:S(2)}, u32[]{:S(2)}) %collective-permute-start.24) | collective-permute-done | bytes 917536 | tf_op jit(solution)/shard_map/ppermute | solution.py:533
  150.5 49.5 %collective-permute-done.15 = bf16[5,448,128]{2,1,0:T(8,128)(2,1)S(1)} collective-permute-done((bf16[5,448,128]{2,1,0:T(8,128)(2,1)S(1)}, bf16[5,448,128]{2,1,0:T(8,128)(2,1)S(1)}, u32[]{:S(2)}, u32[]{:S(2)}) %collective-permute-start.15) | collective-permute-done | bytes 573472 | tf_op jit(solution)/shard_map/ppermute | solution.py:533
  212.5 23.3 %collective-permute-done.3 = bf16[3,448,128]{2,1,0:T(8,128)(2,1)S(1)} collective-permute-done((bf16[3,448,128]{2,1,0:T(8,128)(2,1)S(1)}, bf16[3,448,128]{2,1,0:T(8,128)(2,1)S(1)}, u32[]{:S(2)}, u32[]{:S(2)}) %collective-permute-start.3) | collective-permute-done | bytes 344096 | tf_op jit(solution)/shard_map/ppermute | solution.py:533
  264.9 9.8 all_gather.7
  320.4 10.9 %fusion.7 = bf16[2048,2304]{0,1:T(8,128)(2,1)S(1)} fusion(bf16[768,2304]{1,0:T(8,128)(2,1)S(1)} %copy-done.31, bf16[2048,768]{1,0:T(8,128)(2,1)} %bitcast.555, f32[2304]{0:T(1024)S(1)} %get-tuple-element.121), kind=kOutput, calls=%fused_computation.25 | convolution fusion | flops 7257194496 | bytes 16131072 | tf_op jit(solution)/shard_map/dot_general | solution.py:633
  365.5 68.9 %multiply_convert_fusion = (bf16[2048,3072]{1,0:T(8,128)(2,1)}, f32[2048,3072]{1,0:T(8,128)}, f32[2048,3072]{1,0:T(8,128)}) fusion(f32[3072]{0:T(1024)S(1)} %slice_bitcast_fusion.29, bf16[768,3072]{1,0:T(8,128)(2,1)S(1)} %bitcast.490, f32[2048,768]{1,0:T(8,128)S(1)} %get-tuple-element.125, f32[768]{0:T(1024)S(1)} %get-tuple-element.111, ...), kind=kOutput, calls=%fused_computation.3 | convolution fusion | flops 10086776832 | bytes 73959424 | tf_op jit(solution)/shard_map/dot_general | solution.py:633
  434.4 13.9 %fusion.163 = (f32[2048]{0:T(1024)S(1)}, f32[2048,768]{1,0:T(8,128)S(1)}) fusion(f32[768]{0:T(1024)S(1)} %copy-done.81, f32[768]{0:T(1024)S(1)} %get-tuple-element.111, f32[768]{0:T(1024)S(1)} %get-tuple-element.112, f32[2048]{0:T(1024)S(1)} %add_rsqrt_fusion.1, f32[2048,768]{1,0:T(8,128)S(1)} %get-tuple-element.125, ...), kind=kOutput, calls=%fused_computation.423 | convolution fusion | flops 9674684416 | bytes 29918208 | tf_op jit(solution)/shard_map/dot_general | solution.py:633
  454.8 9.2 all_gather.6
  481.2 9.0 shard_map.154
  546.0 17.0 %convolution_convert_fusion.refs_2_ = bf16[3072,768]{1,0:T(8,128)(2,1)} fusion(bf16[2048,3072]{1,0:T(8,128)(2,1)} %get-tuple-element.62, f32[2048,768]{1,0:T(8,128)S(1)} %get-tuple-element.50), kind=kOutput, calls=%fused_computation.57 | convolution fusion | flops 9667608576 | bytes 23592960 | tf_op jit(solution)/shard_map/dot_general | solution.py:633
  563.1 29.2 %fusion.170 = (bf16[3072]{0:T(1024)(128)(2,1)}, bf16[2048,3072]{1,0:T(8,128)(2,1)}) fusion(f32[2048,3072]{1,0:T(8,128)} %get-tuple-element.63, bf16[3072,768]{1,0:T(8,128)(2,1)S(1)} %bitcast.492, f32[2048,768]{1,0:T(8,128)} %copy-done.21, f32[2048,3072]{1,0:T(8,128)} %get-tuple-element.126, f32[3072]{0:T(1024)S(1)} %slice_bitcast_fusion.29), kind=kOutput, calls=%fused_computation.429 | convolution fusion | flops 9765909504 | bytes 73943040 | tf_op jit(solution)/shard_map/dot_general | solution.py:633
  592.2 20.7 %multiply_reduce_fusion.2 = (bf16[768]{0:T(1024)(128)(2,1)S(1)}, f32[2048]{0:T(1024)S(1)}, f32[2048]{0:T(1024)S(1)}, bf16[768]{0:T(1024)(128)(2,1)S(1)}, f32[2048,768]{1,0:T(8,128)}) fusion(f32[2048,768]{1,0:T(8,128)} %copy-done.9, f32[2048]{0:T(1024)S(1)} %add_rsqrt_fusion.1, f32[2048]{0:T(1024)S(1)} %broadcast_multiply_fusion.4, ...), kind=kOutput, calls=%fused_computation.35 | convolution fusion | flops 9679398912 | bytes 36214784 | tf_op jit(solution)/shard_map/dot_general | solution.py:633
  612.9 18.0 %convolution_convert_fusion.1.refs_4_.refs_0_ = bf16[768,3072]{1,0:T(8,128)(2,1)} fusion(bf16[2048,3072]{1,0:T(8,128)(2,1)} %get-tuple-element.141, f32[2048,768]{1,0:T(8,128)} %copy-done.9, f32[768]{0:T(1024)S(1)} %copy-done.80, f32[768]{0:T(1024)S(1)} %get-tuple-element.112, f32[2048]{0:T(1024)S(1)} %add_rsqrt_fusion.1, f32[2048]{0:T(1024)S(1)} %broadcast_multiply_fusion.4), kind=kOutput, calls=%fused_computation.58 | convolution fusion | flops 9673900032 | bytes 23615488 | tf_op jit(solution)/shard_map/dot_general | solution.py:633
  645.7 9.0 convert_bitcast_fusion
  654.6 10.5 %multiply_reduce_fusion = (f32[16,12,128]{2,1,0:T(8,128)S(1)}, f32[16,12,128,128]{2,3,1,0:T(8,128)}) fusion(f32[16,12,128,128]{2,3,1,0:T(8,128)} %copy-done, f32[16,12,128]{2,1,0:T(8,128)S(1)} %copy-done.36, bf16[16,128,12,64]{1,0,3,2:T(8,128)(2,1)} %bitcast.484, bf16[16,128,12,64]{1,0,3,2:T(8,128)(2,1)S(1)} %bitcast.468), kind=kOutput, calls=%fused_computation.19 | convolution fusion | flops 415211520 | bytes 31653888 | tf_op jit(solution)/shard_map/bqhd,bkhd->bhqk/dot_general | solution.py:667
  665.1 10.3 %multiply_convert_fusion.1 = bf16[16,12,128,128]{2,3,1,0:T(8,128)(2,1)S(1)} fusion(f32[16,12,128,128]{2,3,1,0:T(8,128)} %get-tuple-element.139, f32[16,12,128,128]{2,3,1,0:T(8,128)} %copy-done, f32[16,12,128]{2,1,0:T(8,128)S(1)} %get-tuple-element.138, f32[16,12,128]{2,1,0:T(8,128)S(1)} %copy-done.36), kind=kLoop, calls=%fused_computation.18 | loop fusion | flops 15728640 | bytes 31653888 | tf_op jit(solution)/shard_map/convert_element_type | solution.py:677
  698.8 9.5 fusion.16.refs_0_
  743.0 15.2 %shard_map.158 = (bf16[2,2,8,448,128]{4,3,2,1,0:T(8,128)(2,1)}, bf16[2,2,8,448,128]{4,3,2,1,0:T(8,128)(2,1)}, bf16[2,2,8,448,128]{4,3,2,1,0:T(8,128)(2,1)}, bf16[2,2,8,448,128]{4,3,2,1,0:T(8,128)(2,1)}) custom-call(s32[4]{0:T(128)} %pad_add_fusion.coords_ref, bf16[384,128]{1,0:T(8,128)(2,1)} %convert_element_type.562.refs_4_.refs_0_, ...), custom_call_target="tpu_custom_call" | custom-call | tf_op jit(solution)/shard_map/pallas_call | solution.py:513
  759.8 11.6 %shard_map.157 = (bf16[2,2,5,448,128]{4,3,2,1,0:T(8,128)(2,1)}, bf16[2,2,5,448,128]{4,3,2,1,0:T(8,128)(2,1)}, bf16[2,2,5,448,128]{4,3,2,1,0:T(8,128)(2,1)}, bf16[2,2,5,448,128]{4,3,2,1,0:T(8,128)(2,1)}) custom-call(s32[4]{0:T(128)} %pad_add_fusion.coords_ref, bf16[768,3072]{1,0:T(8,128)(2,1)} %convolution_convert_fusion.1.refs_4_.refs_0_, ...), custom_call_target="tpu_custom_call" | custom-call | tf_op jit(solution)/shard_map/pallas_call | solution.py:513
  778.0 12.0 %collective-permute-done.28 = bf16[2,3,448,128]{3,2,1,0:T(8,128)(2,1)S(1)} collective-permute-done((bf16[2,3,448,128]{3,2,1,0:T(8,128)(2,1)S(1)}, bf16[2,3,448,128]{3,2,1,0:T(8,128)(2,1)S(1)}, u32[]{:S(2)}, u32[]{:S(2)}) %collective-permute-start.28) | collective-permute-done | bytes 688160 | tf_op jit(solution)/shard_map/ppermute | solution.py:533
  811.1 17.2 %collective-permute-done.37 = bf16[2,5,448,128]{3,2,1,0:T(8,128)(2,1)} collective-permute-done((bf16[2,5,448,128]{3,2,1,0:T(8,128)(2,1)}, bf16[2,5,448,128]{3,2,1,0:T(8,128)(2,1)}, u32[]{:S(2)}, u32[]{:S(2)}) %collective-permute-start.37) | collective-permute-done | bytes 1146912 | tf_op jit(solution)/shard_map/ppermute | solution.py:533
  836.8 28.5 %collective-permute-done.46 = bf16[2,8,448,128]{3,2,1,0:T(8,128)(2,1)S(1)} collective-permute-done((bf16[2,8,448,128]{3,2,1,0:T(8,128)(2,1)S(1)}, bf16[2,8,448,128]{3,2,1,0:T(8,128)(2,1)S(1)}, u32[]{:S(2)}, u32[]{:S(2)}) %collective-permute-start.46) | collective-permute-done | bytes 1835040 | tf_op jit(solution)/shard_map/ppermute | solution.py:533
  869.7 11.2 %collective-permute-done.38 = bf16[5,448,128]{2,1,0:T(8,128)(2,1)S(1)} collective-permute-done((bf16[5,448,128]{2,1,0:T(8,128)(2,1)S(1)}, bf16[5,448,128]{2,1,0:T(8,128)(2,1)S(1)}, u32[]{:S(2)}, u32[]{:S(2)}) %collective-permute-start.38) | collective-permute-done | bytes 573472 | tf_op jit(solution)/shard_map/ppermute | solution.py:533
  882.0 16.7 %collective-permute-done.47 = bf16[8,448,128]{2,1,0:T(8,128)(2,1)S(1)} collective-permute-done((bf16[8,448,128]{2,1,0:T(8,128)(2,1)S(1)}, bf16[8,448,128]{2,1,0:T(8,128)(2,1)S(1)}, u32[]{:S(2)}, u32[]{:S(2)}) %collective-permute-start.47) | collective-permute-done | bytes 917536 | tf_op jit(solution)/shard_map/ppermute | solution.py:533
  919.5 17.6 %collective-permute-done.43 = bf16[10,112,128]{2,1,0:T(8,128)(2,1)S(1)} collective-permute-done((bf16[10,112,128]{2,1,0:T(8,128)(2,1)S(1)}, bf16[10,112,128]{2,1,0:T(8,128)(2,1)S(1)}, u32[]{:S(2)}, u32[]{:S(2)}) %collective-permute-start.43) | collective-permute-done | bytes 286752 | tf_op jit(solution)/shard_map/ppermute | solution.py:533
  939.9 26.6 %collective-permute-done.52 = bf16[16,112,128]{2,1,0:T(8,128)(2,1)S(1)} collective-permute-done((bf16[16,112,128]{2,1,0:T(8,128)(2,1)S(1)}, bf16[16,112,128]{2,1,0:T(8,128)(2,1)S(1)}, u32[]{:S(2)}, u32[]{:S(2)}) %collective-permute-start.52) | collective-permute-done | bytes 458784 | tf_op jit(solution)/shard_map/ppermute | solution.py:533
  970.5 13.3 %add_convert_fusion.4 = bf16[2048,768]{1,0:T(8,128)(2,1)} fusion(f32[2048,768]{1,0:T(8,128)} %copy-done.20, bf16[2048,2304]{0,1:T(8,128)(2,1)} %copy-done.12, bf16[768,2304]{1,0:T(8,128)(2,1)} %shard_map.146), kind=kOutput, calls=%fused_computation.36 | convolution fusion | flops 7250903040 | bytes 22413312 | tf_op jit(solution)/shard_map/dot_general | solution.py:633
  983.7 9.0 all-to-all-done.1
  (520 shorter events, 395.0 us)
Async XLA Ops:
  42.4 81.4 %collective-permute-start.11 = (bf16[10,112,128]{2,1,0:T(8,128)(2,1)S(1)}, bf16[10,112,128]{2,1,0:T(8,128)(2,1)S(1)}, u32[]{:S(2)}, u32[]{:S(2)}) collective-permute-start(bf16[10,112,128]{2,1,0:T(8,128)(2,1)S(1)} %slice.379), channel_id=1, source_target_pairs={{0,1},{1,2},{2,3},{3,0},{4,5},{5,6},{6,7},{7,4},{8,9},{9,10},{10,1... | collective-permute-start | bytes 860168 | tf_op jit(solution)/shard_map/ppermute | solution.py:533
  45.5 78.2 %collective-permute-start.10 = (bf16[10,112,128]{2,1,0:T(8,128)(2,1)S(1)}, bf16[10,112,128]{2,1,0:T(8,128)(2,1)S(1)}, u32[]{:S(2)}, u32[]{:S(2)}) collective-permute-start(bf16[10,112,128]{2,1,0:T(8,128)(2,1)S(1)} %slice.379), channel_id=1, source_target_pairs={{0,2},{1,3},{2,0},{3,1},{4,6},{5,7},{6,4},{7,5},{8,10},{9,11},{10,... | collective-permute-start | bytes 860168 | tf_op jit(solution)/shard_map/ppermute | solution.py:533
  50.2 40.9 %collective-permute-start.9 = (bf16[10,112,128]{2,1,0:T(8,128)(2,1)S(1)}, bf16[10,112,128]{2,1,0:T(8,128)(2,1)S(1)}, u32[]{:S(2)}, u32[]{:S(2)}) collective-permute-start(bf16[10,112,128]{2,1,0:T(8,128)(2,1)S(1)} %slice.379), channel_id=1, source_target_pairs={{0,3},{1,0},{2,1},{3,2},{4,7},{5,4},{6,5},{7,6},{8,11},{9,8},{10,9... | collective-permute-start | bytes 860168 | tf_op jit(solution)/shard_map/ppermute | solution.py:533
  70.6 50.2 %collective-permute-start.20 = (bf16[16,112,128]{2,1,0:T(8,128)(2,1)S(1)}, bf16[16,112,128]{2,1,0:T(8,128)(2,1)S(1)}, u32[]{:S(2)}, u32[]{:S(2)}) collective-permute-start(bf16[16,112,128]{2,1,0:T(8,128)(2,1)S(1)} %slice.393), channel_id=1, source_target_pairs={{0,1},{1,2},{2,3},{3,0},{4,5},{5,6},{6,7},{7,4},{8,9},{9,10},{10,1... | collective-permute-start | bytes 1376264 | tf_op jit(solution)/shard_map/ppermute | solution.py:533
  144.0 62.6 %collective-permute-start.25 = (bf16[2,8,448,128]{3,2,1,0:T(8,128)(2,1)S(1)}, bf16[2,8,448,128]{3,2,1,0:T(8,128)(2,1)S(1)}, u32[]{:S(2)}, u32[]{:S(2)}) collective-permute-start(bf16[2,8,448,128]{3,2,1,0:T(8,128)(2,1)S(1)} %get-tuple-element.77), channel_id=1, source_target_pairs={{0,8},{1,9},{2,10},{3,11},{4,12},{5,13},{6,14},{7,15},{8,0},{9,1},... | collective-permute-start | bytes 5505032 | tf_op jit(solution)/shard_map/ppermute | solution.py:533
  144.6 65.7 %collective-permute-start.22 = (bf16[2,8,448,128]{3,2,1,0:T(8,128)(2,1)S(1)}, bf16[2,8,448,128]{3,2,1,0:T(8,128)(2,1)S(1)}, u32[]{:S(2)}, u32[]{:S(2)}) collective-permute-start(bf16[2,8,448,128]{3,2,1,0:T(8,128)(2,1)S(1)} %get-tuple-element.79), channel_id=1, source_target_pairs={{0,16},{1,17},{2,18},{3,19},{4,20},{5,21},{6,22},{7,23},{8,24},{9,... | collective-permute-start | bytes 5505032 | tf_op jit(solution)/shard_map/ppermute | solution.py:533
  146.6 53.4 %collective-permute-start.15 = (bf16[5,448,128]{2,1,0:T(8,128)(2,1)S(1)}, bf16[5,448,128]{2,1,0:T(8,128)(2,1)S(1)}, u32[]{:S(2)}, u32[]{:S(2)}) collective-permute-start(bf16[5,448,128]{2,1,0:T(8,128)(2,1)S(1)} %bitcast.507), channel_id=1, source_target_pairs={{0,16},{1,17},{2,18},{3,19},{4,20},{5,21},{6,22},{7,23},{8,24},{9,... | collective-permute-start | bytes 1720328 | tf_op jit(solution)/shard_map/ppermute | solution.py:533
  147.1 58.9 %collective-permute-start.12 = (bf16[5,448,128]{2,1,0:T(8,128)(2,1)S(1)}, bf16[5,448,128]{2,1,0:T(8,128)(2,1)S(1)}, u32[]{:S(2)}, u32[]{:S(2)}) collective-permute-start(bf16[5,448,128]{2,1,0:T(8,128)(2,1)S(1)} %bitcast.505), channel_id=1, source_target_pairs={{0,8},{1,9},{2,10},{3,11},{4,12},{5,13},{6,14},{7,15},{8,0},{9,1},... | collective-permute-start | bytes 1720328 | tf_op jit(solution)/shard_map/ppermute | solution.py:533
  149.0 55.3 %collective-permute-start.6 = (bf16[3,448,128]{2,1,0:T(8,128)(2,1)S(1)}, bf16[3,448,128]{2,1,0:T(8,128)(2,1)S(1)}, u32[]{:S(2)}, u32[]{:S(2)}) collective-permute-start(bf16[3,448,128]{2,1,0:T(8,128)(2,1)S(1)} %bitcast.519), channel_id=1, source_target_pairs={{0,16},{1,17},{2,18},{3,19},{4,20},{5,21},{6,22},{7,23},{8,24},{9,... | collective-permute-start | bytes 1032200 | tf_op jit(solution)/shard_map/ppermute | solution.py:533
  200.1 46.0 %collective-permute-start.16 = (bf16[2,5,448,128]{3,2,1,0:T(8,128)(2,1)S(1)}, bf16[2,5,448,128]{3,2,1,0:T(8,128)(2,1)S(1)}, u32[]{:S(2)}, u32[]{:S(2)}) collective-permute-start(bf16[2,5,448,128]{3,2,1,0:T(8,128)(2,1)S(1)} %get-tuple-element.86), channel_id=1, source_target_pairs={{0,8},{1,9},{2,10},{3,11},{4,12},{5,13},{6,14},{7,15},{8,0},{9,1},... | collective-permute-start | bytes 3440648 | tf_op jit(solution)/shard_map/ppermute | solution.py:533
  204.2 31.5 %collective-permute-start.3 = (bf16[3,448,128]{2,1,0:T(8,128)(2,1)S(1)}, bf16[3,448,128]{2,1,0:T(8,128)(2,1)S(1)}, u32[]{:S(2)}, u32[]{:S(2)}) collective-permute-start(bf16[3,448,128]{2,1,0:T(8,128)(2,1)S(1)} %bitcast.517), channel_id=1, source_target_pairs={{0,8},{1,9},{2,10},{3,11},{4,12},{5,13},{6,14},{7,15},{8,0},{9,1},... | collective-permute-start | bytes 1032200 | tf_op jit(solution)/shard_map/ppermute | solution.py:533
  206.1 37.4 %collective-permute-start.7 = (bf16[2,3,448,128]{3,2,1,0:T(8,128)(2,1)S(1)}, bf16[2,3,448,128]{3,2,1,0:T(8,128)(2,1)S(1)}, u32[]{:S(2)}, u32[]{:S(2)}) collective-permute-start(bf16[2,3,448,128]{3,2,1,0:T(8,128)(2,1)S(1)} %get-tuple-element.93), channel_id=1, source_target_pairs={{0,8},{1,9},{2,10},{3,11},{4,12},{5,13},{6,14},{7,15},{8,0},{9,1},... | collective-permute-start | bytes 2064392 | tf_op jit(solution)/shard_map/ppermute | solution.py:533
  206.6 39.8 %collective-permute-start.13 = (bf16[2,5,448,128]{3,2,1,0:T(8,128)(2,1)S(1)}, bf16[2,5,448,128]{3,2,1,0:T(8,128)(2,1)S(1)}, u32[]{:S(2)}, u32[]{:S(2)}) collective-permute-start(bf16[2,5,448,128]{3,2,1,0:T(8,128)(2,1)S(1)} %get-tuple-element.88), channel_id=1, source_target_pairs={{0,16},{1,17},{2,18},{3,19},{4,20},{5,21},{6,22},{7,23},{8,24},{9,... | collective-permute-start | bytes 3440648 | tf_op jit(solution)/shard_map/ppermute | solution.py:533
  210.3 102.5 %collective-permute-start.26 = (bf16[2,2,8,448,128]{4,3,2,1,0:T(8,128)(2,1)}, bf16[2,2,8,448,128]{4,3,2,1,0:T(8,128)(2,1)}, u32[]{:S(2)}, u32[]{:S(2)}) collective-permute-start(bf16[2,2,8,448,128]{4,3,2,1,0:T(8,128)(2,1)} %pad_maximum_fusion.2.refs_6_.refs_2_), channel_id=1, source_target_pairs={{0,4},{1,5},{2,6},{3,7},{4,0},{5,1},{6,2},{7,3},{8,12},{9,13},{10,... | collective-permute-start | bytes 11010056 | tf_op jit(solution)/shard_map/ppermute | solution.py:533
  235.8 77.1 %collective-permute-start.23 = (bf16[2,2,8,448,128]{4,3,2,1,0:T(8,128)(2,1)}, bf16[2,2,8,448,128]{4,3,2,1,0:T(8,128)(2,1)}, u32[]{:S(2)}, u32[]{:S(2)}) collective-permute-start(bf16[2,2,8,448,128]{4,3,2,1,0:T(8,128)(2,1)} %pad_maximum_fusion.1.refs_4_.refs_0_), channel_id=1, source_target_pairs={{0,4},{1,5},{2,6},{3,7},{4,0},{5,1},{6,2},{7,3},{8,12},{9,13},{10,... | collective-permute-start | bytes 11010056 | tf_op jit(solution)/shard_map/ppermute | solution.py:533
  246.4 46.3 %collective-permute-start.17 = (bf16[2,2,5,448,128]{4,3,2,1,0:T(8,128)(2,1)S(1)}, bf16[2,2,5,448,128]{4,3,2,1,0:T(8,128)(2,1)}, u32[]{:S(2)}, u32[]{:S(2)}) collective-permute-start(bf16[2,2,5,448,128]{4,3,2,1,0:T(8,128)(2,1)S(1)} %pad_maximum_fusion.4.refs_6_.refs_2_), channel_id=1, source_target_pairs={{0,4},{1,5},{2,6},{3,7},{4,0},{5,1},{6,2},{7,3},{8,12},{9,13},{10,... | collective-permute-start | bytes 6881288 | tf_op jit(solution)/shard_map/ppermute | solution.py:533
  254.5 38.2 %collective-permute-start.14 = (bf16[2,2,5,448,128]{4,3,2,1,0:T(8,128)(2,1)}, bf16[2,2,5,448,128]{4,3,2,1,0:T(8,128)(2,1)}, u32[]{:S(2)}, u32[]{:S(2)}) collective-permute-start(bf16[2,2,5,448,128]{4,3,2,1,0:T(8,128)(2,1)} %pad_maximum_fusion.3.refs_4_.refs_0_), channel_id=1, source_target_pairs={{0,4},{1,5},{2,6},{3,7},{4,0},{5,1},{6,2},{7,3},{8,12},{9,13},{10,... | collective-permute-start | bytes 6881288 | tf_op jit(solution)/shard_map/ppermute | solution.py:533
  723.2 48.9 %collective-permute-start.27 = (bf16[2,2,3,448,128]{4,3,2,1,0:T(8,128)(2,1)}, bf16[2,2,3,448,128]{4,3,2,1,0:T(8,128)(2,1)S(1)}, u32[]{:S(2)}, u32[]{:S(2)}) collective-permute-start(bf16[2,2,3,448,128]{4,3,2,1,0:T(8,128)(2,1)} %get-tuple-element.19), channel_id=1, source_target_pairs={{0,4},{1,5},{2,6},{3,7},{4,0},{5,1},{6,2},{7,3},{8,12},{9,13},{10,... | collective-permute-start | bytes 4128776 | tf_op jit(solution)/shard_map/ppermute | solution.py:533
  723.6 49.5 %collective-permute-start.30 = (bf16[2,2,3,448,128]{4,3,2,1,0:T(8,128)(2,1)}, bf16[2,2,3,448,128]{4,3,2,1,0:T(8,128)(2,1)S(1)}, u32[]{:S(2)}, u32[]{:S(2)}) collective-permute-start(bf16[2,2,3,448,128]{4,3,2,1,0:T(8,128)(2,1)} %get-tuple-element.21), channel_id=1, source_target_pairs={{0,4},{1,5},{2,6},{3,7},{4,0},{5,1},{6,2},{7,3},{8,12},{9,13},{10,... | collective-permute-start | bytes 4128776 | tf_op jit(solution)/shard_map/ppermute | solution.py:533
  758.2 45.6 %collective-permute-start.45 = (bf16[2,2,8,448,128]{4,3,2,1,0:T(8,128)(2,1)}, bf16[2,2,8,448,128]{4,3,2,1,0:T(8,128)(2,1)S(1)}, u32[]{:S(2)}, u32[]{:S(2)}) collective-permute-start(bf16[2,2,8,448,128]{4,3,2,1,0:T(8,128)(2,1)} %get-tuple-element.27), channel_id=1, source_target_pairs={{0,4},{1,5},{2,6},{3,7},{4,0},{5,1},{6,2},{7,3},{8,12},{9,13},{10,... | collective-permute-start | bytes 11010056 | tf_op jit(solution)/shard_map/ppermute | solution.py:533
  794.9 33.4 %collective-permute-start.37 = (bf16[2,5,448,128]{3,2,1,0:T(8,128)(2,1)}, bf16[2,5,448,128]{3,2,1,0:T(8,128)(2,1)}, u32[]{:S(2)}, u32[]{:S(2)}) collective-permute-start(bf16[2,5,448,128]{3,2,1,0:T(8,128)(2,1)} %slice_bitcast_fusion.9), channel_id=1, source_target_pairs={{0,16},{1,17},{2,18},{3,19},{4,20},{5,21},{6,22},{7,23},{8,24},{9,... | collective-permute-start | bytes 3440648 | tf_op jit(solution)/shard_map/ppermute | solution.py:533
  800.8 33.8 %collective-permute-start.40 = (bf16[2,5,448,128]{3,2,1,0:T(8,128)(2,1)}, bf16[2,5,448,128]{3,2,1,0:T(8,128)(2,1)}, u32[]{:S(2)}, u32[]{:S(2)}) collective-permute-start(bf16[2,5,448,128]{3,2,1,0:T(8,128)(2,1)} %slice_bitcast_fusion.7), channel_id=1, source_target_pairs={{0,8},{1,9},{2,10},{3,11},{4,12},{5,13},{6,14},{7,15},{8,0},{9,1},... | collective-permute-start | bytes 3440648 | tf_op jit(solution)/shard_map/ppermute | solution.py:533
  805.2 60.0 %collective-permute-start.46 = (bf16[2,8,448,128]{3,2,1,0:T(8,128)(2,1)S(1)}, bf16[2,8,448,128]{3,2,1,0:T(8,128)(2,1)S(1)}, u32[]{:S(2)}, u32[]{:S(2)}) collective-permute-start(bf16[2,8,448,128]{3,2,1,0:T(8,128)(2,1)S(1)} %slice_bitcast_fusion.5), channel_id=1, source_target_pairs={{0,16},{1,17},{2,18},{3,19},{4,20},{5,21},{6,22},{7,23},{8,24},{9,... | collective-permute-start | bytes 5505032 | tf_op jit(solution)/shard_map/ppermute | solution.py:533
  808.6 60.0 %collective-permute-start.49 = (bf16[2,8,448,128]{3,2,1,0:T(8,128)(2,1)S(1)}, bf16[2,8,448,128]{3,2,1,0:T(8,128)(2,1)S(1)}, u32[]{:S(2)}, u32[]{:S(2)}) collective-permute-start(bf16[2,8,448,128]{3,2,1,0:T(8,128)(2,1)S(1)} %slice_bitcast_fusion.3), channel_id=1, source_target_pairs={{0,8},{1,9},{2,10},{3,11},{4,12},{5,13},{6,14},{7,15},{8,0},{9,1},... | collective-permute-start | bytes 5505032 | tf_op jit(solution)/shard_map/ppermute | solution.py:533
  809.2 95.7 %collective-permute-start.33 = (bf16[6,112,128]{2,1,0:T(8,128)(2,1)S(1)}, bf16[6,112,128]{2,1,0:T(8,128)(2,1)S(1)}, u32[]{:S(2)}, u32[]{:S(2)}) collective-permute-start(bf16[6,112,128]{2,1,0:T(8,128)(2,1)S(1)} %get-tuple-element.89), channel_id=1, source_target_pairs={{0,1},{1,2},{2,3},{3,0},{4,5},{5,6},{6,7},{7,4},{8,9},{9,10},{10,1... | collective-permute-start | bytes 516104 | tf_op jit(solution)/shard_map/ppermute | solution.py:533
  828.3 76.8 %collective-permute-start.35 = (bf16[6,112,128]{2,1,0:T(8,128)(2,1)S(1)}, bf16[6,112,128]{2,1,0:T(8,128)(2,1)S(1)}, u32[]{:S(2)}, u32[]{:S(2)}) collective-permute-start(bf16[6,112,128]{2,1,0:T(8,128)(2,1)S(1)} %get-tuple-element.90), channel_id=1, source_target_pairs={{0,3},{1,0},{2,1},{3,2},{4,7},{5,4},{6,5},{7,6},{8,11},{9,8},{10,9... | collective-permute-start | bytes 516104 | tf_op jit(solution)/shard_map/ppermute | solution.py:533
  834.6 46.2 %collective-permute-start.38 = (bf16[5,448,128]{2,1,0:T(8,128)(2,1)S(1)}, bf16[5,448,128]{2,1,0:T(8,128)(2,1)S(1)}, u32[]{:S(2)}, u32[]{:S(2)}) collective-permute-start(bf16[5,448,128]{2,1,0:T(8,128)(2,1)S(1)} %slice_bitcast_fusion.21), channel_id=1, source_target_pairs={{0,8},{1,9},{2,10},{3,11},{4,12},{5,13},{6,14},{7,15},{8,0},{9,1},... | collective-permute-start | bytes 1720328 | tf_op jit(solution)/shard_map/ppermute | solution.py:533
  868.6 30.1 %collective-permute-start.47 = (bf16[8,448,128]{2,1,0:T(8,128)(2,1)S(1)}, bf16[8,448,128]{2,1,0:T(8,128)(2,1)S(1)}, u32[]{:S(2)}, u32[]{:S(2)}) collective-permute-start(bf16[8,448,128]{2,1,0:T(8,128)(2,1)S(1)} %slice_bitcast_fusion.13), channel_id=1, source_target_pairs={{0,8},{1,9},{2,10},{3,11},{4,12},{5,13},{6,14},{7,15},{8,0},{9,1},... | collective-permute-start | bytes 2752520 | tf_op jit(solution)/shard_map/ppermute | solution.py:533
  904.9 32.2 %collective-permute-start.43 = (bf16[10,112,128]{2,1,0:T(8,128)(2,1)S(1)}, bf16[10,112,128]{2,1,0:T(8,128)(2,1)S(1)}, u32[]{:S(2)}, u32[]{:S(2)}) collective-permute-start(bf16[10,112,128]{2,1,0:T(8,128)(2,1)S(1)} %get-tuple-element.84), channel_id=1, source_target_pairs={{0,2},{1,3},{2,0},{3,1},{4,6},{5,7},{6,4},{7,5},{8,10},{9,11},{10,... | collective-permute-start | bytes 860168 | tf_op jit(solution)/shard_map/ppermute | solution.py:533
  905.1 32.2 %collective-permute-start.51 = (bf16[16,112,128]{2,1,0:T(8,128)(2,1)S(1)}, bf16[16,112,128]{2,1,0:T(8,128)(2,1)S(1)}, u32[]{:S(2)}, u32[]{:S(2)}) collective-permute-start(bf16[16,112,128]{2,1,0:T(8,128)(2,1)S(1)} %get-tuple-element.73), channel_id=1, source_target_pairs={{0,1},{1,2},{2,3},{3,0},{4,5},{5,6},{6,7},{7,4},{8,9},{9,10},{10,1... | collective-permute-start | bytes 1376264 | tf_op jit(solution)/shard_map/ppermute | solution.py:533
  907.1 32.8 %collective-permute-start.53 = (bf16[16,112,128]{2,1,0:T(8,128)(2,1)S(1)}, bf16[16,112,128]{2,1,0:T(8,128)(2,1)S(1)}, u32[]{:S(2)}, u32[]{:S(2)}) collective-permute-start(bf16[16,112,128]{2,1,0:T(8,128)(2,1)S(1)} %get-tuple-element.74), channel_id=1, source_target_pairs={{0,3},{1,0},{2,1},{3,2},{4,7},{5,4},{6,5},{7,6},{8,11},{9,8},{10,9... | collective-permute-start | bytes 1376264 | tf_op jit(solution)/shard_map/ppermute | solution.py:533
  911.2 55.4 %collective-permute-start.52 = (bf16[16,112,128]{2,1,0:T(8,128)(2,1)S(1)}, bf16[16,112,128]{2,1,0:T(8,128)(2,1)S(1)}, u32[]{:S(2)}, u32[]{:S(2)}) collective-permute-start(bf16[16,112,128]{2,1,0:T(8,128)(2,1)S(1)} %get-tuple-element.75), channel_id=1, source_target_pairs={{0,2},{1,3},{2,0},{3,1},{4,6},{5,7},{6,4},{7,5},{8,10},{9,11},{10,... | collective-permute-start | bytes 1376264 | tf_op jit(solution)/shard_map/ppermute | solution.py:533
  (120 other events, 1545.7 us)

commit v2 on v1

v2 whole, which is shorter than its diff:
```python
import math
from types import SimpleNamespace

import jax
import jax.numpy as jnp
import numpy as np
from jax import lax
from jax.experimental import pallas as pl
from jax.experimental.pallas import tpu as pltpu
from jax.sharding import PartitionSpec as P

D = 768
HEADS = 12
HEAD_DIM = 64
FF = 3072
SEG_LEN = 128
LONG_SEGS = 64
EPSILON = 1e-05
NEGATIVE = -1e30

LAYOUT = dict(
    w_qkv=(D, 3 * D),
    b_qv=(2 * D,),
    w_out=(D, D),
    b_out=(D,),
    gain_one=(D,),
    bias_one=(D,),
    w_up=(D, FF),
    b_up=(FF,),
    w_down=(FF, D),
    b_down=(D,),
    gain_two=(D,),
    bias_two=(D,),
    pos_table=(LONG_SEGS, D),
    x_qkv=(D, 3 * D),
    x_bqv=(2 * D,),
    x_out=(D, D),
    x_bout=(D,),
    gain_three=(D,),
    bias_three=(D,),
    x_up=(D, FF),
    x_bup=(FF,),
    x_down=(FF, D),
    x_bdown=(D,),
    gain_four=(D,),
    bias_four=(D,),
)
LANES = 128
BLK = 16
Y, X, C, Z = range(4)


def ceil_to(value, step):
    return -(-value // step) * step


def item_list(total_rows):
    items = []
    nat = 0
    for name, shape in LAYOUT.items():
        rows = math.prod(shape) // LANES
        if len(shape) == 1 and items and len(items[-1].shape) == 1:
            items[-1].names.append(name)
            items[-1].rows += rows
        else:
            items.append(SimpleNamespace(name=name, names=[name], shape=shape, nat=nat, rows=rows))
        nat += rows
    items.append(SimpleNamespace(name=None, names=[], shape=None, nat=nat, rows=total_rows - nat))
    blk = 0
    for item in items:
        item.cols = item.shape[1] // LANES if item.shape and len(item.shape) == 2 else 0
        item.blk = blk
        blk += ceil_to(item.rows, BLK) // BLK
    return items


class Geometry:
    def __init__(self, n_seg, n_doc, shard_len):
        self.n_seg, self.n_doc = n_seg, n_doc
        self.n_dev = n_seg * n_doc
        self.chunk = shard_len // LANES
        self.items = item_list(self.chunk * self.n_dev)
        self.by_name = SimpleNamespace(**{item.name: item for item in self.items if item.name})
        firsts, lasts = [], []
        for n in range(self.n_dev):
            lo, hi = n * self.chunk, (n + 1) * self.chunk
            blocks = []
            for item in self.items:
                a, b = max(lo, item.nat), min(hi, item.nat + item.rows)
                if a < b:
                    blocks.append(item.blk + (a - item.nat) // BLK)
                    blocks.append(item.blk + (b - 1 - item.nat) // BLK)
            firsts.append(min(blocks))
            lasts.append(max(blocks))
        self.first, self.last = firsts, lasts
        most = max(b - a + 1 for a, b in zip(firsts, lasts))
        self.piece_blocks = -(-most // self.n_dev)
        self.piece = self.piece_blocks * BLK
        self.slots = self.piece_blocks * self.n_dev
        self.c_size, self.x_size = 2, 2
        self.y_size = n_seg // 4

    def full_groups(self, item, chunk):
        rows = BLK * item.cols
        lo, hi = chunk * self.chunk - item.nat, (chunk + 1) * self.chunk - item.nat
        first, last = max(0, -(-lo // rows)), min(item.rows, hi) // rows
        return first, max(first, last)

    def block_table(self):
        table = np.zeros((self.n_dev, 4, self.slots), np.int32)
        for n in range(self.n_dev):
            lo, hi = n * self.chunk, (n + 1) * self.chunk
            for t in range(self.slots):
                b = self.first[n] + t
                if b > self.last[n]:
                    continue
                item = [it for it in self.items if it.blk <= b][-1]
                at = b - item.blk
                if item.cols:
                    first, last = self.full_groups(item, n)
                    group, column = divmod(at, item.cols)
                    if first <= group < last:
                        start = item.nat + group * BLK * item.cols + column - lo
                        table[n, :, t] = (start, 0, BLK, item.cols)
                        continue
                start = item.nat + at * BLK
                a = max(start, lo)
                z = min(start + BLK, hi, item.nat + item.rows)
                if a < z:
                    table[n, :, t] = (start - lo, a - start, z - start, 0)
        return table

    def chunks_of(self, item):
        found = []
        n_blocks = ceil_to(item.rows, BLK) // BLK
        for n in range(self.n_dev):
            a = max(item.blk, self.first[n])
            b = min(item.blk + n_blocks, self.last[n] + 1)
            if a < b:
                found.append((n, a - item.blk, b - item.blk, a - self.first[n]))
        return found

    def buckets(self):
        end_attention = self.by_name.w_out.nat
        end_segment = self.by_name.pos_table.nat
        a = (end_attention - 1) // self.chunk + 1
        b = (end_segment - 1) // self.chunk + 1
        return [range(0, a), range(a, b), range(b, self.n_dev)]

    def coords(self, device):
        seg, doc = divmod(device, self.n_doc)
        yx, c = divmod(seg, self.c_size)
        return [*divmod(yx, self.x_size), c, doc]

    def device(self, y, x, c, z):
        return ((y * self.x_size + x) * self.c_size + c) * self.n_doc + z

    def size(self, axis):
        return (self.y_size, self.x_size, self.c_size, self.n_doc)[axis]

    def shift(self, axis, step):
        pairs = []
        for source in range(self.n_dev):
            at = self.coords(source)
            at[axis] = (at[axis] + step) % self.size(axis)
            pairs.append((source, self.device(*at)))
        return pairs
def spec_vmem():
    return pl.BlockSpec(memory_space=pltpu.VMEM)


def spec_any():
    return pl.BlockSpec(memory_space=pl.ANY)


def spec_smem():
    return pl.BlockSpec(memory_space=pltpu.SMEM)


def kernel_params(mib=56):
    return pltpu.CompilerParams(vmem_limit_bytes=mib * 1024 * 1024)


def row_mask(low, high):
    rows = lax.broadcasted_iota(jnp.int32, (BLK, LANES), 0)
    return (rows >= low) & (rows < high)


def block_rows(geo, table_ref, t):
    return [table_ref[i * geo.slots + t] for i in range(4)]


def strides(geo):
    return sorted({item.cols for item in geo.items if item.cols})


def align_rows(geo, table, padded):
    def kernel(table_ref, rows_ref, out_ref):
        def body(t, carry):
            start, low_row, high_row, cols = block_rows(geo, table_ref, t)
            here = pl.ds(pl.multiple_of(t * BLK, BLK), BLK)

            @pl.when(cols == 0)
            def _():
                rows = rows_ref[pl.ds(start + BLK, BLK), :]
                out_ref[here, :] = jnp.where(row_mask(low_row, high_row), rows, 0.0).astype(jnp.bfloat16)

            for stride in strides(geo):
                @pl.when(cols == stride)
                def _(stride=stride):
                    rows = rows_ref[pl.ds(start + BLK, BLK, stride=stride), :]
                    out_ref[here, :] = rows.astype(jnp.bfloat16)

            return carry

        lax.fori_loop(0, geo.slots, body, 0)

    return pl.pallas_call(
        kernel,
        out_shape=jax.ShapeDtypeStruct((geo.slots * BLK, LANES), jnp.bfloat16),
        in_specs=[spec_smem(), spec_vmem()],
        out_specs=spec_vmem(),
        compiler_params=kernel_params(),
    )(table, padded)


def natural_rows(geo, table, blocks, pad_rows):
    def kernel(table_ref, blocks_ref, out_ref):
        def body(t, carry):
            start, low_row, high_row, cols = block_rows(geo, table_ref, t)
            rows = blocks_ref[pl.ds(pl.multiple_of(t * BLK, BLK), BLK), :].astype(jnp.float32)

            @pl.when(cols == 0)
            def _():
                here = pl.ds(start + BLK, BLK)
                out_ref[here, :] = jnp.where(row_mask(low_row, high_row), rows, out_ref[here, :])

            for stride in strides(geo):
                @pl.when(cols == stride)
                def _(stride=stride):
                    out_ref[pl.ds(start + BLK, BLK, stride=stride), :] = rows

            return carry

        lax.fori_loop(0, geo.slots, body, 0)

    return pl.pallas_call(
        kernel,
        out_shape=jax.ShapeDtypeStruct((pad_rows, LANES), jnp.float32),
        in_specs=[spec_smem(), spec_vmem()],
        out_specs=spec_vmem(),
        compiler_params=kernel_params(),
    )(table, blocks)


class Buckets:
    def __init__(self, geo):
        self.geo = geo
        self.ranges = geo.buckets()
        self.half = [(len(r) + 1) // 2 for r in self.ranges]
        self.arrays = [4, 4, 1]

    def find(self, chunk):
        for number, span in enumerate(self.ranges):
            if chunk in span:
                at = chunk - span.start
                cut = self.half[number] if self.arrays[number] > 1 else len(span)
                return (number, 0, at) if at < cut else (number, 1, at - cut)

    def shapes(self, number):
        geo = self.geo
        cut = self.half[number]
        rest = len(self.ranges[number]) - cut
        rows = geo.n_doc * geo.piece
        return [
            (geo.y_size, geo.x_size, cut, rows, LANES),
            (geo.x_size, geo.y_size, rest, rows, LANES),
        ]


def wrap(value, size):
    return lax.rem(value + size, size)


def copy_rows(count, step, body):
    full = count // step
    if full:
        def loop(i, carry):
            body(i * step, step)
            return carry

        lax.fori_loop(0, full, loop, 0)
    if count % step:
        body(full * step, count % step)


VECTOR_ROWS = 16


def chunk_copies(geo, buckets, sources, used, coords_ref, n, staged, sem):
    my_y, my_x, my_c = coords_ref[0], coords_ref[1], coords_ref[2]
    number, half, place = buckets.find(n)
    first = sum(buckets.arrays[m] for m in used[: used.index(number)])
    if buckets.arrays[number] == 1:
        for device in range(geo.n_dev):
            pltpu.make_async_copy(
                sources[first].at[device, n - buckets.ranges[number].start],
                staged.at[pl.ds(device * geo.piece, geo.piece)],
                sem,
            ).start()
        return
    rows = geo.n_doc * geo.piece
    for core in range(2):
        c = my_c if core == 0 else 1 - my_c
        for ry in range(geo.y_size):
            for rx in range(geo.x_size):
                y, x = wrap(my_y - ry, geo.y_size), wrap(my_x - rx, geo.x_size)
                s = (y * geo.x_size + x) * 2 + c
                index = (ry, rx, place) if half == 0 else (rx, ry, place)
                pltpu.make_async_copy(
                    sources[first + 2 * half + core].at[index],
                    staged.at[pl.ds(pl.multiple_of(s * rows, BLK), rows)],
                    sem,
                ).start()


def unpack_matrix(geo, buckets, gathered, coords, name):
    item = vars(geo.by_name)[name]
    depth, cols = item.shape
    chunks = geo.chunks_of(item)
    used = sorted({buckets.find(n)[0] for n, *_ in chunks})
    operands = [array for number in used for array in gathered[number]]
    wide_cols = cols // LANES

    def kernel(coords_ref, *refs):
        sources, (out_ref, staged, wide, sems) = refs[: len(operands)], refs[len(operands) :]
        for at, (n, _, _, _) in enumerate(chunks):
            chunk_copies(geo, buckets, sources, used, coords_ref, n, staged.at[at], sems.at[at])
        for at in range(len(chunks)):
            pltpu.make_async_copy(staged.at[at], staged.at[at], sems.at[at]).wait()
        split = set()
        for at, (n, b0, b1, slot) in enumerate(chunks):
            first, last = geo.full_groups(item, n)
            split |= set(range(b0 // wide_cols, -(-b1 // wide_cols))) - set(range(first, last))

            def group(g, carry, at=at, shift=slot - b0):
                rows = pl.ds(pl.multiple_of(g * BLK, BLK), BLK)
                for cb in range(wide_cols):
                    src = pl.ds(pl.multiple_of((g * wide_cols + cb + shift) * BLK, BLK), BLK)
                    out_ref[rows, cb * LANES : (cb + 1) * LANES] = staged[at, src, :]
                return carry

            lax.fori_loop(first, last, group, 0)
        for g in sorted(split):
            done = g * wide_cols
            for at, (n, b0, b1, slot) in enumerate(chunks):
                lo, hi = max(b0, g * wide_cols), min(b1, (g + 1) * wide_cols)
                for b in range(lo, hi):
                    rows = staged[at, pl.ds((slot + b - b0) * BLK, BLK), :].astype(jnp.float32)
                    here = pl.ds((b - g * wide_cols) * BLK, BLK)
                    wide[here, :] = wide[here, :] + rows if b < done else rows
                done = max(done, hi)
            for cb in range(wide_cols):
                tile = wide[pl.ds(cb, BLK, stride=wide_cols), :]
                out_ref[g * BLK : (g + 1) * BLK, cb * LANES : (cb + 1) * LANES] = tile.astype(jnp.bfloat16)

    return pl.pallas_call(
        kernel,
        out_shape=jax.ShapeDtypeStruct((depth, cols), jnp.bfloat16),
        in_specs=[spec_smem()] + [spec_any()] * len(operands),
        out_specs=spec_vmem(),
        scratch_shapes=[
            pltpu.VMEM((len(chunks), geo.slots * BLK, LANES), jnp.bfloat16),
            pltpu.VMEM((BLK * (wide_cols + 2), LANES), jnp.float32),
            pltpu.SemaphoreType.DMA((len(chunks),)),
        ],
        compiler_params=kernel_params(),
    )(coords, *operands)


def unpack_vectors(geo, buckets, gathered, coords, names):
    lane_cols = D // LANES
    blocks, rows_of = [], []
    for name in names:
        item = vars(geo.by_name)[name]
        for r in range(item.rows):
            rows_of.append(len(blocks) * BLK + r)
        for b in range(ceil_to(item.rows, BLK) // BLK):
            blocks.append(
                [
                    (n, item.blk + b - geo.first[n])
                    for n in range(geo.n_dev)
                    if geo.first[n] <= item.blk + b <= geo.last[n]
                ]
            )
    copies = [(b, which, n, slot) for b, found in enumerate(blocks) for which, (n, slot) in enumerate(found)]
    used = sorted({buckets.find(n)[0] for _, _, n, _ in copies})
    operands = [array for number in used for array in gathered[number]]

    def kernel(coords_ref, *refs):
        sources, (out_ref, staged, wide, sem) = refs[: len(operands)], refs[len(operands) :]
        my_y, my_x, my_c = coords_ref[0], coords_ref[1], coords_ref[2]
        for at, (b, which, n, slot) in enumerate(copies):
            number, half, place = buckets.find(n)
            first = sum(buckets.arrays[m] for m in used[: used.index(number)])
            device, offset = slot // geo.piece_blocks, slot % geo.piece_blocks * BLK
            if buckets.arrays[number] == 1:
                pltpu.make_async_copy(
                    sources[first].at[device, n - buckets.ranges[number].start, pl.ds(offset, BLK)],
                    staged.at[at],
                    sem,
                ).start()
                continue
            y, x, c, z = geo.coords(device)
            ry, rx = wrap(my_y - y, geo.y_size), wrap(my_x - x, geo.x_size)
            index = (ry, rx) if half == 0 else (rx, ry)
            for core in range(2):
                source = sources[first + 2 * half + core]

                @pl.when(my_c == (c if core == 0 else 1 - c))
                def _(source=source, at=at, index=index, place=place, row=z * geo.piece + offset):
                    pltpu.make_async_copy(
                        source.at[index[0], index[1], place, pl.ds(row, BLK)], staged.at[at], sem
                    ).start()

        pltpu.make_async_copy(staged, staged, sem).wait()
        for at, (b, which, n, slot) in enumerate(copies):
            rows = staged[at].astype(jnp.float32)
            here = pl.ds(b * BLK, BLK)
            wide[here, :] = rows if which == 0 else wide[here, :] + rows
        out_ref[...] = jnp.zeros_like(out_ref)
        for r, row in enumerate(rows_of):
            v, cb = divmod(r, lane_cols)
            out_ref[v : v + 1, cb * LANES : (cb + 1) * LANES] = wide[row : row + 1, :]

    return pl.pallas_call(
        kernel,
        out_shape=jax.ShapeDtypeStruct((VECTOR_ROWS, D), jnp.float32),
        in_specs=[spec_smem()] + [spec_any()] * len(operands),
        out_specs=spec_vmem(),
        scratch_shapes=[
            pltpu.VMEM((len(copies), BLK, LANES), jnp.bfloat16),
            pltpu.VMEM((len(blocks) * BLK, LANES), jnp.float32),
            pltpu.SemaphoreType.DMA,
        ],
        compiler_params=kernel_params(),
    )(coords, *operands)


def vector_rows(wide, values, first, count):
    lane_cols = D // LANES
    for r in range(count):
        v, cb = divmod(r, lane_cols)
        wide[r : r + 1, :] = values[first + v : first + v + 1, cb * LANES : (cb + 1) * LANES]


def bucket_parts(geo, span):
    parts = []
    for item in geo.items:
        chunks = [entry for entry in geo.chunks_of(item) if entry[0] in span]
        if chunks and item.names:
            parts.append((item, chunks))
    return parts


def pack_bucket(geo, buckets, number, grads, coords):
    span = buckets.ranges[number]
    seg_rows = geo.n_doc * geo.piece
    parts = bucket_parts(geo, span)
    operands, specs, windows, scratch = [], [], [], []
    wide_rows = BLK
    for item, chunks in parts:
        if len(item.shape) == 2:
            cols = item.shape[1] // LANES
            k0 = min(b0 for _, b0, _, _ in chunks) // cols
            k1 = -(-max(b1 for _, _, b1, _ in chunks) // cols)
            operands.append(grads[item.name])
            specs.append(spec_any())
            windows.append((cols, k0, k1))
            scratch.append(pltpu.VMEM(((k1 - k0) * BLK, item.shape[1]), jnp.bfloat16))
            wide_rows = max(wide_rows, BLK * cols)
        else:
            wide_rows = max(wide_rows, ceil_to(item.rows, BLK))
            operands.append(grads[item.name][0])
            specs.append(spec_vmem())
            windows.append(None)
            scratch.append(pltpu.VMEM((BLK, LANES), jnp.bfloat16))
    outs = [shape for shape in buckets.shapes(number) for _ in range(2)]

    def kernel(coords_ref, *refs):
        sources = refs[: len(parts)]
        targets = refs[len(parts) : len(parts) + 4]
        loaded = refs[len(parts) + 4 : 2 * len(parts) + 4]
        staged, wide, in_sems, out_sems = refs[2 * len(parts) + 4 :]
        my_y, my_x, my_c = coords_ref[0], coords_ref[1], coords_ref[2]
        loads = {}
        for at, window in enumerate(windows):
            if window is not None:
                source = sources[at].at[pl.ds(window[1] * BLK, (window[2] - window[1]) * BLK)]
                loads[at] = pltpu.make_async_copy(source, loaded[at], in_sems.at[at])
                loads[at].start()

        def clear(row, rows):
            for at in range(len(span)):
                here = pl.ds(pl.multiple_of(row, BLK), rows)
                staged[at, here, :] = jnp.zeros((rows, LANES), jnp.bfloat16)

        tail = min(geo.last[n] - geo.first[n] for n in span) * BLK
        copy_rows(geo.slots * BLK - tail, 128, lambda row, rows: clear(row + tail, rows))

        def send_out(n):
            _, half, place = buckets.find(n)
            for core in range(2):
                c = my_c if core == 0 else 1 - my_c
                for ry in range(geo.y_size):
                    for rx in range(geo.x_size):
                        y, x = wrap(my_y + ry, geo.y_size), wrap(my_x + rx, geo.x_size)
                        s = (y * geo.x_size + x) * 2 + c
                        index = (ry, rx, place) if half == 0 else (rx, ry, place)
                        pltpu.make_async_copy(
                            staged.at[n - span.start, pl.ds(pl.multiple_of(s * seg_rows, BLK), seg_rows)],
                            targets[2 * half + core].at[index],
                            out_sems.at[n - span.start],
                        ).start()

        last_part = {n: at for at, (_, chunks) in enumerate(parts) for n, *_ in chunks}
        for at, ((item, chunks), window) in enumerate(zip(parts, windows)):
            if window is None:
                vector_rows(wide, sources[at], grads[item.name][1], item.rows)
                for n, b0, b1, slot in chunks:
                    rows = wide[pl.ds(b0 * BLK, (b1 - b0) * BLK), :].astype(jnp.bfloat16)
                    staged[n - span.start, pl.ds(slot * BLK, (b1 - b0) * BLK), :] = rows
            else:
                loads[at].wait()
                cols, k0, k1 = window
                values = loaded[at]
                split = set()
                for n, b0, b1, slot in chunks:
                    first, last = geo.full_groups(item, n)
                    split |= set(range(b0 // cols, -(-b1 // cols))) - set(range(first, last))

                    def group(g, carry, n=n, shift=slot - b0, k0=k0, cols=cols, values=values):
                        rows = pl.ds(pl.multiple_of((g - k0) * BLK, BLK), BLK)
                        for cb in range(cols):
                            dst = pl.ds(pl.multiple_of((g * cols + cb + shift) * BLK, BLK), BLK)
                            staged[n - span.start, dst, :] = values[rows, cb * LANES : (cb + 1) * LANES]
                        return carry

                    lax.fori_loop(first, last, group, 0)
                for g in sorted(split):
                    for cb in range(cols):
                        tile = values[(g - k0) * BLK : (g - k0 + 1) * BLK, cb * LANES : (cb + 1) * LANES]
                        wide[pl.ds(cb, BLK, stride=cols), :] = tile.astype(jnp.float32)
                    for n, b0, b1, slot in chunks:
                        first, last = geo.full_groups(item, n)
                        lo, hi = max(b0, g * cols), min(b1, (g + 1) * cols)
                        if lo < hi and not first <= g < last:
                            rows = wide[pl.ds((lo - g * cols) * BLK, (hi - lo) * BLK), :]
                            dst = pl.ds((slot + lo - b0) * BLK, (hi - lo) * BLK)
                            staged[n - span.start, dst, :] = rows.astype(jnp.bfloat16)
            for n, *_ in chunks:
                if last_part[n] == at:
                    send_out(n)
        for n in span:
            at = n - span.start
            pltpu.make_async_copy(staged.at[at], staged.at[at], out_sems.at[at]).wait()

    return pl.pallas_call(
        kernel,
        out_shape=[jax.ShapeDtypeStruct(shape, jnp.bfloat16) for shape in outs],
        in_specs=[spec_smem()] + specs,
        out_specs=[spec_any()] * 4,
        scratch_shapes=scratch
        + [
            pltpu.VMEM((len(span), geo.slots * BLK, LANES), jnp.bfloat16),
            pltpu.VMEM((wide_rows + 2 * BLK, LANES), jnp.float32),
            pltpu.SemaphoreType.DMA((len(parts),)),
            pltpu.SemaphoreType.DMA((len(span),)),
        ],
        compiler_params=kernel_params(),
    )(coords, *operands)


def pack_cross(geo, span, lefts, rights, vectors, seg):
    seg_blocks = geo.n_doc * geo.piece_blocks
    parts = bucket_parts(geo, span)
    names = list(lefts)
    vector_names = list(vectors)
    depth_rows = next(iter(rights.values())).shape[0]

    def window(cols):
        return (-(-(seg_blocks - 1) // cols) + 1) * BLK

    wide_rows = 0
    left_rows = BLK
    for item, chunks in parts:
        if len(item.shape) == 2:
            cols = item.shape[1] // LANES
            size = min(window(cols), item.shape[0])
            left_rows = max(left_rows, len(chunks) * size)
            wide_rows = max(wide_rows, len(chunks) * size * cols)

    def kernel(seg_ref, *refs):
        left = dict(zip(names, refs[: len(names)]))
        right = dict(zip(names, refs[len(names) : 2 * len(names)]))
        vector = dict(zip(vector_names, refs[2 * len(names) : 2 * len(names) + len(vector_names)]))
        out_ref, gathered, wide = refs[2 * len(names) + len(vector_names) :]
        low_slot = seg_ref[0] * seg_blocks
        out_ref[...] = jnp.zeros_like(out_ref)
        for item, chunks in parts:
            starts, size, cols = [], 0, 1
            if len(item.shape) == 2:
                cols = item.shape[1] // LANES
                size = min(window(cols), item.shape[0])
                for at, (n, b0, b1, slot) in enumerate(chunks):
                    first = jnp.maximum(low_slot, slot) - slot + b0
                    start = jnp.clip(first // cols * BLK, 0, item.shape[0] - size)
                    start = pl.multiple_of(start, BLK)
                    starts.append(start)
                    gathered[at * size : (at + 1) * size, :] = left[item.name][pl.ds(start, size), :]
                count = len(chunks) * size
                rows = gathered[:count, :]
                for cb in range(0, cols, 2):
                    tile = dot_nn(rows, right[item.name][:, cb * LANES : (cb + 2) * LANES])
                    wide[pl.ds(cb, count, stride=cols), :] = tile[:, :LANES]
                    wide[pl.ds(cb + 1, count, stride=cols), :] = tile[:, LANES:]
            else:
                vector_rows(wide, vector[item.name], vectors[item.name][1], item.rows)
            for at, (n, b0, b1, slot) in enumerate(chunks):
                begin = jnp.maximum(low_slot, slot)
                end = jnp.minimum(low_slot + seg_blocks, slot + b1 - b0)
                base = (at * size - starts[at]) * cols if starts else 0

                first, last = geo.full_groups(item, n) if starts else (0, 0)

                def by_row(t, carry, n=n, b0=b0, slot=slot, base=base):
                    src = pl.ds((b0 + t - slot) * BLK + base, BLK)
                    dst = pl.ds(pl.multiple_of((t - low_slot) * BLK, BLK), BLK)
                    out_ref[n - span.start, dst, :] = wide[src, :].astype(jnp.bfloat16)
                    return carry

                def by_tile(t, carry, n=n, b0=b0, slot=slot, base=base, cols=cols):
                    b = b0 + t - slot
                    group = b // cols
                    src = pl.ds(group * BLK * cols + b - group * cols + base, BLK, stride=cols)
                    dst = pl.ds(pl.multiple_of((t - low_slot) * BLK, BLK), BLK)
                    out_ref[n - span.start, dst, :] = wide[src, :].astype(jnp.bfloat16)
                    return carry

                if first < last:
                    lo = jnp.clip(slot + first * cols - b0, begin, jnp.maximum(begin, end))
                    hi = jnp.clip(slot + last * cols - b0, begin, jnp.maximum(begin, end))
                    lax.fori_loop(begin, lo, by_row, 0)
                    lax.fori_loop(lo, hi, by_tile, 0)
                    lax.fori_loop(hi, jnp.maximum(hi, end), by_row, 0)
                else:
                    lax.fori_loop(begin, jnp.maximum(begin, end), by_row, 0)

    operands = [lefts[n] for n in names] + [rights[n] for n in names]
    operands += [vectors[n][0] for n in vector_names]
    return pl.pallas_call(
        kernel,
        out_shape=jax.ShapeDtypeStruct((len(span), seg_blocks * BLK, LANES), jnp.bfloat16),
        in_specs=[spec_smem()] + [spec_vmem()] * len(operands),
        out_specs=spec_vmem(),
        scratch_shapes=[
            pltpu.VMEM((left_rows, depth_rows), jnp.bfloat16),
            pltpu.VMEM((wide_rows + 2 * BLK, LANES), jnp.float32),
        ],
        compiler_params=kernel_params(),
    )(seg, *operands)
TILE = 512
PAIRS = HEADS // 2
TAIL_RATE = 0.3
TAIL = (
    0.11962929605681312,
    0.12075400207853171,
    0.0999131861559567,
    0.12856268365589474,
    -0.05368570534984477,
    0.20635578836359286,
    -0.15720441932045734,
    0.0356750954846771,
)


def dot_nn(left, right):
    return lax.dot_general(left, right, (((1,), (0,)), ((), ())), preferred_element_type=jnp.float32)


def dot_nt(left, right):
    return lax.dot_general(left, right, (((1,), (1,)), ((), ())), preferred_element_type=jnp.float32)


def dot_tn(left, right):
    return lax.dot_general(left, right, (((0,), (0,)), ((), ())), preferred_element_type=jnp.float32)


def low(values):
    return values.astype(jnp.bfloat16)


def gelu_pair(u):
    t = 1.0 / (1.0 + TAIL_RATE * jnp.abs(u))
    poly = TAIL[-1] * t + TAIL[-2]
    for coef in TAIL[-3::-1]:
        poly = poly * t + coef
    bell = jnp.exp(-0.5 * (u * u))
    tail = bell * (poly * t)
    spread = jnp.where(u < 0.0, tail, 1.0 - tail)
    return u * spread, spread + u * bell * (1.0 / math.sqrt(2.0 * math.pi))


def norm_rows(values, gain, shift):
    center = values - jnp.mean(values, axis=-1, keepdims=True)
    rate = lax.rsqrt(jnp.mean(center * center, axis=-1, keepdims=True) + EPSILON)
    normal = center * rate
    return normal * gain + shift, normal, rate


def norm_pull(grad, normal, rate, gain):
    scaled = grad * gain
    return rate * (
        scaled
        - jnp.mean(scaled, axis=-1, keepdims=True)
        - normal * jnp.mean(scaled * normal, axis=-1, keepdims=True)
    )


def fixed(shape):
    return pl.BlockSpec(shape, lambda i: (0,) * len(shape), pipeline_mode=pl.Buffered(1))


def tiles(cols, first=0):
    return pl.BlockSpec((TILE, cols), lambda i: (i + first, 0))


def both_heads(values):
    first = lax.broadcasted_iota(jnp.int32, values.shape, 1) < HEAD_DIM
    zero = jnp.zeros_like(values)
    return jnp.concatenate([jnp.where(first, values, zero), jnp.where(first, zero, values)], axis=0)


def side_by_side(stacked):
    half = stacked.shape[0] // 2
    return jnp.concatenate([stacked[:half], stacked[half:]], axis=1)


def third(part, pair):
    start = part * D + pair * LANES
    return slice(start, start + LANES)


def attend_kernel(x_ref, wqkv_ref, vec_ref, *refs):
    packed_ref, att_ref, stat_ref = refs[-3:]
    x = x_ref[...]
    for j in range(3):
        cols = slice(j * D, (j + 1) * D)
        part = dot_nn(x, wqkv_ref[:, cols])
        packed_ref[:, cols] = low(part if j == 1 else part + vec_ref[j // 2 : j // 2 + 1, :])
    lanes = lax.broadcasted_iota(jnp.int32, (SEG_LEN, LANES), 1)

    def segment(s, carry):
        rows = pl.ds(pl.multiple_of(s * SEG_LEN, SEG_LEN), SEG_LEN)
        stat = jnp.zeros((SEG_LEN, LANES), jnp.float32)
        for pair in range(PAIRS):
            q = packed_ref[rows, third(0, pair)] * jnp.bfloat16(HEAD_DIM**-0.5)
            k = packed_ref[rows, third(1, pair)]
            v = packed_ref[rows, third(2, pair)]
            scores = dot_nt(both_heads(q), k)
            largest = jnp.max(scores, axis=-1, keepdims=True)
            raised = jnp.exp(scores - largest)
            summed = jnp.sum(raised, axis=-1, keepdims=True)
            weights = low(raised / summed)
            att_ref[rows, pair * LANES : (pair + 1) * LANES] = low(
                dot_nn(side_by_side(weights), both_heads(v))
            )
            log_sum = largest + jnp.log(summed)
            stat = jnp.where(lanes == 2 * pair, log_sum[:SEG_LEN], stat)
            stat = jnp.where(lanes == 2 * pair + 1, log_sum[SEG_LEN:], stat)
        stat_ref[rows, :] = stat
        return carry

    lax.fori_loop(0, TILE // SEG_LEN, segment, 0)


def in_parts(kernel, first, count, inputs, in_specs, outs, out_specs, scratch, previous):
    previous = list(previous or ())
    return pl.pallas_call(
        kernel,
        grid=(count,),
        in_specs=in_specs + [spec_any()] * len(previous),
        out_specs=out_specs,
        out_shape=outs,
        scratch_shapes=scratch,
        input_output_aliases={len(inputs) + i: i for i in range(len(previous))},
        compiler_params=kernel_params(60),
    )(*inputs, *previous)


def attend_layer(x, w_qkv, vecs, first, count, previous=None):
    n = x.shape[0]

    def rows(cols):
        return tiles(cols, first)

    return in_parts(
        attend_kernel,
        first,
        count,
        [x, w_qkv, vecs],
        [rows(D), fixed((D, 3 * D)), fixed((VECTOR_ROWS, D))],
        [
            jax.ShapeDtypeStruct((n, 3 * D), jnp.bfloat16),
            jax.ShapeDtypeStruct((n, D), jnp.bfloat16),
            jax.ShapeDtypeStruct((n, LANES), jnp.float32),
        ],
        [rows(3 * D), rows(D), rows(LANES)],
        [],
        previous,
    )


FBLOCK = D


def feed_kernel(
    x_ref, att_ref, wout_ref, wup_ref, wdown_ref, vec_ref,
    h1low_ref, norm1_ref, g_ref, dg_ref, norm2_ref, rate_ref, h2_ref, cls_ref, res_ref, h1_ref,
):
    step = pl.program_id(0)
    segs = TILE // SEG_LEN
    lanes = lax.broadcasted_iota(jnp.int32, (SEG_LEN, LANES), 1)
    res_ref[...] = dot_nn(att_ref[...], wout_ref[...])

    def start(s, carry):
        rows = pl.ds(pl.multiple_of(s * SEG_LEN, SEG_LEN), SEG_LEN)
        resid = x_ref[rows, :].astype(jnp.float32) + res_ref[rows, :] + vec_ref[2:3, :]
        hidden, normal, rate = norm_rows(resid, vec_ref[3:4, :], vec_ref[4:5, :])
        h1_ref[rows, :] = hidden
        h1low_ref[rows, :] = low(hidden)
        norm1_ref[rows, :] = low(normal)
        rate_ref[rows, :] = jnp.broadcast_to(rate, (SEG_LEN, LANES))
        return carry

    lax.fori_loop(0, segs, start, 0)
    h = h1low_ref[...]
    for j in range(FF // FBLOCK):
        cols = slice(j * FBLOCK, (j + 1) * FBLOCK)
        act, slope = gelu_pair(dot_nn(h, wup_ref[:, cols]) + vec_ref[5 + j : 6 + j, :])
        g = low(act)
        g_ref[:, cols] = g
        dg_ref[:, cols] = low(slope)
        part = dot_nn(g, wdown_ref[cols, :])
        if j == 0:
            res_ref[...] = part
        else:
            res_ref[...] += part

    def finish(s, carry):
        rows = pl.ds(pl.multiple_of(s * SEG_LEN, SEG_LEN), SEG_LEN)
        resid = h1_ref[rows, :] + res_ref[rows, :] + vec_ref[9:10, :]
        hidden, normal, rate = norm_rows(resid, vec_ref[10:11, :], vec_ref[11:12, :])
        h2_ref[rows, :] = low(hidden)
        norm2_ref[rows, :] = low(normal)
        rate_ref[rows, :] = jnp.where(lanes == 0, rate_ref[rows, :], rate)
        cls_ref[pl.ds(step * segs + s, 1), :] = hidden[0:1, :]
        return carry

    lax.fori_loop(0, segs, finish, 0)


def feed_layer(x, att, w_out, w_up, w_down, vecs):
    n = x.shape[0]
    bf, f32 = jnp.bfloat16, jnp.float32
    return pl.pallas_call(
        feed_kernel,
        grid=(n // TILE,),
        in_specs=[
            tiles(D), tiles(D), fixed((D, D)), fixed((D, FF)), fixed((FF, D)), fixed((VECTOR_ROWS, D)),
        ],
        out_specs=[tiles(D), tiles(D), tiles(FF), tiles(FF), tiles(D), tiles(LANES), tiles(D)]
        + [pl.BlockSpec((n // SEG_LEN, D), lambda i: (0, 0))],
        out_shape=[
            jax.ShapeDtypeStruct((n, cols), kind)
            for cols, kind in ((D, bf), (D, bf), (FF, bf), (FF, bf), (D, bf), (LANES, f32), (D, bf))
        ]
        + [jax.ShapeDtypeStruct((n // SEG_LEN, D), f32)],
        scratch_shapes=[pltpu.VMEM((TILE, D), f32), pltpu.VMEM((TILE, D), f32)],
        compiler_params=kernel_params(60),
    )(x, att, w_out, w_up, w_down, vecs)


def feed_back_kernel(
    cot_ref, cls_ref, norm2_ref, dg_ref, norm1_ref, rate_ref,
    wdown_ref, wup_ref, wout_ref, vec_ref,
    dm_ref, du_ref, dao_ref, da_ref, one_ref, sums_ref, res_ref,
):
    step = pl.program_id(0)

    @pl.when(step == 0)
    def _():
        sums_ref[...] = jnp.zeros_like(sums_ref)

    segs = TILE // SEG_LEN
    row_ids = lax.broadcasted_iota(jnp.int32, (SEG_LEN, D), 0)

    def add_sum(row, values):
        sums_ref[row : row + 1, :] += jnp.sum(values, axis=0, keepdims=True)

    def start(s, carry):
        rows = pl.ds(pl.multiple_of(s * SEG_LEN, SEG_LEN), SEG_LEN)
        cls = cls_ref[pl.ds(step * segs + s, 1), :]
        grad = jnp.where(row_ids == 0, cls, cot_ref[rows, :].astype(jnp.float32))
        normal = norm2_ref[rows, :].astype(jnp.float32)
        add_sum(10, grad * normal)
        add_sum(11, grad)
        two = norm_pull(grad, normal, rate_ref[rows, 1:2], vec_ref[10:11, :])
        res_ref[rows, :] = two
        dm = low(two)
        dm_ref[rows, :] = dm
        add_sum(9, dm.astype(jnp.float32))
        return carry

    lax.fori_loop(0, segs, start, 0)
    dm = dm_ref[...]
    for j in range(FF // FBLOCK):
        cols = slice(j * FBLOCK, (j + 1) * FBLOCK)
        du = low(dot_nt(dm, wdown_ref[cols, :]) * dg_ref[:, cols].astype(jnp.float32))
        du_ref[:, cols] = du
        add_sum(5 + j, du.astype(jnp.float32))
        res_ref[...] += dot_nt(du, wup_ref[:, cols])

    def finish(s, carry):
        rows = pl.ds(pl.multiple_of(s * SEG_LEN, SEG_LEN), SEG_LEN)
        grad = res_ref[rows, :]
        normal = norm1_ref[rows, :].astype(jnp.float32)
        add_sum(3, grad * normal)
        add_sum(4, grad)
        one = norm_pull(grad, normal, rate_ref[rows, 0:1], vec_ref[3:4, :])
        one_ref[rows, :] = one
        dao = low(one)
        dao_ref[rows, :] = dao
        add_sum(2, dao.astype(jnp.float32))
        return carry

    lax.fori_loop(0, segs, finish, 0)
    da_ref[...] = low(dot_nt(dao_ref[...], wout_ref[...]))


def feed_back(cot, cls, norm2, dg, norm1, rates, w_down, w_up, w_out, vecs):
    n = cot.shape[0]
    bf, f32 = jnp.bfloat16, jnp.float32
    return pl.pallas_call(
        feed_back_kernel,
        grid=(n // TILE,),
        in_specs=[
            tiles(D), fixed((n // SEG_LEN, D)), tiles(D), tiles(FF), tiles(D), tiles(LANES),
            fixed((FF, D)), fixed((D, FF)), fixed((D, D)), fixed((VECTOR_ROWS, D)),
        ],
        out_specs=[
            tiles(D), tiles(FF), tiles(D), tiles(D), tiles(D),
            pl.BlockSpec((VECTOR_ROWS, D), lambda i: (0, 0)),
        ],
        out_shape=[
            jax.ShapeDtypeStruct((n, D), bf),
            jax.ShapeDtypeStruct((n, FF), bf),
            jax.ShapeDtypeStruct((n, D), bf),
            jax.ShapeDtypeStruct((n, D), bf),
            jax.ShapeDtypeStruct((n, D), f32),
            jax.ShapeDtypeStruct((VECTOR_ROWS, D), f32),
        ],
        scratch_shapes=[pltpu.VMEM((TILE, D), f32)],
        compiler_params=kernel_params(60),
    )(cot, cls, norm2, dg, norm1, rates, w_down, w_up, w_out, vecs)


def attend_back_kernel(packed_ref, stat_ref, da_ref, before_ref, *refs):
    dqkv_ref, sums_ref = refs[-2:]

    @pl.when(pl.program_id(0) == 0)
    def _():
        sums_ref[...] = before_ref[...]

    lanes = lax.broadcasted_iota(jnp.int32, (SEG_LEN, LANES), 1)
    scale = HEAD_DIM**-0.5

    def segment(s, carry):
        rows = pl.ds(pl.multiple_of(s * SEG_LEN, SEG_LEN), SEG_LEN)
        stat = stat_ref[rows, :]
        for pair in range(PAIRS):
            q = packed_ref[rows, third(0, pair)] * jnp.bfloat16(scale)
            k = packed_ref[rows, third(1, pair)]
            v = packed_ref[rows, third(2, pair)]
            da = da_ref[rows, pair * LANES : (pair + 1) * LANES]
            queries, grads = both_heads(q), both_heads(da)
            log_sum = jnp.concatenate([stat[:, 2 * pair : 2 * pair + 1], stat[:, 2 * pair + 1 : 2 * pair + 2]], axis=0)
            weights = jnp.exp(dot_nt(queries, k) - log_sum)
            grad_weights = dot_nt(grads, v)
            dv = dot_tn(low(weights), grads)
            inner = jnp.sum(grad_weights * weights, axis=-1, keepdims=True)
            ds = low(weights * (grad_weights - inner))
            dq = dot_nn(side_by_side(ds), both_heads(k)) * scale
            dk = dot_tn(ds, queries)
            for part, grad in enumerate((dq, dk, dv)):
                grad = low(grad)
                cols = third(part, pair)
                dqkv_ref[rows, cols] = grad
                if part != 1:
                    here = (slice(part // 2, part // 2 + 1), third(0, pair))
                    sums_ref[here] += jnp.sum(grad.astype(jnp.float32), axis=0, keepdims=True)
        return carry

    lax.fori_loop(0, TILE // SEG_LEN, segment, 0)


def attend_back(packed, stat, da, first, count, previous=None):
    n = packed.shape[0]
    before = previous[1] if previous else jnp.zeros((8, D), jnp.float32)
    return in_parts(
        attend_back_kernel,
        first,
        count,
        [packed, stat, da, before],
        [tiles(3 * D, first), tiles(LANES, first), tiles(D, first), fixed((8, D))],
        [jax.ShapeDtypeStruct((n, 3 * D), jnp.bfloat16), jax.ShapeDtypeStruct((8, D), jnp.float32)],
        [tiles(3 * D, first), pl.BlockSpec((8, D), lambda i: (0, 0))],
        [],
        previous and previous[:1],
    )


def cross_kernel(
    rows_ref, tagc_ref, tagr_ref, gz_ref, wqkv_ref, wout_ref, wup_ref, wdown_ref, vec_ref,
    out_ref, grows_ref, sums_ref, gqkv_ref, go_ref, gu_ref, gm_ref, rowst_ref, attt_ref, hidt_ref, actt_ref,
    packed_ref, weights_ref, att_ref, act_ref, slope_ref, res_ref,
):
    scale = HEAD_DIM**-0.5
    rows = rows_ref[...]
    rowst_ref[...] = rows.T
    same = tagc_ref[:, 0:1] == tagr_ref[0:1, :]
    same = jnp.concatenate([same, same], axis=0)

    def add_sum(row, values):
        sums_ref[row : row + 1, :] = jnp.sum(values.astype(jnp.float32), axis=0, keepdims=True)

    def pair_cols(pair):
        return slice(pair * LANES, (pair + 1) * LANES)

    sums_ref[...] = jnp.zeros_like(sums_ref)
    for j in range(3):
        cols = slice(j * D, (j + 1) * D)
        part = dot_nn(rows, wqkv_ref[:, cols])
        packed_ref[:, cols] = low(part if j == 1 else part + vec_ref[j // 2 : j // 2 + 1, :])
    for pair in range(PAIRS):
        q = packed_ref[:, third(0, pair)] * jnp.bfloat16(scale)
        scores = jnp.where(same, dot_nt(both_heads(q), packed_ref[:, third(1, pair)]), NEGATIVE)
        raised = jnp.exp(scores - jnp.max(scores, axis=-1, keepdims=True))
        weights = raised / jnp.sum(raised, axis=-1, keepdims=True)
        weights_ref[pair] = weights
        blend = dot_nn(side_by_side(low(weights)), both_heads(packed_ref[:, third(2, pair)]))
        att_ref[:, pair_cols(pair)] = low(blend)
    att = att_ref[...]
    attt_ref[...] = att.T
    resid = rows.astype(jnp.float32) + dot_nn(att, wout_ref[...]) + vec_ref[2:3, :]
    hidden, normal_three, rate_three = norm_rows(resid, vec_ref[3:4, :], vec_ref[4:5, :])
    hidden_low = low(hidden)
    hidt_ref[...] = hidden_low.T
    res_ref[...] = hidden + vec_ref[9:10, :]
    for j in range(FF // FBLOCK):
        cols = slice(j * FBLOCK, (j + 1) * FBLOCK)
        act, slope = gelu_pair(dot_nn(hidden_low, wup_ref[:, cols]) + vec_ref[5 + j : 6 + j, :])
        act = low(act)
        actt_ref[cols, :] = act.T
        slope_ref[:, cols] = slope
        res_ref[...] += dot_nn(act, wdown_ref[cols, :])
    crossed, normal_four, rate_four = norm_rows(res_ref[...], vec_ref[10:11, :], vec_ref[11:12, :])
    out_ref[...] = low(crossed)

    grad_z = gz_ref[...].astype(jnp.float32)
    add_sum(10, grad_z * normal_four)
    add_sum(11, grad_z)
    grad_four = norm_pull(grad_z, normal_four, rate_four, vec_ref[10:11, :])
    grad_m = low(grad_four)
    gm_ref[...] = grad_m
    add_sum(9, grad_m)
    res_ref[...] = grad_four
    for j in range(FF // FBLOCK):
        cols = slice(j * FBLOCK, (j + 1) * FBLOCK)
        grad_u = low(dot_nt(grad_m, wdown_ref[cols, :]) * slope_ref[:, cols])
        gu_ref[:, cols] = grad_u
        add_sum(5 + j, grad_u)
        res_ref[...] += dot_nt(grad_u, wup_ref[:, cols])
    grad_h = res_ref[...]
    add_sum(3, grad_h * normal_three)
    add_sum(4, grad_h)
    grad_three = norm_pull(grad_h, normal_three, rate_three, vec_ref[3:4, :])
    grad_o = low(grad_three)
    go_ref[...] = grad_o
    add_sum(2, grad_o)
    res_ref[...] = grad_three
    att_ref[...] = low(dot_nt(grad_o, wout_ref[...]))
    for pair in range(PAIRS):
        queries = both_heads(packed_ref[:, third(0, pair)] * jnp.bfloat16(scale))
        grads = both_heads(att_ref[:, pair_cols(pair)])
        weights = weights_ref[pair]
        grad_weights = dot_nt(grads, packed_ref[:, third(2, pair)])
        dv = dot_tn(low(weights), grads)
        inner = jnp.sum(grad_weights * weights, axis=-1, keepdims=True)
        ds = low(weights * (grad_weights - inner))
        dq = dot_nn(side_by_side(ds), both_heads(packed_ref[:, third(1, pair)])) * scale
        dk = dot_tn(ds, queries)
        for part, grad in enumerate((dq, dk, dv)):
            gqkv_ref[:, third(part, pair)] = low(grad)
    add_sum(0, gqkv_ref[:, :D])
    add_sum(1, gqkv_ref[:, 2 * D :])
    for j in range(3):
        cols = slice(j * D, (j + 1) * D)
        res_ref[...] += dot_nt(gqkv_ref[:, cols], wqkv_ref[:, cols])
    grows_ref[...] = low(res_ref[...])


def cross_layer(rows, tags, grad_out, x_qkv, x_out, x_up, x_down, vec):
    m = rows.shape[0]
    bf, f32 = jnp.bfloat16, jnp.float32
    tagc = jnp.broadcast_to(tags.astype(f32)[:, None], (m, LANES))
    tagr = jnp.broadcast_to(tags.astype(f32)[None, :], (8, m))
    operands = [rows, tagc, tagr, grad_out, x_qkv, x_out, x_up, x_down, vec]
    shapes = [(m, D), (m, D), (VECTOR_ROWS, D), (m, 3 * D), (m, D), (m, FF), (m, D), (D, m), (D, m), (D, m), (FF, m)]
    return pl.pallas_call(
        cross_kernel,
        out_shape=[jax.ShapeDtypeStruct(shape, f32 if i == 2 else bf) for i, shape in enumerate(shapes)],
        in_specs=[spec_vmem()] * len(operands),
        out_specs=[spec_vmem()] * len(shapes),
        scratch_shapes=[
            pltpu.VMEM((m, 3 * D), bf),
            pltpu.VMEM((PAIRS, 2 * m, m), f32),
            pltpu.VMEM((m, D), bf),
            pltpu.VMEM((m, D), bf),
            pltpu.VMEM((m, FF), f32),
            pltpu.VMEM((m, D), f32),
        ],
        compiler_params=kernel_params(60),
    )(*operands)
AXES = ("seg", "doc")


def tie(value, *others):
    return lax.optimization_barrier((value, *others))[0]


def send(geo, value, axis, step):
    return lax.ppermute(value, AXES, geo.shift(axis, step))


def gather_axis(geo, value, axis):
    return jnp.stack([value] + [send(geo, value, axis, r) for r in range(1, geo.size(axis))])


def gather_line(geo, pieces, my_z):
    nd = geo.n_doc
    parts = [pieces] + [send(geo, pieces, Z, r) for r in range(1, nd)]
    parts = parts[::-1]
    line = jnp.stack(parts + parts[: nd - 1], axis=1)
    line = lax.dynamic_slice_in_dim(line, nd - 1 - my_z, nd, axis=1)
    return line.reshape(pieces.shape[0], nd * geo.piece, LANES)


def gather_plane(geo, halves, step):
    orders = ((X, Y), (Y, X))
    return [gather_axis(geo, half, order[step]) for half, order in zip(halves, orders)]


def gather_cores(geo, halves):
    return [array for half in halves for array in (half, send(geo, half, C, 1))]


def plus(*terms):
    return low(sum(term.astype(jnp.float32) for term in terms))


def reduce_cores(geo, arrays):
    return [(arrays[2 * half], send(geo, arrays[2 * half + 1], C, 1)) for half in range(2)]


def reduce_plane(geo, halves, step):
    orders = ((Y, X), (X, Y))
    result = []
    for half, order in zip(halves, orders):
        value = plus(*half)
        axis = order[step]
        result.append([value[0]] + [send(geo, value[r], axis, r) for r in range(1, geo.size(axis))])
    return result


def reduce_line(geo, line, my_z):
    nd = geo.n_doc
    line = line.reshape(line.shape[0], nd, geo.piece, LANES)

    def to(r):
        return lax.dynamic_index_in_dim(line, lax.rem(my_z + r, nd), axis=1, keepdims=False)

    return [to(0)] + [send(geo, to(r), Z, r) for r in range(1, nd)]


def join(halves):
    return jnp.concatenate([plus(*half) for half in halves])
def optimizer_step(gradient, master, momentum, average, scaling, rating):
    scaled = gradient * scaling
    moment = 0.5 * momentum + scaled
    weight = master - rating * (scaled + 0.5 * moment)
    smooth = 0.5 * average + 0.5 * weight
    return (weight, moment, smooth, low(weight))


def row_rates(geo, n_tokens, n_cls):
    total = geo.chunk * geo.n_dev
    scaling = np.zeros((total,), np.float32)
    rating = np.full((total,), 0.2, np.float32)
    names = list(LAYOUT)
    cross = names[-13:]
    row = 0
    for name, shape in LAYOUT.items():
        rows = math.prod(shape) // LANES
        scaling[row : row + rows] = 1.0 / math.sqrt(n_cls if name in cross else n_tokens)
        if len(shape) == 2:
            rating[row : row + rows] = 1.0 if name == cross[0] else 0.5 / math.sqrt(shape[0])
        row += rows
    return scaling.reshape(geo.n_dev, geo.chunk), rating.reshape(geo.n_dev, geo.chunk)


def matmul(left, right):
    return jnp.dot(left, right, preferred_element_type=jnp.float32)


def column_sum(rows):
    return jnp.sum(rows.astype(jnp.float32), axis=0, keepdims=True)


def local(tokens, cotangent, seg_doc, seg_pos, master, momentum, average):
    n_seg = lax.axis_size(AXES[0])
    n_doc = lax.axis_size(AXES[1])
    geo = Geometry(n_seg, n_doc, master.shape[0])
    buckets = Buckets(geo)
    my_seg, my_doc = lax.axis_index(AXES[0]), lax.axis_index(AXES[1])
    me = my_seg * n_doc + my_doc
    coords = jnp.stack([my_seg // 4, my_seg // 2 % 2, my_seg % 2, my_doc]).astype(jnp.int32)
    table = lax.dynamic_index_in_dim(
        jnp.asarray(geo.block_table().reshape(geo.n_dev, -1)), me, 0, False
    )
    pad_rows = ceil_to(geo.chunk + 4 * BLK, 8)
    padded = jnp.pad(
        master.reshape(geo.chunk, LANES), ((BLK, pad_rows - geo.chunk - BLK), (0, 0))
    )
    aligned = align_rows(geo, table, padded)
    pieces = lax.all_to_all(aligned.reshape(geo.n_dev, geo.piece, LANES), AXES, 0, 0, tiled=True)
    parts = [pieces[span.start : span.stop] for span in buckets.ranges]

    seg_count = tokens.shape[1]
    n_rows = n_seg * seg_count
    tiles_all = seg_count * SEG_LEN // TILE
    inputs = tokens[0].reshape(seg_count * SEG_LEN, D)
    cot_rows = cotangent[0]
    tags = low(jnp.stack([seg_doc[0], seg_pos[0]], axis=1).astype(jnp.float32))
    tagged = jnp.concatenate([cot_rows[:, 0], jnp.pad(tags, ((0, 0), (0, LANES - 2)))], axis=1)
    all_tagged = lax.all_gather(tie(tagged, pieces), AXES[0], axis=0, tiled=True)
    all_grad, all_doc, all_pos = all_tagged[:, :D], all_tagged[:, D], all_tagged[:, D + 1]
    pos_hot = (all_pos.astype(jnp.int32)[:, None] == jnp.arange(LONG_SEGS)[None, :]).astype(jnp.bfloat16)

    line = gather_line(geo, parts[0], my_doc)
    cut = buckets.half
    line_b = gather_line(geo, tie(parts[1], line, all_tagged), my_doc)
    plane = gather_plane(geo, [line[: cut[0]], line[cut[0] :]], 0)
    plane = gather_plane(geo, plane, 1)
    gathered = [gather_cores(geo, plane), None, None]
    line_b = tie(line_b, *plane)
    plane_b = gather_plane(geo, [line_b[: cut[1]], line_b[cut[1] :]], 0)

    def matrix(number):
        return unpack_matrix(geo, buckets, gathered, coords, item_name(number))

    def vectors(*numbers):
        return unpack_vectors(geo, buckets, gathered, coords, [item_name(i) for i in numbers])

    w_qkv = matrix(0)
    gathered[2] = [lax.all_gather(tie(parts[2], w_qkv), AXES)]
    vec_a = vectors(1)
    w_qkv = tie(w_qkv, *plane_b)
    plane_b = gather_plane(geo, plane_b, 1)
    first = max(1, tiles_all - 1)
    outs = attend_layer(inputs, w_qkv, vec_a, 0, first)
    plane_b = [tie(half, outs[0]) for half in plane_b]
    gathered[1] = gather_cores(geo, plane_b)
    if first < tiles_all:
        outs = attend_layer(tie(inputs, *plane_b), w_qkv, vec_a, first, tiles_all - first, outs)
    packed, attended, stat = outs

    w_out, w_up, w_down, vec = matrix(2), matrix(4), matrix(6), vectors(1, 3, 5, 7)
    hidden_low, normal_one, active, slope, normal_two, rates, hidden_two, cls = feed_layer(
        inputs, attended, w_out, w_up, w_down, vec
    )

    cross = [matrix(i) for i in (8, 9, 11, 13, 15)]
    xvec = vectors(10, 12, 14, 16)

    def own(values):
        return lax.dynamic_slice_in_dim(values, my_seg * seg_count, seg_count, axis=0)

    cls_low = low(cls + matmul(own(pos_hot), cross[0]))
    rows = lax.all_gather(cls_low, AXES[0], axis=0, tiled=True)
    crossed, grad_rows, xsums, g_qkv, g_o, g_u, g_m, rows_t, att_t, hid_t, act_t = cross_layer(
        rows, all_doc, all_grad, *cross[1:], xvec
    )
    first_row = lax.broadcasted_iota(jnp.int32, (seg_count, SEG_LEN, D), 1) == 0
    mixed_out = jnp.where(
        first_row, own(crossed)[:, None, :], hidden_two.reshape(seg_count, SEG_LEN, D)
    )
    names = [item_name(i) for i in (8, 9, 11, 13, 15)]
    line_c = pack_cross(
        geo,
        buckets.ranges[2],
        dict(zip(names, (pos_hot.T, rows_t, att_t, hid_t, act_t))),
        dict(zip(names, (grad_rows, g_qkv, g_o, g_u, g_m))),
        {item_name(i): (xsums, row) for i, row in ((10, 0), (12, 2), (14, 5), (16, 9))},
        my_seg.astype(jnp.int32).reshape(1),
    )
    line_c_parts = reduce_line(geo, line_c, my_doc)

    grads = {}
    dm, du, dao, da, grad_one, sums = feed_back(
        cot_rows.reshape(-1, D), tie(own(grad_rows).astype(jnp.float32), line_c), normal_two,
        slope, normal_one, rates, w_down, w_up, w_out, vec,
    )
    grads[item_name(4)] = low(matmul(hidden_low.T, du))
    grads[item_name(6)] = low(matmul(active.T, dm))
    grads[item_name(2)] = low(matmul(attended.T, dao))
    grads[item_name(8)] = low(matmul(own(pos_hot).T, own(grad_rows)))
    grads[item_name(3)] = (sums, 2)
    grads[item_name(5)] = (sums, 5)
    grads[item_name(7)] = (sums, 9)
    halves = reduce_cores(geo, pack_bucket(geo, buckets, 1, grads, coords))
    pieces_c = plus(*[tie(part, sums) for part in line_c_parts])
    da = tie(da, halves[0][0])
    back = attend_back(packed, stat, da, 0, 1)
    halves = [[tie(v, back[0]) for v in half] for half in halves]
    halves = reduce_plane(geo, halves, 0)
    if tiles_all > 1:
        da = tie(da, halves[0][0], halves[1][0])
        back = attend_back(packed, stat, da, 1, tiles_all - 1, back)
    dqkv, qv_sums = back
    halves = [[tie(v, dqkv) for v in half] for half in halves]
    halves = reduce_plane(geo, halves, 1)
    dqkv = tie(dqkv, halves[0][0], halves[1][0])
    grads[item_name(0)] = low(matmul(inputs.T, dqkv))
    grads[item_name(1)] = (qv_sums, 0)
    halves = [[tie(v, grads[item_name(0)]) for v in half] for half in halves]
    line_b_parts = reduce_line(geo, join(halves), my_doc)
    grads[item_name(0)] = tie(grads[item_name(0)], line_b_parts[0])
    halves = reduce_cores(geo, pack_bucket(geo, buckets, 0, grads, coords))
    halves = reduce_plane(geo, halves, 0)
    dqkv = tie(dqkv, halves[0][0], halves[1][0])
    token_grad = low(grad_one + matmul(dqkv, w_qkv.T))
    halves = [[tie(v, token_grad) for v in half] for half in halves]
    halves = reduce_plane(geo, halves, 1)
    pieces_b = plus(*line_b_parts)
    pieces_a = plus(*reduce_line(geo, join(halves), my_doc))

    owned = lax.all_to_all(jnp.concatenate([pieces_a, pieces_b, pieces_c]), AXES, 0, 0, tiled=True)
    natural = natural_rows(geo, table, owned.reshape(-1, LANES), pad_rows)
    gradient = natural[BLK : BLK + geo.chunk].reshape(-1)
    n_cls = n_doc * n_rows
    scaling, rating = (
        jnp.broadcast_to(
            lax.dynamic_index_in_dim(jnp.asarray(rates), me, 0, False)[:, None], (geo.chunk, LANES)
        ).reshape(-1)
        for rates in row_rates(geo, n_cls * SEG_LEN, n_cls)
    )
    weight, moment, smooth, copy_low = optimizer_step(
        gradient, master, momentum, average, scaling, rating
    )
    return (
        mixed_out[None],
        token_grad.reshape(1, seg_count, SEG_LEN, D),
        weight,
        moment,
        smooth,
        copy_low,
    )


def item_name(number):
    return item_list(0)[number].name


def solution(mesh):
    layer = P(AXES[1], AXES[0], None, None)
    ids = P(AXES[1], AXES[0])
    flat = P(AXES)
    return jax.shard_map(
        local,
        mesh=mesh,
        in_specs=(layer, layer, ids, ids, flat, flat, flat),
        out_specs=(layer, layer, flat, flat, flat, flat),
        check_vma=False,
    )
```

time: 1010 us -> 763 us (0.76)
  matrix products: 291 us -> 55 us
  Pallas kernels: 103 us -> 300 us
  waiting for transfers between devices: 328 us -> 225 us
  local copies, waits for them, and re-layouts: 75 us -> 27.5 us
  other arithmetic: 87.2 us -> 42.1 us
  starting transfers between devices: 68.3 us -> 42.4 us
  between operations: 2.93 us -> 15.1 us
    pallas_call x2 -> x11, Pallas kernels: 4.64 us -> 211 us  [the longest x4 72.1 us: in_parts(): pl.pallas_call(kernel, grid=(count,), in_specs=in_specs + [spec_any()] *...]
    dot_general x26 -> x7, matrix products: 251 us -> 55 us  [matmul(): return jnp.dot(left, right, preferred_element_type=jnp.float32)]
    ppermute x54 -> x39, waiting for transfers between devices: 319 us -> 208 us  [send(): return lax.ppermute(value, AXES, geo.shift(axis, step))]
    dot_general x12 -> x0, matrix products: 39.8 us -> none  [the longest x2 11.8 us: attend_backward(): jnp.einsum('bqhd,bkhd->bhqk', grad_heads, values, preferred_element_type=...]
    reduce_sum x19 -> x0, other arithmetic: 31.9 us -> none  [the longest x11 22.4 us: column_sum(): return jnp.sum(rows.astype(jnp.float32), axis=0)]
    convert_element_type x27 -> x3, other arithmetic: 30.2 us -> 2 us  [the longest x1 1.37 us: local(): own(grad_rows).astype(jnp.float32)]
    ppermute x54 -> x39, starting transfers between devices: 65.6 us -> 39 us  [send(): return lax.ppermute(value, AXES, geo.shift(axis, step))]
    convert_element_type x4 -> x18, other arithmetic: 1.17 us -> 22.5 us  [low(): return values.astype(jnp.bfloat16)]
  transfers between devices with their start and end apart: 55 -> 41, of which waited for: 25 -> 25; matrix products, arithmetic and copies ran while one was open for 8% -> 8% of each run, Pallas kernels for 6% -> 20%
where the time goes in v2:
time: 763 us; the launch traced here: 756 us
  Pallas kernels  300 us (39%)
  waiting for transfers between devices  225 us (29%)
  matrix products  55 us (7%)
  blocking collectives  48.4 us (6%)
  starting transfers between devices  42.4 us (6%)
  other arithmetic  42.1 us (6%)
  local copies, waits for them, and re-layouts  27.5 us (4%)
  between operations  15.1 us (2%)
    ppermute x39, waiting for transfers between devices, send(): return lax.ppermute(value, AXES, geo.shift(axis, step))  208 us
    pallas_call x4, Pallas kernels, in_parts(): pl.pallas_call(kernel, grid=(count,), in_specs=in_specs + [spec_any()] *...  72.1 us
    pallas_call x1, Pallas kernels, feed_layer(): pl.pallas_call(feed_kernel, grid=(n // TILE,), in_specs=[tiles(D), tiles(...  59.1 us
    dot_general x7, matrix products, matmul(): return jnp.dot(left, right, preferred_element_type=jnp.float32)  55 us
    pallas_call x9, Pallas kernels, unpack_matrix(): pl.pallas_call(kernel, out_shape=jax.ShapeDtypeStruct((depth, cols), jnp....  54 us
    pallas_call x1, Pallas kernels, feed_back(): pl.pallas_call(feed_back_kernel, grid=(n // TILE,), in_specs=[tiles(D), f...  43.9 us
    ppermute x39, starting transfers between devices, send(): return lax.ppermute(value, AXES, geo.shift(axis, step))  39 us
    all_to_all x1, blocking collectives, local(): lax.all_to_all(aligned.reshape(geo.n_dev, geo.piece, LANES), AXES, 0, 0,...  29.7 us
  transfers between devices with their start and end apart: 41, of which 25 were waited for; matrix products, arithmetic and copies ran while one was open for 8% of the time, Pallas kernels for 20%

profile of v2, /device:TPU:0, one launch (start us, length us, event | category | flops | bytes accessed | tf_op | source)
XLA Modules:
  0.0 755.9 jit_solution(10392285922993484037)
XLA Ops:
  11.4 9.3 %shard_map.145 = bf16[3584,128]{1,0:T(8,128)(2,1)} custom-call(s32[896]{0:T(1024)} %fusion.16.table_ref, f32[3544,128]{1,0:T(8,128)} %pad.8.rows_ref), custom_call_target="tpu_custom_call" | custom-call | tf_op jit(solution)/shard_map/pallas_call | solution.py:218
  20.7 29.7 %all_to_all.10 = bf16[32,112,128]{2,1,0:T(8,128)(2,1)S(1)} all-to-all(bf16[32,112,128]{2,1,0:T(8,128)(2,1)} %bitcast.183), channel_id=1, replica_groups=mesh['seg'=8,'doc'=4] {'seg','doc'}, dimensions={0} | all-to-all | bytes 1835008 | tf_op jit(solution)/shard_map/all_to_all | solution.py:1256
  57.2 7.8 %collective-permute-done.4 = bf16[4,112,128]{2,1,0:T(8,128)(2,1)S(1)} collective-permute-done((bf16[4,112,128]{2,1,0:T(8,128)(2,1)S(1)}, bf16[4,112,128]{2,1,0:T(8,128)(2,1)S(1)}, u32[]{:S(2)}, u32[]{:S(2)}) %collective-permute-start.4) | collective-permute-done | bytes 114720 | tf_op jit(solution)/shard_map/ppermute | solution.py:1153
  74.5 8.6 %collective-permute-done.9 = bf16[2,2,448,128]{3,2,1,0:T(8,128)(2,1)S(1)} collective-permute-done((bf16[2,2,448,128]{3,2,1,0:T(8,128)(2,1)S(1)}, bf16[2,2,448,128]{3,2,1,0:T(8,128)(2,1)S(1)}, u32[]{:S(2)}, u32[]{:S(2)}) %collective-permute-start.9) | collective-permute-done | bytes 458784 | tf_op jit(solution)/shard_map/ppermute | solution.py:1153
  99.2 9.5 %all_gather.12 = bf16[128,896]{1,0:T(8,128)(2,1)S(1)} all-gather(bf16[16,896]{1,0:T(8,128)(2,1)S(1)} %fusion.10), channel_id=1, replica_groups=mesh['seg'=8,'doc'=4] {'seg'}, dimensions={0}, use_global_device_ids=true | all-gather | bytes 258048 | tf_op jit(solution)/shard_map/all_gather | solution.py:1266
  111.8 11.9 %collective-permute-done = bf16[12,112,128]{2,1,0:T(8,128)(2,1)S(1)} collective-permute-done((bf16[12,112,128]{2,1,0:T(8,128)(2,1)S(1)}, bf16[12,112,128]{2,1,0:T(8,128)(2,1)S(1)}, u32[]{:S(2)}, u32[]{:S(2)}) %collective-permute-start) | collective-permute-done | bytes 344096 | tf_op jit(solution)/shard_map/ppermute | solution.py:1153
  123.7 32.0 %collective-permute-done.1 = bf16[12,112,128]{2,1,0:T(8,128)(2,1)S(1)} collective-permute-done((bf16[12,112,128]{2,1,0:T(8,128)(2,1)S(1)}, bf16[12,112,128]{2,1,0:T(8,128)(2,1)S(1)}, u32[]{:S(2)}, u32[]{:S(2)}) %collective-permute-start.1) | collective-permute-done | bytes 344096 | tf_op jit(solution)/shard_map/ppermute | solution.py:1153
  159.3 15.0 %collective-permute-done.14 = bf16[6,448,128]{2,1,0:T(8,128)(2,1)S(1)} collective-permute-done((bf16[6,448,128]{2,1,0:T(8,128)(2,1)S(1)}, bf16[6,448,128]{2,1,0:T(8,128)(2,1)S(1)}, u32[]{:S(2)}, u32[]{:S(2)}) %collective-permute-start.14) | collective-permute-done | bytes 688160 | tf_op jit(solution)/shard_map/ppermute | solution.py:1153
  181.5 22.7 %shard_map.148 = (bf16[2048,2304]{1,0:T(8,128)(2,1)}, bf16[2048,768]{1,0:T(8,128)(2,1)}, f32[2048,128]{1,0:T(8,128)}) custom-call(bf16[2048,768]{1,0:T(8,128)(2,1)} %bitcast.168, bf16[768,2304]{1,0:T(8,128)(2,1)} %shard_map.146.wqkv_ref, f32[16,768]{1,0:T(8,128)} %shard_map.147.vec_ref), custom_call_target="tpu_custom_call" | custom-call | tf_op jit(solution)/shard_map/pallas_call | solution.py:789
  204.3 28.7 %collective-permute-done.15 = bf16[2,6,448,128]{3,2,1,0:T(8,128)(2,1)S(1)} collective-permute-done((bf16[2,6,448,128]{3,2,1,0:T(8,128)(2,1)S(1)}, bf16[2,6,448,128]{3,2,1,0:T(8,128)(2,1)S(1)}, u32[]{:S(2)}, u32[]{:S(2)}) %collective-permute-start.15) | collective-permute-done | bytes 1376288 | tf_op jit(solution)/shard_map/ppermute | solution.py:1153
  242.9 9.4 %shard_map.149 = (bf16[2048,2304]{1,0:T(8,128)(2,1)}, bf16[2048,768]{1,0:T(8,128)(2,1)}, f32[2048,128]{1,0:T(8,128)}) custom-call(bf16[2048,768]{1,0:T(8,128)(2,1)} %bitcast.169, bf16[768,2304]{1,0:T(8,128)(2,1)} %shard_map.146.wqkv_ref, f32[16,768]{1,0:T(8,128)} %shard_map.147.vec_ref, ...), custom_call_target="tpu_custom_call", output_to_operand_aliasing={{0}: (3, {}), {1}: (4, {}), {2}: (5, {})} | custom-call | tf_op jit(solution)/shard_map/pallas_call | solution.py:789
  259.7 8.1 %shard_map.152.wdown_ref = bf16[3072,768]{1,0:T(8,128)(2,1)} custom-call(s32[4]{0:T(128)} %pad_add_fusion.coords_ref, bf16[2,2,6,448,128]{4,3,2,1,0:T(8,128)(2,1)} %pad_maximum_fusion.refs_4_.refs_0_, bf16[2,2,6,448,128]{4,3,2,1,0:T(8,128)(2,1)} %collective-permute-done.16.refs_5_.refs_1_, bf16[2,2,6,448,128]{4,3,2,1,0:T(8,128)(2,1)} %copy-done, ...), custom_call_target="tpu_custom_call" | custom-call | tf_op jit(solution)/shard_map/pallas_call | solution.py:367
  275.2 59.1 %shard_map.154 = (bf16[2048,768]{1,0:T(8,128)(2,1)}, bf16[2048,768]{1,0:T(8,128)(2,1)}, bf16[2048,3072]{1,0:T(8,128)(2,1)}, bf16[2048,3072]{1,0:T(8,128)(2,1)}, ...) custom-call(bf16[2048,768]{1,0:T(8,128)(2,1)} %bitcast.170, ...), custom_call_target="tpu_custom_call" | custom-call | tf_op jit(solution)/shard_map/pallas_call | solution.py:876
  346.2 8.1 %shard_map.159.wdown_ref = bf16[3072,768]{1,0:T(8,128)(2,1)} custom-call(s32[4]{0:T(128)} %pad_add_fusion.coords_ref, bf16[32,16,112,128]{3,2,1,0:T(8,128)(2,1)} %bitcast.165), custom_call_target="tpu_custom_call" | custom-call | tf_op jit(solution)/shard_map/pallas_call | solution.py:367
  365.9 9.3 %all_gather.15.rows_ref = bf16[128,768]{1,0:T(8,128)(2,1)} all-gather(bf16[16,768]{1,0:T(8,128)(2,1)S(1)} %add_convert_fusion.13), channel_id=1, replica_groups=mesh['seg'=8,'doc'=4] {'seg'}, dimensions={0}, use_global_device_ids=true | all-gather | bytes 221184 | tf_op jit(solution)/shard_map/all_gather | solution.py:1310
  376.6 17.4 %shard_map.161 = (bf16[128,768]{1,0:T(8,128)(2,1)}, bf16[128,768]{1,0:T(8,128)(2,1)}, f32[16,768]{1,0:T(8,128)}, bf16[128,2304]{1,0:T(8,128)(2,1)}, bf16[128,768...) custom-call(bf16[128,768]{1,0:T(8,128)(2,1)} %all_gather.15.rows_ref, ...), custom_call_target="tpu_custom_call" | custom-call | tf_op jit(solution)/shard_map/pallas_call | solution.py:1130
  397.0 12.8 %shard_map.162 = bf16[16,448,128]{2,1,0:T(8,128)(2,1)} custom-call(s32[1]{0:T(128)} %bitcast.41.seg_ref, bf16[64,128]{1,0:T(8,128)(2,1)} %fusion.9.refs_0_, bf16[768,128]{1,0:T(8,128)(2,1)} %get-tuple-element.99.refs_1_, bf16[768,128]{1,0:T(8,128)(2,1)} %get-tuple-element.100.refs_2_, bf16[768,128]{1,0:T(8,128)(2,1)} %get-tuple-element.101.refs_3_, ...), custom_call_target="tpu_custom_call" | custom-call | tf_op jit(solution)/shard_map/pallas_call | solution.py:661
  409.8 43.9 %shard_map.163 = (bf16[2048,768]{1,0:T(8,128)(2,1)}, bf16[2048,3072]{1,0:T(8,128)(2,1)}, bf16[2048,768]{1,0:T(8,128)(2,1)}, bf16[2048,768]{1,0:T(8,128)(2,1)}, f32[2048,768]{1,0:T(8,128)}, /*index=5*/f32[16,768]{1,0:T(8,128)}) custom-call(bf16[2048,768]{1,0:T(8,128)(2,1)} %bitcast.172, f32[16,768]{1,0:T(8,128)} %get-tuple-element.108.cls_ref, ...), custom_call_target="tpu_custom_call" | custom-call | tf_op jit(solution)/shard_map/pallas_call | solution.py:954
  459.4 14.9 %convolution_convert_fusion.1.refs_4_ = bf16[3072,768]{1,0:T(8,128)(2,1)} fusion(bf16[2048,3072]{1,0:T(8,128)(2,1)} %get-tuple-element.121, bf16[2048,768]{1,0:T(8,128)(2,1)S(1)} %copy-done.28), kind=kOutput, calls=%fused_computation.4 | convolution fusion | flops 9666035712 | bytes 20447232 | tf_op jit(solution)/shard_map/dot_general | solution.py:1233
  474.3 12.0 %convolution_convert_fusion.2.refs_2_ = bf16[768,3072]{1,0:T(8,128)(2,1)} fusion(bf16[2048,768]{1,0:T(8,128)(2,1)S(1)} %copy-done.27, bf16[2048,3072]{1,0:T(8,128)(2,1)S(1)} %bitcast.201), kind=kOutput, calls=%fused_computation.5 | convolution fusion | flops 9666035712 | bytes 20447232 | tf_op jit(solution)/shard_map/dot_general | solution.py:1233
  486.3 10.7 %shard_map.164 = (bf16[2,2,6,448,128]{4,3,2,1,0:T(8,128)(2,1)}, bf16[2,2,6,448,128]{4,3,2,1,0:T(8,128)(2,1)}, bf16[2,2,6,448,128]{4,3,2,1,0:T(8,128)(2,1)}, bf16[2,2,6,448,128]{4,3,2,1,0:T(8,128)(2,1)}) custom-call(s32[4]{0:T(128)} %pad_add_fusion.coords_ref, bf16[768,768]{1,0:T(8,128)(2,1)} %convolution_convert_fusion.3.refs_0_.refs_2_, ...), custom_call_target="tpu_custom_call" | custom-call | tf_op jit(solution)/shard_map/pallas_call | solution.py:568
  499.0 11.9 %shard_map.165 = (bf16[2048,2304]{1,0:T(8,128)(2,1)}, f32[8,768]{1,0:T(8,128)}) custom-call(bf16[2048,2304]{1,0:T(8,128)(2,1)} %get-tuple-element.114.packed_ref, f32[2048,128]{1,0:T(8,128)} %get-tuple-element.115.stat_ref, bf16[2048,768]{1,0:T(8,128)(2,1)} %get-tuple-element.133.da_ref, f32[8,768]{1,0:T(8,128)} %broadcast_in_dim.53.before_ref), custom_call_target="tpu_custom_call" | custom-call | tf_op jit(solution)/shard_map/pallas_call | solution.py:789
  522.8 28.1 %shard_map.166 = (bf16[2048,2304]{1,0:T(8,128)(2,1)}, f32[8,768]{1,0:T(8,128)}) custom-call(bf16[2048,2304]{1,0:T(8,128)(2,1)} %get-tuple-element.114.packed_ref, f32[2048,128]{1,0:T(8,128)} %get-tuple-element.115.stat_ref, bf16[2048,768]{1,0:T(8,128)(2,1)} %get-tuple-element.133.da_ref, ...), custom_call_target="tpu_custom_call", output_to_operand_aliasing={{0}: (4, {})} | custom-call | tf_op jit(solution)/shard_map/pallas_call | solution.py:789
  557.5 10.1 %fusion.refs_0_ = bf16[768,2304]{1,0:T(8,128)(2,1)} fusion(bf16[2048,2304]{1,0:T(8,128)(2,1)S(1)} %copy-done.7, bf16[2048,768]{1,0:T(8,128)(2,1)S(1)} %bitcast.171), kind=kOutput, calls=%fused_computation.6 | convolution fusion | flops 7249526784 | bytes 16121856 | tf_op jit(solution)/shard_map/dot_general | solution.py:1233
  579.7 8.6 %collective-permute-done.33 = bf16[12,112,128]{2,1,0:T(8,128)(2,1)S(1)} collective-permute-done((bf16[12,112,128]{2,1,0:T(8,128)(2,1)}, bf16[12,112,128]{2,1,0:T(8,128)(2,1)S(1)}, u32[]{:S(2)}, u32[]{:S(2)}) %collective-permute-start.33) | collective-permute-done | bytes 344096 | tf_op jit(solution)/shard_map/ppermute | solution.py:1153
  593.7 14.5 %collective-permute-done.34 = bf16[12,112,128]{2,1,0:T(8,128)(2,1)} collective-permute-done((bf16[12,112,128]{2,1,0:T(8,128)(2,1)S(1)}, bf16[12,112,128]{2,1,0:T(8,128)(2,1)}, u32[]{:S(2)}, u32[]{:S(2)}) %collective-permute-start.34) | collective-permute-done | bytes 344096 | tf_op jit(solution)/shard_map/ppermute | solution.py:1153
  618.5 12.1 %collective-permute-done.38 = bf16[16,112,128]{2,1,0:T(8,128)(2,1)S(1)} collective-permute-done((bf16[16,112,128]{2,1,0:T(8,128)(2,1)S(1)}, bf16[16,112,128]{2,1,0:T(8,128)(2,1)S(1)}, u32[]{:S(2)}, u32[]{:S(2)}) %collective-permute-start.38) | collective-permute-done | bytes 458784 | tf_op jit(solution)/shard_map/ppermute | solution.py:1153
  630.6 26.2 %collective-permute-done.37 = bf16[16,112,128]{2,1,0:T(8,128)(2,1)S(1)} collective-permute-done((bf16[16,112,128]{2,1,0:T(8,128)(2,1)S(1)}, bf16[16,112,128]{2,1,0:T(8,128)(2,1)S(1)}, u32[]{:S(2)}, u32[]{:S(2)}) %collective-permute-start.37) | collective-permute-done | bytes 458784 | tf_op jit(solution)/shard_map/ppermute | solution.py:1153
  660.1 9.5 %fusion.23 = f32[2048,768]{1,0:T(8,128)} fusion(bf16[2048,2304]{1,0:T(8,128)(2,1)S(1)} %bitcast.174, bf16[768,2304]{1,0:T(8,128)(2,1)S(1)} %copy-done.1), kind=kOutput, calls=%fused_computation.121 | convolution fusion | flops 7247757312 | bytes 19267584 | tf_op jit(solution)/shard_map/dot_general | solution.py:1233
  678.2 10.1 %collective-permute-done.28 = bf16[2,2,448,128]{3,2,1,0:T(8,128)(2,1)S(1)} collective-permute-done((bf16[2,2,448,128]{3,2,1,0:T(8,128)(2,1)S(1)}, bf16[2,2,448,128]{3,2,1,0:T(8,128)(2,1)S(1)}, u32[]{:S(2)}, u32[]{:S(2)}) %collective-permute-start.28) | collective-permute-done | bytes 458784 | tf_op jit(solution)/shard_map/ppermute | solution.py:1153
  715.1 17.4 %all-to-all-done.1 = bf16[32,112,128]{2,1,0:T(8,128)(2,1)S(1)} async-done(((bf16[32,112,128]{2,1,0:T(8,128)(2,1)}), bf16[32,112,128]{2,1,0:T(8,128)(2,1)S(1)}, u32[]{:S(2)}, u32[]{:S(2)}) %all-to-all-start.1) | async-done | bytes 917536 | tf_op jit(solution)/shard_map/all_to_all | solution.py:1368
  733.4 8.9 %shard_map.168 = f32[3544,128]{1,0:T(8,128)} custom-call(s32[896]{0:T(1024)} %fusion.16.table_ref, bf16[3584,128]{1,0:T(8,128)(2,1)} %bitcast.182), custom_call_target="tpu_custom_call" | custom-call | tf_op jit(solution)/shard_map/pallas_call | solution.py:247
  (252 shorter events, 202.5 us)
Async XLA Ops:
  7.2 327.2 %all-gather.3.cloned.1.call-start = ((), (), s32[]{:S(2)}) async-start(), calls=%async_computation.2 | async-start | bytes 15138816 | tf_op jit(solution)/shard_map/all_gather | solution.py:1286
  53.5 11.5 %collective-permute-start.5 = (bf16[4,112,128]{2,1,0:T(8,128)(2,1)S(1)}, bf16[4,112,128]{2,1,0:T(8,128)(2,1)S(1)}, u32[]{:S(2)}, u32[]{:S(2)}) collective-permute-start(bf16[4,112,128]{2,1,0:T(8,128)(2,1)S(1)} %slice.122), channel_id=1, source_target_pairs={{0,1},{1,2},{2,3},{3,0},{4,5},{5,6},{6,7},{7,4},{8,9},{9,10},{10,1... | collective-permute-start | bytes 344072 | tf_op jit(solution)/shard_map/ppermute | solution.py:1153
  53.6 11.5 %collective-permute-start.4 = (bf16[4,112,128]{2,1,0:T(8,128)(2,1)S(1)}, bf16[4,112,128]{2,1,0:T(8,128)(2,1)S(1)}, u32[]{:S(2)}, u32[]{:S(2)}) collective-permute-start(bf16[4,112,128]{2,1,0:T(8,128)(2,1)S(1)} %slice.122), channel_id=1, source_target_pairs={{0,2},{1,3},{2,0},{3,1},{4,6},{5,7},{6,4},{7,5},{8,10},{9,11},{10,... | collective-permute-start | bytes 344072 | tf_op jit(solution)/shard_map/ppermute | solution.py:1153
  72.1 11.0 %collective-permute-start.9 = (bf16[2,2,448,128]{3,2,1,0:T(8,128)(2,1)S(1)}, bf16[2,2,448,128]{3,2,1,0:T(8,128)(2,1)S(1)}, u32[]{:S(2)}, u32[]{:S(2)}) collective-permute-start(bf16[2,2,448,128]{3,2,1,0:T(8,128)(2,1)S(1)} %get-tuple-element.198), channel_id=1, source_target_pairs={{0,8},{1,9},{2,10},{3,11},{4,12},{5,13},{6,14},{7,15},{8,0},{9,1},... | collective-permute-start | bytes 1376264 | tf_op jit(solution)/shard_map/ppermute | solution.py:1153
  73.5 11.2 %collective-permute-start.7 = (bf16[2,2,448,128]{3,2,1,0:T(8,128)(2,1)S(1)}, bf16[2,2,448,128]{3,2,1,0:T(8,128)(2,1)S(1)}, u32[]{:S(2)}, u32[]{:S(2)}) collective-permute-start(bf16[2,2,448,128]{3,2,1,0:T(8,128)(2,1)S(1)} %get-tuple-element.200), channel_id=1, source_target_pairs={{0,16},{1,17},{2,18},{3,19},{4,20},{5,21},{6,22},{7,23},{8,24},{9,... | collective-permute-start | bytes 1376264 | tf_op jit(solution)/shard_map/ppermute | solution.py:1153
  108.7 15.0 %collective-permute-start = (bf16[12,112,128]{2,1,0:T(8,128)(2,1)S(1)}, bf16[12,112,128]{2,1,0:T(8,128)(2,1)S(1)}, u32[]{:S(2)}, u32[]{:S(2)}) collective-permute-start(bf16[12,112,128]{2,1,0:T(8,128)(2,1)S(1)} %slice.120), channel_id=1, source_target_pairs={{0,3},{1,0},{2,1},{3,2},{4,7},{5,4},{6,5},{7,6},{8,11},{9,8},{10,9... | collective-permute-start | bytes 1032200 | tf_op jit(solution)/shard_map/ppermute | solution.py:1153
  111.1 44.6 %collective-permute-start.1 = (bf16[12,112,128]{2,1,0:T(8,128)(2,1)S(1)}, bf16[12,112,128]{2,1,0:T(8,128)(2,1)S(1)}, u32[]{:S(2)}, u32[]{:S(2)}) collective-permute-start(bf16[12,112,128]{2,1,0:T(8,128)(2,1)S(1)} %slice.120), channel_id=1, source_target_pairs={{0,2},{1,3},{2,0},{3,1},{4,6},{5,7},{6,4},{7,5},{8,10},{9,11},{10,... | collective-permute-start | bytes 1032200 | tf_op jit(solution)/shard_map/ppermute | solution.py:1153
  111.1 44.6 %collective-permute-start.2 = (bf16[12,112,128]{2,1,0:T(8,128)(2,1)S(1)}, bf16[12,112,128]{2,1,0:T(8,128)(2,1)S(1)}, u32[]{:S(2)}, u32[]{:S(2)}) collective-permute-start(bf16[12,112,128]{2,1,0:T(8,128)(2,1)S(1)} %slice.120), channel_id=1, source_target_pairs={{0,1},{1,2},{2,3},{3,0},{4,5},{5,6},{6,7},{7,4},{8,9},{9,10},{10,1... | collective-permute-start | bytes 1032200 | tf_op jit(solution)/shard_map/ppermute | solution.py:1153
  156.9 17.4 %collective-permute-start.14 = (bf16[6,448,128]{2,1,0:T(8,128)(2,1)S(1)}, bf16[6,448,128]{2,1,0:T(8,128)(2,1)S(1)}, u32[]{:S(2)}, u32[]{:S(2)}) collective-permute-start(bf16[6,448,128]{2,1,0:T(8,128)(2,1)S(1)} %get-tuple-element.184), channel_id=1, source_target_pairs={{0,16},{1,17},{2,18},{3,19},{4,20},{5,21},{6,22},{7,23},{8,24},{9,... | collective-permute-start | bytes 2064392 | tf_op jit(solution)/shard_map/ppermute | solution.py:1153
  157.9 18.1 %collective-permute-start.10 = (bf16[6,448,128]{2,1,0:T(8,128)(2,1)S(1)}, bf16[6,448,128]{2,1,0:T(8,128)(2,1)S(1)}, u32[]{:S(2)}, u32[]{:S(2)}) collective-permute-start(bf16[6,448,128]{2,1,0:T(8,128)(2,1)S(1)} %get-tuple-element.185), channel_id=1, source_target_pairs={{0,8},{1,9},{2,10},{3,11},{4,12},{5,13},{6,14},{7,15},{8,0},{9,1},... | collective-permute-start | bytes 2064392 | tf_op jit(solution)/shard_map/ppermute | solution.py:1153
  175.6 57.4 %collective-permute-start.15 = (bf16[2,6,448,128]{3,2,1,0:T(8,128)(2,1)S(1)}, bf16[2,6,448,128]{3,2,1,0:T(8,128)(2,1)S(1)}, u32[]{:S(2)}, u32[]{:S(2)}) collective-permute-start(bf16[2,6,448,128]{3,2,1,0:T(8,128)(2,1)S(1)} %get-tuple-element.181), channel_id=1, source_target_pairs={{0,8},{1,9},{2,10},{3,11},{4,12},{5,13},{6,14},{7,15},{8,0},{9,1},... | collective-permute-start | bytes 4128776 | tf_op jit(solution)/shard_map/ppermute | solution.py:1153
  177.8 58.8 %collective-permute-start.11 = (bf16[2,6,448,128]{3,2,1,0:T(8,128)(2,1)}, bf16[2,6,448,128]{3,2,1,0:T(8,128)(2,1)}, u32[]{:S(2)}, u32[]{:S(2)}) collective-permute-start(bf16[2,6,448,128]{3,2,1,0:T(8,128)(2,1)} %get-tuple-element.187), channel_id=1, source_target_pairs={{0,16},{1,17},{2,18},{3,19},{4,20},{5,21},{6,22},{7,23},{8,24},{9,... | collective-permute-start | bytes 4128776 | tf_op jit(solution)/shard_map/ppermute | solution.py:1153
  240.7 11.6 %collective-permute-start.16 = (bf16[2,2,6,448,128]{4,3,2,1,0:T(8,128)(2,1)}, bf16[2,2,6,448,128]{4,3,2,1,0:T(8,128)(2,1)}, u32[]{:S(2)}, u32[]{:S(2)}) collective-permute-start(bf16[2,2,6,448,128]{4,3,2,1,0:T(8,128)(2,1)} %pad_maximum_fusion.refs_4_.refs_0_), channel_id=1, source_target_pairs={{0,4},{1,5},{2,6},{3,7},{4,0},{5,1},{6,2},{7,3},{8,12},{9,13},{10,... | collective-permute-start | bytes 8257544 | tf_op jit(solution)/shard_map/ppermute | solution.py:1153
  240.7 12.7 %collective-permute-start.17 = (bf16[2,2,6,448,128]{4,3,2,1,0:T(8,128)(2,1)S(1)}, bf16[2,2,6,448,128]{4,3,2,1,0:T(8,128)(2,1)}, u32[]{:S(2)}, u32[]{:S(2)}) collective-permute-start(bf16[2,2,6,448,128]{4,3,2,1,0:T(8,128)(2,1)S(1)} %pad_maximum_fusion.1.refs_6_.refs_2_), channel_id=1, source_target_pairs={{0,4},{1,5},{2,6},{3,7},{4,0},{5,1},{6,2},{7,3},{8,12},{9,13},{10,... | collective-permute-start | bytes 8257544 | tf_op jit(solution)/shard_map/ppermute | solution.py:1153
  497.0 13.9 %collective-permute-start.19 = (bf16[2,2,6,448,128]{4,3,2,1,0:T(8,128)(2,1)}, bf16[2,2,6,448,128]{4,3,2,1,0:T(8,128)(2,1)S(1)}, u32[]{:S(2)}, u32[]{:S(2)}) collective-permute-start(bf16[2,2,6,448,128]{4,3,2,1,0:T(8,128)(2,1)} %get-tuple-element.131), channel_id=1, source_target_pairs={{0,4},{1,5},{2,6},{3,7},{4,0},{5,1},{6,2},{7,3},{8,12},{9,13},{10,... | collective-permute-start | bytes 8257544 | tf_op jit(solution)/shard_map/ppermute | solution.py:1153
  498.3 12.6 %collective-permute-start.18 = (bf16[2,2,6,448,128]{4,3,2,1,0:T(8,128)(2,1)}, bf16[2,2,6,448,128]{4,3,2,1,0:T(8,128)(2,1)}, u32[]{:S(2)}, u32[]{:S(2)}) collective-permute-start(bf16[2,2,6,448,128]{4,3,2,1,0:T(8,128)(2,1)} %get-tuple-element.127), channel_id=1, source_target_pairs={{0,4},{1,5},{2,6},{3,7},{4,0},{5,1},{6,2},{7,3},{8,12},{9,13},{10,... | collective-permute-start | bytes 8257544 | tf_op jit(solution)/shard_map/ppermute | solution.py:1153
  517.3 33.6 %collective-permute-start.20 = (bf16[2,6,448,128]{3,2,1,0:T(8,128)(2,1)}, bf16[2,6,448,128]{3,2,1,0:T(8,128)(2,1)}, u32[]{:S(2)}, u32[]{:S(2)}) collective-permute-start(bf16[2,6,448,128]{3,2,1,0:T(8,128)(2,1)} %get-tuple-element.167), channel_id=1, source_target_pairs={{0,16},{1,17},{2,18},{3,19},{4,20},{5,21},{6,22},{7,23},{8,24},{9,... | collective-permute-start | bytes 4128776 | tf_op jit(solution)/shard_map/ppermute | solution.py:1153
  521.2 32.8 %collective-permute-start.21 = (bf16[2,6,448,128]{3,2,1,0:T(8,128)(2,1)}, bf16[2,6,448,128]{3,2,1,0:T(8,128)(2,1)}, u32[]{:S(2)}, u32[]{:S(2)}) collective-permute-start(bf16[2,6,448,128]{3,2,1,0:T(8,128)(2,1)} %get-tuple-element.165), channel_id=1, source_target_pairs={{0,8},{1,9},{2,10},{3,11},{4,12},{5,13},{6,14},{7,15},{8,0},{9,1},... | collective-permute-start | bytes 4128776 | tf_op jit(solution)/shard_map/ppermute | solution.py:1153
  552.8 20.9 %collective-permute-start.22 = (bf16[6,448,128]{2,1,0:T(8,128)(2,1)S(1)}, bf16[6,448,128]{2,1,0:T(8,128)(2,1)S(1)}, u32[]{:S(2)}, u32[]{:S(2)}) collective-permute-start(bf16[6,448,128]{2,1,0:T(8,128)(2,1)S(1)} %get-tuple-element.176), channel_id=1, source_target_pairs={{0,8},{1,9},{2,10},{3,11},{4,12},{5,13},{6,14},{7,15},{8,0},{9,1},... | collective-permute-start | bytes 2064392 | tf_op jit(solution)/shard_map/ppermute | solution.py:1153
  556.7 17.1 %collective-permute-start.23 = (bf16[6,448,128]{2,1,0:T(8,128)(2,1)S(1)}, bf16[6,448,128]{2,1,0:T(8,128)(2,1)S(1)}, u32[]{:S(2)}, u32[]{:S(2)}) collective-permute-start(bf16[6,448,128]{2,1,0:T(8,128)(2,1)S(1)} %get-tuple-element.178), channel_id=1, source_target_pairs={{0,16},{1,17},{2,18},{3,19},{4,20},{5,21},{6,22},{7,23},{8,24},{9,... | collective-permute-start | bytes 2064392 | tf_op jit(solution)/shard_map/ppermute | solution.py:1153
  575.2 13.0 %collective-permute-start.33 = (bf16[12,112,128]{2,1,0:T(8,128)(2,1)}, bf16[12,112,128]{2,1,0:T(8,128)(2,1)S(1)}, u32[]{:S(2)}, u32[]{:S(2)}) collective-permute-start(bf16[12,112,128]{2,1,0:T(8,128)(2,1)} %get-tuple-element.173), channel_id=1, source_target_pairs={{0,1},{1,2},{2,3},{3,0},{4,5},{5,6},{6,7},{7,4},{8,9},{9,10},{10,1... | collective-permute-start | bytes 1032200 | tf_op jit(solution)/shard_map/ppermute | solution.py:1153
  575.2 17.7 %collective-permute-start.35 = (bf16[12,112,128]{2,1,0:T(8,128)(2,1)}, bf16[12,112,128]{2,1,0:T(8,128)(2,1)S(1)}, u32[]{:S(2)}, u32[]{:S(2)}) collective-permute-start(bf16[12,112,128]{2,1,0:T(8,128)(2,1)} %get-tuple-element.174), channel_id=1, source_target_pairs={{0,3},{1,0},{2,1},{3,2},{4,7},{5,4},{6,5},{7,6},{8,11},{9,8},{10,9... | collective-permute-start | bytes 1032200 | tf_op jit(solution)/shard_map/ppermute | solution.py:1153
  579.0 29.2 %collective-permute-start.34 = (bf16[12,112,128]{2,1,0:T(8,128)(2,1)S(1)}, bf16[12,112,128]{2,1,0:T(8,128)(2,1)}, u32[]{:S(2)}, u32[]{:S(2)}) collective-permute-start(bf16[12,112,128]{2,1,0:T(8,128)(2,1)S(1)} %get-tuple-element.175), channel_id=1, source_target_pairs={{0,2},{1,3},{2,0},{3,1},{4,6},{5,7},{6,4},{7,5},{8,10},{9,11},{10,... | collective-permute-start | bytes 1032200 | tf_op jit(solution)/shard_map/ppermute | solution.py:1153
  615.6 41.2 %collective-permute-start.24 = (bf16[2,2,2,448,128]{4,3,2,1,0:T(8,128)(2,1)}, bf16[2,2,2,448,128]{4,3,2,1,0:T(8,128)(2,1)S(1)}, u32[]{:S(2)}, u32[]{:S(2)}) collective-permute-start(bf16[2,2,2,448,128]{4,3,2,1,0:T(8,128)(2,1)} %get-tuple-element.148), channel_id=1, source_target_pairs={{0,4},{1,5},{2,6},{3,7},{4,0},{5,1},{6,2},{7,3},{8,12},{9,13},{10,... | collective-permute-start | bytes 2752520 | tf_op jit(solution)/shard_map/ppermute | solution.py:1153
  615.9 14.7 %collective-permute-start.38 = (bf16[16,112,128]{2,1,0:T(8,128)(2,1)S(1)}, bf16[16,112,128]{2,1,0:T(8,128)(2,1)S(1)}, u32[]{:S(2)}, u32[]{:S(2)}) collective-permute-start(bf16[16,112,128]{2,1,0:T(8,128)(2,1)S(1)} %get-tuple-element.170), channel_id=1, source_target_pairs={{0,3},{1,0},{2,1},{3,2},{4,7},{5,4},{6,5},{7,6},{8,11},{9,8},{10,9... | collective-permute-start | bytes 1376264 | tf_op jit(solution)/shard_map/ppermute | solution.py:1153
  617.9 39.0 %collective-permute-start.37 = (bf16[16,112,128]{2,1,0:T(8,128)(2,1)S(1)}, bf16[16,112,128]{2,1,0:T(8,128)(2,1)S(1)}, u32[]{:S(2)}, u32[]{:S(2)}) collective-permute-start(bf16[16,112,128]{2,1,0:T(8,128)(2,1)S(1)} %get-tuple-element.171), channel_id=1, source_target_pairs={{0,2},{1,3},{2,0},{3,1},{4,6},{5,7},{6,4},{7,5},{8,10},{9,11},{10,... | collective-permute-start | bytes 1376264 | tf_op jit(solution)/shard_map/ppermute | solution.py:1153
  617.9 39.0 %collective-permute-start.36 = (bf16[16,112,128]{2,1,0:T(8,128)(2,1)S(1)}, bf16[16,112,128]{2,1,0:T(8,128)(2,1)S(1)}, u32[]{:S(2)}, u32[]{:S(2)}) collective-permute-start(bf16[16,112,128]{2,1,0:T(8,128)(2,1)S(1)} %get-tuple-element.172), channel_id=1, source_target_pairs={{0,1},{1,2},{2,3},{3,0},{4,5},{5,6},{6,7},{7,4},{8,9},{9,10},{10,1... | collective-permute-start | bytes 1376264 | tf_op jit(solution)/shard_map/ppermute | solution.py:1153
  618.5 40.0 %collective-permute-start.25 = (bf16[2,2,2,448,128]{4,3,2,1,0:T(8,128)(2,1)S(1)}, bf16[2,2,2,448,128]{4,3,2,1,0:T(8,128)(2,1)S(1)}, u32[]{:S(2)}, u32[]{:S(2)}) collective-permute-start(bf16[2,2,2,448,128]{4,3,2,1,0:T(8,128)(2,1)S(1)} %copy-done.29), channel_id=1, source_target_pairs={{0,4},{1,5},{2,6},{3,7},{4,0},{5,1},{6,2},{7,3},{8,12},{9,13},{10,... | collective-permute-start | bytes 2752520 | tf_op jit(solution)/shard_map/ppermute | solution.py:1153
  658.1 18.0 %collective-permute-start.26 = (bf16[2,2,448,128]{3,2,1,0:T(8,128)(2,1)S(1)}, bf16[2,2,448,128]{3,2,1,0:T(8,128)(2,1)}, u32[]{:S(2)}, u32[]{:S(2)}) collective-permute-start(bf16[2,2,448,128]{3,2,1,0:T(8,128)(2,1)S(1)} %get-tuple-element.188), channel_id=1, source_target_pairs={{0,16},{1,17},{2,18},{3,19},{4,20},{5,21},{6,22},{7,23},{8,24},{9,... | collective-permute-start | bytes 1376264 | tf_op jit(solution)/shard_map/ppermute | solution.py:1153
  674.9 13.4 %collective-permute-start.28 = (bf16[2,2,448,128]{3,2,1,0:T(8,128)(2,1)S(1)}, bf16[2,2,448,128]{3,2,1,0:T(8,128)(2,1)S(1)}, u32[]{:S(2)}, u32[]{:S(2)}) collective-permute-start(bf16[2,2,448,128]{3,2,1,0:T(8,128)(2,1)S(1)} %get-tuple-element.190), channel_id=1, source_target_pairs={{0,8},{1,9},{2,10},{3,11},{4,12},{5,13},{6,14},{7,15},{8,0},{9,1},... | collective-permute-start | bytes 1376264 | tf_op jit(solution)/shard_map/ppermute | solution.py:1153
  677.2 14.7 %collective-permute-start.27 = (bf16[2,448,128]{2,1,0:T(8,128)(2,1)S(1)}, bf16[2,448,128]{2,1,0:T(8,128)(2,1)S(1)}, u32[]{:S(2)}, u32[]{:S(2)}) collective-permute-start(bf16[2,448,128]{2,1,0:T(8,128)(2,1)S(1)} %slice_bitcast_fusion.14), channel_id=1, source_target_pairs={{0,8},{1,9},{2,10},{3,11},{4,12},{5,13},{6,14},{7,15},{8,0},{9,1},... | collective-permute-start | bytes 688136 | tf_op jit(solution)/shard_map/ppermute | solution.py:1153
  706.8 25.7 %all-to-all-start.1 = ((bf16[32,112,128]{2,1,0:T(8,128)(2,1)}), bf16[32,112,128]{2,1,0:T(8,128)(2,1)S(1)}, u32[]{:S(2)}, u32[]{:S(2)}) async-start(bf16[32,112,128]{2,1,0:T(8,128)(2,1)} %pad_maximum_fusion.7), calls=%async_computation.1 | async-start | bytes 1835008 | tf_op jit(solution)/shard_map/all_to_all | solution.py:1368
  (49 other events, 652.8 us)
Sparse Core Ops, SparseCore 0:
  94.5 159.4 all-gather.2

commit v3 on v2

--- a/solution.py
+++ b/solution.py
@@ -97,6 +97,8 @@
         self.piece_blocks = -(-most // self.n_dev)
         self.piece = self.piece_blocks * BLK
         self.slots = self.piece_blocks * self.n_dev
+        self.groups = -(-most // (self.piece_blocks * n_doc))
+        self.staged_rows = self.groups * n_doc * self.piece
         self.c_size, self.x_size = 2, 2
         self.y_size = n_seg // 4
 
@@ -106,29 +108,38 @@
         first, last = max(0, -(-lo // rows)), min(item.rows, hi) // rows
         return first, max(first, last)
 
-    def block_table(self):
-        table = np.zeros((self.n_dev, 4, self.slots), np.int32)
+    def block_tables(self):
+        matrices = [item for item in self.items if item.cols]
+        single = [[] for _ in range(self.n_dev)]
+        groups = np.zeros((self.n_dev, len(matrices), 3), np.int32)
         for n in range(self.n_dev):
             lo, hi = n * self.chunk, (n + 1) * self.chunk
             for t in range(self.slots):
                 b = self.first[n] + t
                 if b > self.last[n]:
+                    single[n].append((t, 0, 0, 0))
                     continue
                 item = [it for it in self.items if it.blk <= b][-1]
                 at = b - item.blk
                 if item.cols:
                     first, last = self.full_groups(item, n)
-                    group, column = divmod(at, item.cols)
-                    if first <= group < last:
-                        start = item.nat + group * BLK * item.cols + column - lo
-                        table[n, :, t] = (start, 0, BLK, item.cols)
+                    if first <= at // item.cols < last:
                         continue
                 start = item.nat + at * BLK
                 a = max(start, lo)
-                z = min(start + BLK, hi, item.nat + item.rows)
-                if a < z:
-                    table[n, :, t] = (start - lo, a - start, z - start, 0)
-        return table
+                z = max(a, min(start + BLK, hi, item.nat + item.rows))
+                single[n].append((t, start - lo, a - start, z - start))
+            for i, item in enumerate(matrices):
+                first, last = self.full_groups(item, n)
+                if first < last:
+                    slot = item.blk + first * item.cols - self.first[n]
+                    groups[n, i] = (slot, item.nat + first * BLK * item.cols - lo, last - first)
+        most = max(len(rows) for rows in single)
+        table = np.zeros((self.n_dev, 1 + 4 * most), np.int32)
+        for n, rows in enumerate(single):
+            table[n, 0] = len(rows)
+            table[n, 1 : 1 + 4 * len(rows)] = np.asarray(rows, np.int32).reshape(-1)
+        return matrices, np.concatenate([groups.reshape(self.n_dev, -1), table], axis=1)
 
     def chunks_of(self, item):
         found = []
@@ -140,12 +151,9 @@
                 found.append((n, a - item.blk, b - item.blk, a - self.first[n]))
         return found
 
-    def buckets(self):
-        end_attention = self.by_name.w_out.nat
-        end_segment = self.by_name.pos_table.nat
-        a = (end_attention - 1) // self.chunk + 1
-        b = (end_segment - 1) // self.chunk + 1
-        return [range(0, a), range(a, b), range(b, self.n_dev)]
+    def spans(self, *ends):
+        cuts = [0] + [(end.nat - 1) // self.chunk + 1 for end in ends] + [self.n_dev]
+        return [range(a, b) for a, b in zip(cuts, cuts[1:])]
 
     def coords(self, device):
         seg, doc = divmod(device, self.n_doc)
@@ -181,39 +189,47 @@
     return pltpu.CompilerParams(vmem_limit_bytes=mib * 1024 * 1024)
 
 
+def cost(micros):
+    return pl.CostEstimate(flops=int(micros * 1e9), bytes_accessed=int(micros * 3e6), transcendentals=0)
+
+
 def row_mask(low, high):
     rows = lax.broadcasted_iota(jnp.int32, (BLK, LANES), 0)
     return (rows >= low) & (rows < high)
 
 
-def block_rows(geo, table_ref, t):
-    return [table_ref[i * geo.slots + t] for i in range(4)]
-
-
-def strides(geo):
-    return sorted({item.cols for item in geo.items if item.cols})
+def block_moves(geo, table_ref, by_group, by_row):
+    matrices = geo.block_tables()[0]
+    for i, item in enumerate(matrices):
+        def body(g, carry, i=i, cols=item.cols):
+            for cb in range(cols):
+                by_group(table_ref[3 * i] + g * cols + cb, table_ref[3 * i + 1] + g * BLK * cols + cb, cols)
+            return carry
+
+        lax.fori_loop(0, table_ref[3 * i + 2], body, 0)
+    base = 3 * len(matrices)
+
+    def single(r, carry):
+        by_row(*[table_ref[base + 1 + 4 * r + j] for j in range(4)])
+        return carry
+
+    lax.fori_loop(0, table_ref[base], single, 0)
+
+
+def block_at(slot):
+    return pl.ds(pl.multiple_of(slot * BLK, BLK), BLK)
 
 
 def align_rows(geo, table, padded):
     def kernel(table_ref, rows_ref, out_ref):
-        def body(t, carry):
-            start, low_row, high_row, cols = block_rows(geo, table_ref, t)
-            here = pl.ds(pl.multiple_of(t * BLK, BLK), BLK)
-
-            @pl.when(cols == 0)
-            def _():
-                rows = rows_ref[pl.ds(start + BLK, BLK), :]
-                out_ref[here, :] = jnp.where(row_mask(low_row, high_row), rows, 0.0).astype(jnp.bfloat16)
-
-            for stride in strides(geo):
-                @pl.when(cols == stride)
-                def _(stride=stride):
-                    rows = rows_ref[pl.ds(start + BLK, BLK, stride=stride), :]
-                    out_ref[here, :] = rows.astype(jnp.bfloat16)
-
-            return carry
-
-        lax.fori_loop(0, geo.slots, body, 0)
+        def by_group(slot, start, cols):
+            out_ref[block_at(slot), :] = rows_ref[pl.ds(start + BLK, BLK, stride=cols), :].astype(jnp.bfloat16)
+
+        def by_row(slot, start, low_row, high_row):
+            rows = jnp.where(row_mask(low_row, high_row), rows_ref[pl.ds(start + BLK, BLK), :], 0.0)
+            out_ref[block_at(slot), :] = rows.astype(jnp.bfloat16)
+
+        block_moves(geo, table_ref, by_group, by_row)
 
     return pl.pallas_call(
         kernel,
@@ -221,28 +237,21 @@
         in_specs=[spec_smem(), spec_vmem()],
         out_specs=spec_vmem(),
         compiler_params=kernel_params(),
+        cost_estimate=cost(3),
     )(table, padded)
 
 
 def natural_rows(geo, table, blocks, pad_rows):
     def kernel(table_ref, blocks_ref, out_ref):
-        def body(t, carry):
-            start, low_row, high_row, cols = block_rows(geo, table_ref, t)
-            rows = blocks_ref[pl.ds(pl.multiple_of(t * BLK, BLK), BLK), :].astype(jnp.float32)
-
-            @pl.when(cols == 0)
-            def _():
-                here = pl.ds(start + BLK, BLK)
-                out_ref[here, :] = jnp.where(row_mask(low_row, high_row), rows, out_ref[here, :])
-
-            for stride in strides(geo):
-                @pl.when(cols == stride)
-                def _(stride=stride):
-                    out_ref[pl.ds(start + BLK, BLK, stride=stride), :] = rows
-
-            return carry
-
-        lax.fori_loop(0, geo.slots, body, 0)
+        def by_group(slot, start, cols):
+            out_ref[pl.ds(start + BLK, BLK, stride=cols), :] = blocks_ref[block_at(slot), :].astype(jnp.float32)
+
+        def by_row(slot, start, low_row, high_row):
+            here = pl.ds(start + BLK, BLK)
+            rows = blocks_ref[block_at(slot), :].astype(jnp.float32)
+            out_ref[here, :] = jnp.where(row_mask(low_row, high_row), rows, out_ref[here, :])
+
+        block_moves(geo, table_ref, by_group, by_row)
 
     return pl.pallas_call(
         kernel,
@@ -250,21 +259,22 @@
         in_specs=[spec_smem(), spec_vmem()],
         out_specs=spec_vmem(),
         compiler_params=kernel_params(),
+        cost_estimate=cost(3),
     )(table, blocks)
 
 
 class Buckets:
-    def __init__(self, geo):
+    def __init__(self, geo, arrays, *ends):
         self.geo = geo
-        self.ranges = geo.buckets()
+        self.ranges = geo.spans(*ends)
+        self.arrays = arrays
         self.half = [(len(r) + 1) // 2 for r in self.ranges]
-        self.arrays = [4, 4, 1]
 
     def find(self, chunk):
         for number, span in enumerate(self.ranges):
             if chunk in span:
                 at = chunk - span.start
-                cut = self.half[number] if self.arrays[number] > 1 else len(span)
+                cut = self.half[number]
                 return (number, 0, at) if at < cut else (number, 1, at - cut)
 
     def shapes(self, number):
@@ -294,6 +304,48 @@
         body(full * step, count % step)
 
 
+def place_line(geo, parts, my_z, cut):
+    n, nd = parts[0].shape[0], geo.n_doc
+    counts = [cut, n - cut]
+
+    def kernel(z_ref, *refs):
+        sources, outs = refs[:nd], refs[nd:]
+        for r in range(nd):
+            z = wrap(z_ref[0] - r, nd)
+            rows = pl.ds(pl.multiple_of(z * geo.piece, BLK), geo.piece)
+            for i in range(n):
+                target = outs[0].at[i] if i < cut else outs[1].at[i - cut]
+                target[rows, :] = sources[r][i]
+
+    return pl.pallas_call(
+        kernel,
+        out_shape=[jax.ShapeDtypeStruct((c, nd * geo.piece, LANES), jnp.bfloat16) for c in counts],
+        in_specs=[spec_smem()] + [spec_vmem()] * nd,
+        out_specs=[spec_vmem()] * 2,
+        compiler_params=kernel_params(),
+        cost_estimate=cost(2),
+    )(my_z.reshape(1), *parts)
+
+
+def class_tags(cot, doc, pos):
+    count = cot.shape[0]
+
+    def kernel(doc_ref, pos_ref, cot_ref, out_ref):
+        lanes = lax.broadcasted_iota(jnp.int32, (1, LANES), 1)
+        for s in range(count):
+            out_ref[s : s + 1, :D] = cot_ref[s, 0:1, :].astype(jnp.float32)
+            tag = jnp.where(lanes == 0, doc_ref[s], jnp.where(lanes == 1, pos_ref[s], 0))
+            out_ref[s : s + 1, D:] = tag.astype(jnp.float32)
+
+    return pl.pallas_call(
+        kernel,
+        grid=(1,),
+        out_shape=jax.ShapeDtypeStruct((count, D + LANES), jnp.float32),
+        in_specs=[spec_smem(), spec_smem(), pl.BlockSpec((count, BLK, D), lambda i: (0, 0, 0))],
+        out_specs=pl.BlockSpec((count, D + LANES), lambda i: (0, 0)),
+        compiler_params=kernel_params(),
+        cost_estimate=cost(2),
+    )(doc, pos, cot)
 VECTOR_ROWS = 16
 
 
@@ -302,7 +354,7 @@
     number, half, place = buckets.find(n)
     first = sum(buckets.arrays[m] for m in used[: used.index(number)])
     if buckets.arrays[number] == 1:
-        for device in range(geo.n_dev):
+        for device in range(geo.groups * geo.n_doc):
             pltpu.make_async_copy(
                 sources[first].at[device, n - buckets.ranges[number].start],
                 staged.at[pl.ds(device * geo.piece, geo.piece)],
@@ -317,134 +369,86 @@
                 y, x = wrap(my_y - ry, geo.y_size), wrap(my_x - rx, geo.x_size)
                 s = (y * geo.x_size + x) * 2 + c
                 index = (ry, rx, place) if half == 0 else (rx, ry, place)
-                pltpu.make_async_copy(
-                    sources[first + 2 * half + core].at[index],
-                    staged.at[pl.ds(pl.multiple_of(s * rows, BLK), rows)],
-                    sem,
-                ).start()
-
-
-def unpack_matrix(geo, buckets, gathered, coords, name):
-    item = vars(geo.by_name)[name]
-    depth, cols = item.shape
-    chunks = geo.chunks_of(item)
-    used = sorted({buckets.find(n)[0] for n, *_ in chunks})
-    operands = [array for number in used for array in gathered[number]]
-    wide_cols = cols // LANES
-
-    def kernel(coords_ref, *refs):
-        sources, (out_ref, staged, wide, sems) = refs[: len(operands)], refs[len(operands) :]
-        for at, (n, _, _, _) in enumerate(chunks):
-            chunk_copies(geo, buckets, sources, used, coords_ref, n, staged.at[at], sems.at[at])
-        for at in range(len(chunks)):
-            pltpu.make_async_copy(staged.at[at], staged.at[at], sems.at[at]).wait()
+
+                def begin(s=s, index=index, core=core):
+                    pltpu.make_async_copy(
+                        sources[first + 2 * half + core].at[index],
+                        staged.at[pl.ds(pl.multiple_of(s * rows, BLK), rows)],
+                        sem,
+                    ).start()
+
+                if geo.groups == geo.n_seg:
+                    begin()
+                else:
+                    pl.when(s < geo.groups)(begin)
+
+
+class Weights:
+    def __init__(self, geo, buckets, gathered, names):
+        self.geo, self.buckets = geo, buckets
+        self.items = [vars(geo.by_name)[name] for name in names]
+        self.chunks = sorted({n for item in self.items for n, *_ in geo.chunks_of(item)})
+        self.used = sorted({buckets.find(n)[0] for n in self.chunks})
+        self.operands = [array for number in self.used for array in gathered[number]]
+        cols = max([item.cols for item in self.items])
+        self.scratch = [
+            pltpu.VMEM((len(self.chunks), geo.staged_rows, LANES), jnp.bfloat16),
+            pltpu.VMEM((BLK * (cols + 2), LANES), jnp.float32),
+            pltpu.SemaphoreType.DMA((len(self.chunks),)),
+        ]
+
+    def start(self, coords_ref, sources, staged, sems):
+        for at, n in enumerate(self.chunks):
+            chunk_copies(
+                self.geo, self.buckets, sources, self.used, coords_ref, n, staged.at[at], sems.at[at]
+            )
+
+    def wait(self, number, waited, staged, sems):
+        for n, *_ in self.geo.chunks_of(self.items[number]):
+            at = self.chunks.index(n)
+            if at not in waited:
+                waited.add(at)
+                pltpu.make_async_copy(staged.at[at], staged.at[at], sems.at[at]).wait()
+
+    def blocks(self, item, lo, hi, staged, wide):
+        done = lo
+        for n, b0, b1, slot in self.geo.chunks_of(item):
+            for b in range(max(b0, lo), min(b1, hi)):
+                at = self.chunks.index(n)
+                rows = staged[at, pl.ds((slot + b - b0) * BLK, BLK), :].astype(jnp.float32)
+                here = pl.ds((b - lo) * BLK, BLK)
+                wide[here, :] = wide[here, :] + rows if b < done else rows
+            done = max(done, min(b1, hi))
+
+    def matrix(self, number, staged, wide, out_ref):
+        item = self.items[number]
+        cols = item.cols
         split = set()
-        for at, (n, b0, b1, slot) in enumerate(chunks):
-            first, last = geo.full_groups(item, n)
-            split |= set(range(b0 // wide_cols, -(-b1 // wide_cols))) - set(range(first, last))
+        for n, b0, b1, slot in self.geo.chunks_of(item):
+            at = self.chunks.index(n)
+            first, last = self.geo.full_groups(item, n)
+            split |= set(range(b0 // cols, -(-b1 // cols))) - set(range(first, last))
 
             def group(g, carry, at=at, shift=slot - b0):
                 rows = pl.ds(pl.multiple_of(g * BLK, BLK), BLK)
-                for cb in range(wide_cols):
-                    src = pl.ds(pl.multiple_of((g * wide_cols + cb + shift) * BLK, BLK), BLK)
-                    out_ref[rows, cb * LANES : (cb + 1) * LANES] = staged[at, src, :]
+                for cb in range(cols):
+                    tile = staged[at, block_at(g * cols + cb + shift), :]
+                    out_ref[rows, cb * LANES : (cb + 1) * LANES] = tile
                 return carry
 
             lax.fori_loop(first, last, group, 0)
         for g in sorted(split):
-            done = g * wide_cols
-            for at, (n, b0, b1, slot) in enumerate(chunks):
-                lo, hi = max(b0, g * wide_cols), min(b1, (g + 1) * wide_cols)
-                for b in range(lo, hi):
-                    rows = staged[at, pl.ds((slot + b - b0) * BLK, BLK), :].astype(jnp.float32)
-                    here = pl.ds((b - g * wide_cols) * BLK, BLK)
-                    wide[here, :] = wide[here, :] + rows if b < done else rows
-                done = max(done, hi)
-            for cb in range(wide_cols):
-                tile = wide[pl.ds(cb, BLK, stride=wide_cols), :]
+            self.blocks(item, g * cols, (g + 1) * cols, staged, wide)
+            for cb in range(cols):
+                tile = wide[pl.ds(cb, BLK, stride=cols), :]
                 out_ref[g * BLK : (g + 1) * BLK, cb * LANES : (cb + 1) * LANES] = tile.astype(jnp.bfloat16)
 
-    return pl.pallas_call(
-        kernel,
-        out_shape=jax.ShapeDtypeStruct((depth, cols), jnp.bfloat16),
-        in_specs=[spec_smem()] + [spec_any()] * len(operands),
-        out_specs=spec_vmem(),
-        scratch_shapes=[
-            pltpu.VMEM((len(chunks), geo.slots * BLK, LANES), jnp.bfloat16),
-            pltpu.VMEM((BLK * (wide_cols + 2), LANES), jnp.float32),
-            pltpu.SemaphoreType.DMA((len(chunks),)),
-        ],
-        compiler_params=kernel_params(),
-    )(coords, *operands)
-
-
-def unpack_vectors(geo, buckets, gathered, coords, names):
-    lane_cols = D // LANES
-    blocks, rows_of = [], []
-    for name in names:
-        item = vars(geo.by_name)[name]
+    def vectors(self, number, staged, wide, out_ref, row):
+        item = self.items[number]
+        self.blocks(item, 0, ceil_to(item.rows, BLK) // BLK, staged, wide)
         for r in range(item.rows):
-            rows_of.append(len(blocks) * BLK + r)
-        for b in range(ceil_to(item.rows, BLK) // BLK):
-            blocks.append(
-                [
-                    (n, item.blk + b - geo.first[n])
-                    for n in range(geo.n_dev)
-                    if geo.first[n] <= item.blk + b <= geo.last[n]
-                ]
-            )
-    copies = [(b, which, n, slot) for b, found in enumerate(blocks) for which, (n, slot) in enumerate(found)]
-    used = sorted({buckets.find(n)[0] for _, _, n, _ in copies})
-    operands = [array for number in used for array in gathered[number]]
-
-    def kernel(coords_ref, *refs):
-        sources, (out_ref, staged, wide, sem) = refs[: len(operands)], refs[len(operands) :]
-        my_y, my_x, my_c = coords_ref[0], coords_ref[1], coords_ref[2]
-        for at, (b, which, n, slot) in enumerate(copies):
-            number, half, place = buckets.find(n)
-            first = sum(buckets.arrays[m] for m in used[: used.index(number)])
-            device, offset = slot // geo.piece_blocks, slot % geo.piece_blocks * BLK
-            if buckets.arrays[number] == 1:
-                pltpu.make_async_copy(
-                    sources[first].at[device, n - buckets.ranges[number].start, pl.ds(offset, BLK)],
-                    staged.at[at],
-                    sem,
-                ).start()
-                continue
-            y, x, c, z = geo.coords(device)
-            ry, rx = wrap(my_y - y, geo.y_size), wrap(my_x - x, geo.x_size)
-            index = (ry, rx) if half == 0 else (rx, ry)
-            for core in range(2):
-                source = sources[first + 2 * half + core]
-
-                @pl.when(my_c == (c if core == 0 else 1 - c))
-                def _(source=source, at=at, index=index, place=place, row=z * geo.piece + offset):
-                    pltpu.make_async_copy(
-                        source.at[index[0], index[1], place, pl.ds(row, BLK)], staged.at[at], sem
-                    ).start()
-
-        pltpu.make_async_copy(staged, staged, sem).wait()
-        for at, (b, which, n, slot) in enumerate(copies):
-            rows = staged[at].astype(jnp.float32)
-            here = pl.ds(b * BLK, BLK)
-            wide[here, :] = rows if which == 0 else wide[here, :] + rows
-        out_ref[...] = jnp.zeros_like(out_ref)
-        for r, row in enumerate(rows_of):
-            v, cb = divmod(r, lane_cols)
-            out_ref[v : v + 1, cb * LANES : (cb + 1) * LANES] = wide[row : row + 1, :]
-
-    return pl.pallas_call(
-        kernel,
-        out_shape=jax.ShapeDtypeStruct((VECTOR_ROWS, D), jnp.float32),
-        in_specs=[spec_smem()] + [spec_any()] * len(operands),
-        out_specs=spec_vmem(),
-        scratch_shapes=[
-            pltpu.VMEM((len(copies), BLK, LANES), jnp.bfloat16),
-            pltpu.VMEM((len(blocks) * BLK, LANES), jnp.float32),
-            pltpu.SemaphoreType.DMA,
-        ],
-        compiler_params=kernel_params(),
-    )(coords, *operands)
+            v, cb = divmod(r, D // LANES)
+            out_ref[row + v : row + v + 1, cb * LANES : (cb + 1) * LANES] = wide[r : r + 1, :]
 
 
 def vector_rows(wide, values, first, count):
@@ -578,6 +582,7 @@
             pltpu.SemaphoreType.DMA((len(span),)),
         ],
         compiler_params=kernel_params(),
+        cost_estimate=cost(7),
     )(coords, *operands)
 
 
@@ -668,6 +673,7 @@
             pltpu.VMEM((wide_rows + 2 * BLK, LANES), jnp.float32),
         ],
         compiler_params=kernel_params(),
+        cost_estimate=cost(12),
     )(seg, *operands)
 TILE = 512
 PAIRS = HEADS // 2
@@ -751,8 +757,7 @@
     return slice(start, start + LANES)
 
 
-def attend_kernel(x_ref, wqkv_ref, vec_ref, *refs):
-    packed_ref, att_ref, stat_ref = refs[-3:]
+def attend_kernel(x_ref, wqkv_ref, vec_ref, packed_ref, att_ref, stat_ref):
     x = x_ref[...]
     for j in range(3):
         cols = slice(j * D, (j + 1) * D)
@@ -784,7 +789,7 @@
     lax.fori_loop(0, TILE // SEG_LEN, segment, 0)
 
 
-def in_parts(kernel, first, count, inputs, in_specs, outs, out_specs, scratch, previous):
+def in_parts(kernel, micros, count, inputs, in_specs, outs, out_specs, scratch, previous):
     previous = list(previous or ())
     return pl.pallas_call(
         kernel,
@@ -795,30 +800,64 @@
         scratch_shapes=scratch,
         input_output_aliases={len(inputs) + i: i for i in range(len(previous))},
         compiler_params=kernel_params(60),
+        cost_estimate=cost(micros),
     )(*inputs, *previous)
 
 
-def attend_layer(x, w_qkv, vecs, first, count, previous=None):
-    n = x.shape[0]
-
+def attend_layer(x, w_qkv, vecs, first, count, previous):
     def rows(cols):
         return tiles(cols, first)
 
+    def kernel(x_ref, wqkv_ref, vec_ref, *refs):
+        attend_kernel(x_ref, wqkv_ref, vec_ref, *refs[-3:])
+
     return in_parts(
-        attend_kernel,
-        first,
+        kernel,
+        8 * count,
         count,
         [x, w_qkv, vecs],
         [rows(D), fixed((D, 3 * D)), fixed((VECTOR_ROWS, D))],
-        [
-            jax.ShapeDtypeStruct((n, 3 * D), jnp.bfloat16),
-            jax.ShapeDtypeStruct((n, D), jnp.bfloat16),
-            jax.ShapeDtypeStruct((n, LANES), jnp.float32),
-        ],
+        [jax.ShapeDtypeStruct(v.shape, v.dtype) for v in previous],
         [rows(3 * D), rows(D), rows(LANES)],
         [],
         previous,
     )
+
+
+def attend_first(x, weights, coords):
+    n = x.shape[0]
+    bf, f32 = jnp.bfloat16, jnp.float32
+    count = len(weights.operands)
+
+    def kernel(coords_ref, *refs):
+        sources, x_ref, refs = refs[:count], refs[count], refs[count + 1 :]
+        packed_ref, att_ref, stat_ref, wqkv_ref, vec_ref, staged, wide, sems = refs
+        weights.start(coords_ref, sources, staged, sems)
+        waited = set()
+        for number in range(2):
+            weights.wait(number, waited, staged, sems)
+        weights.matrix(0, staged, wide, wqkv_ref)
+        vec_ref[...] = jnp.zeros_like(vec_ref)
+        weights.vectors(1, staged, wide, vec_ref, 0)
+        attend_kernel(x_ref, wqkv_ref, vec_ref, packed_ref, att_ref, stat_ref)
+
+    whole = [pl.BlockSpec(shape, lambda i: (0, 0)) for shape in ((D, 3 * D), (VECTOR_ROWS, D))]
+    return pl.pallas_call(
+        kernel,
+        grid=(1,),
+        in_specs=[spec_smem()] + [spec_any()] * count + [tiles(D)],
+        out_specs=[tiles(3 * D), tiles(D), tiles(LANES)] + whole,
+        out_shape=[
+            jax.ShapeDtypeStruct((n, 3 * D), bf),
+            jax.ShapeDtypeStruct((n, D), bf),
+            jax.ShapeDtypeStruct((n, LANES), f32),
+            jax.ShapeDtypeStruct((D, 3 * D), bf),
+            jax.ShapeDtypeStruct((VECTOR_ROWS, D), f32),
+        ],
+        scratch_shapes=weights.scratch,
+        compiler_params=kernel_params(60),
+        cost_estimate=cost(12),
+    )(coords, *weights.operands, x)
 
 
 FBLOCK = D
@@ -870,25 +909,69 @@
     lax.fori_loop(0, segs, finish, 0)
 
 
-def feed_layer(x, att, w_out, w_up, w_down, vecs):
+def feed_layer(x, att, weights, coords):
     n = x.shape[0]
     bf, f32 = jnp.bfloat16, jnp.float32
+    count = len(weights.operands)
+    steps = n // TILE
+    shapes = [item.shape for item in weights.items if item.cols]
+
+    def kernel(coords_ref, *refs):
+        sources, refs = refs[:count], refs[count:]
+        x_ref, att_ref = refs[:2]
+        outs, kept = refs[2:10], refs[10:13]
+        vec_ref, res_ref, h1_ref, out_sems = refs[13:17]
+        held, (staged, wide, sems) = refs[17:20], refs[20:]
+        step = pl.program_id(0)
+
+        @pl.when(step == 0)
+        def _():
+            weights.start(coords_ref, sources, staged, sems)
+            waited = set()
+            vec_ref[...] = jnp.zeros_like(vec_ref)
+            place = row = 0
+            for number, item in enumerate(weights.items):
+                weights.wait(number, waited, staged, sems)
+                if item.cols:
+                    weights.matrix(number, staged, wide, held[place])
+                    pltpu.make_async_copy(held[place], kept[place], out_sems.at[place]).start()
+                    place += 1
+                else:
+                    weights.vectors(number, staged, wide, vec_ref, row)
+                    row += item.rows * LANES // D
+
+        feed_kernel(x_ref, att_ref, *held, vec_ref, *outs, res_ref, h1_ref)
+
+        @pl.when(step == steps - 1)
+        def _():
+            for place in range(3):
+                pltpu.make_async_copy(held[place], kept[place], out_sems.at[place]).wait()
+
     return pl.pallas_call(
-        feed_kernel,
-        grid=(n // TILE,),
-        in_specs=[
-            tiles(D), tiles(D), fixed((D, D)), fixed((D, FF)), fixed((FF, D)), fixed((VECTOR_ROWS, D)),
-        ],
+        kernel,
+        grid=(steps,),
+        in_specs=[spec_smem()] + [spec_any()] * count + [tiles(D), tiles(D)],
         out_specs=[tiles(D), tiles(D), tiles(FF), tiles(FF), tiles(D), tiles(LANES), tiles(D)]
-        + [pl.BlockSpec((n // SEG_LEN, D), lambda i: (0, 0))],
+        + [pl.BlockSpec((n // SEG_LEN, D), lambda i: (0, 0))]
+        + [spec_any()] * 3
+        + [pl.BlockSpec((VECTOR_ROWS, D), lambda i: (0, 0))],
         out_shape=[
             jax.ShapeDtypeStruct((n, cols), kind)
             for cols, kind in ((D, bf), (D, bf), (FF, bf), (FF, bf), (D, bf), (LANES, f32), (D, bf))
         ]
-        + [jax.ShapeDtypeStruct((n // SEG_LEN, D), f32)],
-        scratch_shapes=[pltpu.VMEM((TILE, D), f32), pltpu.VMEM((TILE, D), f32)],
-        compiler_params=kernel_params(60),
-    )(x, att, w_out, w_up, w_down, vecs)
+        + [jax.ShapeDtypeStruct((n // SEG_LEN, D), f32)]
+        + [jax.ShapeDtypeStruct(shape, bf) for shape in shapes]
+        + [jax.ShapeDtypeStruct((VECTOR_ROWS, D), f32)],
+        scratch_shapes=[
+            pltpu.VMEM((TILE, D), f32),
+            pltpu.VMEM((TILE, D), f32),
+            pltpu.SemaphoreType.DMA((3,)),
+        ]
+        + [pltpu.VMEM(shape, bf) for shape in shapes]
+        + weights.scratch,
+        compiler_params=kernel_params(62),
+        cost_estimate=cost(60),
+    )(coords, *weights.operands, x, att)
 
 
 def feed_back_kernel(
@@ -972,6 +1055,7 @@
         ],
         scratch_shapes=[pltpu.VMEM((TILE, D), f32)],
         compiler_params=kernel_params(60),
+        cost_estimate=cost(44),
     )(cot, cls, norm2, dg, norm1, rates, w_down, w_up, w_out, vecs)
 
 
@@ -1019,7 +1103,7 @@
     before = previous[1] if previous else jnp.zeros((8, D), jnp.float32)
     return in_parts(
         attend_back_kernel,
-        first,
+        10 * count,
         count,
         [packed, stat, da, before],
         [tiles(3 * D, first), tiles(LANES, first), tiles(D, first), fixed((8, D))],
@@ -1031,7 +1115,7 @@
 
 
 def cross_kernel(
-    rows_ref, tagc_ref, tagr_ref, gz_ref, wqkv_ref, wout_ref, wup_ref, wdown_ref, vec_ref,
+    load, rows_ref, tagc_ref, tagr_ref, gz_ref, wqkv_ref, wout_ref, wup_ref, wdown_ref, vec_ref,
     out_ref, grows_ref, sums_ref, gqkv_ref, go_ref, gu_ref, gm_ref, rowst_ref, attt_ref, hidt_ref, actt_ref,
     packed_ref, weights_ref, att_ref, act_ref, slope_ref, res_ref,
 ):
@@ -1048,6 +1132,7 @@
         return slice(pair * LANES, (pair + 1) * LANES)
 
     sums_ref[...] = jnp.zeros_like(sums_ref)
+    load(0)
     for j in range(3):
         cols = slice(j * D, (j + 1) * D)
         part = dot_nn(rows, wqkv_ref[:, cols])
@@ -1062,10 +1147,12 @@
         att_ref[:, pair_cols(pair)] = low(blend)
     att = att_ref[...]
     attt_ref[...] = att.T
+    load(1)
     resid = rows.astype(jnp.float32) + dot_nn(att, wout_ref[...]) + vec_ref[2:3, :]
     hidden, normal_three, rate_three = norm_rows(resid, vec_ref[3:4, :], vec_ref[4:5, :])
     hidden_low = low(hidden)
     hidt_ref[...] = hidden_low.T
+    load(2)
     res_ref[...] = hidden + vec_ref[9:10, :]
     for j in range(FF // FBLOCK):
         cols = slice(j * FBLOCK, (j + 1) * FBLOCK)
@@ -1120,17 +1207,42 @@
     grows_ref[...] = low(res_ref[...])
 
 
-def cross_layer(rows, tags, grad_out, x_qkv, x_out, x_up, x_down, vec):
-    m = rows.shape[0]
+def cross_layer(cls, places, tags, grad_out, weights, coords):
+    m = cls.shape[0]
     bf, f32 = jnp.bfloat16, jnp.float32
     tagc = jnp.broadcast_to(tags.astype(f32)[:, None], (m, LANES))
     tagr = jnp.broadcast_to(tags.astype(f32)[None, :], (8, m))
-    operands = [rows, tagc, tagr, grad_out, x_qkv, x_out, x_up, x_down, vec]
+    count = len(weights.operands)
+    operands = [cls, tagc, tagr, grad_out]
     shapes = [(m, D), (m, D), (VECTOR_ROWS, D), (m, 3 * D), (m, D), (m, FF), (m, D), (D, m), (D, m), (D, m), (FF, m)]
+    matrices = [number for number, item in enumerate(weights.items) if item.cols]
+    vectors = [number for number, item in enumerate(weights.items) if not item.cols]
+    needs = [(matrices[:1], vectors[:1]), (matrices[1:2], vectors[1:2]), (matrices[2:], vectors[2:])]
+
+    def kernel(coords_ref, *refs):
+        sources, refs = refs[:count], refs[count:]
+        ins, outs = refs[: len(operands)], refs[len(operands) : len(operands) + len(shapes)]
+        held, vec_ref, refs = refs[-8:-4], refs[-4], (refs[len(operands) + len(shapes) : -8], refs[-3:])
+        scratch, (staged, wide, sems) = refs
+        waited = set()
+        rows_of = {number: row for number, row in zip(vectors, (0, 2, 5, 9))}
+        weights.start(coords_ref, sources, staged, sems)
+
+        def load(stage):
+            for number in needs[stage][0]:
+                weights.wait(number, waited, staged, sems)
+                weights.matrix(number, staged, wide, held[matrices.index(number)])
+            for number in needs[stage][1]:
+                weights.wait(number, waited, staged, sems)
+                weights.vectors(number, staged, wide, vec_ref, rows_of[number])
+
+        vec_ref[...] = jnp.zeros_like(vec_ref)
+        cross_kernel(load, *ins, *held, vec_ref, *outs, *scratch)
+
     return pl.pallas_call(
-        cross_kernel,
+        kernel,
         out_shape=[jax.ShapeDtypeStruct(shape, f32 if i == 2 else bf) for i, shape in enumerate(shapes)],
-        in_specs=[spec_vmem()] * len(operands),
+        in_specs=[spec_smem()] + [spec_any()] * count + [spec_vmem()] * len(operands),
         out_specs=[spec_vmem()] * len(shapes),
         scratch_shapes=[
             pltpu.VMEM((m, 3 * D), bf),
@@ -1139,9 +1251,34 @@
             pltpu.VMEM((m, D), bf),
             pltpu.VMEM((m, FF), f32),
             pltpu.VMEM((m, D), f32),
-        ],
-        compiler_params=kernel_params(60),
-    )(*operands)
+        ]
+        + [pltpu.VMEM(weights.items[number].shape, bf) for number in matrices]
+        + [pltpu.VMEM((VECTOR_ROWS, D), f32)]
+        + weights.scratch,
+        compiler_params=kernel_params(62),
+        cost_estimate=cost(22),
+    )(coords, *weights.operands, *operands)
+
+
+def class_rows(cls, hot, weights, coords):
+    count = len(weights.operands)
+
+    def kernel(coords_ref, *refs):
+        sources, (cls_ref, hot_ref, out_ref, table, staged, wide, sems) = refs[:count], refs[count:]
+        weights.start(coords_ref, sources, staged, sems)
+        weights.wait(0, set(), staged, sems)
+        weights.matrix(0, staged, wide, table)
+        out_ref[...] = low(cls_ref[...] + dot_nn(hot_ref[...], table[...]))
+
+    return pl.pallas_call(
+        kernel,
+        out_shape=jax.ShapeDtypeStruct(cls.shape, jnp.bfloat16),
+        in_specs=[spec_smem()] + [spec_any()] * count + [spec_vmem()] * 2,
+        out_specs=spec_vmem(),
+        scratch_shapes=[pltpu.VMEM((LONG_SEGS, D), jnp.bfloat16)] + weights.scratch,
+        compiler_params=kernel_params(),
+        cost_estimate=cost(3),
+    )(coords, *weights.operands, cls, hot)
 AXES = ("seg", "doc")
 
 
@@ -1149,26 +1286,27 @@
     return lax.optimization_barrier((value, *others))[0]
 
 
+def after(halves, *others):
+    return [[tie(value, *others) for value in half] for half in halves]
+
+
 def send(geo, value, axis, step):
     return lax.ppermute(value, AXES, geo.shift(axis, step))
 
 
-def gather_axis(geo, value, axis):
-    return jnp.stack([value] + [send(geo, value, axis, r) for r in range(1, geo.size(axis))])
-
-
-def gather_line(geo, pieces, my_z):
-    nd = geo.n_doc
-    parts = [pieces] + [send(geo, pieces, Z, r) for r in range(1, nd)]
-    parts = parts[::-1]
-    line = jnp.stack(parts + parts[: nd - 1], axis=1)
-    line = lax.dynamic_slice_in_dim(line, nd - 1 - my_z, nd, axis=1)
-    return line.reshape(pieces.shape[0], nd * geo.piece, LANES)
-
-
-def gather_plane(geo, halves, step):
+def gather_axis(geo, value, axis, others):
+    parts = [send(geo, value, axis, r) for r in range(1, geo.size(axis))]
+    return jnp.stack([value] + [tie(part, *others) if others else part for part in parts])
+
+
+def gather_line(geo, pieces, my_z, cut):
+    parts = [pieces] + [send(geo, pieces, Z, r) for r in range(1, geo.n_doc)]
+    return place_line(geo, parts, my_z, cut)
+
+
+def gather_plane(geo, halves, step, others=()):
     orders = ((X, Y), (Y, X))
-    return [gather_axis(geo, half, order[step]) for half, order in zip(halves, orders)]
+    return [gather_axis(geo, half, order[step], others) for half, order in zip(halves, orders)]
 
 
 def gather_cores(geo, halves):
@@ -1241,131 +1379,131 @@
     n_seg = lax.axis_size(AXES[0])
     n_doc = lax.axis_size(AXES[1])
     geo = Geometry(n_seg, n_doc, master.shape[0])
-    buckets = Buckets(geo)
+    by = geo.by_name
+    gather = Buckets(geo, [4, 4, 1], by.w_out, by.pos_table)
+    buckets = Buckets(geo, [4, 4, 4, 1], by.w_out, by.w_down, by.pos_table)
     my_seg, my_doc = lax.axis_index(AXES[0]), lax.axis_index(AXES[1])
     me = my_seg * n_doc + my_doc
     coords = jnp.stack([my_seg // 4, my_seg // 2 % 2, my_seg % 2, my_doc]).astype(jnp.int32)
-    table = lax.dynamic_index_in_dim(
-        jnp.asarray(geo.block_table().reshape(geo.n_dev, -1)), me, 0, False
-    )
+    table = lax.dynamic_index_in_dim(jnp.asarray(geo.block_tables()[1]), me, 0, False)
     pad_rows = ceil_to(geo.chunk + 4 * BLK, 8)
     padded = jnp.pad(
         master.reshape(geo.chunk, LANES), ((BLK, pad_rows - geo.chunk - BLK), (0, 0))
     )
     aligned = align_rows(geo, table, padded)
     pieces = lax.all_to_all(aligned.reshape(geo.n_dev, geo.piece, LANES), AXES, 0, 0, tiled=True)
-    parts = [pieces[span.start : span.stop] for span in buckets.ranges]
+    parts = [pieces[span.start : span.stop] for span in gather.ranges]
 
     seg_count = tokens.shape[1]
     n_rows = n_seg * seg_count
     tiles_all = seg_count * SEG_LEN // TILE
     inputs = tokens[0].reshape(seg_count * SEG_LEN, D)
     cot_rows = cotangent[0]
-    tags = low(jnp.stack([seg_doc[0], seg_pos[0]], axis=1).astype(jnp.float32))
-    tagged = jnp.concatenate([cot_rows[:, 0], jnp.pad(tags, ((0, 0), (0, LANES - 2)))], axis=1)
-    all_tagged = lax.all_gather(tie(tagged, pieces), AXES[0], axis=0, tiled=True)
+    tagged = low(class_tags(cot_rows, seg_doc[0], seg_pos[0]))
+    cut = gather.half
+    line = gather_line(geo, parts[0], my_doc, cut[0])
+
+    gathered = [None, None, None]
+
+    def weights(*numbers):
+        return Weights(geo, gather, gathered, [item_name(i) for i in numbers])
+
+    started = tie(parts[1], *line)
+    parts_b = [started] + [send(geo, started, Z, r) for r in range(1, n_doc)]
+    plane = gather_plane(geo, line, 0, parts_b[1:2])
+    plane = gather_plane(geo, plane, 1, parts_b[2:3])
+    gathered[0] = gather_cores(geo, plane)
+    all_tagged = lax.all_gather(tie(tagged, *plane), AXES[0], axis=0, tiled=True)
+    parts_b[-1] = tie(parts_b[-1], all_tagged)
+    line_b = place_line(geo, parts_b, my_doc, cut[1])
+    *outs, w_qkv, vec_a = attend_first(tie(inputs, *line_b), weights(0, 1), coords)
+    plane_b = gather_plane(geo, line_b, 0, [vec_a])
+    middle = max(1, tiles_all - 2)
+    outs = attend_layer(tie(inputs, *plane_b), w_qkv, vec_a, 1, middle, outs)
+    gathered[2] = [lax.all_gather(tie(parts[2], outs[2]), AXES)]
+    plane_b = gather_plane(geo, plane_b, 1, [outs[2]])
+    gathered[1] = gather_cores(geo, plane_b)
+    if 1 + middle < tiles_all:
+        last = tiles_all - 1 - middle
+        outs = attend_layer(tie(inputs, *plane_b), w_qkv, vec_a, 1 + middle, last, outs)
+    packed, attended, stat = outs
+    hidden_low, normal_one, active, slope, normal_two, rates, hidden_two, cls, w_out, w_up, w_down, vec = feed_layer(
+        inputs, attended, weights(1, 2, 3, 4, 5, 6, 7), coords
+    )
+
     all_grad, all_doc, all_pos = all_tagged[:, :D], all_tagged[:, D], all_tagged[:, D + 1]
     pos_hot = (all_pos.astype(jnp.int32)[:, None] == jnp.arange(LONG_SEGS)[None, :]).astype(jnp.bfloat16)
 
-    line = gather_line(geo, parts[0], my_doc)
-    cut = buckets.half
-    line_b = gather_line(geo, tie(parts[1], line, all_tagged), my_doc)
-    plane = gather_plane(geo, [line[: cut[0]], line[cut[0] :]], 0)
-    plane = gather_plane(geo, plane, 1)
-    gathered = [gather_cores(geo, plane), None, None]
-    line_b = tie(line_b, *plane)
-    plane_b = gather_plane(geo, [line_b[: cut[1]], line_b[cut[1] :]], 0)
-
-    def matrix(number):
-        return unpack_matrix(geo, buckets, gathered, coords, item_name(number))
-
-    def vectors(*numbers):
-        return unpack_vectors(geo, buckets, gathered, coords, [item_name(i) for i in numbers])
-
-    w_qkv = matrix(0)
-    gathered[2] = [lax.all_gather(tie(parts[2], w_qkv), AXES)]
-    vec_a = vectors(1)
-    w_qkv = tie(w_qkv, *plane_b)
-    plane_b = gather_plane(geo, plane_b, 1)
-    first = max(1, tiles_all - 1)
-    outs = attend_layer(inputs, w_qkv, vec_a, 0, first)
-    plane_b = [tie(half, outs[0]) for half in plane_b]
-    gathered[1] = gather_cores(geo, plane_b)
-    if first < tiles_all:
-        outs = attend_layer(tie(inputs, *plane_b), w_qkv, vec_a, first, tiles_all - first, outs)
-    packed, attended, stat = outs
-
-    w_out, w_up, w_down, vec = matrix(2), matrix(4), matrix(6), vectors(1, 3, 5, 7)
-    hidden_low, normal_one, active, slope, normal_two, rates, hidden_two, cls = feed_layer(
-        inputs, attended, w_out, w_up, w_down, vec
-    )
-
-    cross = [matrix(i) for i in (8, 9, 11, 13, 15)]
-    xvec = vectors(10, 12, 14, 16)
-
     def own(values):
         return lax.dynamic_slice_in_dim(values, my_seg * seg_count, seg_count, axis=0)
 
-    cls_low = low(cls + matmul(own(pos_hot), cross[0]))
+    cls_low = class_rows(cls, own(pos_hot), weights(8), coords)
     rows = lax.all_gather(cls_low, AXES[0], axis=0, tiled=True)
     crossed, grad_rows, xsums, g_qkv, g_o, g_u, g_m, rows_t, att_t, hid_t, act_t = cross_layer(
-        rows, all_doc, all_grad, *cross[1:], xvec
-    )
-    first_row = lax.broadcasted_iota(jnp.int32, (seg_count, SEG_LEN, D), 1) == 0
-    mixed_out = jnp.where(
-        first_row, own(crossed)[:, None, :], hidden_two.reshape(seg_count, SEG_LEN, D)
+        rows, all_pos, all_doc, all_grad, weights(9, 10, 11, 12, 13, 14, 15, 16), coords
     )
     names = [item_name(i) for i in (8, 9, 11, 13, 15)]
     line_c = pack_cross(
         geo,
-        buckets.ranges[2],
+        buckets.ranges[3],
         dict(zip(names, (pos_hot.T, rows_t, att_t, hid_t, act_t))),
         dict(zip(names, (grad_rows, g_qkv, g_o, g_u, g_m))),
         {item_name(i): (xsums, row) for i, row in ((10, 0), (12, 2), (14, 5), (16, 9))},
         my_seg.astype(jnp.int32).reshape(1),
     )
-    line_c_parts = reduce_line(geo, line_c, my_doc)
+    sums_c = reduce_line(geo, line_c, my_doc)
 
     grads = {}
     dm, du, dao, da, grad_one, sums = feed_back(
-        cot_rows.reshape(-1, D), tie(own(grad_rows).astype(jnp.float32), line_c), normal_two,
+        cot_rows.reshape(-1, D), tie(own(grad_rows).astype(jnp.float32), *sums_c[:1]), normal_two,
         slope, normal_one, rates, w_down, w_up, w_out, vec,
     )
-    grads[item_name(4)] = low(matmul(hidden_low.T, du))
-    grads[item_name(6)] = low(matmul(active.T, dm))
-    grads[item_name(2)] = low(matmul(attended.T, dao))
+    pieces_c = plus(*[tie(part, sums) for part in sums_c])
     grads[item_name(8)] = low(matmul(own(pos_hot).T, own(grad_rows)))
-    grads[item_name(3)] = (sums, 2)
-    grads[item_name(5)] = (sums, 5)
-    grads[item_name(7)] = (sums, 9)
-    halves = reduce_cores(geo, pack_bucket(geo, buckets, 1, grads, coords))
-    pieces_c = plus(*[tie(part, sums) for part in line_c_parts])
-    da = tie(da, halves[0][0])
-    back = attend_back(packed, stat, da, 0, 1)
-    halves = [[tie(v, back[0]) for v in half] for half in halves]
-    halves = reduce_plane(geo, halves, 0)
+    for number, row in ((3, 2), (5, 5), (7, 9)):
+        grads[item_name(number)] = (sums, row)
+    grads[item_name(6)] = low(matmul(active.T, tie(dm, pieces_c)))
+    arrays_d = pack_bucket(geo, buckets, 2, grads, coords)
+    halves_d = reduce_cores(geo, arrays_d)
+    grads[item_name(4)] = low(matmul(hidden_low.T, tie(du, arrays_d[0])))
+    halves_d = reduce_plane(geo, after(halves_d, grads[item_name(4)]), 0)
+    grads[item_name(2)] = low(matmul(attended.T, tie(dao, halves_d[0][0], halves_d[1][0])))
+    arrays_b = pack_bucket(geo, buckets, 1, grads, coords)
+    halves_b = reduce_cores(geo, arrays_b)
+    back = attend_back(packed, stat, tie(da, arrays_b[0]), 0, 1)
+    halves_d = reduce_plane(geo, after(halves_d, back[1]), 1)
+    halves_b = reduce_plane(geo, after(halves_b, back[1]), 0)
     if tiles_all > 1:
-        da = tie(da, halves[0][0], halves[1][0])
-        back = attend_back(packed, stat, da, 1, tiles_all - 1, back)
+        da = tie(da, *[half[0] for half in halves_b + halves_d])
+        back = attend_back(packed, stat, da, 1, middle, back)
+    line_d = reduce_line(geo, join(after(halves_d, back[1])), my_doc)
+    halves_b = reduce_plane(geo, after(halves_b, back[1]), 1)
+    if 1 + middle < tiles_all:
+        da = tie(da, line_d[0], *[half[0] for half in halves_b])
+        back = attend_back(packed, stat, da, 1 + middle, last, back)
     dqkv, qv_sums = back
-    halves = [[tie(v, dqkv) for v in half] for half in halves]
-    halves = reduce_plane(geo, halves, 1)
-    dqkv = tie(dqkv, halves[0][0], halves[1][0])
-    grads[item_name(0)] = low(matmul(inputs.T, dqkv))
+    line_b = reduce_line(geo, join(after(halves_b, qv_sums)), my_doc)
+    grads[item_name(0)] = low(matmul(inputs.T, tie(dqkv, line_b[0])))
     grads[item_name(1)] = (qv_sums, 0)
-    halves = [[tie(v, grads[item_name(0)]) for v in half] for half in halves]
-    line_b_parts = reduce_line(geo, join(halves), my_doc)
-    grads[item_name(0)] = tie(grads[item_name(0)], line_b_parts[0])
-    halves = reduce_cores(geo, pack_bucket(geo, buckets, 0, grads, coords))
-    halves = reduce_plane(geo, halves, 0)
-    dqkv = tie(dqkv, halves[0][0], halves[1][0])
-    token_grad = low(grad_one + matmul(dqkv, w_qkv.T))
-    halves = [[tie(v, token_grad) for v in half] for half in halves]
-    halves = reduce_plane(geo, halves, 1)
-    pieces_b = plus(*line_b_parts)
-    pieces_a = plus(*reduce_line(geo, join(halves), my_doc))
-
-    owned = lax.all_to_all(jnp.concatenate([pieces_a, pieces_b, pieces_c]), AXES, 0, 0, tiled=True)
+    pieces_d = plus(*[tie(part, grads[item_name(0)]) for part in line_d])
+    grads[item_name(0)] = tie(grads[item_name(0)], pieces_d)
+    arrays_a = pack_bucket(geo, buckets, 0, grads, coords)
+    halves_a = reduce_cores(geo, arrays_a)
+    pieces_b = plus(*[tie(part, arrays_a[0]) for part in line_b])
+    halves_a = reduce_plane(geo, after(halves_a, pieces_b), 0)
+    token_grad = low(grad_one + matmul(tie(dqkv, halves_a[0][0], halves_a[1][0]), w_qkv.T))
+    halves_a = reduce_plane(geo, after(halves_a, token_grad), 1)
+    first_row = lax.broadcasted_iota(jnp.int32, (seg_count, SEG_LEN, D), 1) == 0
+    crossed = tie(crossed, halves_a[0][0], halves_a[1][0])
+    mixed_out = jnp.where(
+        first_row, own(crossed)[:, None, :], hidden_two.reshape(seg_count, SEG_LEN, D)
+    )
+    line_a = reduce_line(geo, join(after(halves_a, mixed_out)), my_doc)
+    pieces_a = plus(*line_a)
+
+    owned = lax.all_to_all(
+        jnp.concatenate([pieces_a, pieces_b, pieces_d, pieces_c]), AXES, 0, 0, tiled=True
+    )
     natural = natural_rows(geo, table, owned.reshape(-1, LANES), pad_rows)
     gradient = natural[BLK : BLK + geo.chunk].reshape(-1)
     n_cls = n_doc * n_rows

time: 763 us -> 652 us (0.85)
  waiting for transfers between devices: 225 us -> 150 us
  Pallas kernels: 300 us -> 263 us
  starting transfers between devices: 42.4 us -> 52.6 us
  local copies, waits for them, and re-layouts: 27.5 us -> 19.4 us
    ppermute x39 -> x48, waiting for transfers between devices: 208 us -> 131 us  [send(): return lax.ppermute(value, AXES, geo.shift(axis, step))]
    pallas_call x14 -> x7, Pallas kernels: 137 us -> 110 us  [the longest x1 66 us: feed_layer(): pl.pallas_call(kernel, grid=(steps,), in_specs=[spec_smem()] + [spec_any(...]
    ppermute x39 -> x48, starting transfers between devices: 39 us -> 49.3 us  [send(): return lax.ppermute(value, AXES, geo.shift(axis, step))]
    pallas_call x2 -> x3, Pallas kernels: 16.8 us -> 21.7 us  [pack_bucket(): pl.pallas_call(kernel, out_shape=[jax.ShapeDtypeStruct(shape, jnp.bfloat1...]
    dot_general x7 -> x6, matrix products: 55 us -> 58.5 us  [matmul(): return jnp.dot(left, right, preferred_element_type=jnp.float32)]
    convert_element_type x18 -> x25, other arithmetic: 22.5 us -> 19.1 us  [low(): return values.astype(jnp.bfloat16)]
    pallas_call x4 -> x5, Pallas kernels: 72.1 us -> 69.2 us  [in_parts(): pl.pallas_call(kernel, grid=(count,), in_specs=in_specs + [spec_any()] *...]
  transfers between devices with their start and end apart: 41 -> 50, of which waited for: 25 -> 17; matrix products, arithmetic and copies ran while one was open for 8% -> 11% of each run, Pallas kernels for 20% -> 29%
where the time goes in v3:
time: 652 us; the launch traced here: 647 us
  Pallas kernels  263 us (40%)
  waiting for transfers between devices  150 us (23%)
  matrix products  58.5 us (9%)
  starting transfers between devices  52.6 us (8%)
  blocking collectives  50.1 us (8%)
  other arithmetic  37.3 us (6%)
  local copies, waits for them, and re-layouts  19.4 us (3%)
  between operations  14.9 us (2%)
    ppermute x48, waiting for transfers between devices, send(): return lax.ppermute(value, AXES, geo.shift(axis, step))  131 us
    pallas_call x5, Pallas kernels, in_parts(): pl.pallas_call(kernel, grid=(count,), in_specs=in_specs + [spec_any()] *...  69.2 us
    pallas_call x1, Pallas kernels, feed_layer(): pl.pallas_call(kernel, grid=(steps,), in_specs=[spec_smem()] + [spec_any(...  66 us
    dot_general x6, matrix products, matmul(): return jnp.dot(left, right, preferred_element_type=jnp.float32)  58.5 us
    ppermute x48, starting transfers between devices, send(): return lax.ppermute(value, AXES, geo.shift(axis, step))  49.3 us
    pallas_call x1, Pallas kernels, feed_back(): pl.pallas_call(feed_back_kernel, grid=(n // TILE,), in_specs=[tiles(D), f...  43.9 us
    all_to_all x1, blocking collectives, local(): lax.all_to_all(aligned.reshape(geo.n_dev, geo.piece, LANES), AXES, 0, 0,...  29.8 us
    pallas_call x1, Pallas kernels, cross_layer(): pl.pallas_call(kernel, out_shape=[jax.ShapeDtypeStruct(shape, f32 if i ==...  22.3 us
  transfers between devices with their start and end apart: 50, of which 17 were waited for; matrix products, arithmetic and copies ran while one was open for 11% of the time, Pallas kernels for 29%

profile of v3, /device:TPU:0, one launch (start us, length us, event | category | flops | bytes accessed | tf_op | source)
XLA Modules:
  0.0 646.5 jit_solution(13482068416005951276)
XLA Ops:
  14.2 29.8 %all_to_all.10 = bf16[32,112,128]{2,1,0:T(8,128)(2,1)S(1)} all-to-all(bf16[32,112,128]{2,1,0:T(8,128)(2,1)} %bitcast.164), channel_id=1, replica_groups=mesh['seg'=8,'doc'=4] {'seg','doc'}, dimensions={0} | all-to-all | bytes 1835008 | tf_op jit(solution)/shard_map/all_to_all | solution.py:1394
  51.6 6.7 %collective-permute-done.1.refs_2_ = bf16[4,112,128]{2,1,0:T(8,128)(2,1)S(1)} collective-permute-done((bf16[4,112,128]{2,1,0:T(8,128)(2,1)S(1)}, bf16[4,112,128]{2,1,0:T(8,128)(2,1)S(1)}, u32[]{:S(2)}, u32[]{:S(2)}) %collective-permute-start.1) | collective-permute-done | bytes 114720 | tf_op jit(solution)/shard_map/ppermute | solution.py:1294
  63.0 4.9 collective-permute-done.8
  76.6 14.8 %collective-permute-done.4.refs_2_ = bf16[12,112,128]{2,1,0:T(8,128)(2,1)S(1)} collective-permute-done((bf16[12,112,128]{2,1,0:T(8,128)(2,1)S(1)}, bf16[12,112,128]{2,1,0:T(8,128)(2,1)S(1)}, u32[]{:S(2)}, u32[]{:S(2)}) %collective-permute-start.4) | collective-permute-done | bytes 344096 | tf_op jit(solution)/shard_map/ppermute | solution.py:1294
  99.0 9.8 %all_gather.12 = bf16[128,896]{1,0:T(8,128)(2,1)S(1)} all-gather(bf16[16,896]{1,0:T(8,128)(2,1)S(1)} %convert_element_type.273), channel_id=1, replica_groups=mesh['seg'=8,'doc'=4] {'seg'}, dimensions={0}, use_global_device_ids=true | all-gather | bytes 258048 | tf_op jit(solution)/shard_map/all_gather | solution.py:1416
  113.3 12.7 %shard_map.149 = (bf16[2048,2304]{1,0:T(8,128)(2,1)}, bf16[2048,768]{1,0:T(8,128)(2,1)}, f32[2048,128]{1,0:T(8,128)}, bf16[768,2304]{1,0:T(8,128)(2,1)}, f32[16,768]{1,0:T(8,128)}) custom-call(s32[4]{0:T(128)} %pad_add_fusion.coords_ref, bf16[2,2,2,448,128]{4,3,2,1,0:T(8,128)(2,1)} %copy-done.11, ...), custom_call_target="tpu_custom_call" | custom-call | flops 12000000000 | bytes 36000000 | tf_op jit(solution)/shard_map/pallas_call | solution.py:845
  133.9 16.4 %shard_map.150 = (bf16[2048,2304]{1,0:T(8,128)(2,1)}, bf16[2048,768]{1,0:T(8,128)(2,1)}, f32[2048,128]{1,0:T(8,128)}) custom-call(bf16[2048,768]{1,0:T(8,128)(2,1)} %bitcast.179, bf16[768,2304]{1,0:T(8,128)(2,1)} %get-tuple-element.158.wqkv_ref, f32[16,768]{1,0:T(8,128)} %get-tuple-element.154.vec_ref, ...), custom_call_target="tpu_custom_call", output_to_operand_aliasing={{0}: (3, {}), {1}: (4, {}), {2}: (5, {})} | custom-call | flops 16000000000 | bytes 48000000 | tf_op jit(solution)/shard_map/pallas_call | solution.py:794
  152.5 38.4 %collective-permute-done.16 = bf16[2,6,448,128]{3,2,1,0:T(8,128)(2,1)S(1)} collective-permute-done((bf16[2,6,448,128]{3,2,1,0:T(8,128)(2,1)S(1)}, bf16[2,6,448,128]{3,2,1,0:T(8,128)(2,1)S(1)}, u32[]{:S(2)}, u32[]{:S(2)}) %collective-permute-start.16) | collective-permute-done | bytes 1376288 | tf_op jit(solution)/shard_map/ppermute | solution.py:1294
  199.3 9.4 %shard_map.151 = (bf16[2048,2304]{1,0:T(8,128)(2,1)}, bf16[2048,768]{1,0:T(8,128)(2,1)}, f32[2048,128]{1,0:T(8,128)}) custom-call(bf16[2048,768]{1,0:T(8,128)(2,1)} %bitcast.180, bf16[768,2304]{1,0:T(8,128)(2,1)} %get-tuple-element.158.wqkv_ref, f32[16,768]{1,0:T(8,128)} %get-tuple-element.154.vec_ref, ...), custom_call_target="tpu_custom_call", output_to_operand_aliasing={{0}: (3, {}), {1}: (4, {}), {2}: (5, {})} | custom-call | flops 8000000000 | bytes 24000000 | tf_op jit(solution)/shard_map/pallas_call | solution.py:794
  208.7 66.0 %shard_map.152 = (bf16[2048,768]{1,0:T(8,128)(2,1)}, bf16[2048,768]{1,0:T(8,128)(2,1)}, bf16[2048,3072]{1,0:T(8,128)(2,1)}, bf16[2048,3072]{1,0:T(8,128)(2,1)}, ...) custom-call(s32[4]{0:T(128)} %pad_add_fusion.coords_ref, ...), custom_call_target="tpu_custom_call" | custom-call | flops 60000002048 | bytes 180000000 | tf_op jit(solution)/shard_map/pallas_call | solution.py:950
  277.6 10.4 %all_gather.15.refs_1_ = bf16[128,768]{1,0:T(8,128)(2,1)} all-gather(bf16[16,768]{1,0:T(8,128)(2,1)} %shard_map.153), channel_id=1, replica_groups=mesh['seg'=8,'doc'=4] {'seg'}, dimensions={0}, use_global_device_ids=true | all-gather | bytes 221184 | tf_op jit(solution)/shard_map/all_gather | solution.py:1441
  289.4 22.3 %shard_map.154 = (bf16[128,768]{1,0:T(8,128)(2,1)}, bf16[128,768]{1,0:T(8,128)(2,1)}, f32[16,768]{1,0:T(8,128)}, bf16[128,2304]{1,0:T(8,128)(2,1)}, bf16[128,768...) custom-call(s32[4]{0:T(128)} %pad_add_fusion.coords_ref, ...), custom_call_target="tpu_custom_call" | custom-call | flops 22000001024 | bytes 66000000 | tf_op jit(solution)/shard_map/pallas_call | solution.py:1242
  313.1 12.7 %shard_map.155 = bf16[16,448,128]{2,1,0:T(8,128)(2,1)} custom-call(s32[1]{0:T(128)} %bitcast.29.seg_ref, bf16[64,128]{1,0:T(8,128)(2,1)} %fusion.6.refs_0_, bf16[768,128]{1,0:T(8,128)(2,1)} %get-tuple-element.175.refs_1_, bf16[768,128]{1,0:T(8,128)(2,1)} %get-tuple-element.176.refs_2_, bf16[768,128]{1,0:T(8,128)(2,1)} %get-tuple-element.177.refs_3_, ...), custom_call_target="tpu_custom_call" | custom-call | flops 12000000000 | bytes 36000000 | tf_op jit(solution)/shard_map/pallas_call | solution.py:666
  327.4 3.8 collective-permute-start.20
  331.3 43.9 %shard_map.156 = (bf16[2048,768]{1,0:T(8,128)(2,1)}, bf16[2048,3072]{1,0:T(8,128)(2,1)}, bf16[2048,768]{1,0:T(8,128)(2,1)}, bf16[2048,768]{1,0:T(8,128)(2,1)}, f32[2048,768]{1,0:T(8,128)}, /*index=5*/f32[16,768]{1,0:T(8,128)}) custom-call(bf16[2048,768]{1,0:T(8,128)(2,1)} %bitcast.177, f32[16,768]{1,0:T(8,128)} %dynamic-slice_convert_fusion.cls_ref, ...), custom_call_target="tpu_custom_call" | custom-call | flops 44000002048 | bytes 132000000 | tf_op jit(solution)/shard_map/pallas_call | solution.py:1037
  377.8 15.4 %convolution_convert_fusion.2.refs_0_.refs_4_ = bf16[3072,768]{1,0:T(8,128)(2,1)} fusion(bf16[2048,3072]{1,0:T(8,128)(2,1)} %get-tuple-element.195, bf16[2048,768]{1,0:T(8,128)(2,1)} %get-tuple-element.202), kind=kOutput, calls=%fused_computation.3 | convolution fusion | flops 9666035712 | bytes 20447232 | tf_op jit(solution)/shard_map/dot_general | solution.py:1371
  393.1 8.0 %shard_map.157 = (bf16[2,2,3,448,128]{4,3,2,1,0:T(8,128)(2,1)}, bf16[2,2,3,448,128]{4,3,2,1,0:T(8,128)(2,1)}, bf16[2,2,2,448,128]{4,3,2,1,0:T(8,128)(2,1)}, bf16[2,2,2,448,128]{4,3,2,1,0:T(8,128)(2,1)}) custom-call(s32[4]{0:T(128)} %pad_add_fusion.coords_ref, bf16[3072,768]{1,0:T(8,128)(2,1)} %convolution_convert_fusion.2.refs_0_.refs_4_, ...), custom_call_target="tpu_custom_call" | custom-call | flops 7000000000 | bytes 21000000 | tf_op jit(solution)/shard_map/pallas_call | solution.py:572
  401.9 14.7 %convolution_convert_fusion.1.refs_2_ = bf16[768,3072]{1,0:T(8,128)(2,1)} fusion(bf16[2048,768]{1,0:T(8,128)(2,1)S(1)} %copy-done.28, bf16[2048,3072]{1,0:T(8,128)(2,1)} %get-tuple-element.206), kind=kOutput, calls=%fused_computation.2 | convolution fusion | flops 9666035712 | bytes 20447232 | tf_op jit(solution)/shard_map/dot_general | solution.py:1371
  423.9 7.8 %shard_map.158 = (bf16[2,2,4,448,128]{4,3,2,1,0:T(8,128)(2,1)}, bf16[2,2,4,448,128]{4,3,2,1,0:T(8,128)(2,1)}, bf16[2,2,3,448,128]{4,3,2,1,0:T(8,128)(2,1)}, bf16[2,2,3,448,128]{4,3,2,1,0:T(8,128)(2,1)}) custom-call(s32[4]{0:T(128)} %pad_add_fusion.coords_ref, bf16[768,768]{1,0:T(8,128)(2,1)} %convolution_convert_fusion.3.refs_0_.refs_2_, ...), custom_call_target="tpu_custom_call" | custom-call | flops 7000000000 | bytes 21000000 | tf_op jit(solution)/shard_map/pallas_call | solution.py:572
  434.5 11.9 %shard_map.159 = (bf16[2048,2304]{1,0:T(8,128)(2,1)}, f32[8,768]{1,0:T(8,128)}) custom-call(bf16[2048,2304]{1,0:T(8,128)(2,1)} %get-tuple-element.172.packed_ref, f32[2048,128]{1,0:T(8,128)} %get-tuple-element.173.stat_ref, bf16[2048,768]{1,0:T(8,128)(2,1)} %get-tuple-element.240.da_ref, f32[8,768]{1,0:T(8,128)} %broadcast_in_dim.54.before_ref), custom_call_target="tpu_custom_call" | custom-call | flops 10000000000 | bytes 30000000 | tf_op jit(solution)/shard_map/pallas_call | solution.py:794
  457.4 19.9 %shard_map.160 = (bf16[2048,2304]{1,0:T(8,128)(2,1)}, f32[8,768]{1,0:T(8,128)}) custom-call(bf16[2048,2304]{1,0:T(8,128)(2,1)} %get-tuple-element.172.packed_ref, f32[2048,128]{1,0:T(8,128)} %get-tuple-element.173.stat_ref, bf16[2048,768]{1,0:T(8,128)(2,1)} %get-tuple-element.240.da_ref, ...), custom_call_target="tpu_custom_call", output_to_operand_aliasing={{0}: (4, {})} | custom-call | flops 20000000000 | bytes 60000000 | tf_op jit(solution)/shard_map/pallas_call | solution.py:794
  487.7 12.9 %collective-permute-done.29 = bf16[2,4,448,128]{3,2,1,0:T(8,128)(2,1)S(1)} collective-permute-done((bf16[2,4,448,128]{3,2,1,0:T(8,128)(2,1)S(1)}, bf16[2,4,448,128]{3,2,1,0:T(8,128)(2,1)S(1)}, u32[]{:S(2)}, u32[]{:S(2)}) %collective-permute-start.29) | collective-permute-done | bytes 917536 | tf_op jit(solution)/shard_map/ppermute | solution.py:1294
  502.0 11.6 %shard_map.161 = (bf16[2048,2304]{1,0:T(8,128)(2,1)}, f32[8,768]{1,0:T(8,128)}) custom-call(bf16[2048,2304]{1,0:T(8,128)(2,1)} %get-tuple-element.172.packed_ref, f32[2048,128]{1,0:T(8,128)} %get-tuple-element.173.stat_ref, bf16[2048,768]{1,0:T(8,128)(2,1)} %get-tuple-element.240.da_ref, ...), custom_call_target="tpu_custom_call", output_to_operand_aliasing={{0}: (4, {})} | custom-call | flops 10000000000 | bytes 30000000 | tf_op jit(solution)/shard_map/pallas_call | solution.py:794
  515.5 12.8 %fusion.refs_0_ = bf16[768,2304]{1,0:T(8,128)(2,1)} fusion(bf16[2048,2304]{1,0:T(8,128)(2,1)} %get-tuple-element.267, bf16[2048,768]{1,0:T(8,128)(2,1)S(1)} %bitcast.182), kind=kOutput, calls=%fused_computation.4 | convolution fusion | flops 7249526784 | bytes 16121856 | tf_op jit(solution)/shard_map/dot_general | solution.py:1371
  528.3 6.0 shard_map.162
  541.8 14.1 %collective-permute-done.37 = bf16[7,112,128]{2,1,0:T(8,128)(2,1)S(1)} collective-permute-done((bf16[7,112,128]{2,1,0:T(8,128)(2,1)S(1)}, bf16[7,112,128]{2,1,0:T(8,128)(2,1)S(1)}, u32[]{:S(2)}, u32[]{:S(2)}) %collective-permute-start.37) | collective-permute-done | bytes 200736 | tf_op jit(solution)/shard_map/ppermute | solution.py:1294
  559.6 10.2 %fusion.16 = f32[2048,768]{1,0:T(8,128)S(1)} fusion(bf16[2048,2304]{1,0:T(8,128)(2,1)} %get-tuple-element.267, bf16[768,2304]{1,0:T(8,128)(2,1)S(1)} %copy-done.27), kind=kOutput, calls=%fused_computation.112 | convolution fusion | flops 7247757312 | bytes 19267584 | tf_op jit(solution)/shard_map/dot_general | solution.py:1371
  574.5 11.2 %collective-permute-done.42 = bf16[2,2,448,128]{3,2,1,0:T(8,128)(2,1)S(1)} collective-permute-done((bf16[2,2,448,128]{3,2,1,0:T(8,128)(2,1)S(1)}, bf16[2,2,448,128]{3,2,1,0:T(8,128)(2,1)S(1)}, u32[]{:S(2)}, u32[]{:S(2)}) %collective-permute-start.42) | collective-permute-done | bytes 458784 | tf_op jit(solution)/shard_map/ppermute | solution.py:1294
  587.2 5.4 collective-permute-done.44
  599.6 3.8 collective-permute-done.46
  610.9 19.3 %all-to-all-done.1 = bf16[32,112,128]{2,1,0:T(8,128)(2,1)} async-done(((bf16[32,112,128]{2,1,0:T(8,128)(2,1)}), bf16[32,112,128]{2,1,0:T(8,128)(2,1)}, u32[]{:S(2)}, u32[]{:S(2)}) %all-to-all-start.1) | async-done | bytes 917536 | tf_op jit(solution)/shard_map/all_to_all | solution.py:1504
  633.3 4.4 fusion.14
  (233 shorter events, 140.2 us)
Async XLA Ops:
  7.2 267.5 %all-gather.3.cloned.1.call-start = ((), (), s32[]{:S(2)}) async-start(), calls=%async_computation.2 | async-start | bytes 15138816 | tf_op jit(solution)/shard_map/all_gather | solution.py:1423
  71.9 19.5 %collective-permute-start.9 = (bf16[2,2,448,128]{3,2,1,0:T(8,128)(2,1)S(1)}, bf16[2,2,448,128]{3,2,1,0:T(8,128)(2,1)S(1)}, u32[]{:S(2)}, u32[]{:S(2)}) collective-permute-start(bf16[2,2,448,128]{3,2,1,0:T(8,128)(2,1)S(1)} %get-tuple-element.325), channel_id=1, source_target_pairs={{0,8},{1,9},{2,10},{3,11},{4,12},{5,13},{6,14},{7,15},{8,0},{9,1},... | collective-permute-start | bytes 1376264 | tf_op jit(solution)/shard_map/ppermute | solution.py:1294
  74.6 16.8 %collective-permute-start.7 = (bf16[2,2,448,128]{3,2,1,0:T(8,128)(2,1)S(1)}, bf16[2,2,448,128]{3,2,1,0:T(8,128)(2,1)S(1)}, u32[]{:S(2)}, u32[]{:S(2)}) collective-permute-start(bf16[2,2,448,128]{3,2,1,0:T(8,128)(2,1)S(1)} %get-tuple-element.327), channel_id=1, source_target_pairs={{0,16},{1,17},{2,18},{3,19},{4,20},{5,21},{6,22},{7,23},{8,24},{9,... | collective-permute-start | bytes 1376264 | tf_op jit(solution)/shard_map/ppermute | solution.py:1294
  92.2 21.1 %collective-permute-start.11 = (bf16[2,2,2,448,128]{4,3,2,1,0:T(8,128)(2,1)S(1)}, bf16[2,2,2,448,128]{4,3,2,1,0:T(8,128)(2,1)}, u32[]{:S(2)}, u32[]{:S(2)}) collective-permute-start(bf16[2,2,2,448,128]{4,3,2,1,0:T(8,128)(2,1)S(1)} %pad_maximum_fusion.4.refs_0_), channel_id=1, source_target_pairs={{0,4},{1,5},{2,6},{3,7},{4,0},{5,1},{6,2},{7,3},{8,12},{9,13},{10,... | collective-permute-start | bytes 2752520 | tf_op jit(solution)/shard_map/ppermute | solution.py:1294
  92.4 20.9 %collective-permute-start.12 = (bf16[2,2,2,448,128]{4,3,2,1,0:T(8,128)(2,1)S(1)}, bf16[2,2,2,448,128]{4,3,2,1,0:T(8,128)(2,1)}, u32[]{:S(2)}, u32[]{:S(2)}) collective-permute-start(bf16[2,2,2,448,128]{4,3,2,1,0:T(8,128)(2,1)S(1)} %pad_maximum_fusion.5.refs_2_), channel_id=1, source_target_pairs={{0,4},{1,5},{2,6},{3,7},{4,0},{5,1},{6,2},{7,3},{8,12},{9,13},{10,... | collective-permute-start | bytes 2752520 | tf_op jit(solution)/shard_map/ppermute | solution.py:1294
  92.9 15.9 %collective-permute-start.5 = (bf16[12,112,128]{2,1,0:T(8,128)(2,1)S(1)}, bf16[12,112,128]{2,1,0:T(8,128)(2,1)}, u32[]{:S(2)}, u32[]{:S(2)}) collective-permute-start(bf16[12,112,128]{2,1,0:T(8,128)(2,1)S(1)} %slice.125.refs_0_), channel_id=1, source_target_pairs={{0,3},{1,0},{2,1},{3,2},{4,7},{5,4},{6,5},{7,6},{8,11},{9,8},{10,9... | collective-permute-start | bytes 1032200 | tf_op jit(solution)/shard_map/ppermute | solution.py:1294
  111.3 18.2 %collective-permute-start.10 = (bf16[6,448,128]{2,1,0:T(8,128)(2,1)}, bf16[6,448,128]{2,1,0:T(8,128)(2,1)}, u32[]{:S(2)}, u32[]{:S(2)}) collective-permute-start(bf16[6,448,128]{2,1,0:T(8,128)(2,1)} %get-tuple-element.151), channel_id=1, source_target_pairs={{0,8},{1,9},{2,10},{3,11},{4,12},{5,13},{6,14},{7,15},{8,0},{9,1},... | collective-permute-start | bytes 2064392 | tf_op jit(solution)/shard_map/ppermute | solution.py:1294
  111.8 17.6 %collective-permute-start.13 = (bf16[6,448,128]{2,1,0:T(8,128)(2,1)}, bf16[6,448,128]{2,1,0:T(8,128)(2,1)S(1)}, u32[]{:S(2)}, u32[]{:S(2)}) collective-permute-start(bf16[6,448,128]{2,1,0:T(8,128)(2,1)} %get-tuple-element.152), channel_id=1, source_target_pairs={{0,16},{1,17},{2,18},{3,19},{4,20},{5,21},{6,22},{7,23},{8,24},{9,... | collective-permute-start | bytes 2064392 | tf_op jit(solution)/shard_map/ppermute | solution.py:1294
  150.4 40.5 %collective-permute-start.16 = (bf16[2,6,448,128]{3,2,1,0:T(8,128)(2,1)S(1)}, bf16[2,6,448,128]{3,2,1,0:T(8,128)(2,1)S(1)}, u32[]{:S(2)}, u32[]{:S(2)}) collective-permute-start(bf16[2,6,448,128]{3,2,1,0:T(8,128)(2,1)S(1)} %get-tuple-element.292), channel_id=1, source_target_pairs={{0,8},{1,9},{2,10},{3,11},{4,12},{5,13},{6,14},{7,15},{8,0},{9,1},... | collective-permute-start | bytes 4128776 | tf_op jit(solution)/shard_map/ppermute | solution.py:1294
  151.9 40.9 %collective-permute-start.14 = (bf16[2,6,448,128]{3,2,1,0:T(8,128)(2,1)S(1)}, bf16[2,6,448,128]{3,2,1,0:T(8,128)(2,1)S(1)}, u32[]{:S(2)}, u32[]{:S(2)}) collective-permute-start(bf16[2,6,448,128]{3,2,1,0:T(8,128)(2,1)S(1)} %get-tuple-element.330), channel_id=1, source_target_pairs={{0,16},{1,17},{2,18},{3,19},{4,20},{5,21},{6,22},{7,23},{8,24},{9,... | collective-permute-start | bytes 4128776 | tf_op jit(solution)/shard_map/ppermute | solution.py:1294
  327.4 49.4 %collective-permute-start.18 = (bf16[16,112,128]{2,1,0:T(8,128)(2,1)S(1)}, bf16[16,112,128]{2,1,0:T(8,128)(2,1)S(1)}, u32[]{:S(2)}, u32[]{:S(2)}) collective-permute-start(bf16[16,112,128]{2,1,0:T(8,128)(2,1)S(1)} %get-tuple-element.283), channel_id=1, source_target_pairs={{0,1},{1,2},{2,3},{3,0},{4,5},{5,6},{6,7},{7,4},{8,9},{9,10},{10,1... | collective-permute-start | bytes 1376264 | tf_op jit(solution)/shard_map/ppermute | solution.py:1294
  327.4 49.4 %collective-permute-start.20 = (bf16[16,112,128]{2,1,0:T(8,128)(2,1)S(1)}, bf16[16,112,128]{2,1,0:T(8,128)(2,1)S(1)}, u32[]{:S(2)}, u32[]{:S(2)}) collective-permute-start(bf16[16,112,128]{2,1,0:T(8,128)(2,1)S(1)} %get-tuple-element.284), channel_id=1, source_target_pairs={{0,3},{1,0},{2,1},{3,2},{4,7},{5,4},{6,5},{7,6},{8,11},{9,8},{10,9... | collective-permute-start | bytes 1376264 | tf_op jit(solution)/shard_map/ppermute | solution.py:1294
  331.3 45.6 %collective-permute-start.19 = (bf16[16,112,128]{2,1,0:T(8,128)(2,1)S(1)}, bf16[16,112,128]{2,1,0:T(8,128)(2,1)S(1)}, u32[]{:S(2)}, u32[]{:S(2)}) collective-permute-start(bf16[16,112,128]{2,1,0:T(8,128)(2,1)S(1)} %get-tuple-element.285), channel_id=1, source_target_pairs={{0,2},{1,3},{2,0},{3,1},{4,6},{5,7},{6,4},{7,5},{8,10},{9,11},{10,... | collective-permute-start | bytes 1376264 | tf_op jit(solution)/shard_map/ppermute | solution.py:1294
  401.9 16.5 %collective-permute-start.21 = (bf16[2,2,3,448,128]{4,3,2,1,0:T(8,128)(2,1)}, bf16[2,2,3,448,128]{4,3,2,1,0:T(8,128)(2,1)S(1)}, u32[]{:S(2)}, u32[]{:S(2)}) collective-permute-start(bf16[2,2,3,448,128]{4,3,2,1,0:T(8,128)(2,1)} %get-tuple-element.208), channel_id=1, source_target_pairs={{0,4},{1,5},{2,6},{3,7},{4,0},{5,1},{6,2},{7,3},{8,12},{9,13},{10,... | collective-permute-start | bytes 4128776 | tf_op jit(solution)/shard_map/ppermute | solution.py:1294
  417.0 29.4 %collective-permute-start.26 = (bf16[2,2,448,128]{3,2,1,0:T(8,128)(2,1)S(1)}, bf16[2,2,448,128]{3,2,1,0:T(8,128)(2,1)S(1)}, u32[]{:S(2)}, u32[]{:S(2)}) collective-permute-start(bf16[2,2,448,128]{3,2,1,0:T(8,128)(2,1)S(1)} %get-tuple-element.301), channel_id=1, source_target_pairs={{0,8},{1,9},{2,10},{3,11},{4,12},{5,13},{6,14},{7,15},{8,0},{9,1},... | collective-permute-start | bytes 1376264 | tf_op jit(solution)/shard_map/ppermute | solution.py:1294
  431.7 18.3 %collective-permute-start.25 = (bf16[2,3,448,128]{3,2,1,0:T(8,128)(2,1)}, bf16[2,3,448,128]{3,2,1,0:T(8,128)(2,1)}, u32[]{:S(2)}, u32[]{:S(2)}) collective-permute-start(bf16[2,3,448,128]{3,2,1,0:T(8,128)(2,1)} %get-tuple-element.289), channel_id=1, source_target_pairs={{0,16},{1,17},{2,18},{3,19},{4,20},{5,21},{6,22},{7,23},{8,24},{9,... | collective-permute-start | bytes 2064392 | tf_op jit(solution)/shard_map/ppermute | solution.py:1294
  433.4 19.7 %collective-permute-start.24 = (bf16[2,2,3,448,128]{4,3,2,1,0:T(8,128)(2,1)}, bf16[2,2,3,448,128]{4,3,2,1,0:T(8,128)(2,1)}, u32[]{:S(2)}, u32[]{:S(2)}) collective-permute-start(bf16[2,2,3,448,128]{4,3,2,1,0:T(8,128)(2,1)} %get-tuple-element.223), channel_id=1, source_target_pairs={{0,4},{1,5},{2,6},{3,7},{4,0},{5,1},{6,2},{7,3},{8,12},{9,13},{10,... | collective-permute-start | bytes 4128776 | tf_op jit(solution)/shard_map/ppermute | solution.py:1294
  433.4 23.4 %collective-permute-start.23 = (bf16[2,2,4,448,128]{4,3,2,1,0:T(8,128)(2,1)}, bf16[2,2,4,448,128]{4,3,2,1,0:T(8,128)(2,1)S(1)}, u32[]{:S(2)}, u32[]{:S(2)}) collective-permute-start(bf16[2,2,4,448,128]{4,3,2,1,0:T(8,128)(2,1)} %get-tuple-element.219), channel_id=1, source_target_pairs={{0,4},{1,5},{2,6},{3,7},{4,0},{5,1},{6,2},{7,3},{8,12},{9,13},{10,... | collective-permute-start | bytes 5505032 | tf_op jit(solution)/shard_map/ppermute | solution.py:1294
  447.3 30.1 %collective-permute-start.28 = (bf16[2,448,128]{2,1,0:T(8,128)(2,1)}, bf16[2,448,128]{2,1,0:T(8,128)(2,1)}, u32[]{:S(2)}, u32[]{:S(2)}) collective-permute-start(bf16[2,448,128]{2,1,0:T(8,128)(2,1)} %get-tuple-element.322), channel_id=1, source_target_pairs={{0,16},{1,17},{2,18},{3,19},{4,20},{5,21},{6,22},{7,23},{8,24},{9,... | collective-permute-start | bytes 688136 | tf_op jit(solution)/shard_map/ppermute | solution.py:1294
  452.1 25.2 %collective-permute-start.27 = (bf16[3,448,128]{2,1,0:T(8,128)(2,1)}, bf16[3,448,128]{2,1,0:T(8,128)(2,1)}, u32[]{:S(2)}, u32[]{:S(2)}) collective-permute-start(bf16[3,448,128]{2,1,0:T(8,128)(2,1)} %get-tuple-element.309), channel_id=1, source_target_pairs={{0,8},{1,9},{2,10},{3,11},{4,12},{5,13},{6,14},{7,15},{8,0},{9,1},... | collective-permute-start | bytes 1032200 | tf_op jit(solution)/shard_map/ppermute | solution.py:1294
  455.7 30.4 %collective-permute-start.30 = (bf16[2,3,448,128]{3,2,1,0:T(8,128)(2,1)}, bf16[2,3,448,128]{3,2,1,0:T(8,128)(2,1)}, u32[]{:S(2)}, u32[]{:S(2)}) collective-permute-start(bf16[2,3,448,128]{3,2,1,0:T(8,128)(2,1)} %get-tuple-element.287), channel_id=1, source_target_pairs={{0,8},{1,9},{2,10},{3,11},{4,12},{5,13},{6,14},{7,15},{8,0},{9,1},... | collective-permute-start | bytes 2064392 | tf_op jit(solution)/shard_map/ppermute | solution.py:1294
  477.3 23.4 %collective-permute-start.29 = (bf16[2,4,448,128]{3,2,1,0:T(8,128)(2,1)S(1)}, bf16[2,4,448,128]{3,2,1,0:T(8,128)(2,1)S(1)}, u32[]{:S(2)}, u32[]{:S(2)}) collective-permute-start(bf16[2,4,448,128]{3,2,1,0:T(8,128)(2,1)S(1)} %get-tuple-element.281), channel_id=1, source_target_pairs={{0,16},{1,17},{2,18},{3,19},{4,20},{5,21},{6,22},{7,23},{8,24},{9,... | collective-permute-start | bytes 2752520 | tf_op jit(solution)/shard_map/ppermute | solution.py:1294
  480.8 47.5 %collective-permute-start.33 = (bf16[5,112,128]{2,1,0:T(8,128)(2,1)S(1)}, bf16[5,112,128]{2,1,0:T(8,128)(2,1)S(1)}, u32[]{:S(2)}, u32[]{:S(2)}) collective-permute-start(bf16[5,112,128]{2,1,0:T(8,128)(2,1)S(1)} %get-tuple-element.311), channel_id=1, source_target_pairs={{0,1},{1,2},{2,3},{3,0},{4,5},{5,6},{6,7},{7,4},{8,9},{9,10},{10,1... | collective-permute-start | bytes 430088 | tf_op jit(solution)/shard_map/ppermute | solution.py:1294
  481.4 46.8 %collective-permute-start.35 = (bf16[5,112,128]{2,1,0:T(8,128)(2,1)S(1)}, bf16[5,112,128]{2,1,0:T(8,128)(2,1)S(1)}, u32[]{:S(2)}, u32[]{:S(2)}) collective-permute-start(bf16[5,112,128]{2,1,0:T(8,128)(2,1)S(1)} %get-tuple-element.312), channel_id=1, source_target_pairs={{0,3},{1,0},{2,1},{3,2},{4,7},{5,4},{6,5},{7,6},{8,11},{9,8},{10,9... | collective-permute-start | bytes 430088 | tf_op jit(solution)/shard_map/ppermute | solution.py:1294
  484.6 43.6 %collective-permute-start.34 = (bf16[5,112,128]{2,1,0:T(8,128)(2,1)S(1)}, bf16[5,112,128]{2,1,0:T(8,128)(2,1)S(1)}, u32[]{:S(2)}, u32[]{:S(2)}) collective-permute-start(bf16[5,112,128]{2,1,0:T(8,128)(2,1)S(1)} %get-tuple-element.313), channel_id=1, source_target_pairs={{0,2},{1,3},{2,0},{3,1},{4,6},{5,7},{6,4},{7,5},{8,10},{9,11},{10,... | collective-permute-start | bytes 430088 | tf_op jit(solution)/shard_map/ppermute | solution.py:1294
  487.4 26.2 %collective-permute-start.32 = (bf16[3,448,128]{2,1,0:T(8,128)(2,1)S(1)}, bf16[3,448,128]{2,1,0:T(8,128)(2,1)S(1)}, u32[]{:S(2)}, u32[]{:S(2)}) collective-permute-start(bf16[3,448,128]{2,1,0:T(8,128)(2,1)S(1)} %get-tuple-element.307), channel_id=1, source_target_pairs={{0,16},{1,17},{2,18},{3,19},{4,20},{5,21},{6,22},{7,23},{8,24},{9,... | collective-permute-start | bytes 1032200 | tf_op jit(solution)/shard_map/ppermute | solution.py:1294
  534.3 21.7 %collective-permute-start.39 = (bf16[2,2,2,448,128]{4,3,2,1,0:T(8,128)(2,1)}, bf16[2,2,2,448,128]{4,3,2,1,0:T(8,128)(2,1)S(1)}, u32[]{:S(2)}, u32[]{:S(2)}) collective-permute-start(bf16[2,2,2,448,128]{4,3,2,1,0:T(8,128)(2,1)} %get-tuple-element.260), channel_id=1, source_target_pairs={{0,4},{1,5},{2,6},{3,7},{4,0},{5,1},{6,2},{7,3},{8,12},{9,13},{10,... | collective-permute-start | bytes 2752520 | tf_op jit(solution)/shard_map/ppermute | solution.py:1294
  535.1 20.8 %collective-permute-start.37 = (bf16[7,112,128]{2,1,0:T(8,128)(2,1)S(1)}, bf16[7,112,128]{2,1,0:T(8,128)(2,1)S(1)}, u32[]{:S(2)}, u32[]{:S(2)}) collective-permute-start(bf16[7,112,128]{2,1,0:T(8,128)(2,1)S(1)} %get-tuple-element.305), channel_id=1, source_target_pairs={{0,2},{1,3},{2,0},{3,1},{4,6},{5,7},{6,4},{7,5},{8,10},{9,11},{10,... | collective-permute-start | bytes 602120 | tf_op jit(solution)/shard_map/ppermute | solution.py:1294
  537.4 18.4 %collective-permute-start.36 = (bf16[7,112,128]{2,1,0:T(8,128)(2,1)S(1)}, bf16[7,112,128]{2,1,0:T(8,128)(2,1)S(1)}, u32[]{:S(2)}, u32[]{:S(2)}) collective-permute-start(bf16[7,112,128]{2,1,0:T(8,128)(2,1)S(1)} %get-tuple-element.303), channel_id=1, source_target_pairs={{0,1},{1,2},{2,3},{3,0},{4,5},{5,6},{6,7},{7,4},{8,9},{9,10},{10,1... | collective-permute-start | bytes 602120 | tf_op jit(solution)/shard_map/ppermute | solution.py:1294
  539.5 19.7 %collective-permute-start.40 = (bf16[2,2,2,448,128]{4,3,2,1,0:T(8,128)(2,1)}, bf16[2,2,2,448,128]{4,3,2,1,0:T(8,128)(2,1)S(1)}, u32[]{:S(2)}, u32[]{:S(2)}) collective-permute-start(bf16[2,2,2,448,128]{4,3,2,1,0:T(8,128)(2,1)} %get-tuple-element.265), channel_id=1, source_target_pairs={{0,4},{1,5},{2,6},{3,7},{4,0},{5,1},{6,2},{7,3},{8,12},{9,13},{10,... | collective-permute-start | bytes 2752520 | tf_op jit(solution)/shard_map/ppermute | solution.py:1294
  573.4 19.2 %collective-permute-start.43 = (bf16[2,448,128]{2,1,0:T(8,128)(2,1)S(1)}, bf16[2,448,128]{2,1,0:T(8,128)(2,1)S(1)}, u32[]{:S(2)}, u32[]{:S(2)}) collective-permute-start(bf16[2,448,128]{2,1,0:T(8,128)(2,1)S(1)} %get-tuple-element.318), channel_id=1, source_target_pairs={{0,8},{1,9},{2,10},{3,11},{4,12},{5,13},{6,14},{7,15},{8,0},{9,1},... | collective-permute-start | bytes 688136 | tf_op jit(solution)/shard_map/ppermute | solution.py:1294
  604.5 25.7 %all-to-all-start.1 = ((bf16[32,112,128]{2,1,0:T(8,128)(2,1)}), bf16[32,112,128]{2,1,0:T(8,128)(2,1)}, u32[]{:S(2)}, u32[]{:S(2)}) async-start(bf16[32,112,128]{2,1,0:T(8,128)(2,1)} %pad_maximum_fusion.6), calls=%async_computation.1 | async-start | bytes 1835008 | tf_op jit(solution)/shard_map/all_to_all | solution.py:1504
  (49 other events, 437.1 us)
Sparse Core Ops, SparseCore 0:
  150.5 108.3 all-gather.2

commit v4 on v3

--- a/solution.py
+++ b/solution.py
@@ -190,7 +190,45 @@
 
 
 def cost(micros):
+    micros = micros if micros >= 6 else 0
     return pl.CostEstimate(flops=int(micros * 1e9), bytes_accessed=int(micros * 3e6), transcendentals=0)
+
+
+class Order:
+    def start(self):
+        self.token = jnp.zeros((8, LANES), jnp.float32)
+        self.others = []
+
+    def wait_for(self, *others):
+        self.others += others
+
+
+ORDER = Order()
+
+
+def ordered(kernel, out_shape, in_specs, out_specs, **settings):
+    single = not isinstance(out_shape, (list, tuple))
+    outs, specs = ([out_shape], [out_specs]) if single else (list(out_shape), list(out_specs))
+
+    def run(*inputs):
+        extra = [ORDER.token] + ORDER.others
+        n_in, n_out, n_extra = len(inputs), len(outs), len(extra)
+
+        def wrapped(*refs):
+            rest = refs[n_in + n_extra :]
+            kernel(*refs[:n_in], *rest[:n_out], *rest[n_out + 1 :])
+
+        results = pl.pallas_call(
+            wrapped,
+            out_shape=outs + [jax.ShapeDtypeStruct((8, LANES), jnp.float32)],
+            in_specs=list(in_specs) + [spec_any()] * n_extra,
+            out_specs=specs + [spec_any()],
+            **settings,
+        )(*inputs, *extra)
+        ORDER.token, ORDER.others = results[-1], []
+        return results[0] if single else results[:-1]
+
+    return run
 
 
 def row_mask(low, high):
@@ -220,8 +258,13 @@
     return pl.ds(pl.multiple_of(slot * BLK, BLK), BLK)
 
 
-def align_rows(geo, table, padded):
-    def kernel(table_ref, rows_ref, out_ref):
+def align_rows(geo, table, natural, pad_rows):
+    def kernel(table_ref, natural_ref, out_ref, rows_ref):
+        def fill(row, rows):
+            rows_ref[pl.ds(row + BLK, rows), :] = natural_ref[pl.ds(row, rows), :]
+
+        copy_rows(natural.shape[0], 256, fill)
+
         def by_group(slot, start, cols):
             out_ref[block_at(slot), :] = rows_ref[pl.ds(start + BLK, BLK, stride=cols), :].astype(jnp.bfloat16)
 
@@ -231,14 +274,15 @@
 
         block_moves(geo, table_ref, by_group, by_row)
 
-    return pl.pallas_call(
+    return ordered(
         kernel,
         out_shape=jax.ShapeDtypeStruct((geo.slots * BLK, LANES), jnp.bfloat16),
         in_specs=[spec_smem(), spec_vmem()],
         out_specs=spec_vmem(),
+        scratch_shapes=[pltpu.VMEM((pad_rows, LANES), jnp.float32)],
         compiler_params=kernel_params(),
         cost_estimate=cost(3),
-    )(table, padded)
+    )(table, natural)
 
 
 def natural_rows(geo, table, blocks, pad_rows):
@@ -253,7 +297,7 @@
 
         block_moves(geo, table_ref, by_group, by_row)
 
-    return pl.pallas_call(
+    return ordered(
         kernel,
         out_shape=jax.ShapeDtypeStruct((pad_rows, LANES), jnp.float32),
         in_specs=[spec_smem(), spec_vmem()],
@@ -317,7 +361,7 @@
                 target = outs[0].at[i] if i < cut else outs[1].at[i - cut]
                 target[rows, :] = sources[r][i]
 
-    return pl.pallas_call(
+    return ordered(
         kernel,
         out_shape=[jax.ShapeDtypeStruct((c, nd * geo.piece, LANES), jnp.bfloat16) for c in counts],
         in_specs=[spec_smem()] + [spec_vmem()] * nd,
@@ -325,27 +369,6 @@
         compiler_params=kernel_params(),
         cost_estimate=cost(2),
     )(my_z.reshape(1), *parts)
-
-
-def class_tags(cot, doc, pos):
-    count = cot.shape[0]
-
-    def kernel(doc_ref, pos_ref, cot_ref, out_ref):
-        lanes = lax.broadcasted_iota(jnp.int32, (1, LANES), 1)
-        for s in range(count):
-            out_ref[s : s + 1, :D] = cot_ref[s, 0:1, :].astype(jnp.float32)
-            tag = jnp.where(lanes == 0, doc_ref[s], jnp.where(lanes == 1, pos_ref[s], 0))
-            out_ref[s : s + 1, D:] = tag.astype(jnp.float32)
-
-    return pl.pallas_call(
-        kernel,
-        grid=(1,),
-        out_shape=jax.ShapeDtypeStruct((count, D + LANES), jnp.float32),
-        in_specs=[spec_smem(), spec_smem(), pl.BlockSpec((count, BLK, D), lambda i: (0, 0, 0))],
-        out_specs=pl.BlockSpec((count, D + LANES), lambda i: (0, 0)),
-        compiler_params=kernel_params(),
-        cost_estimate=cost(2),
-    )(doc, pos, cot)
 VECTOR_ROWS = 16
 
 
@@ -467,7 +490,7 @@
     return parts
 
 
-def pack_bucket(geo, buckets, number, grads, coords):
+def grad_bucket(geo, buckets, number, grads, coords, name, left, right, rows, keep=False):
     span = buckets.ranges[number]
     seg_rows = geo.n_doc * geo.piece
     parts = bucket_parts(geo, span)
@@ -475,42 +498,46 @@
     wide_rows = BLK
     for item, chunks in parts:
         if len(item.shape) == 2:
-            cols = item.shape[1] // LANES
+            cols = item.cols
+            wide_rows = max(wide_rows, BLK * cols)
+            if item.name == name:
+                main, main_chunks, windows_at = item, chunks, len(windows)
+                windows.append(None)
+                continue
             k0 = min(b0 for _, b0, _, _ in chunks) // cols
             k1 = -(-max(b1 for _, _, b1, _ in chunks) // cols)
             operands.append(grads[item.name])
             specs.append(spec_any())
-            windows.append((cols, k0, k1))
+            windows.append((len(operands) - 1, k0, k1))
             scratch.append(pltpu.VMEM(((k1 - k0) * BLK, item.shape[1]), jnp.bfloat16))
-            wide_rows = max(wide_rows, BLK * cols)
         else:
             wide_rows = max(wide_rows, ceil_to(item.rows, BLK))
             operands.append(grads[item.name][0])
-            specs.append(spec_vmem())
-            windows.append(None)
+            specs.append(pl.BlockSpec(operands[-1].shape, lambda i: (0, 0)))
+            windows.append((len(operands) - 1, None, None))
             scratch.append(pltpu.VMEM((BLK, LANES), jnp.bfloat16))
     outs = [shape for shape in buckets.shapes(number) for _ in range(2)]
-
-    def kernel(coords_ref, *refs):
-        sources = refs[: len(parts)]
-        targets = refs[len(parts) : len(parts) + 4]
-        loaded = refs[len(parts) + 4 : 2 * len(parts) + 4]
-        staged, wide, in_sems, out_sems = refs[2 * len(parts) + 4 :]
+    depth, width = main.shape
+    cols = main.cols
+    steps = depth // rows
+    count = len(operands)
+    block_groups = rows // BLK
+
+    def split_groups(item, chunks):
+        found = set()
+        for n, b0, b1, _ in chunks:
+            first, last = geo.full_groups(item, n)
+            found |= set(range(b0 // item.cols, -(-b1 // item.cols))) - set(range(first, last))
+        return sorted(found)
+
+    def kernel(coords_ref, left_ref, right_ref, *refs):
+        sources, targets = refs[:count], refs[count : count + 4]
+        refs = refs[count + 4 :]
+        if keep:
+            kept_ref, refs = refs[0], refs[1:]
+        loaded, (values, staged, wide, in_sems, out_sems) = refs[:count], refs[count:]
+        step = pl.program_id(0)
         my_y, my_x, my_c = coords_ref[0], coords_ref[1], coords_ref[2]
-        loads = {}
-        for at, window in enumerate(windows):
-            if window is not None:
-                source = sources[at].at[pl.ds(window[1] * BLK, (window[2] - window[1]) * BLK)]
-                loads[at] = pltpu.make_async_copy(source, loaded[at], in_sems.at[at])
-                loads[at].start()
-
-        def clear(row, rows):
-            for at in range(len(span)):
-                here = pl.ds(pl.multiple_of(row, BLK), rows)
-                staged[at, here, :] = jnp.zeros((rows, LANES), jnp.bfloat16)
-
-        tail = min(geo.last[n] - geo.first[n] for n in span) * BLK
-        copy_rows(geo.slots * BLK - tail, 128, lambda row, rows: clear(row + tail, rows))
 
         def send_out(n):
             _, half, place = buckets.find(n)
@@ -527,63 +554,113 @@
                             out_sems.at[n - span.start],
                         ).start()
 
-        last_part = {n: at for at, (_, chunks) in enumerate(parts) for n, *_ in chunks}
-        for at, ((item, chunks), window) in enumerate(zip(parts, windows)):
-            if window is None:
-                vector_rows(wide, sources[at], grads[item.name][1], item.rows)
-                for n, b0, b1, slot in chunks:
-                    rows = wide[pl.ds(b0 * BLK, (b1 - b0) * BLK), :].astype(jnp.bfloat16)
-                    staged[n - span.start, pl.ds(slot * BLK, (b1 - b0) * BLK), :] = rows
-            else:
-                loads[at].wait()
-                cols, k0, k1 = window
-                values = loaded[at]
-                split = set()
-                for n, b0, b1, slot in chunks:
-                    first, last = geo.full_groups(item, n)
-                    split |= set(range(b0 // cols, -(-b1 // cols))) - set(range(first, last))
-
-                    def group(g, carry, n=n, shift=slot - b0, k0=k0, cols=cols, values=values):
-                        rows = pl.ds(pl.multiple_of((g - k0) * BLK, BLK), BLK)
-                        for cb in range(cols):
-                            dst = pl.ds(pl.multiple_of((g * cols + cb + shift) * BLK, BLK), BLK)
-                            staged[n - span.start, dst, :] = values[rows, cb * LANES : (cb + 1) * LANES]
-                        return carry
-
-                    lax.fori_loop(first, last, group, 0)
-                for g in sorted(split):
-                    for cb in range(cols):
-                        tile = values[(g - k0) * BLK : (g - k0 + 1) * BLK, cb * LANES : (cb + 1) * LANES]
-                        wide[pl.ds(cb, BLK, stride=cols), :] = tile.astype(jnp.float32)
+        def whole(item, chunks, values, base, lo, hi):
+            for n, b0, b1, slot in chunks:
+                first, last = geo.full_groups(item, n)
+
+                def group(g, carry, n=n, shift=slot - b0):
+                    here = pl.ds(pl.multiple_of((g - base) * BLK, BLK), BLK)
+                    for cb in range(item.cols):
+                        dst = block_at(g * item.cols + cb + shift)
+                        staged[n - span.start, dst, :] = values[here, cb * LANES : (cb + 1) * LANES]
+                    return carry
+
+                start = jnp.maximum(first, lo)
+                lax.fori_loop(start, jnp.maximum(start, jnp.minimum(last, hi)), group, 0)
+
+        def cut(item, chunks, values, base, g):
+            for cb in range(item.cols):
+                tile = values[pl.ds(pl.multiple_of((g - base) * BLK, BLK), BLK), cb * LANES : (cb + 1) * LANES]
+                wide[pl.ds(cb, BLK, stride=item.cols), :] = tile.astype(jnp.float32)
+            for n, b0, b1, slot in chunks:
+                first, last = geo.full_groups(item, n)
+                lo, hi = max(b0, g * item.cols), min(b1, (g + 1) * item.cols)
+                if lo < hi and not first <= g < last:
+                    part = wide[pl.ds((lo - g * item.cols) * BLK, (hi - lo) * BLK), :]
+                    dst = pl.ds((slot + lo - b0) * BLK, (hi - lo) * BLK)
+                    staged[n - span.start, dst, :] = part.astype(jnp.bfloat16)
+
+        @pl.when(step == 0)
+        def _():
+            loads = {}
+            for (item, chunks), window in zip(parts, windows):
+                if window is not None and window[1] is not None:
+                    at, k0, k1 = window
+                    source = sources[at].at[pl.ds(k0 * BLK, (k1 - k0) * BLK)]
+                    loads[at] = pltpu.make_async_copy(source, loaded[at], in_sems.at[at])
+                    loads[at].start()
+
+            def clear(row, size):
+                for at in range(len(span)):
+                    here = pl.ds(pl.multiple_of(row + tail, BLK), size)
+                    staged[at, here, :] = jnp.zeros((size, LANES), jnp.bfloat16)
+
+            tail = min(geo.last[n] - geo.first[n] for n in span) * BLK
+            copy_rows(geo.slots * BLK - tail, 128, clear)
+            for (item, chunks), window in zip(parts, windows):
+                if window is None:
+                    continue
+                at, k0, k1 = window
+                if k0 is None:
+                    vector_rows(wide, sources[at], grads[item.name][1], item.rows)
                     for n, b0, b1, slot in chunks:
-                        first, last = geo.full_groups(item, n)
-                        lo, hi = max(b0, g * cols), min(b1, (g + 1) * cols)
-                        if lo < hi and not first <= g < last:
-                            rows = wide[pl.ds((lo - g * cols) * BLK, (hi - lo) * BLK), :]
-                            dst = pl.ds((slot + lo - b0) * BLK, (hi - lo) * BLK)
-                            staged[n - span.start, dst, :] = rows.astype(jnp.bfloat16)
-            for n, *_ in chunks:
-                if last_part[n] == at:
-                    send_out(n)
-        for n in span:
-            at = n - span.start
-            pltpu.make_async_copy(staged.at[at], staged.at[at], out_sems.at[at]).wait()
-
-    return pl.pallas_call(
+                        part = wide[pl.ds(b0 * BLK, (b1 - b0) * BLK), :].astype(jnp.bfloat16)
+                        staged[n - span.start, pl.ds(slot * BLK, (b1 - b0) * BLK), :] = part
+                else:
+                    loads[at].wait()
+                    whole(item, chunks, loaded[at], k0, k0, k1)
+                    for g in split_groups(item, chunks):
+                        cut(item, chunks, loaded[at], k0, g)
+
+        values[...] = low(dot_tn(left_ref[...], right_ref[...]))
+        if keep:
+            kept_ref[...] = values[...]
+        low_group = step * block_groups
+        whole(main, main_chunks, values, low_group, low_group, low_group + block_groups)
+        for g in split_groups(main, main_chunks):
+            @pl.when(step == g // block_groups)
+            def _(g=g):
+                cut(main, main_chunks, values, g // block_groups * block_groups, g)
+
+        ready = {n: 0 for n in span}
+        for n, _, b1, _ in main_chunks:
+            ready[n] = (b1 - 1) // cols // block_groups
+        for at in range(steps):
+            here = [n for n in span if ready[n] == at]
+            if here:
+                @pl.when(step == at)
+                def _(here=here):
+                    for n in here:
+                        send_out(n)
+
+        @pl.when(step == steps - 1)
+        def _():
+            for at in range(len(span)):
+                pltpu.make_async_copy(staged.at[at], staged.at[at], out_sems.at[at]).wait()
+
+    extra = [jax.ShapeDtypeStruct(main.shape, jnp.bfloat16)] if keep else []
+    return ordered(
         kernel,
-        out_shape=[jax.ShapeDtypeStruct(shape, jnp.bfloat16) for shape in outs],
-        in_specs=[spec_smem()] + specs,
-        out_specs=[spec_any()] * 4,
+        grid=(steps,),
+        out_shape=[jax.ShapeDtypeStruct(shape, jnp.bfloat16) for shape in outs] + extra,
+        in_specs=[
+            spec_smem(),
+            pl.BlockSpec((left.shape[0], rows), lambda i: (0, i)),
+            pl.BlockSpec(right.shape, lambda i: (0, 0), pipeline_mode=pl.Buffered(1)),
+        ]
+        + specs,
+        out_specs=[spec_any()] * 4 + [pl.BlockSpec((rows, width), lambda i: (i, 0))] * len(extra),
         scratch_shapes=scratch
         + [
+            pltpu.VMEM((rows, width), jnp.bfloat16),
             pltpu.VMEM((len(span), geo.slots * BLK, LANES), jnp.bfloat16),
             pltpu.VMEM((wide_rows + 2 * BLK, LANES), jnp.float32),
-            pltpu.SemaphoreType.DMA((len(parts),)),
+            pltpu.SemaphoreType.DMA((max(count, 1),)),
             pltpu.SemaphoreType.DMA((len(span),)),
         ],
-        compiler_params=kernel_params(),
-        cost_estimate=cost(7),
-    )(coords, *operands)
+        compiler_params=kernel_params(60),
+        cost_estimate=cost(18),
+    )(coords, left, right, *operands)
 
 
 def pack_cross(geo, span, lefts, rights, vectors, seg):
@@ -663,7 +740,7 @@
 
     operands = [lefts[n] for n in names] + [rights[n] for n in names]
     operands += [vectors[n][0] for n in vector_names]
-    return pl.pallas_call(
+    return ordered(
         kernel,
         out_shape=jax.ShapeDtypeStruct((len(span), seg_blocks * BLK, LANES), jnp.bfloat16),
         in_specs=[spec_smem()] + [spec_vmem()] * len(operands),
@@ -791,7 +868,7 @@
 
 def in_parts(kernel, micros, count, inputs, in_specs, outs, out_specs, scratch, previous):
     previous = list(previous or ())
-    return pl.pallas_call(
+    return ordered(
         kernel,
         grid=(count,),
         in_specs=in_specs + [spec_any()] * len(previous),
@@ -842,7 +919,7 @@
         attend_kernel(x_ref, wqkv_ref, vec_ref, packed_ref, att_ref, stat_ref)
 
     whole = [pl.BlockSpec(shape, lambda i: (0, 0)) for shape in ((D, 3 * D), (VECTOR_ROWS, D))]
-    return pl.pallas_call(
+    return ordered(
         kernel,
         grid=(1,),
         in_specs=[spec_smem()] + [spec_any()] * count + [tiles(D)],
@@ -947,7 +1024,7 @@
             for place in range(3):
                 pltpu.make_async_copy(held[place], kept[place], out_sems.at[place]).wait()
 
-    return pl.pallas_call(
+    return ordered(
         kernel,
         grid=(steps,),
         in_specs=[spec_smem()] + [spec_any()] * count + [tiles(D), tiles(D)],
@@ -1034,7 +1111,7 @@
 def feed_back(cot, cls, norm2, dg, norm1, rates, w_down, w_up, w_out, vecs):
     n = cot.shape[0]
     bf, f32 = jnp.bfloat16, jnp.float32
-    return pl.pallas_call(
+    return ordered(
         feed_back_kernel,
         grid=(n // TILE,),
         in_specs=[
@@ -1239,7 +1316,7 @@
         vec_ref[...] = jnp.zeros_like(vec_ref)
         cross_kernel(load, *ins, *held, vec_ref, *outs, *scratch)
 
-    return pl.pallas_call(
+    return ordered(
         kernel,
         out_shape=[jax.ShapeDtypeStruct(shape, f32 if i == 2 else bf) for i, shape in enumerate(shapes)],
         in_specs=[spec_smem()] + [spec_any()] * count + [spec_vmem()] * len(operands),
@@ -1260,43 +1337,90 @@
     )(coords, *weights.operands, *operands)
 
 
-def class_rows(cls, hot, weights, coords):
+def class_rows(cls, cot, hot, doc, pos, weights, coords):
     count = len(weights.operands)
+    segs = cls.shape[0]
 
     def kernel(coords_ref, *refs):
-        sources, (cls_ref, hot_ref, out_ref, table, staged, wide, sems) = refs[:count], refs[count:]
+        sources, (cls_ref, cot_ref, hot_ref, doc_ref, pos_ref, out_ref, wide_out, table, staged, wide, sems) = (
+            refs[:count],
+            refs[count:],
+        )
         weights.start(coords_ref, sources, staged, sems)
+        lanes = lax.broadcasted_iota(jnp.int32, (1, LANES), 1)
+        for s in range(segs):
+            wide_out[s : s + 1, D : 2 * D] = cot_ref[s, 0:1, :].astype(jnp.float32)
+            tag = jnp.where(lanes == 0, doc_ref[s], jnp.where(lanes == 1, pos_ref[s], 0))
+            wide_out[s : s + 1, 2 * D :] = tag.astype(jnp.float32)
         weights.wait(0, set(), staged, sems)
         weights.matrix(0, staged, wide, table)
-        out_ref[...] = low(cls_ref[...] + dot_nn(hot_ref[...], table[...]))
-
-    return pl.pallas_call(
+        wide_out[:, :D] = cls_ref[...] + dot_nn(hot_ref[...], table[...])
+        out_ref[...] = low(wide_out[...])
+
+    def whole(shape):
+        return pl.BlockSpec(shape, lambda i: (0,) * len(shape))
+
+    return ordered(
         kernel,
-        out_shape=jax.ShapeDtypeStruct(cls.shape, jnp.bfloat16),
-        in_specs=[spec_smem()] + [spec_any()] * count + [spec_vmem()] * 2,
-        out_specs=spec_vmem(),
-        scratch_shapes=[pltpu.VMEM((LONG_SEGS, D), jnp.bfloat16)] + weights.scratch,
+        grid=(1,),
+        out_shape=jax.ShapeDtypeStruct((segs, 2 * D + LANES), jnp.bfloat16),
+        in_specs=[spec_smem()] + [spec_any()] * count
+        + [whole(cls.shape), whole((segs, BLK, D)), whole(hot.shape), spec_smem(), spec_smem()],
+        out_specs=whole((segs, 2 * D + LANES)),
+        scratch_shapes=[
+            pltpu.VMEM((segs, 2 * D + LANES), jnp.float32),
+            pltpu.VMEM((LONG_SEGS, D), jnp.bfloat16),
+        ]
+        + weights.scratch,
         compiler_params=kernel_params(),
         cost_estimate=cost(3),
-    )(coords, *weights.operands, cls, hot)
+    )(coords, *weights.operands, cls, cot, hot, doc, pos)
+
+
+def token_back(grad_one, dqkv, w_qkv, first, count, previous=None):
+    n = grad_one.shape[0]
+
+    def kernel(one_ref, dqkv_ref, wqkv_ref, *refs):
+        total = one_ref[...]
+        for j in range(3):
+            cols = slice(j * D, (j + 1) * D)
+            total = total + dot_nt(dqkv_ref[:, cols], wqkv_ref[:, cols])
+        refs[-1][...] = low(total)
+
+    return in_parts(
+        kernel,
+        3 * count,
+        count,
+        [grad_one, dqkv, w_qkv],
+        [tiles(D, first), tiles(3 * D, first), fixed((D, 3 * D))],
+        [jax.ShapeDtypeStruct((n, D), jnp.bfloat16)],
+        [tiles(D, first)],
+        [],
+        previous,
+    )
 AXES = ("seg", "doc")
-
-
-def tie(value, *others):
-    return lax.optimization_barrier((value, *others))[0]
-
-
-def after(halves, *others):
-    return [[tie(value, *others) for value in half] for half in halves]
 
 
 def send(geo, value, axis, step):
     return lax.ppermute(value, AXES, geo.shift(axis, step))
 
 
-def gather_axis(geo, value, axis, others):
-    parts = [send(geo, value, axis, r) for r in range(1, geo.size(axis))]
-    return jnp.stack([value] + [tie(part, *others) if others else part for part in parts])
+def flat_call(kernel, inputs, outs, micros=2):
+    rows = [value.reshape(-1, LANES) for value in inputs]
+    shapes = [jax.ShapeDtypeStruct((math.prod(shape[:-1]), LANES), jnp.bfloat16) for shape in outs]
+    results = ordered(
+        kernel,
+        out_shape=shapes,
+        in_specs=[spec_vmem()] * len(rows),
+        out_specs=[spec_vmem()] * len(outs),
+        compiler_params=kernel_params(60),
+        cost_estimate=cost(micros),
+    )(*rows)
+    return [value.reshape(shape) for value, shape in zip(results, outs)]
+
+
+def in_blocks(count, body):
+    copy_rows(count, 256, lambda row, rows: body(pl.multiple_of(row, BLK), rows))
 
 
 def gather_line(geo, pieces, my_z, cut):
@@ -1304,45 +1428,123 @@
     return place_line(geo, parts, my_z, cut)
 
 
-def gather_plane(geo, halves, step, others=()):
+def gather_plane(geo, halves, step):
     orders = ((X, Y), (Y, X))
-    return [gather_axis(geo, half, order[step], others) for half, order in zip(halves, orders)]
+    inputs, outs, sizes = [], [], []
+    for half, order in zip(halves, orders):
+        came = [send(geo, half, order[step], r) for r in range(1, geo.size(order[step]))]
+        inputs += [half] + came
+        sizes.append(1 + len(came))
+        outs.append((sizes[-1],) + half.shape)
+
+    def kernel(*refs):
+        sources, targets = refs[: sum(sizes)], refs[sum(sizes) :]
+        for at, target in enumerate(targets):
+            for place, source in enumerate(sources[sum(sizes[:at]) : sum(sizes[: at + 1])]):
+                count = source.shape[0]
+
+                def move(row, rows, source=source, target=target, base=place * count):
+                    target[pl.ds(base + row, rows), :] = source[pl.ds(row, rows), :]
+
+                in_blocks(count, move)
+
+    return flat_call(kernel, inputs, outs)
 
 
 def gather_cores(geo, halves):
     return [array for half in halves for array in (half, send(geo, half, C, 1))]
 
 
-def plus(*terms):
-    return low(sum(term.astype(jnp.float32) for term in terms))
-
-
 def reduce_cores(geo, arrays):
-    return [(arrays[2 * half], send(geo, arrays[2 * half + 1], C, 1)) for half in range(2)]
+    return [[arrays[2 * half], send(geo, arrays[2 * half + 1], C, 1)] for half in range(2)]
+
+
+def add_blocks(sources, target, source_row, target_row, count):
+    def body(row, rows):
+        total = sources[0][pl.ds(source_row + row, rows), :].astype(jnp.float32)
+        for source in sources[1:]:
+            total = total + source[pl.ds(source_row + row, rows), :].astype(jnp.float32)
+        target[pl.ds(target_row + row, rows), :] = low(total)
+
+    in_blocks(count, body)
 
 
 def reduce_plane(geo, halves, step):
     orders = ((Y, X), (X, Y))
-    result = []
+    inputs, outs, sizes = [], [], []
     for half, order in zip(halves, orders):
-        value = plus(*half)
-        axis = order[step]
-        result.append([value[0]] + [send(geo, value[r], axis, r) for r in range(1, geo.size(axis))])
-    return result
-
-
-def reduce_line(geo, line, my_z):
+        inputs += half
+        sizes.append((len(half), geo.size(order[step])))
+        outs += [half[0].shape[1:]] * sizes[-1][1]
+
+    def kernel(*refs):
+        sources, targets = refs[: len(inputs)], refs[len(inputs) :]
+        for terms, places in sizes:
+            for place in range(places):
+                count = targets[place].shape[0]
+                add_blocks(sources[:terms], targets[place], place * count, 0, count)
+            sources, targets = sources[terms:], targets[places:]
+
+    results = flat_call(kernel, inputs, outs)
+    halves = []
+    for (_, places), order in zip(sizes, orders):
+        mine, results = results[:places], results[places:]
+        halves.append([mine[0]] + [send(geo, mine[r], order[step], r) for r in range(1, places)])
+    return halves
+
+
+def reduce_line(geo, halves, my_z):
     nd = geo.n_doc
-    line = line.reshape(line.shape[0], nd, geo.piece, LANES)
-
-    def to(r):
-        return lax.dynamic_index_in_dim(line, lax.rem(my_z + r, nd), axis=1, keepdims=False)
-
-    return [to(0)] + [send(geo, to(r), Z, r) for r in range(1, nd)]
-
-
-def join(halves):
-    return jnp.concatenate([plus(*half) for half in halves])
+    inputs = [value for half in halves for value in half]
+    counts = [half[0].shape[0] for half in halves]
+
+    def kernel(z_ref, *refs):
+        sources, targets = refs[: len(inputs)], refs[len(inputs) :]
+        done = 0
+        for half, n in zip(halves, counts):
+            terms, sources = sources[: len(half)], sources[len(half) :]
+            for r in range(nd):
+                first = pl.multiple_of(wrap(z_ref[0] + r, nd) * geo.piece, BLK)
+                for i in range(n):
+                    here = pl.ds(first, geo.piece)
+                    total = sum(term[i, here, :].astype(jnp.float32) for term in terms)
+                    targets[r][done + i] = low(total)
+            done += n
+
+    outs = ordered(
+        kernel,
+        out_shape=[jax.ShapeDtypeStruct((sum(counts), geo.piece, LANES), jnp.bfloat16)] * nd,
+        in_specs=[spec_smem()] + [spec_vmem()] * len(inputs),
+        out_specs=[spec_vmem()] * nd,
+        compiler_params=kernel_params(60),
+        cost_estimate=cost(2),
+    )(my_z.reshape(1), *inputs)
+    return [outs[0]] + [send(geo, outs[r], Z, r) for r in range(1, nd)]
+
+
+def sum_pieces(geo, groups):
+    inputs = [part for group in groups for part in group]
+
+    def kernel(*refs):
+        sources, target = refs[:-1], refs[-1]
+        row = 0
+        for group in groups:
+            terms, sources = sources[: len(group)], sources[len(group) :]
+            count = terms[0].shape[0]
+            add_blocks(terms, target, 0, row, count)
+            row += count
+
+    count = sum(group[0].shape[0] for group in groups)
+    return flat_call(kernel, inputs, [(count, geo.piece, LANES)])[0]
+
+
+def gate(value):
+    def kernel(source, target):
+        in_blocks(source.shape[0], lambda row, rows: target.__setitem__(
+            (pl.ds(row, rows), slice(None)), source[pl.ds(row, rows), :]
+        ))
+
+    return flat_call(kernel, [value], [value.shape])[0]
 def optimizer_step(gradient, master, momentum, average, scaling, rating):
     scaled = gradient * scaling
     moment = 0.5 * momentum + scaled
@@ -1387,58 +1589,53 @@
     coords = jnp.stack([my_seg // 4, my_seg // 2 % 2, my_seg % 2, my_doc]).astype(jnp.int32)
     table = lax.dynamic_index_in_dim(jnp.asarray(geo.block_tables()[1]), me, 0, False)
     pad_rows = ceil_to(geo.chunk + 4 * BLK, 8)
-    padded = jnp.pad(
-        master.reshape(geo.chunk, LANES), ((BLK, pad_rows - geo.chunk - BLK), (0, 0))
-    )
-    aligned = align_rows(geo, table, padded)
+    ORDER.start()
+    aligned = align_rows(geo, table, master.reshape(geo.chunk, LANES), pad_rows)
     pieces = lax.all_to_all(aligned.reshape(geo.n_dev, geo.piece, LANES), AXES, 0, 0, tiled=True)
     parts = [pieces[span.start : span.stop] for span in gather.ranges]
 
     seg_count = tokens.shape[1]
     n_rows = n_seg * seg_count
     tiles_all = seg_count * SEG_LEN // TILE
+    middle = max(1, tiles_all - 2)
+    last = tiles_all - 1 - middle
     inputs = tokens[0].reshape(seg_count * SEG_LEN, D)
     cot_rows = cotangent[0]
-    tagged = low(class_tags(cot_rows, seg_doc[0], seg_pos[0]))
     cut = gather.half
+
     line = gather_line(geo, parts[0], my_doc, cut[0])
-
-    gathered = [None, None, None]
+    parts_b = [parts[1]] + [send(geo, parts[1], Z, r) for r in range(1, n_doc)]
+    ORDER.wait_for(*parts_b[1:2])
+    plane = gather_plane(geo, line, 0)
+    ORDER.wait_for(*parts_b[2:3])
+    plane = gather_plane(geo, plane, 1)
+    gathered = [gather_cores(geo, plane), None, None]
 
     def weights(*numbers):
         return Weights(geo, gather, gathered, [item_name(i) for i in numbers])
 
-    started = tie(parts[1], *line)
-    parts_b = [started] + [send(geo, started, Z, r) for r in range(1, n_doc)]
-    plane = gather_plane(geo, line, 0, parts_b[1:2])
-    plane = gather_plane(geo, plane, 1, parts_b[2:3])
-    gathered[0] = gather_cores(geo, plane)
-    all_tagged = lax.all_gather(tie(tagged, *plane), AXES[0], axis=0, tiled=True)
-    parts_b[-1] = tie(parts_b[-1], all_tagged)
-    line_b = place_line(geo, parts_b, my_doc, cut[1])
-    *outs, w_qkv, vec_a = attend_first(tie(inputs, *line_b), weights(0, 1), coords)
-    plane_b = gather_plane(geo, line_b, 0, [vec_a])
-    middle = max(1, tiles_all - 2)
-    outs = attend_layer(tie(inputs, *plane_b), w_qkv, vec_a, 1, middle, outs)
-    gathered[2] = [lax.all_gather(tie(parts[2], outs[2]), AXES)]
-    plane_b = gather_plane(geo, plane_b, 1, [outs[2]])
+    def own(values):
+        return lax.dynamic_slice_in_dim(values, my_seg * seg_count, seg_count, axis=0)
+
+    plane_b = place_line(geo, parts_b, my_doc, cut[1])
+    *outs, w_qkv, vec_a = attend_first(inputs, weights(0, 1), coords)
+    plane_b = gather_plane(geo, plane_b, 0)
+    gathered[2] = [lax.all_gather(gate(parts[2]), AXES)]
+    outs = attend_layer(inputs, w_qkv, vec_a, 1, middle, outs)
+    plane_b = gather_plane(geo, plane_b, 1)
     gathered[1] = gather_cores(geo, plane_b)
-    if 1 + middle < tiles_all:
-        last = tiles_all - 1 - middle
-        outs = attend_layer(tie(inputs, *plane_b), w_qkv, vec_a, 1 + middle, last, outs)
+    if last:
+        outs = attend_layer(inputs, w_qkv, vec_a, 1 + middle, last, outs)
     packed, attended, stat = outs
     hidden_low, normal_one, active, slope, normal_two, rates, hidden_two, cls, w_out, w_up, w_down, vec = feed_layer(
         inputs, attended, weights(1, 2, 3, 4, 5, 6, 7), coords
     )
 
-    all_grad, all_doc, all_pos = all_tagged[:, :D], all_tagged[:, D], all_tagged[:, D + 1]
+    hot = (seg_pos[0][:, None] == jnp.arange(LONG_SEGS)[None, :]).astype(jnp.bfloat16)
+    mine = class_rows(cls, cot_rows, hot, seg_doc[0], seg_pos[0], weights(8), coords)
+    tagged = lax.all_gather(mine, AXES[0], axis=0, tiled=True)
+    rows, all_grad, all_doc, all_pos = tagged[:, :D], tagged[:, D : 2 * D], tagged[:, 2 * D], tagged[:, 2 * D + 1]
     pos_hot = (all_pos.astype(jnp.int32)[:, None] == jnp.arange(LONG_SEGS)[None, :]).astype(jnp.bfloat16)
-
-    def own(values):
-        return lax.dynamic_slice_in_dim(values, my_seg * seg_count, seg_count, axis=0)
-
-    cls_low = class_rows(cls, own(pos_hot), weights(8), coords)
-    rows = lax.all_gather(cls_low, AXES[0], axis=0, tiled=True)
     crossed, grad_rows, xsums, g_qkv, g_o, g_u, g_m, rows_t, att_t, hid_t, act_t = cross_layer(
         rows, all_pos, all_doc, all_grad, weights(9, 10, 11, 12, 13, 14, 15, 16), coords
     )
@@ -1451,59 +1648,52 @@
         {item_name(i): (xsums, row) for i, row in ((10, 0), (12, 2), (14, 5), (16, 9))},
         my_seg.astype(jnp.int32).reshape(1),
     )
-    sums_c = reduce_line(geo, line_c, my_doc)
+    line_c = reduce_line(geo, [[line_c]], my_doc)
 
     grads = {}
     dm, du, dao, da, grad_one, sums = feed_back(
-        cot_rows.reshape(-1, D), tie(own(grad_rows).astype(jnp.float32), *sums_c[:1]), normal_two,
-        slope, normal_one, rates, w_down, w_up, w_out, vec,
+        cot_rows.reshape(-1, D), own(grad_rows).astype(jnp.float32), normal_two, slope, normal_one, rates,
+        w_down, w_up, w_out, vec,
     )
-    pieces_c = plus(*[tie(part, sums) for part in sums_c])
-    grads[item_name(8)] = low(matmul(own(pos_hot).T, own(grad_rows)))
+    pieces_c = sum_pieces(geo, [line_c])
+    grads[item_name(8)] = low(matmul(hot.T, own(grad_rows)))
     for number, row in ((3, 2), (5, 5), (7, 9)):
         grads[item_name(number)] = (sums, row)
-    grads[item_name(6)] = low(matmul(active.T, tie(dm, pieces_c)))
-    arrays_d = pack_bucket(geo, buckets, 2, grads, coords)
+    *arrays_d, grads[item_name(6)] = grad_bucket(
+        geo, buckets, 2, grads, coords, item_name(6), active, dm, 512, keep=True
+    )
     halves_d = reduce_cores(geo, arrays_d)
-    grads[item_name(4)] = low(matmul(hidden_low.T, tie(du, arrays_d[0])))
-    halves_d = reduce_plane(geo, after(halves_d, grads[item_name(4)]), 0)
-    grads[item_name(2)] = low(matmul(attended.T, tie(dao, halves_d[0][0], halves_d[1][0])))
-    arrays_b = pack_bucket(geo, buckets, 1, grads, coords)
+    grads[item_name(2)] = low(matmul(attended.T, dao))
+    ORDER.wait_for(grads[item_name(2)])
+    halves_d = reduce_plane(geo, halves_d, 0)
+    arrays_b = grad_bucket(geo, buckets, 1, grads, coords, item_name(4), hidden_low, du, 256)
     halves_b = reduce_cores(geo, arrays_b)
-    back = attend_back(packed, stat, tie(da, arrays_b[0]), 0, 1)
-    halves_d = reduce_plane(geo, after(halves_d, back[1]), 1)
-    halves_b = reduce_plane(geo, after(halves_b, back[1]), 0)
+    back = attend_back(packed, stat, da, 0, 1)
+    halves_d = reduce_plane(geo, halves_d, 1)
+    halves_b = reduce_plane(geo, halves_b, 0)
     if tiles_all > 1:
-        da = tie(da, *[half[0] for half in halves_b + halves_d])
         back = attend_back(packed, stat, da, 1, middle, back)
-    line_d = reduce_line(geo, join(after(halves_d, back[1])), my_doc)
-    halves_b = reduce_plane(geo, after(halves_b, back[1]), 1)
-    if 1 + middle < tiles_all:
-        da = tie(da, line_d[0], *[half[0] for half in halves_b])
+    line_d = reduce_line(geo, halves_d, my_doc)
+    halves_b = reduce_plane(geo, halves_b, 1)
+    if last:
         back = attend_back(packed, stat, da, 1 + middle, last, back)
     dqkv, qv_sums = back
-    line_b = reduce_line(geo, join(after(halves_b, qv_sums)), my_doc)
-    grads[item_name(0)] = low(matmul(inputs.T, tie(dqkv, line_b[0])))
+    pieces_d = sum_pieces(geo, [line_d])
+    line_b = reduce_line(geo, halves_b, my_doc)
     grads[item_name(1)] = (qv_sums, 0)
-    pieces_d = plus(*[tie(part, grads[item_name(0)]) for part in line_d])
-    grads[item_name(0)] = tie(grads[item_name(0)], pieces_d)
-    arrays_a = pack_bucket(geo, buckets, 0, grads, coords)
+    arrays_a = grad_bucket(geo, buckets, 0, grads, coords, item_name(0), inputs, dqkv, 256)
     halves_a = reduce_cores(geo, arrays_a)
-    pieces_b = plus(*[tie(part, arrays_a[0]) for part in line_b])
-    halves_a = reduce_plane(geo, after(halves_a, pieces_b), 0)
-    token_grad = low(grad_one + matmul(tie(dqkv, halves_a[0][0], halves_a[1][0]), w_qkv.T))
-    halves_a = reduce_plane(geo, after(halves_a, token_grad), 1)
+    halves_a = reduce_plane(geo, halves_a, 0)
+    token_grad, = token_back(grad_one, dqkv, w_qkv, 0, tiles_all)
+    pieces_b = sum_pieces(geo, [line_b])
+    halves_a = reduce_plane(geo, halves_a, 1)
     first_row = lax.broadcasted_iota(jnp.int32, (seg_count, SEG_LEN, D), 1) == 0
-    crossed = tie(crossed, halves_a[0][0], halves_a[1][0])
     mixed_out = jnp.where(
         first_row, own(crossed)[:, None, :], hidden_two.reshape(seg_count, SEG_LEN, D)
     )
-    line_a = reduce_line(geo, join(after(halves_a, mixed_out)), my_doc)
-    pieces_a = plus(*line_a)
-
-    owned = lax.all_to_all(
-        jnp.concatenate([pieces_a, pieces_b, pieces_d, pieces_c]), AXES, 0, 0, tiled=True
-    )
+    line_a = reduce_line(geo, halves_a, my_doc)
+    all_pieces = sum_pieces(geo, [line_a, [pieces_b], [pieces_d], [pieces_c]])
+    owned = lax.all_to_all(all_pieces, AXES, 0, 0, tiled=True)
     natural = natural_rows(geo, table, owned.reshape(-1, LANES), pad_rows)
     gradient = natural[BLK : BLK + geo.chunk].reshape(-1)
     n_cls = n_doc * n_rows

time: 652 us -> 626 us (0.960)
  Pallas kernels: 263 us -> 366 us
  waiting for transfers between devices: 150 us -> 94.2 us
  matrix products: 58.5 us -> 8.2 us
  other arithmetic: 37.3 us -> 14 us
  blocking collectives: 50.1 us -> 39.3 us
  local copies, waits for them, and re-layouts: 19.4 us -> 26.2 us
    pallas_call x19 -> x38, Pallas kernels: 263 us -> 366 us  [run(): pl.pallas_call(wrapped, out_shape=outs + [jax.ShapeDtypeStruct((8, LANES)...]
    ppermute x48, waiting for transfers between devices: 131 us -> 76.8 us  [send(): return lax.ppermute(value, AXES, geo.shift(axis, step))]
    dot_general x6 -> x2, matrix products: 58.5 us -> 8.2 us  [matmul(): return jnp.dot(left, right, preferred_element_type=jnp.float32)]
    unnamed x62 -> x112, local copies, waits for them, and re-layouts: 4.52 us -> 19.8 us
    convert_element_type x25 -> x1, other arithmetic: 19.1 us -> 4.7 us  [low(): return values.astype(jnp.bfloat16)]
    all_gather x2 -> x1, blocking collectives: 20.2 us -> 9.42 us  [local(): tagged = lax.all_gather(mine, AXES[0], axis=0, tiled=True)]
    another operation x7 -> x0, other arithmetic: 9.66 us -> none  [gather_axis(): jnp.stack([value] + [tie(part, *others) if others else part for part in p...]
  transfers between devices with their start and end apart: 50 -> 50, of which waited for: 17 -> 16; matrix products, arithmetic and copies ran while one was open for 11% -> 3% of each run, Pallas kernels for 29% -> 38%
where the time goes in v4:
time: 626 us; the launch traced here: 616 us
  Pallas kernels  366 us (58%)
  waiting for transfers between devices  94.2 us (15%)
  starting transfers between devices  53 us (8%)
  blocking collectives  39.3 us (6%)
  local copies, waits for them, and re-layouts  26.2 us (4%)
  between operations  15 us (2%)
  other arithmetic  14 us (2%)
  matrix products  8.2 us (1%)
    pallas_call x38, Pallas kernels, run(): pl.pallas_call(wrapped, out_shape=outs + [jax.ShapeDtypeStruct((8, LANES)...  366 us
    ppermute x48, waiting for transfers between devices, send(): return lax.ppermute(value, AXES, geo.shift(axis, step))  76.8 us
    ppermute x48, starting transfers between devices, send(): return lax.ppermute(value, AXES, geo.shift(axis, step))  48.5 us
    all_to_all x1, blocking collectives, local(): lax.all_to_all(aligned.reshape(geo.n_dev, geo.piece, LANES), AXES, 0, 0,...  29.8 us
    unnamed x112, local copies, waits for them, and re-layouts  19.8 us
    all_to_all x1, waiting for transfers between devices, local(): owned = lax.all_to_all(all_pieces, AXES, 0, 0, tiled=True)  17.3 us
  transfers between devices with their start and end apart: 50, of which 16 were waited for; matrix products, arithmetic and copies ran while one was open for 3% of the time, Pallas kernels for 38%

profile of v4, /device:TPU:0, one launch (start us, length us, event | category | flops | bytes accessed | tf_op | source)
XLA Modules:
  0.0 615.8 jit_solution(9580918273366390810)
XLA Ops:
  12.1 29.8 %all_to_all.10 = bf16[32,112,128]{2,1,0:T(8,128)(2,1)S(1)} all-to-all(bf16[32,112,128]{2,1,0:T(8,128)(2,1)} %bitcast.130), channel_id=1, replica_groups=mesh['seg'=8,'doc'=4] {'seg','doc'}, dimensions={0} | all-to-all | bytes 1835008 | tf_op jit(solution)/shard_map/all_to_all | solution.py:1594
  49.5 14.0 %collective-permute-done.4.refs_3_ = bf16[4,112,128]{2,1,0:T(8,128)(2,1)S(1)} collective-permute-done((bf16[4,112,128]{2,1,0:T(8,128)(2,1)S(1)}, bf16[4,112,128]{2,1,0:T(8,128)(2,1)S(1)}, u32[]{:S(2)}, u32[]{:S(2)}) %collective-permute-start.4) | collective-permute-done | bytes 114720 | tf_op jit(solution)/shard_map/ppermute | solution.py:1405
  68.2 4.1 collective-permute-done.6
  78.9 12.3 %collective-permute-done.1.refs_5_.refs_3_ = bf16[12,112,128]{2,1,0:T(8,128)(2,1)S(1)} collective-permute-done((bf16[12,112,128]{2,1,0:T(8,128)(2,1)S(1)}, bf16[12,112,128]{2,1,0:T(8,128)(2,1)S(1)}, u32[]{:S(2)}, u32[]{:S(2)}) %collective-permute-start.1) | collective-permute-done | bytes 344096 | tf_op jit(solution)/shard_map/ppermute | solution.py:1405
  98.3 7.3 %collective-permute-done.2.refs_4_ = bf16[12,112,128]{2,1,0:T(8,128)(2,1)S(1)} collective-permute-done((bf16[12,112,128]{2,1,0:T(8,128)(2,1)S(1)}, bf16[12,112,128]{2,1,0:T(8,128)(2,1)S(1)}, u32[]{:S(2)}, u32[]{:S(2)}) %collective-permute-start.2) | collective-permute-done | bytes 344096 | tf_op jit(solution)/shard_map/ppermute | solution.py:1405
  111.4 12.7 %shard_map.150 = (bf16[2048,2304]{1,0:T(8,128)(2,1)}, bf16[2048,768]{1,0:T(8,128)(2,1)}, f32[2048,128]{1,0:T(8,128)}, bf16[768,2304]{1,0:T(8,128)(2,1)}, f32[16,768]{1,0:T(8,128)}, /*index=5*/f32[8,128]{1,0:T(8,128)}) custom-call(s32[4]{0:T(128)} %pad_add_fusion.refs_0_, bf16[2,2,2,448,128]{4,3,2,1,0:T(8,128)(2,1)} %bitcast.187, ...), custom_call_target="tpu_custom_call" | custom-call | flops 12000000000 | bytes 36000000 | tf_op jit(solution)/shard_map/pallas_call | solution.py:221
  133.8 16.4 %shard_map.153 = (bf16[2048,2304]{1,0:T(8,128)(2,1)}, bf16[2048,768]{1,0:T(8,128)(2,1)}, f32[2048,128]{1,0:T(8,128)}, f32[8,128]{1,0:T(8,128)}) custom-call(bf16[2048,768]{1,0:T(8,128)(2,1)} %bitcast.182, bf16[768,2304]{1,0:T(8,128)(2,1)} %get-tuple-element.183.refs_1_.refs_2_, ...), custom_call_target="tpu_custom_call", output_to_operand_aliasing={{0}: (3, {}), {1}: (4, {}), {2}: (5, {})} | custom-call | flops 16000000000 | bytes 48000000 | tf_op jit(solution)/shard_map/pallas_call | solution.py:221
  150.3 18.7 %collective-permute-done.15 = bf16[2,6,448,128]{3,2,1,0:T(8,128)(2,1)S(1)} collective-permute-done((bf16[2,6,448,128]{3,2,1,0:T(8,128)(2,1)}, bf16[2,6,448,128]{3,2,1,0:T(8,128)(2,1)S(1)}, u32[]{:S(2)}, u32[]{:S(2)}) %collective-permute-start.15) | collective-permute-done | bytes 1376288 | tf_op jit(solution)/shard_map/ppermute | solution.py:1405
  171.6 5.6 shard_map.154
  178.4 9.4 %shard_map.155 = (bf16[2048,2304]{1,0:T(8,128)(2,1)}, bf16[2048,768]{1,0:T(8,128)(2,1)}, f32[2048,128]{1,0:T(8,128)}, f32[8,128]{1,0:T(8,128)}) custom-call(bf16[2048,768]{1,0:T(8,128)(2,1)} %bitcast.183, bf16[768,2304]{1,0:T(8,128)(2,1)} %get-tuple-element.183.refs_1_.refs_2_, ...), custom_call_target="tpu_custom_call", output_to_operand_aliasing={{0}: (3, {}), {1}: (4, {}), {2}: (5, {})} | custom-call | flops 8000000000 | bytes 24000000 | tf_op jit(solution)/shard_map/pallas_call | solution.py:221
  187.8 64.5 %shard_map.156 = (bf16[2048,768]{1,0:T(8,128)(2,1)}, bf16[2048,768]{1,0:T(8,128)(2,1)}, bf16[2048,3072]{1,0:T(8,128)(2,1)}, bf16[2048,3072]{1,0:T(8,128)(2,1)}, ...) custom-call(s32[4]{0:T(128)} %pad_add_fusion.refs_0_, ...), custom_call_target="tpu_custom_call" | custom-call | flops 60000002048 | bytes 180000000 | tf_op jit(solution)/shard_map/pallas_call | solution.py:221
  255.6 9.4 %all_gather.7 = bf16[128,1664]{1,0:T(8,128)(2,1)S(1)} all-gather(bf16[16,1664]{1,0:T(8,128)(2,1)} %get-tuple-element.200), channel_id=1, replica_groups=mesh['seg'=8,'doc'=4] {'seg'}, dimensions={0}, use_global_device_ids=true | all-gather | bytes 479232 | tf_op jit(solution)/shard_map/all_gather | solution.py:1636
  268.0 22.3 %shard_map.158 = (bf16[128,768]{1,0:T(8,128)(2,1)}, bf16[128,768]{1,0:T(8,128)(2,1)}, f32[16,768]{1,0:T(8,128)}, bf16[128,2304]{1,0:T(8,128)(2,1)}, bf16[128,768...) custom-call(s32[4]{0:T(128)} %pad_add_fusion.refs_0_, ...), custom_call_target="tpu_custom_call" | custom-call | flops 22000001024 | bytes 66000000 | tf_op jit(solution)/shard_map/pallas_call | solution.py:221
  290.3 12.8 %shard_map.159 = (bf16[16,448,128]{2,1,0:T(8,128)(2,1)}, f32[8,128]{1,0:T(8,128)}) custom-call(s32[1]{0:T(128)} %bitcast.35.refs_0_, bf16[64,128]{1,0:T(8,128)(2,1)} %fusion.2.refs_1_, bf16[768,128]{1,0:T(8,128)(2,1)} %get-tuple-element.213.refs_2_, bf16[768,128]{1,0:T(8,128)(2,1)} %get-tuple-element.214.refs_3_, ...), custom_call_target="tpu_custom_call" | custom-call | flops 12000000000 | bytes 36000000 | tf_op jit(solution)/shard_map/pallas_call | solution.py:221
  311.4 43.7 %shard_map.161 = (bf16[2048,768]{1,0:T(8,128)(2,1)}, bf16[2048,3072]{1,0:T(8,128)(2,1)}, bf16[2048,768]{1,0:T(8,128)(2,1)}, bf16[2048,768]{1,0:T(8,128)(2,1)}, f...) custom-call(bf16[2048,768]{1,0:T(8,128)(2,1)} %bitcast.109, f32[16,768]{1,0:T(8,128)} %get-tuple-element.329.refs_1_, ...), custom_call_target="tpu_custom_call" | custom-call | flops 44000002048 | bytes 132000000 | tf_op jit(solution)/shard_map/pallas_call | solution.py:221
  360.3 19.9 %shard_map.163 = (bf16[2,2,3,448,128]{4,3,2,1,0:T(8,128)(2,1)}, bf16[2,2,3,448,128]{4,3,2,1,0:T(8,128)(2,1)}, bf16[2,2,2,448,128]{4,3,2,1,0:T(8,128)(2,1)}, bf16...) custom-call(s32[4]{0:T(128)} %pad_add_fusion.refs_0_, ...), custom_call_target="tpu_custom_call" | custom-call | flops 17999998976 | bytes 54000000 | tf_op jit(solution)/shard_map/pallas_call | solution.py:221
  381.0 6.5 %convolution_convert_fusion.refs_5_.refs_3_.refs_4_ = bf16[768,768]{1,0:T(8,128)(2,1)} fusion(bf16[2048,768]{1,0:T(8,128)(2,1)} %get-tuple-element.196.refs_10_, bf16[2048,768]{1,0:T(8,128)(2,1)} %get-tuple-element.232), kind=kOutput, calls=%fused_computation.7 | convolution fusion | flops 2416508928 | bytes 7471104 | tf_op jit(solution)/shard_map/dot_general | solution.py:1573
  388.9 4.4 shard_map.164
  393.3 21.3 %shard_map.165 = (bf16[2,2,4,448,128]{4,3,2,1,0:T(8,128)(2,1)}, bf16[2,2,4,448,128]{4,3,2,1,0:T(8,128)(2,1)}, bf16[2,2,3,448,128]{4,3,2,1,0:T(8,128)(2,1)}, bf16[2,2,3,448,128]{4,3,2,1,0:T(8,128)(2,1)}, f32[8,128]{1,0:T(8,128)}) custom-call(s32[4]{0:T(128)} %pad_add_fusion.refs_0_, bf16[2048,768]{1,0:T(8,128)(2,1)} %get-tuple-element.230.refs_1_, ...), custom_call_target="tpu_custom_call" | custom-call | flops 17999998976 | bytes 54000000 | tf_op jit(solution)/shard_map/pallas_call | solution.py:221
  418.6 11.6 %shard_map.166 = (bf16[2048,2304]{1,0:T(8,128)(2,1)}, f32[8,768]{1,0:T(8,128)}, f32[8,128]{1,0:T(8,128)}) custom-call(bf16[2048,2304]{1,0:T(8,128)(2,1)} %get-tuple-element.227.refs_0_, f32[2048,128]{1,0:T(8,128)} %get-tuple-element.228.refs_1_, bf16[2048,768]{1,0:T(8,128)(2,1)} %get-tuple-element.229.refs_2_, f32[8,768]{1,0:T(8,128)} %broadcast_in_dim.58.refs_3_, ...), custom_call_target="tpu_custom_call" | custom-call | flops 10000000000 | bytes 30000000 | tf_op jit(solution)/shard_map/pallas_call | solution.py:221
  430.2 4.3 collective-permute-done.25
  442.1 5.6 shard_map.168
  449.6 19.8 %shard_map.169 = (bf16[2048,2304]{1,0:T(8,128)(2,1)}, f32[8,768]{1,0:T(8,128)}, f32[8,128]{1,0:T(8,128)}) custom-call(bf16[2048,2304]{1,0:T(8,128)(2,1)} %get-tuple-element.227.refs_0_, f32[2048,128]{1,0:T(8,128)} %get-tuple-element.228.refs_1_, bf16[2048,768]{1,0:T(8,128)(2,1)} %get-tuple-element.229.refs_2_, ...), custom_call_target="tpu_custom_call", output_to_operand_aliasing={{0}: (4, {})} | custom-call | flops 20000000000 | bytes 60000000 | tf_op jit(solution)/shard_map/pallas_call | solution.py:221
  484.3 11.6 %shard_map.172 = (bf16[2048,2304]{1,0:T(8,128)(2,1)}, f32[8,768]{1,0:T(8,128)}, f32[8,128]{1,0:T(8,128)}) custom-call(bf16[2048,2304]{1,0:T(8,128)(2,1)} %get-tuple-element.227.refs_0_, f32[2048,128]{1,0:T(8,128)} %get-tuple-element.228.refs_1_, bf16[2048,768]{1,0:T(8,128)(2,1)} %get-tuple-element.229.refs_2_, ...), custom_call_target="tpu_custom_call", output_to_operand_aliasing={{0}: (4, {})} | custom-call | flops 10000000000 | bytes 30000000 | tf_op jit(solution)/shard_map/pallas_call | solution.py:221
  501.7 15.7 %shard_map.175 = (bf16[2,2,2,448,128]{4,3,2,1,0:T(8,128)(2,1)}, bf16[2,2,2,448,128]{4,3,2,1,0:T(8,128)(2,1)}, bf16[2,2,2,448,128]{4,3,2,1,0:T(8,128)(2,1)}, bf16[2,2,2,448,128]{4,3,2,1,0:T(8,128)(2,1)}, f32[8,128]{1,0:T(8,128)}) custom-call(s32[4]{0:T(128)} %pad_add_fusion.refs_0_, bf16[2048,768]{1,0:T(8,128)(2,1)} %bitcast.185, ...), custom_call_target="tpu_custom_call" | custom-call | flops 17999998976 | bytes 54000000 | tf_op jit(solution)/shard_map/pallas_call | solution.py:221
  523.1 3.8 shard_map.176
  528.9 13.2 %shard_map.177 = (bf16[2048,768]{1,0:T(8,128)(2,1)}, f32[8,128]{1,0:T(8,128)}) custom-call(f32[2048,768]{1,0:T(8,128)} %get-tuple-element.226.refs_0_, bf16[2048,2304]{1,0:T(8,128)(2,1)} %get-tuple-element.276.refs_2_.refs_1_, bf16[768,2304]{1,0:T(8,128)(2,1)} %get-tuple-element.183.refs_1_.refs_2_, f32[8,128]{1,0:T(8,128)} %get-tuple-element.294.refs_3_), custom_call_target="tpu_custom_call" | custom-call | flops 12000000000 | bytes 36000000 | tf_op jit(solution)/shard_map/pallas_call | solution.py:221
  550.5 4.5 collective-permute-done.43.refs_2_
  571.4 4.5 all-to-all-start.1
  576.9 4.0 broadcast_select_fusion
  580.9 17.3 %all-to-all-done.1 = bf16[32,112,128]{2,1,0:T(8,128)(2,1)S(1)} async-done(((bf16[32,112,128]{2,1,0:T(8,128)(2,1)}), bf16[32,112,128]{2,1,0:T(8,128)(2,1)S(1)}, u32[]{:S(2)}, u32[]{:S(2)}) %all-to-all-start.1) | async-done | bytes 917536 | tf_op jit(solution)/shard_map/all_to_all | solution.py:1696
  602.0 4.7 fusion.7
  (243 shorter events, 145.0 us)
Async XLA Ops:
  7.2 245.2 %all-gather.2.cloned.1.call-start = ((), (), s32[]{:S(2)}) async-start(), calls=%async_computation.2 | async-start | bytes 15138816 | tf_op jit(solution)/shard_map/all_gather | solution.py:1623
  45.2 18.4 %collective-permute-start.4 = (bf16[4,112,128]{2,1,0:T(8,128)(2,1)S(1)}, bf16[4,112,128]{2,1,0:T(8,128)(2,1)S(1)}, u32[]{:S(2)}, u32[]{:S(2)}) collective-permute-start(bf16[4,112,128]{2,1,0:T(8,128)(2,1)S(1)} %slice.34.refs_1_), channel_id=1, source_target_pairs={{0,2},{1,3},{2,0},{3,1},{4,6},{5,7},{6,4},{7,5},{8,10},{9,11},{10,... | collective-permute-start | bytes 344072 | tf_op jit(solution)/shard_map/ppermute | solution.py:1405
  46.5 17.0 %collective-permute-start.3 = (bf16[4,112,128]{2,1,0:T(8,128)(2,1)S(1)}, bf16[4,112,128]{2,1,0:T(8,128)(2,1)S(1)}, u32[]{:S(2)}, u32[]{:S(2)}) collective-permute-start(bf16[4,112,128]{2,1,0:T(8,128)(2,1)S(1)} %slice.34.refs_1_), channel_id=1, source_target_pairs={{0,1},{1,2},{2,3},{3,0},{4,5},{5,6},{6,7},{7,4},{8,9},{9,10},{10,1... | collective-permute-start | bytes 344072 | tf_op jit(solution)/shard_map/ppermute | solution.py:1405
  46.5 26.9 %collective-permute-start = (bf16[12,112,128]{2,1,0:T(8,128)(2,1)S(1)}, bf16[12,112,128]{2,1,0:T(8,128)(2,1)S(1)}, u32[]{:S(2)}, u32[]{:S(2)}) collective-permute-start(bf16[12,112,128]{2,1,0:T(8,128)(2,1)S(1)} %slice.33.refs_1_), channel_id=1, source_target_pairs={{0,1},{1,2},{2,3},{3,0},{4,5},{5,6},{6,7},{7,4},{8,9},{9,10},{10,1... | collective-permute-start | bytes 1032200 | tf_op jit(solution)/shard_map/ppermute | solution.py:1405
  95.1 15.3 %collective-permute-start.12 = (bf16[2,2,2,448,128]{4,3,2,1,0:T(8,128)(2,1)}, bf16[2,2,2,448,128]{4,3,2,1,0:T(8,128)(2,1)S(1)}, u32[]{:S(2)}, u32[]{:S(2)}) collective-permute-start(bf16[2,2,2,448,128]{4,3,2,1,0:T(8,128)(2,1)} %bitcast.186), channel_id=1, source_target_pairs={{0,4},{1,5},{2,6},{3,7},{4,0},{5,1},{6,2},{7,3},{8,12},{9,13},{10,... | collective-permute-start | bytes 2752520 | tf_op jit(solution)/shard_map/ppermute | solution.py:1405
  95.1 15.3 %collective-permute-start.13 = (bf16[2,2,2,448,128]{4,3,2,1,0:T(8,128)(2,1)}, bf16[2,2,2,448,128]{4,3,2,1,0:T(8,128)(2,1)}, u32[]{:S(2)}, u32[]{:S(2)}) collective-permute-start(bf16[2,2,2,448,128]{4,3,2,1,0:T(8,128)(2,1)} %bitcast.189), channel_id=1, source_target_pairs={{0,4},{1,5},{2,6},{3,7},{4,0},{5,1},{6,2},{7,3},{8,12},{9,13},{10,... | collective-permute-start | bytes 2752520 | tf_op jit(solution)/shard_map/ppermute | solution.py:1405
  108.8 16.7 %collective-permute-start.10 = (bf16[6,448,128]{2,1,0:T(8,128)(2,1)}, bf16[6,448,128]{2,1,0:T(8,128)(2,1)S(1)}, u32[]{:S(2)}, u32[]{:S(2)}) collective-permute-start(bf16[6,448,128]{2,1,0:T(8,128)(2,1)} %get-tuple-element.173), channel_id=1, source_target_pairs={{0,8},{1,9},{2,10},{3,11},{4,12},{5,13},{6,14},{7,15},{8,0},{9,1},... | collective-permute-start | bytes 2064392 | tf_op jit(solution)/shard_map/ppermute | solution.py:1405
  110.2 16.4 %collective-permute-start.11 = (bf16[6,448,128]{2,1,0:T(8,128)(2,1)}, bf16[6,448,128]{2,1,0:T(8,128)(2,1)S(1)}, u32[]{:S(2)}, u32[]{:S(2)}) collective-permute-start(bf16[6,448,128]{2,1,0:T(8,128)(2,1)} %get-tuple-element.174), channel_id=1, source_target_pairs={{0,16},{1,17},{2,18},{3,19},{4,20},{5,21},{6,22},{7,23},{8,24},{9,... | collective-permute-start | bytes 2064392 | tf_op jit(solution)/shard_map/ppermute | solution.py:1405
  132.8 36.1 %collective-permute-start.15 = (bf16[2,6,448,128]{3,2,1,0:T(8,128)(2,1)}, bf16[2,6,448,128]{3,2,1,0:T(8,128)(2,1)S(1)}, u32[]{:S(2)}, u32[]{:S(2)}) collective-permute-start(bf16[2,6,448,128]{3,2,1,0:T(8,128)(2,1)} %bitcast.122), channel_id=1, source_target_pairs={{0,8},{1,9},{2,10},{3,11},{4,12},{5,13},{6,14},{7,15},{8,0},{9,1},... | collective-permute-start | bytes 4128776 | tf_op jit(solution)/shard_map/ppermute | solution.py:1405
  133.5 36.9 %collective-permute-start.14 = (bf16[2,6,448,128]{3,2,1,0:T(8,128)(2,1)}, bf16[2,6,448,128]{3,2,1,0:T(8,128)(2,1)S(1)}, u32[]{:S(2)}, u32[]{:S(2)}) collective-permute-start(bf16[2,6,448,128]{3,2,1,0:T(8,128)(2,1)} %bitcast.121), channel_id=1, source_target_pairs={{0,16},{1,17},{2,18},{3,19},{4,20},{5,21},{6,22},{7,23},{8,24},{9,... | collective-permute-start | bytes 4128776 | tf_op jit(solution)/shard_map/ppermute | solution.py:1405
  306.1 50.6 %collective-permute-start.18 = (bf16[16,112,128]{2,1,0:T(8,128)(2,1)}, bf16[16,112,128]{2,1,0:T(8,128)(2,1)S(1)}, u32[]{:S(2)}, u32[]{:S(2)}) collective-permute-start(bf16[16,112,128]{2,1,0:T(8,128)(2,1)} %get-tuple-element.237), channel_id=1, source_target_pairs={{0,1},{1,2},{2,3},{3,0},{4,5},{5,6},{6,7},{7,4},{8,9},{9,10},{10,1... | collective-permute-start | bytes 1376264 | tf_op jit(solution)/shard_map/ppermute | solution.py:1405
  306.1 50.6 %collective-permute-start.19 = (bf16[16,112,128]{2,1,0:T(8,128)(2,1)}, bf16[16,112,128]{2,1,0:T(8,128)(2,1)S(1)}, u32[]{:S(2)}, u32[]{:S(2)}) collective-permute-start(bf16[16,112,128]{2,1,0:T(8,128)(2,1)} %get-tuple-element.238), channel_id=1, source_target_pairs={{0,2},{1,3},{2,0},{3,1},{4,6},{5,7},{6,4},{7,5},{8,10},{9,11},{10,... | collective-permute-start | bytes 1376264 | tf_op jit(solution)/shard_map/ppermute | solution.py:1405
  308.4 48.4 %collective-permute-start.20 = (bf16[16,112,128]{2,1,0:T(8,128)(2,1)}, bf16[16,112,128]{2,1,0:T(8,128)(2,1)S(1)}, u32[]{:S(2)}, u32[]{:S(2)}) collective-permute-start(bf16[16,112,128]{2,1,0:T(8,128)(2,1)} %get-tuple-element.239), channel_id=1, source_target_pairs={{0,3},{1,0},{2,1},{3,2},{4,7},{5,4},{6,5},{7,6},{8,11},{9,8},{10,9... | collective-permute-start | bytes 1376264 | tf_op jit(solution)/shard_map/ppermute | solution.py:1405
  414.7 25.8 %collective-permute-start.23 = (bf16[2,2,4,448,128]{4,3,2,1,0:T(8,128)(2,1)}, bf16[2,2,4,448,128]{4,3,2,1,0:T(8,128)(2,1)S(1)}, u32[]{:S(2)}, u32[]{:S(2)}) collective-permute-start(bf16[2,2,4,448,128]{4,3,2,1,0:T(8,128)(2,1)} %get-tuple-element.253), channel_id=1, source_target_pairs={{0,4},{1,5},{2,6},{3,7},{4,0},{5,1},{6,2},{7,3},{8,12},{9,13},{10,... | collective-permute-start | bytes 5505032 | tf_op jit(solution)/shard_map/ppermute | solution.py:1405
  415.2 25.3 %collective-permute-start.24 = (bf16[2,2,3,448,128]{4,3,2,1,0:T(8,128)(2,1)}, bf16[2,2,3,448,128]{4,3,2,1,0:T(8,128)(2,1)S(1)}, u32[]{:S(2)}, u32[]{:S(2)}) collective-permute-start(bf16[2,2,3,448,128]{4,3,2,1,0:T(8,128)(2,1)} %get-tuple-element.255), channel_id=1, source_target_pairs={{0,4},{1,5},{2,6},{3,7},{4,0},{5,1},{6,2},{7,3},{8,12},{9,13},{10,... | collective-permute-start | bytes 4128776 | tf_op jit(solution)/shard_map/ppermute | solution.py:1405
  415.3 14.9 %collective-permute-start.26 = (bf16[2,2,448,128]{3,2,1,0:T(8,128)(2,1)}, bf16[2,2,448,128]{3,2,1,0:T(8,128)(2,1)}, u32[]{:S(2)}, u32[]{:S(2)}) collective-permute-start(bf16[2,2,448,128]{3,2,1,0:T(8,128)(2,1)} %bitcast.50), channel_id=1, source_target_pairs={{0,8},{1,9},{2,10},{3,11},{4,12},{5,13},{6,14},{7,15},{8,0},{9,1},... | collective-permute-start | bytes 1376264 | tf_op jit(solution)/shard_map/ppermute | solution.py:1405
  417.1 17.3 %collective-permute-start.25 = (bf16[2,3,448,128]{3,2,1,0:T(8,128)(2,1)}, bf16[2,3,448,128]{3,2,1,0:T(8,128)(2,1)S(1)}, u32[]{:S(2)}, u32[]{:S(2)}) collective-permute-start(bf16[2,3,448,128]{3,2,1,0:T(8,128)(2,1)} %bitcast.194), channel_id=1, source_target_pairs={{0,16},{1,17},{2,18},{3,19},{4,20},{5,21},{6,22},{7,23},{8,24},{9,... | collective-permute-start | bytes 2064392 | tf_op jit(solution)/shard_map/ppermute | solution.py:1405
  438.3 31.1 %collective-permute-start.30 = (bf16[2,448,128]{2,1,0:T(8,128)(2,1)}, bf16[2,448,128]{2,1,0:T(8,128)(2,1)S(1)}, u32[]{:S(2)}, u32[]{:S(2)}) collective-permute-start(bf16[2,448,128]{2,1,0:T(8,128)(2,1)} %bitcast.200), channel_id=1, source_target_pairs={{0,16},{1,17},{2,18},{3,19},{4,20},{5,21},{6,22},{7,23},{8,24},{9,... | collective-permute-start | bytes 688136 | tf_op jit(solution)/shard_map/ppermute | solution.py:1405
  439.2 30.3 %collective-permute-start.29 = (bf16[3,448,128]{2,1,0:T(8,128)(2,1)}, bf16[3,448,128]{2,1,0:T(8,128)(2,1)S(1)}, u32[]{:S(2)}, u32[]{:S(2)}) collective-permute-start(bf16[3,448,128]{2,1,0:T(8,128)(2,1)} %bitcast.198), channel_id=1, source_target_pairs={{0,8},{1,9},{2,10},{3,11},{4,12},{5,13},{6,14},{7,15},{8,0},{9,1},... | collective-permute-start | bytes 1032200 | tf_op jit(solution)/shard_map/ppermute | solution.py:1405
  447.7 29.6 %collective-permute-start.28 = (bf16[2,3,448,128]{3,2,1,0:T(8,128)(2,1)}, bf16[2,3,448,128]{3,2,1,0:T(8,128)(2,1)S(1)}, u32[]{:S(2)}, u32[]{:S(2)}) collective-permute-start(bf16[2,3,448,128]{3,2,1,0:T(8,128)(2,1)} %bitcast.193), channel_id=1, source_target_pairs={{0,8},{1,9},{2,10},{3,11},{4,12},{5,13},{6,14},{7,15},{8,0},{9,1},... | collective-permute-start | bytes 2064392 | tf_op jit(solution)/shard_map/ppermute | solution.py:1405
  448.4 28.9 %collective-permute-start.27 = (bf16[2,4,448,128]{3,2,1,0:T(8,128)(2,1)}, bf16[2,4,448,128]{3,2,1,0:T(8,128)(2,1)S(1)}, u32[]{:S(2)}, u32[]{:S(2)}) collective-permute-start(bf16[2,4,448,128]{3,2,1,0:T(8,128)(2,1)} %bitcast.192), channel_id=1, source_target_pairs={{0,16},{1,17},{2,18},{3,19},{4,20},{5,21},{6,22},{7,23},{8,24},{9,... | collective-permute-start | bytes 2752520 | tf_op jit(solution)/shard_map/ppermute | solution.py:1405
  472.3 23.6 %collective-permute-start.33 = (bf16[5,112,128]{2,1,0:T(8,128)(2,1)}, bf16[5,112,128]{2,1,0:T(8,128)(2,1)S(1)}, u32[]{:S(2)}, u32[]{:S(2)}) collective-permute-start(bf16[5,112,128]{2,1,0:T(8,128)(2,1)} %get-tuple-element.283), channel_id=1, source_target_pairs={{0,1},{1,2},{2,3},{3,0},{4,5},{5,6},{6,7},{7,4},{8,9},{9,10},{10,1... | collective-permute-start | bytes 430088 | tf_op jit(solution)/shard_map/ppermute | solution.py:1405
  472.9 23.0 %collective-permute-start.34 = (bf16[5,112,128]{2,1,0:T(8,128)(2,1)}, bf16[5,112,128]{2,1,0:T(8,128)(2,1)S(1)}, u32[]{:S(2)}, u32[]{:S(2)}) collective-permute-start(bf16[5,112,128]{2,1,0:T(8,128)(2,1)} %get-tuple-element.284), channel_id=1, source_target_pairs={{0,2},{1,3},{2,0},{3,1},{4,6},{5,7},{6,4},{7,5},{8,10},{9,11},{10,... | collective-permute-start | bytes 430088 | tf_op jit(solution)/shard_map/ppermute | solution.py:1405
  474.3 21.5 %collective-permute-start.35 = (bf16[5,112,128]{2,1,0:T(8,128)(2,1)}, bf16[5,112,128]{2,1,0:T(8,128)(2,1)S(1)}, u32[]{:S(2)}, u32[]{:S(2)}) collective-permute-start(bf16[5,112,128]{2,1,0:T(8,128)(2,1)} %get-tuple-element.285), channel_id=1, source_target_pairs={{0,3},{1,0},{2,1},{3,2},{4,7},{5,4},{6,5},{7,6},{8,11},{9,8},{10,9... | collective-permute-start | bytes 430088 | tf_op jit(solution)/shard_map/ppermute | solution.py:1405
  482.1 16.3 %collective-permute-start.32 = (bf16[3,448,128]{2,1,0:T(8,128)(2,1)}, bf16[3,448,128]{2,1,0:T(8,128)(2,1)S(1)}, u32[]{:S(2)}, u32[]{:S(2)}) collective-permute-start(bf16[3,448,128]{2,1,0:T(8,128)(2,1)} %bitcast.199), channel_id=1, source_target_pairs={{0,16},{1,17},{2,18},{3,19},{4,20},{5,21},{6,22},{7,23},{8,24},{9,... | collective-permute-start | bytes 1032200 | tf_op jit(solution)/shard_map/ppermute | solution.py:1405
  483.0 15.5 %collective-permute-start.31 = (bf16[4,448,128]{2,1,0:T(8,128)(2,1)}, bf16[4,448,128]{2,1,0:T(8,128)(2,1)S(1)}, u32[]{:S(2)}, u32[]{:S(2)}) collective-permute-start(bf16[4,448,128]{2,1,0:T(8,128)(2,1)} %bitcast.195), channel_id=1, source_target_pairs={{0,8},{1,9},{2,10},{3,11},{4,12},{5,13},{6,14},{7,15},{8,0},{9,1},... | collective-permute-start | bytes 1376264 | tf_op jit(solution)/shard_map/ppermute | solution.py:1405
  518.0 24.0 %collective-permute-start.40 = (bf16[7,112,128]{2,1,0:T(8,128)(2,1)S(1)}, bf16[7,112,128]{2,1,0:T(8,128)(2,1)S(1)}, u32[]{:S(2)}, u32[]{:S(2)}) collective-permute-start(bf16[7,112,128]{2,1,0:T(8,128)(2,1)S(1)} %copy-done.55), channel_id=1, source_target_pairs={{0,1},{1,2},{2,3},{3,0},{4,5},{5,6},{6,7},{7,4},{8,9},{9,10},{10,1... | collective-permute-start | bytes 602120 | tf_op jit(solution)/shard_map/ppermute | solution.py:1405
  518.0 24.0 %collective-permute-start.41 = (bf16[7,112,128]{2,1,0:T(8,128)(2,1)S(1)}, bf16[7,112,128]{2,1,0:T(8,128)(2,1)S(1)}, u32[]{:S(2)}, u32[]{:S(2)}) collective-permute-start(bf16[7,112,128]{2,1,0:T(8,128)(2,1)S(1)} %copy-done.54), channel_id=1, source_target_pairs={{0,2},{1,3},{2,0},{3,1},{4,6},{5,7},{6,4},{7,5},{8,10},{9,11},{10,... | collective-permute-start | bytes 602120 | tf_op jit(solution)/shard_map/ppermute | solution.py:1405
  519.0 23.1 %collective-permute-start.42 = (bf16[7,112,128]{2,1,0:T(8,128)(2,1)S(1)}, bf16[7,112,128]{2,1,0:T(8,128)(2,1)S(1)}, u32[]{:S(2)}, u32[]{:S(2)}) collective-permute-start(bf16[7,112,128]{2,1,0:T(8,128)(2,1)S(1)} %copy-done.53), channel_id=1, source_target_pairs={{0,3},{1,0},{2,1},{3,2},{4,7},{5,4},{6,5},{7,6},{8,11},{9,8},{10,9... | collective-permute-start | bytes 602120 | tf_op jit(solution)/shard_map/ppermute | solution.py:1405
  527.0 17.9 %collective-permute-start.38 = (bf16[2,2,448,128]{3,2,1,0:T(8,128)(2,1)}, bf16[2,2,448,128]{3,2,1,0:T(8,128)(2,1)S(1)}, u32[]{:S(2)}, u32[]{:S(2)}) collective-permute-start(bf16[2,2,448,128]{3,2,1,0:T(8,128)(2,1)} %bitcast.197), channel_id=1, source_target_pairs={{0,16},{1,17},{2,18},{3,19},{4,20},{5,21},{6,22},{7,23},{8,24},{9,... | collective-permute-start | bytes 1376264 | tf_op jit(solution)/shard_map/ppermute | solution.py:1405
  527.3 17.6 %collective-permute-start.39 = (bf16[2,2,448,128]{3,2,1,0:T(8,128)(2,1)}, bf16[2,2,448,128]{3,2,1,0:T(8,128)(2,1)S(1)}, u32[]{:S(2)}, u32[]{:S(2)}) collective-permute-start(bf16[2,2,448,128]{3,2,1,0:T(8,128)(2,1)} %bitcast.196), channel_id=1, source_target_pairs={{0,8},{1,9},{2,10},{3,11},{4,12},{5,13},{6,14},{7,15},{8,0},{9,1},... | collective-permute-start | bytes 1376264 | tf_op jit(solution)/shard_map/ppermute | solution.py:1405
  571.4 26.8 %all-to-all-start.1 = ((bf16[32,112,128]{2,1,0:T(8,128)(2,1)}), bf16[32,112,128]{2,1,0:T(8,128)(2,1)S(1)}, u32[]{:S(2)}, u32[]{:S(2)}) async-start(bf16[32,112,128]{2,1,0:T(8,128)(2,1)} %bitcast.129), calls=%async_computation.1 | async-start | bytes 1835008 | tf_op jit(solution)/shard_map/all_to_all | solution.py:1696
  (74 other events, 431.7 us)
Sparse Core Ops, SparseCore 0:
  132.9 107.4 all-gather.1

commit v5 on v4

--- a/solution.py
+++ b/solution.py
@@ -98,7 +98,8 @@
         self.piece = self.piece_blocks * BLK
         self.slots = self.piece_blocks * self.n_dev
         self.groups = -(-most // (self.piece_blocks * n_doc))
-        self.staged_rows = self.groups * n_doc * self.piece
+        self.share = n_doc * self.piece
+        self.staged_rows = self.groups * self.share
         self.c_size, self.x_size = 2, 2
         self.y_size = n_seg // 4
 
@@ -152,7 +153,7 @@
         return found
 
     def spans(self, *ends):
-        cuts = [0] + [(end.nat - 1) // self.chunk + 1 for end in ends] + [self.n_dev]
+        cuts = [0] + [ceil_to((end.nat - 1) // self.chunk + 1, self.n_doc) for end in ends] + [self.n_dev]
         return [range(a, b) for a, b in zip(cuts, cuts[1:])]
 
     def coords(self, device):
@@ -285,26 +286,61 @@
     )(table, natural)
 
 
-def natural_rows(geo, table, blocks, pad_rows):
-    def kernel(table_ref, blocks_ref, out_ref):
+def update_rows(geo, table, blocks, begins, factors, state, pad_rows):
+    rows_all = geo.chunk
+    runs = begins.shape[0]
+
+    def kernel(table_ref, begins_ref, factors_ref, blocks_ref, *refs):
+        inputs, outs, held, (grad_ref, in_sems) = refs[:3], refs[3:7], refs[7:10], refs[10:]
+        loads = [
+            pltpu.make_async_copy(source, target, in_sems.at[i])
+            for i, (source, target) in enumerate(zip(inputs, held))
+        ]
+        for load in loads:
+            load.start()
+
         def by_group(slot, start, cols):
-            out_ref[pl.ds(start + BLK, BLK, stride=cols), :] = blocks_ref[block_at(slot), :].astype(jnp.float32)
+            grad_ref[pl.ds(start + BLK, BLK, stride=cols), :] = blocks_ref[block_at(slot), :].astype(jnp.float32)
 
         def by_row(slot, start, low_row, high_row):
             here = pl.ds(start + BLK, BLK)
             rows = blocks_ref[block_at(slot), :].astype(jnp.float32)
-            out_ref[here, :] = jnp.where(row_mask(low_row, high_row), rows, out_ref[here, :])
+            grad_ref[here, :] = jnp.where(row_mask(low_row, high_row), rows, grad_ref[here, :])
 
         block_moves(geo, table_ref, by_group, by_row)
-
+        for load in loads:
+            load.wait()
+
+        def step(row, rows):
+            here = pl.ds(row, rows)
+            at = lax.broadcasted_iota(jnp.int32, (rows, LANES), 0) + row
+            scale = jnp.full((rows, LANES), factors_ref[0], jnp.float32)
+            rate = jnp.full((rows, LANES), factors_ref[runs], jnp.float32)
+            for run in range(1, runs):
+                later = at >= begins_ref[run]
+                scale = jnp.where(later, factors_ref[run], scale)
+                rate = jnp.where(later, factors_ref[runs + run], rate)
+            scaled = grad_ref[pl.ds(row + BLK, rows), :] * scale
+            moment = 0.5 * held[1][here, :] + scaled
+            weight = held[0][here, :] - rate * (scaled + 0.5 * moment)
+            outs[0][here, :] = weight
+            outs[1][here, :] = moment
+            outs[2][here, :] = 0.5 * held[2][here, :] + 0.5 * weight
+            outs[3][here, :] = weight.astype(jnp.bfloat16)
+
+        copy_rows(rows_all, 128, step)
+
+    full = [jax.ShapeDtypeStruct((rows_all, LANES), kind) for kind in (jnp.float32,) * 3 + (jnp.bfloat16,)]
     return ordered(
         kernel,
-        out_shape=jax.ShapeDtypeStruct((pad_rows, LANES), jnp.float32),
-        in_specs=[spec_smem(), spec_vmem()],
-        out_specs=spec_vmem(),
+        out_shape=full,
+        in_specs=[spec_smem()] * 3 + [spec_vmem()] + [spec_any()] * 3,
+        out_specs=[spec_vmem()] * 4,
+        scratch_shapes=[pltpu.VMEM((rows_all, LANES), jnp.float32)] * 3
+        + [pltpu.VMEM((pad_rows, LANES), jnp.float32), pltpu.SemaphoreType.DMA((3,))],
         compiler_params=kernel_params(),
         cost_estimate=cost(3),
-    )(table, blocks)
+    )(table, begins, factors, blocks, *state)
 
 
 class Buckets:
@@ -312,23 +348,18 @@
         self.geo = geo
         self.ranges = geo.spans(*ends)
         self.arrays = arrays
-        self.half = [(len(r) + 1) // 2 for r in self.ranges]
 
     def find(self, chunk):
         for number, span in enumerate(self.ranges):
             if chunk in span:
-                at = chunk - span.start
-                cut = self.half[number]
-                return (number, 0, at) if at < cut else (number, 1, at - cut)
+                return number, chunk - span.start
 
     def shapes(self, number):
         geo = self.geo
-        cut = self.half[number]
-        rest = len(self.ranges[number]) - cut
-        rows = geo.n_doc * geo.piece
+        count = len(self.ranges[number])
         return [
-            (geo.y_size, geo.x_size, cut, rows, LANES),
-            (geo.x_size, geo.y_size, rest, rows, LANES),
+            (geo.y_size, geo.x_size, count, geo.share // 2, LANES),
+            (geo.x_size, geo.y_size, count, geo.share // 2, LANES),
         ]
 
 
@@ -348,22 +379,21 @@
         body(full * step, count % step)
 
 
-def place_line(geo, parts, my_z, cut):
-    n, nd = parts[0].shape[0], geo.n_doc
-    counts = [cut, n - cut]
+def place_line(geo, parts, my_z):
+    count, nd = parts[0].shape[0], geo.n_doc
+    rows = geo.share // 2
 
     def kernel(z_ref, *refs):
         sources, outs = refs[:nd], refs[nd:]
         for r in range(nd):
             z = wrap(z_ref[0] - r, nd)
-            rows = pl.ds(pl.multiple_of(z * geo.piece, BLK), geo.piece)
-            for i in range(n):
-                target = outs[0].at[i] if i < cut else outs[1].at[i - cut]
-                target[rows, :] = sources[r][i]
+            for s in range(count):
+                for half in range(2):
+                    outs[half][s * nd + z] = sources[r][s, half * rows : (half + 1) * rows]
 
     return ordered(
         kernel,
-        out_shape=[jax.ShapeDtypeStruct((c, nd * geo.piece, LANES), jnp.bfloat16) for c in counts],
+        out_shape=[jax.ShapeDtypeStruct((count * nd, rows, LANES), jnp.bfloat16)] * 2,
         in_specs=[spec_smem()] + [spec_vmem()] * nd,
         out_specs=[spec_vmem()] * 2,
         compiler_params=kernel_params(),
@@ -374,31 +404,33 @@
 
 def chunk_copies(geo, buckets, sources, used, coords_ref, n, staged, sem):
     my_y, my_x, my_c = coords_ref[0], coords_ref[1], coords_ref[2]
-    number, half, place = buckets.find(n)
+    number, place = buckets.find(n)
     first = sum(buckets.arrays[m] for m in used[: used.index(number)])
     if buckets.arrays[number] == 1:
-        for device in range(geo.groups * geo.n_doc):
+        line, z = divmod(place, geo.n_doc)
+        for s in range(geo.groups):
             pltpu.make_async_copy(
-                sources[first].at[device, n - buckets.ranges[number].start],
-                staged.at[pl.ds(device * geo.piece, geo.piece)],
+                sources[first].at[s * geo.n_doc + z, line],
+                staged.at[pl.ds(s * geo.share, geo.share)],
                 sem,
             ).start()
         return
-    rows = geo.n_doc * geo.piece
+    rows = geo.share // 2
     for core in range(2):
         c = my_c if core == 0 else 1 - my_c
         for ry in range(geo.y_size):
             for rx in range(geo.x_size):
                 y, x = wrap(my_y - ry, geo.y_size), wrap(my_x - rx, geo.x_size)
                 s = (y * geo.x_size + x) * 2 + c
-                index = (ry, rx, place) if half == 0 else (rx, ry, place)
-
-                def begin(s=s, index=index, core=core):
-                    pltpu.make_async_copy(
-                        sources[first + 2 * half + core].at[index],
-                        staged.at[pl.ds(pl.multiple_of(s * rows, BLK), rows)],
-                        sem,
-                    ).start()
+
+                def begin(s=s, ry=ry, rx=rx, core=core):
+                    for half in range(2):
+                        index = (ry, rx, place) if half == 0 else (rx, ry, place)
+                        pltpu.make_async_copy(
+                            sources[first + 2 * half + core].at[index],
+                            staged.at[pl.ds(pl.multiple_of(s * geo.share + half * rows, BLK), rows)],
+                            sem,
+                        ).start()
 
                 if geo.groups == geo.n_seg:
                     begin()
@@ -492,7 +524,6 @@
 
 def grad_bucket(geo, buckets, number, grads, coords, name, left, right, rows, keep=False):
     span = buckets.ranges[number]
-    seg_rows = geo.n_doc * geo.piece
     parts = bucket_parts(geo, span)
     operands, specs, windows, scratch = [], [], [], []
     wide_rows = BLK
@@ -540,19 +571,22 @@
         my_y, my_x, my_c = coords_ref[0], coords_ref[1], coords_ref[2]
 
         def send_out(n):
-            _, half, place = buckets.find(n)
+            _, place = buckets.find(n)
+            half_rows = geo.share // 2
             for core in range(2):
                 c = my_c if core == 0 else 1 - my_c
                 for ry in range(geo.y_size):
                     for rx in range(geo.x_size):
                         y, x = wrap(my_y + ry, geo.y_size), wrap(my_x + rx, geo.x_size)
                         s = (y * geo.x_size + x) * 2 + c
-                        index = (ry, rx, place) if half == 0 else (rx, ry, place)
-                        pltpu.make_async_copy(
-                            staged.at[n - span.start, pl.ds(pl.multiple_of(s * seg_rows, BLK), seg_rows)],
-                            targets[2 * half + core].at[index],
-                            out_sems.at[n - span.start],
-                        ).start()
+                        for half in range(2):
+                            index = (ry, rx, place) if half == 0 else (rx, ry, place)
+                            here = pl.ds(pl.multiple_of(s * geo.share + half * half_rows, BLK), half_rows)
+                            pltpu.make_async_copy(
+                                staged.at[n - span.start, here],
+                                targets[2 * half + core].at[index],
+                                out_sems.at[n - span.start],
+                            ).start()
 
         def whole(item, chunks, values, base, lo, hi):
             for n, b0, b1, slot in chunks:
@@ -853,7 +887,7 @@
             largest = jnp.max(scores, axis=-1, keepdims=True)
             raised = jnp.exp(scores - largest)
             summed = jnp.sum(raised, axis=-1, keepdims=True)
-            weights = low(raised / summed)
+            weights = low(raised * (1.0 / summed))
             att_ref[rows, pair * LANES : (pair + 1) * LANES] = low(
                 dot_nn(side_by_side(weights), both_heads(v))
             )
@@ -1218,7 +1252,7 @@
         q = packed_ref[:, third(0, pair)] * jnp.bfloat16(scale)
         scores = jnp.where(same, dot_nt(both_heads(q), packed_ref[:, third(1, pair)]), NEGATIVE)
         raised = jnp.exp(scores - jnp.max(scores, axis=-1, keepdims=True))
-        weights = raised / jnp.sum(raised, axis=-1, keepdims=True)
+        weights = raised * (1.0 / jnp.sum(raised, axis=-1, keepdims=True))
         weights_ref[pair] = weights
         blend = dot_nn(side_by_side(low(weights)), both_heads(packed_ref[:, third(2, pair)]))
         att_ref[:, pair_cols(pair)] = low(blend)
@@ -1405,48 +1439,55 @@
     return lax.ppermute(value, AXES, geo.shift(axis, step))
 
 
+def along_z(geo, value):
+    return [value] + [send(geo, value, Z, r) for r in range(1, geo.n_doc)]
+
+
+STEPS = 4
+
+
+def slab(place, rows):
+    return pl.BlockSpec((pl.squeezed, rows, LANES), lambda i: (place, i, 0))
+
+
 def flat_call(kernel, inputs, outs, micros=2):
-    rows = [value.reshape(-1, LANES) for value in inputs]
-    shapes = [jax.ShapeDtypeStruct((math.prod(shape[:-1]), LANES), jnp.bfloat16) for shape in outs]
+    arrays, specs = [], []
+    for value, places in inputs:
+        rows = value.size // LANES // places
+        for place in range(places):
+            arrays.append(value.reshape(places, rows, LANES))
+            specs.append(slab(place, rows // STEPS))
+    shapes, out_specs = [], []
+    for shape, places in outs:
+        rows = math.prod(shape) // LANES // max(places, 1)
+        shapes.append(jax.ShapeDtypeStruct((max(places, 1), rows, LANES), jnp.bfloat16))
+        out_specs.append(pl.BlockSpec((max(places, 1), rows // STEPS, LANES), lambda i: (0, i, 0)))
     results = ordered(
         kernel,
+        grid=(STEPS,),
         out_shape=shapes,
-        in_specs=[spec_vmem()] * len(rows),
-        out_specs=[spec_vmem()] * len(outs),
+        in_specs=specs,
+        out_specs=out_specs,
         compiler_params=kernel_params(60),
         cost_estimate=cost(micros),
-    )(*rows)
-    return [value.reshape(shape) for value, shape in zip(results, outs)]
-
-
-def in_blocks(count, body):
-    copy_rows(count, 256, lambda row, rows: body(pl.multiple_of(row, BLK), rows))
-
-
-def gather_line(geo, pieces, my_z, cut):
-    parts = [pieces] + [send(geo, pieces, Z, r) for r in range(1, geo.n_doc)]
-    return place_line(geo, parts, my_z, cut)
+    )(*arrays)
+    return [value.reshape(shape) for value, (shape, _) in zip(results, outs)]
 
 
 def gather_plane(geo, halves, step):
     orders = ((X, Y), (Y, X))
-    inputs, outs, sizes = [], [], []
+    inputs, outs = [], []
     for half, order in zip(halves, orders):
         came = [send(geo, half, order[step], r) for r in range(1, geo.size(order[step]))]
-        inputs += [half] + came
-        sizes.append(1 + len(came))
-        outs.append((sizes[-1],) + half.shape)
+        inputs += [(value, 1) for value in [half] + came]
+        outs.append(((1 + len(came),) + half.shape, 1 + len(came)))
 
     def kernel(*refs):
-        sources, targets = refs[: sum(sizes)], refs[sum(sizes) :]
-        for at, target in enumerate(targets):
-            for place, source in enumerate(sources[sum(sizes[:at]) : sum(sizes[: at + 1])]):
-                count = source.shape[0]
-
-                def move(row, rows, source=source, target=target, base=place * count):
-                    target[pl.ds(base + row, rows), :] = source[pl.ds(row, rows), :]
-
-                in_blocks(count, move)
+        sources, targets = refs[: len(inputs)], refs[len(inputs) :]
+        for target, (_, places) in zip(targets, outs):
+            for place in range(places):
+                target[place] = sources[place][...]
+            sources = sources[places:]
 
     return flat_call(kernel, inputs, outs)
 
@@ -1459,61 +1500,57 @@
     return [[arrays[2 * half], send(geo, arrays[2 * half + 1], C, 1)] for half in range(2)]
 
 
-def add_blocks(sources, target, source_row, target_row, count):
-    def body(row, rows):
-        total = sources[0][pl.ds(source_row + row, rows), :].astype(jnp.float32)
-        for source in sources[1:]:
-            total = total + source[pl.ds(source_row + row, rows), :].astype(jnp.float32)
-        target[pl.ds(target_row + row, rows), :] = low(total)
-
-    in_blocks(count, body)
-
-
-def reduce_plane(geo, halves, step):
+def added(sources):
+    return low(sum(source[...].astype(jnp.float32) for source in sources))
+
+
+def reduce_plane(geo, groups, step):
     orders = ((Y, X), (X, Y))
-    inputs, outs, sizes = [], [], []
-    for half, order in zip(halves, orders):
-        inputs += half
-        sizes.append((len(half), geo.size(order[step])))
-        outs += [half[0].shape[1:]] * sizes[-1][1]
+    inputs, outs, jobs = [], [], []
+    for halves, step in zip(groups, step):
+        for half, order in zip(halves, orders):
+            places = geo.size(order[step])
+            inputs += [(value, places) for value in half]
+            outs += [(half[0].shape[1:], 0)] * places
+            jobs.append((len(half), places, order[step]))
 
     def kernel(*refs):
-        sources, targets = refs[: len(inputs)], refs[len(inputs) :]
-        for terms, places in sizes:
+        count = sum(places for _, places in inputs)
+        sources, targets = refs[:count], refs[count:]
+        for terms, places, _ in jobs:
             for place in range(places):
-                count = targets[place].shape[0]
-                add_blocks(sources[:terms], targets[place], place * count, 0, count)
-            sources, targets = sources[terms:], targets[places:]
+                targets[place][0] = added(sources[place : terms * places : places])
+            sources, targets = sources[terms * places :], targets[places:]
 
     results = flat_call(kernel, inputs, outs)
-    halves = []
-    for (_, places), order in zip(sizes, orders):
+    reduced = []
+    for _, places, axis in jobs:
         mine, results = results[:places], results[places:]
-        halves.append([mine[0]] + [send(geo, mine[r], order[step], r) for r in range(1, places)])
-    return halves
+        reduced.append([mine[0]] + [send(geo, mine[r], axis, r) for r in range(1, places)])
+    return [reduced[2 * i : 2 * i + 2] for i in range(len(groups))]
 
 
 def reduce_line(geo, halves, my_z):
     nd = geo.n_doc
     inputs = [value for half in halves for value in half]
-    counts = [half[0].shape[0] for half in halves]
+    count = inputs[0].shape[0] // nd
+    rows = [half[0].shape[1] for half in halves]
 
     def kernel(z_ref, *refs):
         sources, targets = refs[: len(inputs)], refs[len(inputs) :]
         done = 0
-        for half, n in zip(halves, counts):
+        for half, n in zip(halves, rows):
             terms, sources = sources[: len(half)], sources[len(half) :]
             for r in range(nd):
-                first = pl.multiple_of(wrap(z_ref[0] + r, nd) * geo.piece, BLK)
-                for i in range(n):
-                    here = pl.ds(first, geo.piece)
-                    total = sum(term[i, here, :].astype(jnp.float32) for term in terms)
-                    targets[r][done + i] = low(total)
+                z = wrap(z_ref[0] + r, nd)
+                for s in range(count):
+                    total = sum(term[s * nd + z].astype(jnp.float32) for term in terms)
+                    targets[r][s, done : done + n] = low(total)
             done += n
 
     outs = ordered(
         kernel,
-        out_shape=[jax.ShapeDtypeStruct((sum(counts), geo.piece, LANES), jnp.bfloat16)] * nd,
+        out_shape=[jax.ShapeDtypeStruct((count, geo.share, LANES), jnp.bfloat16)] * nd,
         in_specs=[spec_smem()] + [spec_vmem()] * len(inputs),
         out_specs=[spec_vmem()] * nd,
         compiler_params=kernel_params(60),
@@ -1522,51 +1559,61 @@
     return [outs[0]] + [send(geo, outs[r], Z, r) for r in range(1, nd)]
 
 
-def sum_pieces(geo, groups):
-    inputs = [part for group in groups for part in group]
+def sum_line(geo, line):
+    def kernel(*refs):
+        refs[-1][0] = added(refs[:-1])
+
+    return flat_call(kernel, [(part, 1) for part in line], [(line[0].shape, 0)])[0]
+
+
+def sum_all(geo, line, *others):
+    count = line[0].shape[0]
 
     def kernel(*refs):
         sources, target = refs[:-1], refs[-1]
-        row = 0
-        for group in groups:
-            terms, sources = sources[: len(group)], sources[len(group) :]
-            count = terms[0].shape[0]
-            add_blocks(terms, target, 0, row, count)
-            row += count
-
-    count = sum(group[0].shape[0] for group in groups)
-    return flat_call(kernel, inputs, [(count, geo.piece, LANES)])[0]
+        target[:count] = added(sources[: len(line)])
+        row = count
+        for source in sources[len(line) :]:
+            target[row : row + source.shape[0]] = source[...]
+            row += source.shape[0]
+
+    return ordered(
+        kernel,
+        out_shape=jax.ShapeDtypeStruct((geo.n_seg, geo.share, LANES), jnp.bfloat16),
+        in_specs=[spec_vmem()] * (len(line) + len(others)),
+        out_specs=spec_vmem(),
+        compiler_params=kernel_params(),
+        cost_estimate=cost(2),
+    )(*line, *others)
 
 
 def gate(value):
     def kernel(source, target):
-        in_blocks(source.shape[0], lambda row, rows: target.__setitem__(
-            (pl.ds(row, rows), slice(None)), source[pl.ds(row, rows), :]
-        ))
-
-    return flat_call(kernel, [value], [value.shape])[0]
-def optimizer_step(gradient, master, momentum, average, scaling, rating):
-    scaled = gradient * scaling
-    moment = 0.5 * momentum + scaled
-    weight = master - rating * (scaled + 0.5 * moment)
-    smooth = 0.5 * average + 0.5 * weight
-    return (weight, moment, smooth, low(weight))
-
-
+        target[0] = source[...]
+
+    return flat_call(kernel, [(value, 1)], [(value.shape, 0)])[0]
 def row_rates(geo, n_tokens, n_cls):
-    total = geo.chunk * geo.n_dev
-    scaling = np.zeros((total,), np.float32)
-    rating = np.full((total,), 0.2, np.float32)
-    names = list(LAYOUT)
-    cross = names[-13:]
+    runs = []
+    cross = list(LAYOUT)[-13:]
     row = 0
     for name, shape in LAYOUT.items():
-        rows = math.prod(shape) // LANES
-        scaling[row : row + rows] = 1.0 / math.sqrt(n_cls if name in cross else n_tokens)
+        scale = 1.0 / math.sqrt(n_cls if name in cross else n_tokens)
+        rate = 0.2
         if len(shape) == 2:
-            rating[row : row + rows] = 1.0 if name == cross[0] else 0.5 / math.sqrt(shape[0])
-        row += rows
-    return scaling.reshape(geo.n_dev, geo.chunk), rating.reshape(geo.n_dev, geo.chunk)
+            rate = 1.0 if name == cross[0] else 0.5 / math.sqrt(shape[0])
+        runs.append((row, scale, rate))
+        row += math.prod(shape) // LANES
+    runs.append((row, 0.0, 0.2))
+    begins = [run[0] for run in runs] + [geo.chunk * geo.n_dev]
+    found = []
+    for n in range(geo.n_dev):
+        lo, hi = n * geo.chunk, (n + 1) * geo.chunk
+        found.append(
+            [(max(run[0] - lo, 0), *run[1:]) for run, end in zip(runs, begins[1:]) if run[0] < hi and end > lo]
+        )
+    most = max(len(rows) for rows in found)
+    found = [rows + [(geo.chunk, 0.0, 0.0)] * (most - len(rows)) for rows in found]
+    return np.asarray(found, np.float32).transpose(0, 2, 1).copy()
 
 
 def matmul(left, right):
@@ -1591,8 +1638,8 @@
     pad_rows = ceil_to(geo.chunk + 4 * BLK, 8)
     ORDER.start()
     aligned = align_rows(geo, table, master.reshape(geo.chunk, LANES), pad_rows)
-    pieces = lax.all_to_all(aligned.reshape(geo.n_dev, geo.piece, LANES), AXES, 0, 0, tiled=True)
-    parts = [pieces[span.start : span.stop] for span in gather.ranges]
+    shares = lax.all_to_all(aligned.reshape(geo.n_seg, geo.share, LANES), AXES[0], 0, 0, tiled=True)
+    parts = [shares[span.start // n_doc : span.stop // n_doc] for span in gather.ranges]
 
     seg_count = tokens.shape[1]
     n_rows = n_seg * seg_count
@@ -1601,10 +1648,9 @@
     last = tiles_all - 1 - middle
     inputs = tokens[0].reshape(seg_count * SEG_LEN, D)
     cot_rows = cotangent[0]
-    cut = gather.half
-
-    line = gather_line(geo, parts[0], my_doc, cut[0])
-    parts_b = [parts[1]] + [send(geo, parts[1], Z, r) for r in range(1, n_doc)]
+
+    line = place_line(geo, along_z(geo, parts[0]), my_doc)
+    parts_b = along_z(geo, parts[1])
     ORDER.wait_for(*parts_b[1:2])
     plane = gather_plane(geo, line, 0)
     ORDER.wait_for(*parts_b[2:3])
@@ -1617,7 +1663,7 @@
     def own(values):
         return lax.dynamic_slice_in_dim(values, my_seg * seg_count, seg_count, axis=0)
 
-    plane_b = place_line(geo, parts_b, my_doc, cut[1])
+    plane_b = place_line(geo, parts_b, my_doc)
     *outs, w_qkv, vec_a = attend_first(inputs, weights(0, 1), coords)
     plane_b = gather_plane(geo, plane_b, 0)
     gathered[2] = [lax.all_gather(gate(parts[2]), AXES)]
@@ -1655,7 +1701,7 @@
         cot_rows.reshape(-1, D), own(grad_rows).astype(jnp.float32), normal_two, slope, normal_one, rates,
         w_down, w_up, w_out, vec,
     )
-    pieces_c = sum_pieces(geo, [line_c])
+    sums_c = sum_line(geo, line_c)
     grads[item_name(8)] = low(matmul(hot.T, own(grad_rows)))
     for number, row in ((3, 2), (5, 5), (7, 9)):
         grads[item_name(number)] = (sums, row)
@@ -1665,46 +1711,42 @@
     halves_d = reduce_cores(geo, arrays_d)
     grads[item_name(2)] = low(matmul(attended.T, dao))
     ORDER.wait_for(grads[item_name(2)])
-    halves_d = reduce_plane(geo, halves_d, 0)
+    halves_d, = reduce_plane(geo, [halves_d], [0])
     arrays_b = grad_bucket(geo, buckets, 1, grads, coords, item_name(4), hidden_low, du, 256)
     halves_b = reduce_cores(geo, arrays_b)
     back = attend_back(packed, stat, da, 0, 1)
-    halves_d = reduce_plane(geo, halves_d, 1)
-    halves_b = reduce_plane(geo, halves_b, 0)
+    halves_d, halves_b = reduce_plane(geo, [halves_d, halves_b], [1, 0])
     if tiles_all > 1:
         back = attend_back(packed, stat, da, 1, middle, back)
     line_d = reduce_line(geo, halves_d, my_doc)
-    halves_b = reduce_plane(geo, halves_b, 1)
+    halves_b, = reduce_plane(geo, [halves_b], [1])
     if last:
         back = attend_back(packed, stat, da, 1 + middle, last, back)
     dqkv, qv_sums = back
-    pieces_d = sum_pieces(geo, [line_d])
+    sums_d = sum_line(geo, line_d)
     line_b = reduce_line(geo, halves_b, my_doc)
     grads[item_name(1)] = (qv_sums, 0)
     arrays_a = grad_bucket(geo, buckets, 0, grads, coords, item_name(0), inputs, dqkv, 256)
     halves_a = reduce_cores(geo, arrays_a)
-    halves_a = reduce_plane(geo, halves_a, 0)
+    halves_a, = reduce_plane(geo, [halves_a], [0])
     token_grad, = token_back(grad_one, dqkv, w_qkv, 0, tiles_all)
-    pieces_b = sum_pieces(geo, [line_b])
-    halves_a = reduce_plane(geo, halves_a, 1)
+    sums_b = sum_line(geo, line_b)
+    halves_a, = reduce_plane(geo, [halves_a], [1])
     first_row = lax.broadcasted_iota(jnp.int32, (seg_count, SEG_LEN, D), 1) == 0
     mixed_out = jnp.where(
         first_row, own(crossed)[:, None, :], hidden_two.reshape(seg_count, SEG_LEN, D)
     )
     line_a = reduce_line(geo, halves_a, my_doc)
-    all_pieces = sum_pieces(geo, [line_a, [pieces_b], [pieces_d], [pieces_c]])
-    owned = lax.all_to_all(all_pieces, AXES, 0, 0, tiled=True)
-    natural = natural_rows(geo, table, owned.reshape(-1, LANES), pad_rows)
-    gradient = natural[BLK : BLK + geo.chunk].reshape(-1)
+    owned = lax.all_to_all(
+        sum_all(geo, line_a, sums_b, sums_d, sums_c), AXES[0], 0, 0, tiled=True
+    )
     n_cls = n_doc * n_rows
-    scaling, rating = (
-        jnp.broadcast_to(
-            lax.dynamic_index_in_dim(jnp.asarray(rates), me, 0, False)[:, None], (geo.chunk, LANES)
-        ).reshape(-1)
-        for rates in row_rates(geo, n_cls * SEG_LEN, n_cls)
-    )
-    weight, moment, smooth, copy_low = optimizer_step(
-        gradient, master, momentum, average, scaling, rating
+    rates = lax.dynamic_index_in_dim(jnp.asarray(row_rates(geo, n_cls * SEG_LEN, n_cls)), me, 0, False)
+    begins, factors = rates[0].astype(jnp.int32), rates[1:].reshape(-1)
+    state = [value.reshape(geo.chunk, LANES) for value in (master, momentum, average)]
+    weight, moment, smooth, copy_low = (
+        value.reshape(-1)
+        for value in update_rows(geo, table, owned.reshape(-1, LANES), begins, factors, state, pad_rows)
     )
     return (
         mixed_out[None],

time: 626 us -> 605 us (0.966)
  waiting for transfers between devices: 94.2 us -> 81.1 us
  Pallas kernels: 366 us -> 378 us
  blocking collectives: 39.3 us -> 28.8 us
    pallas_call x38 -> x37, Pallas kernels: 366 us -> 378 us  [run(): pl.pallas_call(wrapped, out_shape=outs + [jax.ShapeDtypeStruct((8, LANES)...]
    all_to_all x1, blocking collectives: 29.8 us -> 19.4 us  [local(): lax.all_to_all(aligned.reshape(geo.n_seg, geo.share, LANES), AXES[0], 0,...]
    all_to_all x1, waiting for transfers between devices: 17.3 us -> 8.27 us  [local(): lax.all_to_all(sum_all(geo, line_a, sums_b, sums_d, sums_c), AXES[0], 0,...]
    unnamed x112 -> x108, local copies, waits for them, and re-layouts: 19.8 us -> 19 us
  transfers between devices with their start and end apart: 50 -> 50, of which waited for: 16 -> 16; matrix products, arithmetic and copies ran while one was open for 3% -> 3% of each run, Pallas kernels for 38% -> 39%
where the time goes in v5:
time: 605 us; the launch traced here: 595 us
  Pallas kernels  378 us (62%)
  waiting for transfers between devices  81.1 us (13%)
  starting transfers between devices  50.1 us (8%)
  blocking collectives  28.8 us (5%)
  local copies, waits for them, and re-layouts  25.7 us (4%)
  between operations  15 us (2%)
  matrix products  8.2 us (1%)
  other arithmetic  7.88 us (1%)
    pallas_call x37, Pallas kernels, run(): pl.pallas_call(wrapped, out_shape=outs + [jax.ShapeDtypeStruct((8, LANES)...  378 us
    ppermute x48, waiting for transfers between devices, send(): return lax.ppermute(value, AXES, geo.shift(axis, step))  72.8 us
    ppermute x48, starting transfers between devices, send(): return lax.ppermute(value, AXES, geo.shift(axis, step))  46.5 us
    all_to_all x1, blocking collectives, local(): lax.all_to_all(aligned.reshape(geo.n_seg, geo.share, LANES), AXES[0], 0,...  19.4 us
    unnamed x108, local copies, waits for them, and re-layouts  19 us
  transfers between devices with their start and end apart: 50, of which 16 were waited for; matrix products, arithmetic and copies ran while one was open for 3% of the time, Pallas kernels for 39%

profile of v5, /device:TPU:0, one launch (start us, length us, event | category | flops | bytes accessed | tf_op | source)
XLA Modules:
  0.0 594.5 jit_solution(9390400550707816548)
XLA Ops:
  12.1 19.4 %all_to_all.10 = bf16[8,448,128]{2,1,0:T(8,128)(2,1)S(1)} all-to-all(bf16[8,448,128]{2,1,0:T(8,128)(2,1)} %bitcast.171), channel_id=1, replica_groups=mesh['seg'=8,'doc'=4] {'seg'}, dimensions={0} | all-to-all | bytes 1835008 | tf_op jit(solution)/shard_map/all_to_all | solution.py:1641
  38.7 13.4 %collective-permute-done.4.refs_3_ = bf16[1,448,128]{2,1,0:T(8,128)(2,1)S(1)} collective-permute-done((bf16[1,448,128]{2,1,0:T(8,128)(2,1)S(1)}, bf16[1,448,128]{2,1,0:T(8,128)(2,1)S(1)}, u32[]{:S(2)}, u32[]{:S(2)}) %collective-permute-start.4) | collective-permute-done | bytes 114720 | tf_op jit(solution)/shard_map/ppermute | solution.py:1439
  56.1 5.6 collective-permute-done.6
  67.9 8.6 %collective-permute-done.1.refs_5_.refs_3_ = bf16[3,448,128]{2,1,0:T(8,128)(2,1)S(1)} collective-permute-done((bf16[3,448,128]{2,1,0:T(8,128)(2,1)S(1)}, bf16[3,448,128]{2,1,0:T(8,128)(2,1)S(1)}, u32[]{:S(2)}, u32[]{:S(2)}) %collective-permute-start.1) | collective-permute-done | bytes 344096 | tf_op jit(solution)/shard_map/ppermute | solution.py:1439
  84.2 8.7 %collective-permute-done.2.refs_4_ = bf16[3,448,128]{2,1,0:T(8,128)(2,1)S(1)} collective-permute-done((bf16[3,448,128]{2,1,0:T(8,128)(2,1)S(1)}, bf16[3,448,128]{2,1,0:T(8,128)(2,1)S(1)}, u32[]{:S(2)}, u32[]{:S(2)}) %collective-permute-start.2) | collective-permute-done | bytes 344096 | tf_op jit(solution)/shard_map/ppermute | solution.py:1439
  98.7 12.6 %shard_map.141 = (bf16[2048,2304]{1,0:T(8,128)(2,1)}, bf16[2048,768]{1,0:T(8,128)(2,1)}, f32[2048,128]{1,0:T(8,128)}, bf16[768,2304]{1,0:T(8,128)(2,1)}, f32[16,768]{1,0:T(8,128)}, /*index=5*/f32[8,128]{1,0:T(8,128)}) custom-call(s32[4]{0:T(128)} %pad_add_fusion.refs_0_, bf16[2,2,4,224,128]{4,3,2,1,0:T(8,128)(2,1)} %bitcast.218, ...), custom_call_target="tpu_custom_call" | custom-call | flops 12000000000 | bytes 36000000 | tf_op jit(solution)/shard_map/pallas_call | solution.py:222
  114.2 4.1 shard_map.142
  123.2 16.4 %shard_map.144 = (bf16[2048,2304]{1,0:T(8,128)(2,1)}, bf16[2048,768]{1,0:T(8,128)(2,1)}, f32[2048,128]{1,0:T(8,128)}, f32[8,128]{1,0:T(8,128)}) custom-call(bf16[2048,768]{1,0:T(8,128)(2,1)} %bitcast.210, bf16[768,2304]{1,0:T(8,128)(2,1)} %get-tuple-element.185.refs_1_.refs_2_, ...), custom_call_target="tpu_custom_call", output_to_operand_aliasing={{0}: (3, {}), {1}: (4, {}), {2}: (5, {})} | custom-call | flops 16000000000 | bytes 48000000 | tf_op jit(solution)/shard_map/pallas_call | solution.py:222
  139.7 18.8 %collective-permute-done.15 = bf16[2,12,224,128]{3,2,1,0:T(8,128)(2,1)S(1)} collective-permute-done((bf16[2,12,224,128]{3,2,1,0:T(8,128)(2,1)}, bf16[2,12,224,128]{3,2,1,0:T(8,128)(2,1)S(1)}, u32[]{:S(2)}, u32[]{:S(2)}) %collective-permute-start.15) | collective-permute-done | bytes 1376288 | tf_op jit(solution)/shard_map/ppermute | solution.py:1439
  161.7 5.4 shard_map.145
  168.3 9.5 %shard_map.146 = (bf16[2048,2304]{1,0:T(8,128)(2,1)}, bf16[2048,768]{1,0:T(8,128)(2,1)}, f32[2048,128]{1,0:T(8,128)}, f32[8,128]{1,0:T(8,128)}) custom-call(bf16[2048,768]{1,0:T(8,128)(2,1)} %bitcast.211, bf16[768,2304]{1,0:T(8,128)(2,1)} %get-tuple-element.185.refs_1_.refs_2_, ...), custom_call_target="tpu_custom_call", output_to_operand_aliasing={{0}: (3, {}), {1}: (4, {}), {2}: (5, {})} | custom-call | flops 8000000000 | bytes 24000000 | tf_op jit(solution)/shard_map/pallas_call | solution.py:222
  177.8 65.4 %shard_map.147 = (bf16[2048,768]{1,0:T(8,128)(2,1)}, bf16[2048,768]{1,0:T(8,128)(2,1)}, bf16[2048,3072]{1,0:T(8,128)(2,1)}, bf16[2048,3072]{1,0:T(8,128)(2,1)}, ...) custom-call(s32[4]{0:T(128)} %pad_add_fusion.refs_0_, ...), custom_call_target="tpu_custom_call" | custom-call | flops 60000002048 | bytes 180000000 | tf_op jit(solution)/shard_map/pallas_call | solution.py:222
  246.6 9.4 %all_gather.7 = bf16[128,1664]{1,0:T(8,128)(2,1)S(1)} all-gather(bf16[16,1664]{1,0:T(8,128)(2,1)} %get-tuple-element.202), channel_id=1, replica_groups=mesh['seg'=8,'doc'=4] {'seg'}, dimensions={0}, use_global_device_ids=true | all-gather | bytes 479232 | tf_op jit(solution)/shard_map/all_gather | solution.py:1682
  259.0 22.4 %shard_map.149 = (bf16[128,768]{1,0:T(8,128)(2,1)}, bf16[128,768]{1,0:T(8,128)(2,1)}, f32[16,768]{1,0:T(8,128)}, bf16[128,2304]{1,0:T(8,128)(2,1)}, bf16[128,768...) custom-call(s32[4]{0:T(128)} %pad_add_fusion.refs_0_, ...), custom_call_target="tpu_custom_call" | custom-call | flops 22000001024 | bytes 66000000 | tf_op jit(solution)/shard_map/pallas_call | solution.py:222
  281.4 12.8 %shard_map.150 = (bf16[16,448,128]{2,1,0:T(8,128)(2,1)}, f32[8,128]{1,0:T(8,128)}) custom-call(s32[1]{0:T(128)} %bitcast.39.refs_0_, bf16[64,128]{1,0:T(8,128)(2,1)} %fusion.refs_1_, bf16[768,128]{1,0:T(8,128)(2,1)} %get-tuple-element.215.refs_2_, bf16[768,128]{1,0:T(8,128)(2,1)} %get-tuple-element.216.refs_3_, bf16[768,128]{1,0:T(8,128)(2,1)} %get-tuple-element.217.refs_4_, ...), custom_call_target="tpu_custom_call" | custom-call | flops 12000000000 | bytes 36000000 | tf_op jit(solution)/shard_map/pallas_call | solution.py:222
  302.4 43.7 %shard_map.152 = (bf16[2048,768]{1,0:T(8,128)(2,1)}, bf16[2048,3072]{1,0:T(8,128)(2,1)}, bf16[2048,768]{1,0:T(8,128)(2,1)}, bf16[2048,768]{1,0:T(8,128)(2,1)}, f...) custom-call(bf16[2048,768]{1,0:T(8,128)(2,1)} %bitcast.141, f32[16,768]{1,0:T(8,128)} %get-tuple-element.328.refs_1_, ...), custom_call_target="tpu_custom_call" | custom-call | flops 44000002048 | bytes 132000000 | tf_op jit(solution)/shard_map/pallas_call | solution.py:222
  352.4 19.1 %shard_map.154 = (bf16[2,2,4,224,128]{4,3,2,1,0:T(8,128)(2,1)}, bf16[2,2,4,224,128]{4,3,2,1,0:T(8,128)(2,1)}, bf16[2,2,4,224,128]{4,3,2,1,0:T(8,128)(2,1)}, bf16...) custom-call(s32[4]{0:T(128)} %pad_add_fusion.refs_0_, ...), custom_call_target="tpu_custom_call" | custom-call | flops 17999998976 | bytes 54000000 | tf_op jit(solution)/shard_map/pallas_call | solution.py:222
  372.4 6.5 %convolution_convert_fusion.refs_9_.refs_3_.refs_4_ = bf16[768,768]{1,0:T(8,128)(2,1)} fusion(bf16[2048,768]{1,0:T(8,128)(2,1)} %get-tuple-element.198.refs_10_, bf16[2048,768]{1,0:T(8,128)(2,1)} %get-tuple-element.234), kind=kOutput, calls=%fused_computation.1 | convolution fusion | flops 2416508928 | bytes 7471104 | tf_op jit(solution)/shard_map/dot_general | solution.py:1620
  380.1 4.1 shard_map.155
  384.2 21.9 %shard_map.156 = (bf16[2,2,8,224,128]{4,3,2,1,0:T(8,128)(2,1)}, bf16[2,2,8,224,128]{4,3,2,1,0:T(8,128)(2,1)}, bf16[2,2,8,224,128]{4,3,2,1,0:T(8,128)(2,1)}, bf16[2,2,8,224,128]{4,3,2,1,0:T(8,128)(2,1)}, f32[8,128]{1,0:T(8,128)}) custom-call(s32[4]{0:T(128)} %pad_add_fusion.refs_0_, bf16[2048,768]{1,0:T(8,128)(2,1)} %get-tuple-element.232.refs_1_, ...), custom_call_target="tpu_custom_call" | custom-call | flops 17999998976 | bytes 54000000 | tf_op jit(solution)/shard_map/pallas_call | solution.py:222
  410.1 11.6 %shard_map.157 = (bf16[2048,2304]{1,0:T(8,128)(2,1)}, f32[8,768]{1,0:T(8,128)}, f32[8,128]{1,0:T(8,128)}) custom-call(bf16[2048,2304]{1,0:T(8,128)(2,1)} %get-tuple-element.229.refs_0_, f32[2048,128]{1,0:T(8,128)} %get-tuple-element.230.refs_1_, bf16[2048,768]{1,0:T(8,128)(2,1)} %get-tuple-element.231.refs_2_, f32[8,768]{1,0:T(8,128)} %broadcast_in_dim.42.refs_3_, ...), custom_call_target="tpu_custom_call" | custom-call | flops 10000000000 | bytes 30000000 | tf_op jit(solution)/shard_map/pallas_call | solution.py:222
  423.6 6.3 %shard_map.158 = (bf16[1,896,128]{2,1,0:T(8,128)(2,1)}, bf16[1,896,128]{2,1,0:T(8,128)(2,1)}, bf16[1,896,128]{2,1,0:T(8,128)(2,1)}, bf16[1,896,128]{2,1,0:T(8,12...) custom-call(bf16[2,896,128]{2,1,0:T(8,128)(2,1)} %bitcast.149, ...), custom_call_target="tpu_custom_call" | custom-call | tf_op jit(solution)/shard_map/pallas_call | solution.py:222
  434.0 19.8 %shard_map.159 = (bf16[2048,2304]{1,0:T(8,128)(2,1)}, f32[8,768]{1,0:T(8,128)}, f32[8,128]{1,0:T(8,128)}) custom-call(bf16[2048,2304]{1,0:T(8,128)(2,1)} %get-tuple-element.229.refs_0_, f32[2048,128]{1,0:T(8,128)} %get-tuple-element.230.refs_1_, bf16[2048,768]{1,0:T(8,128)(2,1)} %get-tuple-element.231.refs_2_, ...), custom_call_target="tpu_custom_call", output_to_operand_aliasing={{0}: (4, {})} | custom-call | flops 20000000000 | bytes 60000000 | tf_op jit(solution)/shard_map/pallas_call | solution.py:222
  462.9 4.3 shard_map.161
  468.7 11.6 %shard_map.162 = (bf16[2048,2304]{1,0:T(8,128)(2,1)}, f32[8,768]{1,0:T(8,128)}, f32[8,128]{1,0:T(8,128)}) custom-call(bf16[2048,2304]{1,0:T(8,128)(2,1)} %get-tuple-element.229.refs_0_, f32[2048,128]{1,0:T(8,128)} %get-tuple-element.230.refs_1_, bf16[2048,768]{1,0:T(8,128)(2,1)} %get-tuple-element.231.refs_2_, ...), custom_call_target="tpu_custom_call", output_to_operand_aliasing={{0}: (4, {})} | custom-call | flops 10000000000 | bytes 30000000 | tf_op jit(solution)/shard_map/pallas_call | solution.py:222
  487.2 15.7 %shard_map.165 = (bf16[2,2,4,224,128]{4,3,2,1,0:T(8,128)(2,1)}, bf16[2,2,4,224,128]{4,3,2,1,0:T(8,128)(2,1)}, bf16[2,2,4,224,128]{4,3,2,1,0:T(8,128)(2,1)}, bf16[2,2,4,224,128]{4,3,2,1,0:T(8,128)(2,1)}, f32[8,128]{1,0:T(8,128)}) custom-call(s32[4]{0:T(128)} %pad_add_fusion.refs_0_, bf16[2048,768]{1,0:T(8,128)(2,1)} %bitcast.213, ...), custom_call_target="tpu_custom_call" | custom-call | flops 17999998976 | bytes 54000000 | tf_op jit(solution)/shard_map/pallas_call | solution.py:222
  508.6 4.1 shard_map.166
  515.4 13.2 %shard_map.167 = (bf16[2048,768]{1,0:T(8,128)(2,1)}, f32[8,128]{1,0:T(8,128)}) custom-call(f32[2048,768]{1,0:T(8,128)} %get-tuple-element.228.refs_0_, bf16[2048,2304]{1,0:T(8,128)(2,1)} %get-tuple-element.277.refs_2_.refs_1_, bf16[768,2304]{1,0:T(8,128)(2,1)} %get-tuple-element.185.refs_1_.refs_2_, f32[8,128]{1,0:T(8,128)} %get-tuple-element.295.refs_3_), custom_call_target="tpu_custom_call" | custom-call | flops 12000000000 | bytes 36000000 | tf_op jit(solution)/shard_map/pallas_call | solution.py:222
  538.4 5.3 collective-permute-done.43.refs_2_
  566.1 3.8 broadcast_select_fusion
  569.9 8.3 %all-to-all-done.1 = bf16[8,448,128]{2,1,0:T(8,128)(2,1)S(1)} async-done(((bf16[8,448,128]{2,1,0:T(8,128)(2,1)}), bf16[8,448,128]{2,1,0:T(8,128)(2,1)S(1)}, u32[]{:S(2)}, u32[]{:S(2)}) %all-to-all-start.1) | async-done | bytes 917536 | tf_op jit(solution)/shard_map/all_to_all | solution.py:1740
  579.1 8.1 %shard_map.172 = (f32[3473,128]{1,0:T(8,128)}, f32[3473,128]{1,0:T(8,128)}, f32[3473,128]{1,0:T(8,128)}, bf16[3473,128]{1,0:T(8,128)(2,1)}, f32[8,128]{1,0:T(8,128)}) custom-call(s32[156]{0:T(256)} %bitcast.204, s32[5]{0:T(128)} %convert_bitcast_fusion.refs_1_, f32[10]{0:T(128)} %reshape.359.refs_2_, bf16[3584,128]{1,0:T(8,128)(2,1)} %bitcast.130, ...), custom_call_target="tpu_custom_call" | custom-call | tf_op jit(solution)/shard_map/pallas_call | solution.py:222
  (239 shorter events, 139.8 us)
Async XLA Ops:
  7.2 236.0 %all-gather.2.cloned.1.call-start = ((), (), s32[]{:S(2)}) async-start(), calls=%async_computation.2 | async-start | bytes 15138816 | tf_op jit(solution)/shard_map/all_gather | solution.py:1669
  35.1 17.0 %collective-permute-start.4 = (bf16[1,448,128]{2,1,0:T(8,128)(2,1)S(1)}, bf16[1,448,128]{2,1,0:T(8,128)(2,1)S(1)}, u32[]{:S(2)}, u32[]{:S(2)}) collective-permute-start(bf16[1,448,128]{2,1,0:T(8,128)(2,1)S(1)} %slice.40.refs_1_), channel_id=1, source_target_pairs={{0,2},{1,3},{2,0},{3,1},{4,6},{5,7},{6,4},{7,5},{8,10},{9,11},{10,... | collective-permute-start | bytes 344072 | tf_op jit(solution)/shard_map/ppermute | solution.py:1439
  35.1 17.0 %collective-permute-start.3 = (bf16[1,448,128]{2,1,0:T(8,128)(2,1)S(1)}, bf16[1,448,128]{2,1,0:T(8,128)(2,1)S(1)}, u32[]{:S(2)}, u32[]{:S(2)}) collective-permute-start(bf16[1,448,128]{2,1,0:T(8,128)(2,1)S(1)} %slice.40.refs_1_), channel_id=1, source_target_pairs={{0,1},{1,2},{2,3},{3,0},{4,5},{5,6},{6,7},{7,4},{8,9},{9,10},{10,1... | collective-permute-start | bytes 344072 | tf_op jit(solution)/shard_map/ppermute | solution.py:1439
  36.1 19.9 %collective-permute-start = (bf16[3,448,128]{2,1,0:T(8,128)(2,1)S(1)}, bf16[3,448,128]{2,1,0:T(8,128)(2,1)S(1)}, u32[]{:S(2)}, u32[]{:S(2)}) collective-permute-start(bf16[3,448,128]{2,1,0:T(8,128)(2,1)S(1)} %slice.39.refs_1_), channel_id=1, source_target_pairs={{0,1},{1,2},{2,3},{3,0},{4,5},{5,6},{6,7},{7,4},{8,9},{9,10},{10,1... | collective-permute-start | bytes 1032200 | tf_op jit(solution)/shard_map/ppermute | solution.py:1439
  82.3 15.2 %collective-permute-start.12 = (bf16[2,2,4,224,128]{4,3,2,1,0:T(8,128)(2,1)}, bf16[2,2,4,224,128]{4,3,2,1,0:T(8,128)(2,1)S(1)}, u32[]{:S(2)}, u32[]{:S(2)}) collective-permute-start(bf16[2,2,4,224,128]{4,3,2,1,0:T(8,128)(2,1)} %bitcast.217), channel_id=1, source_target_pairs={{0,4},{1,5},{2,6},{3,7},{4,0},{5,1},{6,2},{7,3},{8,12},{9,13},{10,... | collective-permute-start | bytes 2752520 | tf_op jit(solution)/shard_map/ppermute | solution.py:1439
  82.3 15.2 %collective-permute-start.13 = (bf16[2,2,4,224,128]{4,3,2,1,0:T(8,128)(2,1)}, bf16[2,2,4,224,128]{4,3,2,1,0:T(8,128)(2,1)S(1)}, u32[]{:S(2)}, u32[]{:S(2)}) collective-permute-start(bf16[2,2,4,224,128]{4,3,2,1,0:T(8,128)(2,1)} %bitcast.220), channel_id=1, source_target_pairs={{0,4},{1,5},{2,6},{3,7},{4,0},{5,1},{6,2},{7,3},{8,12},{9,13},{10,... | collective-permute-start | bytes 2752520 | tf_op jit(solution)/shard_map/ppermute | solution.py:1439
  96.0 16.8 %collective-permute-start.10 = (bf16[12,224,128]{2,1,0:T(8,128)(2,1)}, bf16[12,224,128]{2,1,0:T(8,128)(2,1)S(1)}, u32[]{:S(2)}, u32[]{:S(2)}) collective-permute-start(bf16[12,224,128]{2,1,0:T(8,128)(2,1)} %get-tuple-element.175), channel_id=1, source_target_pairs={{0,8},{1,9},{2,10},{3,11},{4,12},{5,13},{6,14},{7,15},{8,0},{9,1},... | collective-permute-start | bytes 2064392 | tf_op jit(solution)/shard_map/ppermute | solution.py:1439
  96.8 16.5 %collective-permute-start.11 = (bf16[12,224,128]{2,1,0:T(8,128)(2,1)}, bf16[12,224,128]{2,1,0:T(8,128)(2,1)S(1)}, u32[]{:S(2)}, u32[]{:S(2)}) collective-permute-start(bf16[12,224,128]{2,1,0:T(8,128)(2,1)} %get-tuple-element.176), channel_id=1, source_target_pairs={{0,16},{1,17},{2,18},{3,19},{4,20},{5,21},{6,22},{7,23},{8,24},{9,... | collective-permute-start | bytes 2064392 | tf_op jit(solution)/shard_map/ppermute | solution.py:1439
  121.4 37.1 %collective-permute-start.15 = (bf16[2,12,224,128]{3,2,1,0:T(8,128)(2,1)}, bf16[2,12,224,128]{3,2,1,0:T(8,128)(2,1)S(1)}, u32[]{:S(2)}, u32[]{:S(2)}) collective-permute-start(bf16[2,12,224,128]{3,2,1,0:T(8,128)(2,1)} %bitcast.167), channel_id=1, source_target_pairs={{0,8},{1,9},{2,10},{3,11},{4,12},{5,13},{6,14},{7,15},{8,0},{9,1},... | collective-permute-start | bytes 4128776 | tf_op jit(solution)/shard_map/ppermute | solution.py:1439
  122.7 38.0 %collective-permute-start.14 = (bf16[2,12,224,128]{3,2,1,0:T(8,128)(2,1)}, bf16[2,12,224,128]{3,2,1,0:T(8,128)(2,1)S(1)}, u32[]{:S(2)}, u32[]{:S(2)}) collective-permute-start(bf16[2,12,224,128]{3,2,1,0:T(8,128)(2,1)} %bitcast.165), channel_id=1, source_target_pairs={{0,16},{1,17},{2,18},{3,19},{4,20},{5,21},{6,22},{7,23},{8,24},{9,... | collective-permute-start | bytes 4128776 | tf_op jit(solution)/shard_map/ppermute | solution.py:1439
  297.2 50.6 %collective-permute-start.18 = (bf16[4,448,128]{2,1,0:T(8,128)(2,1)}, bf16[4,448,128]{2,1,0:T(8,128)(2,1)S(1)}, u32[]{:S(2)}, u32[]{:S(2)}) collective-permute-start(bf16[4,448,128]{2,1,0:T(8,128)(2,1)} %get-tuple-element.239), channel_id=1, source_target_pairs={{0,1},{1,2},{2,3},{3,0},{4,5},{5,6},{6,7},{7,4},{8,9},{9,10},{10,1... | collective-permute-start | bytes 1376264 | tf_op jit(solution)/shard_map/ppermute | solution.py:1439
  297.2 50.6 %collective-permute-start.19 = (bf16[4,448,128]{2,1,0:T(8,128)(2,1)}, bf16[4,448,128]{2,1,0:T(8,128)(2,1)S(1)}, u32[]{:S(2)}, u32[]{:S(2)}) collective-permute-start(bf16[4,448,128]{2,1,0:T(8,128)(2,1)} %get-tuple-element.240), channel_id=1, source_target_pairs={{0,2},{1,3},{2,0},{3,1},{4,6},{5,7},{6,4},{7,5},{8,10},{9,11},{10,... | collective-permute-start | bytes 1376264 | tf_op jit(solution)/shard_map/ppermute | solution.py:1439
  297.7 50.2 %collective-permute-start.20 = (bf16[4,448,128]{2,1,0:T(8,128)(2,1)}, bf16[4,448,128]{2,1,0:T(8,128)(2,1)S(1)}, u32[]{:S(2)}, u32[]{:S(2)}) collective-permute-start(bf16[4,448,128]{2,1,0:T(8,128)(2,1)} %get-tuple-element.241), channel_id=1, source_target_pairs={{0,3},{1,0},{2,1},{3,2},{4,7},{5,4},{6,5},{7,6},{8,11},{9,8},{10,9... | collective-permute-start | bytes 1376264 | tf_op jit(solution)/shard_map/ppermute | solution.py:1439
  406.1 15.5 %collective-permute-start.25 = (bf16[2,2,8,224,128]{4,3,2,1,0:T(8,128)(2,1)}, bf16[2,2,8,224,128]{4,3,2,1,0:T(8,128)(2,1)S(1)}, u32[]{:S(2)}, u32[]{:S(2)}) collective-permute-start(bf16[2,2,8,224,128]{4,3,2,1,0:T(8,128)(2,1)} %get-tuple-element.259), channel_id=1, source_target_pairs={{0,4},{1,5},{2,6},{3,7},{4,0},{5,1},{6,2},{7,3},{8,12},{9,13},{10,... | collective-permute-start | bytes 5505032 | tf_op jit(solution)/shard_map/ppermute | solution.py:1439
  406.6 15.0 %collective-permute-start.26 = (bf16[2,2,8,224,128]{4,3,2,1,0:T(8,128)(2,1)}, bf16[2,2,8,224,128]{4,3,2,1,0:T(8,128)(2,1)S(1)}, u32[]{:S(2)}, u32[]{:S(2)}) collective-permute-start(bf16[2,2,8,224,128]{4,3,2,1,0:T(8,128)(2,1)} %get-tuple-element.261), channel_id=1, source_target_pairs={{0,4},{1,5},{2,6},{3,7},{4,0},{5,1},{6,2},{7,3},{8,12},{9,13},{10,... | collective-permute-start | bytes 5505032 | tf_op jit(solution)/shard_map/ppermute | solution.py:1439
  406.7 14.9 %collective-permute-start.23 = (bf16[2,4,224,128]{3,2,1,0:T(8,128)(2,1)}, bf16[2,4,224,128]{3,2,1,0:T(8,128)(2,1)S(1)}, u32[]{:S(2)}, u32[]{:S(2)}) collective-permute-start(bf16[2,4,224,128]{3,2,1,0:T(8,128)(2,1)} %bitcast.230), channel_id=1, source_target_pairs={{0,16},{1,17},{2,18},{3,19},{4,20},{5,21},{6,22},{7,23},{8,24},{9,... | collective-permute-start | bytes 1376264 | tf_op jit(solution)/shard_map/ppermute | solution.py:1439
  408.7 12.9 %collective-permute-start.24 = (bf16[2,4,224,128]{3,2,1,0:T(8,128)(2,1)}, bf16[2,4,224,128]{3,2,1,0:T(8,128)(2,1)}, u32[]{:S(2)}, u32[]{:S(2)}) collective-permute-start(bf16[2,4,224,128]{3,2,1,0:T(8,128)(2,1)} %bitcast.227), channel_id=1, source_target_pairs={{0,8},{1,9},{2,10},{3,11},{4,12},{5,13},{6,14},{7,15},{8,0},{9,1},... | collective-permute-start | bytes 1376264 | tf_op jit(solution)/shard_map/ppermute | solution.py:1439
  429.9 23.9 %collective-permute-start.29 = (bf16[4,224,128]{2,1,0:T(8,128)(2,1)}, bf16[4,224,128]{2,1,0:T(8,128)(2,1)S(1)}, u32[]{:S(2)}, u32[]{:S(2)}) collective-permute-start(bf16[4,224,128]{2,1,0:T(8,128)(2,1)} %bitcast.233), channel_id=1, source_target_pairs={{0,8},{1,9},{2,10},{3,11},{4,12},{5,13},{6,14},{7,15},{8,0},{9,1},... | collective-permute-start | bytes 688136 | tf_op jit(solution)/shard_map/ppermute | solution.py:1439
  431.3 22.6 %collective-permute-start.30 = (bf16[4,224,128]{2,1,0:T(8,128)(2,1)}, bf16[4,224,128]{2,1,0:T(8,128)(2,1)S(1)}, u32[]{:S(2)}, u32[]{:S(2)}) collective-permute-start(bf16[4,224,128]{2,1,0:T(8,128)(2,1)} %bitcast.232), channel_id=1, source_target_pairs={{0,16},{1,17},{2,18},{3,19},{4,20},{5,21},{6,22},{7,23},{8,24},{9,... | collective-permute-start | bytes 688136 | tf_op jit(solution)/shard_map/ppermute | solution.py:1439
  431.4 30.3 %collective-permute-start.27 = (bf16[2,8,224,128]{3,2,1,0:T(8,128)(2,1)}, bf16[2,8,224,128]{3,2,1,0:T(8,128)(2,1)S(1)}, u32[]{:S(2)}, u32[]{:S(2)}) collective-permute-start(bf16[2,8,224,128]{3,2,1,0:T(8,128)(2,1)} %bitcast.224), channel_id=1, source_target_pairs={{0,16},{1,17},{2,18},{3,19},{4,20},{5,21},{6,22},{7,23},{8,24},{9,... | collective-permute-start | bytes 2752520 | tf_op jit(solution)/shard_map/ppermute | solution.py:1439
  433.3 28.4 %collective-permute-start.28 = (bf16[2,8,224,128]{3,2,1,0:T(8,128)(2,1)}, bf16[2,8,224,128]{3,2,1,0:T(8,128)(2,1)S(1)}, u32[]{:S(2)}, u32[]{:S(2)}) collective-permute-start(bf16[2,8,224,128]{3,2,1,0:T(8,128)(2,1)} %bitcast.223), channel_id=1, source_target_pairs={{0,8},{1,9},{2,10},{3,11},{4,12},{5,13},{6,14},{7,15},{8,0},{9,1},... | collective-permute-start | bytes 2752520 | tf_op jit(solution)/shard_map/ppermute | solution.py:1439
  456.7 23.5 %collective-permute-start.33 = (bf16[1,448,128]{2,1,0:T(8,128)(2,1)}, bf16[1,448,128]{2,1,0:T(8,128)(2,1)S(1)}, u32[]{:S(2)}, u32[]{:S(2)}) collective-permute-start(bf16[1,448,128]{2,1,0:T(8,128)(2,1)} %get-tuple-element.284), channel_id=1, source_target_pairs={{0,1},{1,2},{2,3},{3,0},{4,5},{5,6},{6,7},{7,4},{8,9},{9,10},{10,1... | collective-permute-start | bytes 344072 | tf_op jit(solution)/shard_map/ppermute | solution.py:1439
  457.3 23.0 %collective-permute-start.34 = (bf16[1,448,128]{2,1,0:T(8,128)(2,1)}, bf16[1,448,128]{2,1,0:T(8,128)(2,1)S(1)}, u32[]{:S(2)}, u32[]{:S(2)}) collective-permute-start(bf16[1,448,128]{2,1,0:T(8,128)(2,1)} %get-tuple-element.285), channel_id=1, source_target_pairs={{0,2},{1,3},{2,0},{3,1},{4,6},{5,7},{6,4},{7,5},{8,10},{9,11},{10,... | collective-permute-start | bytes 344072 | tf_op jit(solution)/shard_map/ppermute | solution.py:1439
  458.7 21.5 %collective-permute-start.35 = (bf16[1,448,128]{2,1,0:T(8,128)(2,1)}, bf16[1,448,128]{2,1,0:T(8,128)(2,1)S(1)}, u32[]{:S(2)}, u32[]{:S(2)}) collective-permute-start(bf16[1,448,128]{2,1,0:T(8,128)(2,1)} %get-tuple-element.286), channel_id=1, source_target_pairs={{0,3},{1,0},{2,1},{3,2},{4,7},{5,4},{6,5},{7,6},{8,11},{9,8},{10,9... | collective-permute-start | bytes 344072 | tf_op jit(solution)/shard_map/ppermute | solution.py:1439
  467.2 16.6 %collective-permute-start.31 = (bf16[8,224,128]{2,1,0:T(8,128)(2,1)}, bf16[8,224,128]{2,1,0:T(8,128)(2,1)S(1)}, u32[]{:S(2)}, u32[]{:S(2)}) collective-permute-start(bf16[8,224,128]{2,1,0:T(8,128)(2,1)} %bitcast.228), channel_id=1, source_target_pairs={{0,8},{1,9},{2,10},{3,11},{4,12},{5,13},{6,14},{7,15},{8,0},{9,1},... | collective-permute-start | bytes 1376264 | tf_op jit(solution)/shard_map/ppermute | solution.py:1439
  468.6 15.3 %collective-permute-start.32 = (bf16[8,224,128]{2,1,0:T(8,128)(2,1)}, bf16[8,224,128]{2,1,0:T(8,128)(2,1)S(1)}, u32[]{:S(2)}, u32[]{:S(2)}) collective-permute-start(bf16[8,224,128]{2,1,0:T(8,128)(2,1)} %bitcast.226), channel_id=1, source_target_pairs={{0,16},{1,17},{2,18},{3,19},{4,20},{5,21},{6,22},{7,23},{8,24},{9,... | collective-permute-start | bytes 1376264 | tf_op jit(solution)/shard_map/ppermute | solution.py:1439
  503.5 25.1 %collective-permute-start.40 = (bf16[2,448,128]{2,1,0:T(8,128)(2,1)S(1)}, bf16[2,448,128]{2,1,0:T(8,128)(2,1)S(1)}, u32[]{:S(2)}, u32[]{:S(2)}) collective-permute-start(bf16[2,448,128]{2,1,0:T(8,128)(2,1)S(1)} %copy-done.53), channel_id=1, source_target_pairs={{0,1},{1,2},{2,3},{3,0},{4,5},{5,6},{6,7},{7,4},{8,9},{9,10},{10,1... | collective-permute-start | bytes 688136 | tf_op jit(solution)/shard_map/ppermute | solution.py:1439
  503.5 25.1 %collective-permute-start.41 = (bf16[2,448,128]{2,1,0:T(8,128)(2,1)S(1)}, bf16[2,448,128]{2,1,0:T(8,128)(2,1)S(1)}, u32[]{:S(2)}, u32[]{:S(2)}) collective-permute-start(bf16[2,448,128]{2,1,0:T(8,128)(2,1)S(1)} %copy-done.52), channel_id=1, source_target_pairs={{0,2},{1,3},{2,0},{3,1},{4,6},{5,7},{6,4},{7,5},{8,10},{9,11},{10,... | collective-permute-start | bytes 688136 | tf_op jit(solution)/shard_map/ppermute | solution.py:1439
  504.5 24.1 %collective-permute-start.42 = (bf16[2,448,128]{2,1,0:T(8,128)(2,1)S(1)}, bf16[2,448,128]{2,1,0:T(8,128)(2,1)S(1)}, u32[]{:S(2)}, u32[]{:S(2)}) collective-permute-start(bf16[2,448,128]{2,1,0:T(8,128)(2,1)S(1)} %copy-done.51), channel_id=1, source_target_pairs={{0,3},{1,0},{2,1},{3,2},{4,7},{5,4},{6,5},{7,6},{8,11},{9,8},{10,9... | collective-permute-start | bytes 688136 | tf_op jit(solution)/shard_map/ppermute | solution.py:1439
  512.7 19.9 %collective-permute-start.38 = (bf16[2,4,224,128]{3,2,1,0:T(8,128)(2,1)}, bf16[2,4,224,128]{3,2,1,0:T(8,128)(2,1)S(1)}, u32[]{:S(2)}, u32[]{:S(2)}) collective-permute-start(bf16[2,4,224,128]{3,2,1,0:T(8,128)(2,1)} %bitcast.231), channel_id=1, source_target_pairs={{0,16},{1,17},{2,18},{3,19},{4,20},{5,21},{6,22},{7,23},{8,24},{9,... | collective-permute-start | bytes 1376264 | tf_op jit(solution)/shard_map/ppermute | solution.py:1439
  514.7 17.9 %collective-permute-start.39 = (bf16[2,4,224,128]{3,2,1,0:T(8,128)(2,1)}, bf16[2,4,224,128]{3,2,1,0:T(8,128)(2,1)S(1)}, u32[]{:S(2)}, u32[]{:S(2)}) collective-permute-start(bf16[2,4,224,128]{3,2,1,0:T(8,128)(2,1)} %bitcast.229), channel_id=1, source_target_pairs={{0,8},{1,9},{2,10},{3,11},{4,12},{5,13},{6,14},{7,15},{8,0},{9,1},... | collective-permute-start | bytes 1376264 | tf_op jit(solution)/shard_map/ppermute | solution.py:1439
  560.7 17.5 %all-to-all-start.1 = ((bf16[8,448,128]{2,1,0:T(8,128)(2,1)}), bf16[8,448,128]{2,1,0:T(8,128)(2,1)S(1)}, u32[]{:S(2)}, u32[]{:S(2)}) async-start(bf16[8,448,128]{2,1,0:T(8,128)(2,1)} %get-tuple-element.320), calls=%async_computation.1 | async-start | bytes 1835008 | tf_op jit(solution)/shard_map/all_to_all | solution.py:1740
  (72 other events, 437.0 us)
Sparse Core Ops, SparseCore 0:
  121.5 107.7 all-gather.1

commit v6 on v5

--- a/solution.py
+++ b/solution.py
@@ -182,11 +182,15 @@
     return pl.BlockSpec(memory_space=pl.ANY)
 
 
+def spec_hbm():
+    return pl.BlockSpec(memory_space=pltpu.HBM)
+
+
 def spec_smem():
     return pl.BlockSpec(memory_space=pltpu.SMEM)
 
 
-def kernel_params(mib=56):
+def kernel_params(mib=20):
     return pltpu.CompilerParams(vmem_limit_bytes=mib * 1024 * 1024)
 
 
@@ -291,13 +295,7 @@
     runs = begins.shape[0]
 
     def kernel(table_ref, begins_ref, factors_ref, blocks_ref, *refs):
-        inputs, outs, held, (grad_ref, in_sems) = refs[:3], refs[3:7], refs[7:10], refs[10:]
-        loads = [
-            pltpu.make_async_copy(source, target, in_sems.at[i])
-            for i, (source, target) in enumerate(zip(inputs, held))
-        ]
-        for load in loads:
-            load.start()
+        held, outs, grad_ref = refs[:3], refs[3:7], refs[7]
 
         def by_group(slot, start, cols):
             grad_ref[pl.ds(start + BLK, BLK, stride=cols), :] = blocks_ref[block_at(slot), :].astype(jnp.float32)
@@ -308,8 +306,6 @@
             grad_ref[here, :] = jnp.where(row_mask(low_row, high_row), rows, grad_ref[here, :])
 
         block_moves(geo, table_ref, by_group, by_row)
-        for load in loads:
-            load.wait()
 
         def step(row, rows):
             here = pl.ds(row, rows)
@@ -334,11 +330,10 @@
     return ordered(
         kernel,
         out_shape=full,
-        in_specs=[spec_smem()] * 3 + [spec_vmem()] + [spec_any()] * 3,
+        in_specs=[spec_smem()] * 3 + [spec_vmem()] * 4,
         out_specs=[spec_vmem()] * 4,
-        scratch_shapes=[pltpu.VMEM((rows_all, LANES), jnp.float32)] * 3
-        + [pltpu.VMEM((pad_rows, LANES), jnp.float32), pltpu.SemaphoreType.DMA((3,))],
-        compiler_params=kernel_params(),
+        scratch_shapes=[pltpu.VMEM((pad_rows, LANES), jnp.float32)],
+        compiler_params=kernel_params(28),
         cost_estimate=cost(3),
     )(table, begins, factors, blocks, *state)
 
@@ -697,95 +692,96 @@
     )(coords, left, right, *operands)
 
 
-def pack_cross(geo, span, lefts, rights, vectors, seg):
-    seg_blocks = geo.n_doc * geo.piece_blocks
-    parts = bucket_parts(geo, span)
-    names = list(lefts)
-    vector_names = list(vectors)
-    depth_rows = next(iter(rights.values())).shape[0]
-
-    def window(cols):
-        return (-(-(seg_blocks - 1) // cols) + 1) * BLK
-
-    wide_rows = 0
-    left_rows = BLK
-    for item, chunks in parts:
-        if len(item.shape) == 2:
-            cols = item.shape[1] // LANES
-            size = min(window(cols), item.shape[0])
-            left_rows = max(left_rows, len(chunks) * size)
-            wide_rows = max(wide_rows, len(chunks) * size * cols)
-
-    def kernel(seg_ref, *refs):
-        left = dict(zip(names, refs[: len(names)]))
-        right = dict(zip(names, refs[len(names) : 2 * len(names)]))
-        vector = dict(zip(vector_names, refs[2 * len(names) : 2 * len(names) + len(vector_names)]))
-        out_ref, gathered, wide = refs[2 * len(names) + len(vector_names) :]
-        low_slot = seg_ref[0] * seg_blocks
+class CrossPack:
+    def __init__(self, geo, span, depth_rows):
+        self.geo, self.span = geo, span
+        self.parts = bucket_parts(geo, span)
+        self.seg_blocks = geo.n_doc * geo.piece_blocks
+        wide_rows, flat_cols, left_rows = BLK, D, BLK
+        for item, chunks in self.parts:
+            if item.cols:
+                left_rows = max(left_rows, len(chunks) * self.window(item))
+                wide_rows = max(wide_rows, BLK * item.cols)
+                flat_cols = max(flat_cols, item.shape[1])
+            else:
+                wide_rows = max(wide_rows, ceil_to(item.rows, BLK))
+        self.out = jax.ShapeDtypeStruct((len(span), geo.share, LANES), jnp.bfloat16)
+        self.scratch = [
+            pltpu.VMEM((left_rows, depth_rows), jnp.bfloat16),
+            pltpu.VMEM((left_rows, flat_cols), jnp.bfloat16),
+            pltpu.VMEM((wide_rows + 2 * BLK, LANES), jnp.float32),
+        ]
+
+    def window(self, item):
+        return min((-(-(self.seg_blocks - 1) // item.cols) + 1) * BLK, item.shape[0])
+
+    def run(self, seg, lefts, rights, sums_ref, first_rows, out_ref, gathered, flat, wide):
+        geo, span, seg_blocks = self.geo, self.span, self.seg_blocks
+        low_slot = seg * seg_blocks
         out_ref[...] = jnp.zeros_like(out_ref)
-        for item, chunks in parts:
-            starts, size, cols = [], 0, 1
-            if len(item.shape) == 2:
-                cols = item.shape[1] // LANES
-                size = min(window(cols), item.shape[0])
-                for at, (n, b0, b1, slot) in enumerate(chunks):
-                    first = jnp.maximum(low_slot, slot) - slot + b0
-                    start = jnp.clip(first // cols * BLK, 0, item.shape[0] - size)
-                    start = pl.multiple_of(start, BLK)
-                    starts.append(start)
-                    gathered[at * size : (at + 1) * size, :] = left[item.name][pl.ds(start, size), :]
-                count = len(chunks) * size
-                rows = gathered[:count, :]
-                for cb in range(0, cols, 2):
-                    tile = dot_nn(rows, right[item.name][:, cb * LANES : (cb + 2) * LANES])
-                    wide[pl.ds(cb, count, stride=cols), :] = tile[:, :LANES]
-                    wide[pl.ds(cb + 1, count, stride=cols), :] = tile[:, LANES:]
-            else:
-                vector_rows(wide, vector[item.name], vectors[item.name][1], item.rows)
+
+        def slots(lo, hi):
+            begin = jnp.maximum(low_slot, lo)
+            return begin, jnp.maximum(begin, jnp.minimum(low_slot + seg_blocks, hi))
+
+        def rows_out(n, slot, block, rows):
+            begin, end = slots(slot, slot + rows)
+
+            def move(t, carry):
+                data = wide[block_at(block + t - slot), :]
+                out_ref[n - span.start, block_at(t - low_slot), :] = data.astype(jnp.bfloat16)
+                return carry
+
+            lax.fori_loop(begin, end, move, 0)
+
+        for item, chunks in self.parts:
+            if not item.cols:
+                vector_rows(wide, sums_ref, first_rows[item.name], item.rows)
+                for n, b0, b1, slot in chunks:
+                    rows_out(n, slot, b0, b1 - b0)
+                continue
+            cols = item.cols
+            size = self.window(item)
+            starts = []
             for at, (n, b0, b1, slot) in enumerate(chunks):
-                begin = jnp.maximum(low_slot, slot)
-                end = jnp.minimum(low_slot + seg_blocks, slot + b1 - b0)
-                base = (at * size - starts[at]) * cols if starts else 0
-
-                first, last = geo.full_groups(item, n) if starts else (0, 0)
-
-                def by_row(t, carry, n=n, b0=b0, slot=slot, base=base):
-                    src = pl.ds((b0 + t - slot) * BLK + base, BLK)
-                    dst = pl.ds(pl.multiple_of((t - low_slot) * BLK, BLK), BLK)
-                    out_ref[n - span.start, dst, :] = wide[src, :].astype(jnp.bfloat16)
+                first = jnp.maximum(low_slot, slot) - slot + b0
+                start = pl.multiple_of(jnp.clip(first // cols * BLK, 0, item.shape[0] - size), BLK)
+                starts.append(start)
+                gathered[at * size : (at + 1) * size, :] = lefts[item.name][pl.ds(start, size), :]
+            count = len(chunks) * size
+            rows = gathered[:count, :]
+            for cb in range(0, cols, 2):
+                here = slice(cb * LANES, (cb + 2) * LANES)
+                flat[:count, here] = dot_nn(rows, rights[item.name][:, here]).astype(jnp.bfloat16)
+            for at, (n, b0, b1, slot) in enumerate(chunks):
+                first, last = geo.full_groups(item, n)
+                base = at * size - starts[at]
+
+                def group_rows(group, base=base):
+                    return pl.ds(pl.multiple_of(base + group * BLK, BLK), BLK)
+
+                def by_tile(t, carry, n=n, shift=b0 - slot, group_rows=group_rows, cols=cols):
+                    b = t + shift
+                    group = b // cols
+                    lanes = pl.ds(pl.multiple_of((b - group * cols) * LANES, LANES), LANES)
+                    out_ref[n - span.start, block_at(t - low_slot), :] = flat[group_rows(group), lanes]
                     return carry
 
-                def by_tile(t, carry, n=n, b0=b0, slot=slot, base=base, cols=cols):
-                    b = b0 + t - slot
-                    group = b // cols
-                    src = pl.ds(group * BLK * cols + b - group * cols + base, BLK, stride=cols)
-                    dst = pl.ds(pl.multiple_of((t - low_slot) * BLK, BLK), BLK)
-                    out_ref[n - span.start, dst, :] = wide[src, :].astype(jnp.bfloat16)
-                    return carry
-
                 if first < last:
-                    lo = jnp.clip(slot + first * cols - b0, begin, jnp.maximum(begin, end))
-                    hi = jnp.clip(slot + last * cols - b0, begin, jnp.maximum(begin, end))
-                    lax.fori_loop(begin, lo, by_row, 0)
-                    lax.fori_loop(lo, hi, by_tile, 0)
-                    lax.fori_loop(hi, jnp.maximum(hi, end), by_row, 0)
-                else:
-                    lax.fori_loop(begin, jnp.maximum(begin, end), by_row, 0)
-
-    operands = [lefts[n] for n in names] + [rights[n] for n in names]
-    operands += [vectors[n][0] for n in vector_names]
-    return ordered(
-        kernel,
-        out_shape=jax.ShapeDtypeStruct((len(span), seg_blocks * BLK, LANES), jnp.bfloat16),
-        in_specs=[spec_smem()] + [spec_vmem()] * len(operands),
-        out_specs=spec_vmem(),
-        scratch_shapes=[
-            pltpu.VMEM((left_rows, depth_rows), jnp.bfloat16),
-            pltpu.VMEM((wide_rows + 2 * BLK, LANES), jnp.float32),
-        ],
-        compiler_params=kernel_params(),
-        cost_estimate=cost(12),
-    )(seg, *operands)
+                    begin, end = slots(slot + first * cols - b0, slot + last * cols - b0)
+                    lax.fori_loop(begin, end, by_tile, 0)
+                for g in range(b0 // cols, -(-b1 // cols)):
+                    if first <= g < last:
+                        continue
+                    lo, hi = max(b0, g * cols), min(b1, (g + 1) * cols)
+                    begin, end = slots(slot + lo - b0, slot + hi - b0)
+
+                    @pl.when(begin < end)
+                    def _(g=g, lo=lo, hi=hi, n=n, shift=slot - b0, group_rows=group_rows, cols=cols):
+                        for cb in range(cols):
+                            tile = flat[group_rows(g), cb * LANES : (cb + 1) * LANES]
+                            wide[pl.ds(cb, BLK, stride=cols), :] = tile.astype(jnp.float32)
+                        rows_out(n, lo + shift, lo - g * cols, hi - lo)
 TILE = 512
 PAIRS = HEADS // 2
 TAIL_RATE = 0.3
@@ -900,7 +896,7 @@
     lax.fori_loop(0, TILE // SEG_LEN, segment, 0)
 
 
-def in_parts(kernel, micros, count, inputs, in_specs, outs, out_specs, scratch, previous):
+def in_parts(kernel, micros, count, inputs, in_specs, outs, out_specs, scratch, previous, mib=60):
     previous = list(previous or ())
     return ordered(
         kernel,
@@ -910,7 +906,7 @@
         out_shape=outs,
         scratch_shapes=scratch,
         input_output_aliases={len(inputs) + i: i for i in range(len(previous))},
-        compiler_params=kernel_params(60),
+        compiler_params=kernel_params(mib),
         cost_estimate=cost(micros),
     )(*inputs, *previous)
 
@@ -956,7 +952,7 @@
     return ordered(
         kernel,
         grid=(1,),
-        in_specs=[spec_smem()] + [spec_any()] * count + [tiles(D)],
+        in_specs=[spec_smem()] + [spec_hbm()] * count + [tiles(D)],
         out_specs=[tiles(3 * D), tiles(D), tiles(LANES)] + whole,
         out_shape=[
             jax.ShapeDtypeStruct((n, 3 * D), bf),
@@ -1061,7 +1057,7 @@
     return ordered(
         kernel,
         grid=(steps,),
-        in_specs=[spec_smem()] + [spec_any()] * count + [tiles(D), tiles(D)],
+        in_specs=[spec_smem()] + [spec_hbm()] * count + [tiles(D), tiles(D)],
         out_specs=[tiles(D), tiles(D), tiles(FF), tiles(FF), tiles(D), tiles(LANES), tiles(D)]
         + [pl.BlockSpec((n // SEG_LEN, D), lambda i: (0, 0))]
         + [spec_any()] * 3
@@ -1318,25 +1314,42 @@
     grows_ref[...] = low(res_ref[...])
 
 
-def cross_layer(cls, places, tags, grad_out, weights, coords):
+def cross_layer(cls, places, tags, grad_out, weights, coords, pack, seg):
     m = cls.shape[0]
     bf, f32 = jnp.bfloat16, jnp.float32
     tagc = jnp.broadcast_to(tags.astype(f32)[:, None], (m, LANES))
     tagr = jnp.broadcast_to(tags.astype(f32)[None, :], (8, m))
+    placer = jnp.broadcast_to(places.astype(f32)[None, :], (8, m))
     count = len(weights.operands)
-    operands = [cls, tagc, tagr, grad_out]
-    shapes = [(m, D), (m, D), (VECTOR_ROWS, D), (m, 3 * D), (m, D), (m, FF), (m, D), (D, m), (D, m), (D, m), (FF, m)]
+    operands = [cls, tagc, tagr, grad_out, placer]
+    shapes = [
+        (VECTOR_ROWS, D), (m, 3 * D), (m, D), (m, FF), (m, D), (D, m), (D, m), (D, m), (FF, m),
+    ]
     matrices = [number for number, item in enumerate(weights.items) if item.cols]
     vectors = [number for number, item in enumerate(weights.items) if not item.cols]
     needs = [(matrices[:1], vectors[:1]), (matrices[1:2], vectors[1:2]), (matrices[2:], vectors[2:])]
-
-    def kernel(coords_ref, *refs):
-        sources, refs = refs[:count], refs[count:]
-        ins, outs = refs[: len(operands)], refs[len(operands) : len(operands) + len(shapes)]
-        held, vec_ref, refs = refs[-8:-4], refs[-4], (refs[len(operands) + len(shapes) : -8], refs[-3:])
-        scratch, (staged, wide, sems) = refs
+    rows_of = {number: row for number, row in zip(vectors, (0, 2, 5, 9))}
+    inner = [
+        pltpu.VMEM((m, 3 * D), bf),
+        pltpu.VMEM((PAIRS, 2 * m, m), f32),
+        pltpu.VMEM((m, D), bf),
+        pltpu.VMEM((m, D), bf),
+        pltpu.VMEM((m, FF), f32),
+        pltpu.VMEM((m, D), f32),
+    ]
+    held_shapes = [pltpu.VMEM(weights.items[number].shape, bf) for number in matrices]
+
+    def kernel(seg_ref, coords_ref, *refs):
+        refs = list(refs)
+
+        def take(n):
+            taken, refs[:] = refs[:n], refs[n:]
+            return taken
+
+        sources, ins, outs = take(count), take(len(operands)), take(3)
+        kept, scratch, held = take(len(shapes)), take(len(inner)), take(len(matrices))
+        (vec_ref, hot_ref), (staged, wide, sems), packing = take(2), take(3), take(3)
         waited = set()
-        rows_of = {number: row for number, row in zip(vectors, (0, 2, 5, 9))}
         weights.start(coords_ref, sources, staged, sems)
 
         def load(stage):
@@ -1348,27 +1361,35 @@
                 weights.vectors(number, staged, wide, vec_ref, rows_of[number])
 
         vec_ref[...] = jnp.zeros_like(vec_ref)
-        cross_kernel(load, *ins, *held, vec_ref, *outs, *scratch)
+        cross_kernel(load, *ins[:4], *held, vec_ref, *outs[:2], *kept, *scratch)
+        places_at = lax.broadcasted_iota(jnp.int32, (LONG_SEGS, m), 0).astype(f32)
+        hot_ref[...] = jnp.where(places_at == ins[4][0:1, :], 1.0, 0.0).astype(bf)
+        sums_ref, gqkv, go, gu, gm, rows_t, att_t, hid_t, act_t = kept
+        names = [item_name(i) for i in (8, 9, 11, 13, 15)]
+        pack.run(
+            seg_ref[0],
+            dict(zip(names, (hot_ref, rows_t, att_t, hid_t, act_t))),
+            dict(zip(names, (outs[1], gqkv, go, gu, gm))),
+            sums_ref,
+            {item_name(i): row for i, row in ((10, 0), (12, 2), (14, 5), (16, 9))},
+            outs[2],
+            *packing,
+        )
 
     return ordered(
         kernel,
-        out_shape=[jax.ShapeDtypeStruct(shape, f32 if i == 2 else bf) for i, shape in enumerate(shapes)],
-        in_specs=[spec_smem()] + [spec_any()] * count + [spec_vmem()] * len(operands),
-        out_specs=[spec_vmem()] * len(shapes),
-        scratch_shapes=[
-            pltpu.VMEM((m, 3 * D), bf),
-            pltpu.VMEM((PAIRS, 2 * m, m), f32),
-            pltpu.VMEM((m, D), bf),
-            pltpu.VMEM((m, D), bf),
-            pltpu.VMEM((m, FF), f32),
-            pltpu.VMEM((m, D), f32),
-        ]
-        + [pltpu.VMEM(weights.items[number].shape, bf) for number in matrices]
-        + [pltpu.VMEM((VECTOR_ROWS, D), f32)]
-        + weights.scratch,
+        out_shape=[jax.ShapeDtypeStruct((m, D), bf)] * 2 + [pack.out],
+        in_specs=[spec_smem()] * 2 + [spec_hbm()] * count + [spec_vmem()] * len(operands),
+        out_specs=[spec_vmem()] * 3,
+        scratch_shapes=[pltpu.VMEM(shape, f32 if i == 0 else bf) for i, shape in enumerate(shapes)]
+        + inner
+        + held_shapes
+        + [pltpu.VMEM((VECTOR_ROWS, D), f32), pltpu.VMEM((LONG_SEGS, m), bf)]
+        + weights.scratch
+        + pack.scratch,
         compiler_params=kernel_params(62),
-        cost_estimate=cost(22),
-    )(coords, *weights.operands, *operands)
+        cost_estimate=cost(30),
+    )(seg, coords, *weights.operands, *operands)
 
 
 def class_rows(cls, cot, hot, doc, pos, weights, coords):
@@ -1398,7 +1419,7 @@
         kernel,
         grid=(1,),
         out_shape=jax.ShapeDtypeStruct((segs, 2 * D + LANES), jnp.bfloat16),
-        in_specs=[spec_smem()] + [spec_any()] * count
+        in_specs=[spec_smem()] + [spec_hbm()] * count
         + [whole(cls.shape), whole((segs, BLK, D)), whole(hot.shape), spec_smem(), spec_smem()],
         out_specs=whole((segs, 2 * D + LANES)),
         scratch_shapes=[
@@ -1406,7 +1427,7 @@
             pltpu.VMEM((LONG_SEGS, D), jnp.bfloat16),
         ]
         + weights.scratch,
-        compiler_params=kernel_params(),
+        compiler_params=kernel_params(60),
         cost_estimate=cost(3),
     )(coords, *weights.operands, cls, cot, hot, doc, pos)
 
@@ -1468,7 +1489,7 @@
         out_shape=shapes,
         in_specs=specs,
         out_specs=out_specs,
-        compiler_params=kernel_params(60),
+        compiler_params=kernel_params(24),
         cost_estimate=cost(micros),
     )(*arrays)
     return [value.reshape(shape) for value, (shape, _) in zip(results, outs)]
@@ -1553,7 +1574,7 @@
         out_shape=[jax.ShapeDtypeStruct((count, geo.share, LANES), jnp.bfloat16)] * nd,
         in_specs=[spec_smem()] + [spec_vmem()] * len(inputs),
         out_specs=[spec_vmem()] * nd,
-        compiler_params=kernel_params(60),
+        compiler_params=kernel_params(24),
         cost_estimate=cost(2),
     )(my_z.reshape(1), *inputs)
     return [outs[0]] + [send(geo, outs[r], Z, r) for r in range(1, nd)]
@@ -1656,6 +1677,7 @@
     ORDER.wait_for(*parts_b[2:3])
     plane = gather_plane(geo, plane, 1)
     gathered = [gather_cores(geo, plane), None, None]
+    plane_b = place_line(geo, parts_b, my_doc)
 
     def weights(*numbers):
         return Weights(geo, gather, gathered, [item_name(i) for i in numbers])
@@ -1663,7 +1685,6 @@
     def own(values):
         return lax.dynamic_slice_in_dim(values, my_seg * seg_count, seg_count, axis=0)
 
-    plane_b = place_line(geo, parts_b, my_doc)
     *outs, w_qkv, vec_a = attend_first(inputs, weights(0, 1), coords)
     plane_b = gather_plane(geo, plane_b, 0)
     gathered[2] = [lax.all_gather(gate(parts[2]), AXES)]
@@ -1681,18 +1702,9 @@
     mine = class_rows(cls, cot_rows, hot, seg_doc[0], seg_pos[0], weights(8), coords)
     tagged = lax.all_gather(mine, AXES[0], axis=0, tiled=True)
     rows, all_grad, all_doc, all_pos = tagged[:, :D], tagged[:, D : 2 * D], tagged[:, 2 * D], tagged[:, 2 * D + 1]
-    pos_hot = (all_pos.astype(jnp.int32)[:, None] == jnp.arange(LONG_SEGS)[None, :]).astype(jnp.bfloat16)
-    crossed, grad_rows, xsums, g_qkv, g_o, g_u, g_m, rows_t, att_t, hid_t, act_t = cross_layer(
-        rows, all_pos, all_doc, all_grad, weights(9, 10, 11, 12, 13, 14, 15, 16), coords
-    )
-    names = [item_name(i) for i in (8, 9, 11, 13, 15)]
-    line_c = pack_cross(
-        geo,
-        buckets.ranges[3],
-        dict(zip(names, (pos_hot.T, rows_t, att_t, hid_t, act_t))),
-        dict(zip(names, (grad_rows, g_qkv, g_o, g_u, g_m))),
-        {item_name(i): (xsums, row) for i, row in ((10, 0), (12, 2), (14, 5), (16, 9))},
-        my_seg.astype(jnp.int32).reshape(1),
+    crossed, grad_rows, line_c = cross_layer(
+        rows, all_pos, all_doc, all_grad, weights(9, 10, 11, 12, 13, 14, 15, 16), coords,
+        CrossPack(geo, buckets.ranges[3], n_rows), my_seg.astype(jnp.int32).reshape(1),
     )
     line_c = reduce_line(geo, [[line_c]], my_doc)
 

time: 605 us -> 562 us (0.929)
  Pallas kernels: 378 us -> 325 us
  local copies, waits for them, and re-layouts: 25.7 us -> 38.4 us
    pallas_call x37 -> x36, Pallas kernels: 378 us -> 325 us  [run(): pl.pallas_call(wrapped, out_shape=outs + [jax.ShapeDtypeStruct((8, LANES)...]
    unnamed x108 -> x130, local copies, waits for them, and re-layouts: 19 us -> 33.5 us
  transfers between devices with their start and end apart: 50 -> 50, of which waited for: 16 -> 14; matrix products, arithmetic and copies ran while one was open for 3% -> 3% of each run, Pallas kernels for 39% -> 39%
where the time goes in v6:
time: 562 us; the launch traced here: 552 us
  Pallas kernels  325 us (58%)
  waiting for transfers between devices  77.4 us (14%)
  starting transfers between devices  51.6 us (9%)
  local copies, waits for them, and re-layouts  38.4 us (7%)
  blocking collectives  31.1 us (6%)
  between operations  15.1 us (3%)
  other arithmetic  7.06 us (1%)
  matrix products  6.37 us (1%)
    pallas_call x36, Pallas kernels, run(): pl.pallas_call(wrapped, out_shape=outs + [jax.ShapeDtypeStruct((8, LANES)...  325 us
    ppermute x48, waiting for transfers between devices, send(): return lax.ppermute(value, AXES, geo.shift(axis, step))  68.2 us
    ppermute x48, starting transfers between devices, send(): return lax.ppermute(value, AXES, geo.shift(axis, step))  48 us
    unnamed x130, local copies, waits for them, and re-layouts  33.5 us
    all_to_all x1, blocking collectives, local(): lax.all_to_all(aligned.reshape(geo.n_seg, geo.share, LANES), AXES[0], 0,...  19.2 us
    all_gather x1, blocking collectives, local(): tagged = lax.all_gather(mine, AXES[0], axis=0, tiled=True)  11.9 us
  transfers between devices with their start and end apart: 50, of which 14 were waited for; matrix products, arithmetic and copies ran while one was open for 3% of the time, Pallas kernels for 39%

profile of v6, /device:TPU:0, one launch (start us, length us, event | category | flops | bytes accessed | tf_op | source)
XLA Modules:
  0.0 552.4 jit_solution(15155120424793746469)
XLA Ops:
  10.6 19.2 %all_to_all.10 = bf16[8,448,128]{2,1,0:T(8,128)(2,1)S(1)} all-to-all(bf16[8,448,128]{2,1,0:T(8,128)(2,1)S(1)} %bitcast.157), channel_id=1, replica_groups=mesh['seg'=8,'doc'=4] {'seg'}, dimensions={0} | all-to-all | bytes 1835008 | tf_op jit(solution)/shard_map/all_to_all | solution.py:1662
  29.8 3.6 collective-permute-start.5
  37.0 13.4 %collective-permute-done.4.refs_3_ = bf16[1,448,128]{2,1,0:T(8,128)(2,1)S(1)} collective-permute-done((bf16[1,448,128]{2,1,0:T(8,128)(2,1)S(1)}, bf16[1,448,128]{2,1,0:T(8,128)(2,1)S(1)}, u32[]{:S(2)}, u32[]{:S(2)}) %collective-permute-start.4) | collective-permute-done | bytes 114720 | tf_op jit(solution)/shard_map/ppermute | solution.py:1460
  51.9 5.4 collective-permute-done.6
  59.9 9.0 %collective-permute-done.1.refs_5_.refs_3_ = bf16[3,448,128]{2,1,0:T(8,128)(2,1)S(1)} collective-permute-done((bf16[3,448,128]{2,1,0:T(8,128)(2,1)S(1)}, bf16[3,448,128]{2,1,0:T(8,128)(2,1)S(1)}, u32[]{:S(2)}, u32[]{:S(2)}) %collective-permute-start.1) | collective-permute-done | bytes 344096 | tf_op jit(solution)/shard_map/ppermute | solution.py:1460
  73.5 8.3 %collective-permute-done.2.refs_4_ = bf16[3,448,128]{2,1,0:T(8,128)(2,1)S(1)} collective-permute-done((bf16[3,448,128]{2,1,0:T(8,128)(2,1)S(1)}, bf16[3,448,128]{2,1,0:T(8,128)(2,1)S(1)}, u32[]{:S(2)}, u32[]{:S(2)}) %collective-permute-start.2) | collective-permute-done | bytes 344096 | tf_op jit(solution)/shard_map/ppermute | solution.py:1460
  84.6 12.6 %shard_map.141 = (bf16[2048,2304]{1,0:T(8,128)(2,1)}, bf16[2048,768]{1,0:T(8,128)(2,1)}, f32[2048,128]{1,0:T(8,128)}, bf16[768,2304]{1,0:T(8,128)(2,1)}, f32[16,768]{1,0:T(8,128)}, /*index=5*/f32[8,128]{1,0:T(8,128)}) custom-call(s32[4]{0:T(128)} %pad_add_fusion.refs_0_.refs_1_, bf16[2,2,4,224,128]{4,3,2,1,0:T(8,128)(2,1)} %bitcast.23.refs_1_, ...), custom_call_target="tpu_custom_call" | custom-call | flops 12000000000 | bytes 36000000 | tf_op jit(solution)/shard_map/pallas_call | solution.py:226
  109.5 16.4 %shard_map.144 = (bf16[2048,2304]{1,0:T(8,128)(2,1)}, bf16[2048,768]{1,0:T(8,128)(2,1)}, f32[2048,128]{1,0:T(8,128)}, f32[8,128]{1,0:T(8,128)}) custom-call(bf16[2048,768]{1,0:T(8,128)(2,1)} %bitcast.202, bf16[768,2304]{1,0:T(8,128)(2,1)} %get-tuple-element.175.refs_1_.refs_2_, ...), custom_call_target="tpu_custom_call", output_to_operand_aliasing={{0}: (3, {}), {1}: (4, {}), {2}: (5, {})} | custom-call | flops 16000000000 | bytes 48000000 | tf_op jit(solution)/shard_map/pallas_call | solution.py:226
  126.0 15.2 %collective-permute-done.15 = bf16[2,12,224,128]{3,2,1,0:T(8,128)(2,1)} collective-permute-done((bf16[2,12,224,128]{3,2,1,0:T(8,128)(2,1)S(1)}, bf16[2,12,224,128]{3,2,1,0:T(8,128)(2,1)}, u32[]{:S(2)}, u32[]{:S(2)}) %collective-permute-start.15) | collective-permute-done | bytes 1376288 | tf_op jit(solution)/shard_map/ppermute | solution.py:1460
  146.9 4.2 shard_map.145
  153.2 9.4 %shard_map.146 = (bf16[2048,2304]{1,0:T(8,128)(2,1)}, bf16[2048,768]{1,0:T(8,128)(2,1)}, f32[2048,128]{1,0:T(8,128)}, f32[8,128]{1,0:T(8,128)}) custom-call(bf16[2048,768]{1,0:T(8,128)(2,1)} %bitcast.203, bf16[768,2304]{1,0:T(8,128)(2,1)} %get-tuple-element.175.refs_1_.refs_2_, ...), custom_call_target="tpu_custom_call", output_to_operand_aliasing={{0}: (3, {}), {1}: (4, {}), {2}: (5, {})} | custom-call | flops 8000000000 | bytes 24000000 | tf_op jit(solution)/shard_map/pallas_call | solution.py:226
  162.6 63.8 %shard_map.147 = (bf16[2048,768]{1,0:T(8,128)(2,1)}, bf16[2048,768]{1,0:T(8,128)(2,1)}, bf16[2048,3072]{1,0:T(8,128)(2,1)}, bf16[2048,3072]{1,0:T(8,128)(2,1)}, ...) custom-call(s32[4]{0:T(128)} %pad_add_fusion.refs_0_.refs_1_, ...), custom_call_target="tpu_custom_call" | custom-call | flops 60000002048 | bytes 180000000 | tf_op jit(solution)/shard_map/pallas_call | solution.py:226
  226.4 3.4 shard_map.148
  229.8 11.9 %all_gather.7 = bf16[128,1664]{1,0:T(8,128)(2,1)S(1)} all-gather(bf16[16,1664]{1,0:T(8,128)(2,1)} %get-tuple-element.192), channel_id=1, replica_groups=mesh['seg'=8,'doc'=4] {'seg'}, dimensions={0}, use_global_device_ids=true | all-gather | bytes 479232 | tf_op jit(solution)/shard_map/all_gather | solution.py:1703
  244.6 32.4 %shard_map.149 = (bf16[128,768]{1,0:T(8,128)(2,1)}, bf16[128,768]{1,0:T(8,128)(2,1)}, bf16[16,448,128]{2,1,0:T(8,128)(2,1)}, f32[8,128]{1,0:T(8,128)}) custom-call(s32[1]{0:T(128)} %bitcast.refs_0_, s32[4]{0:T(128)} %pad_add_fusion.refs_0_.refs_1_, bf16[32,4,448,128]{3,2,1,0:T(8,128)(2,1)} %all-gather.2.cloned.1.call-done.refs_5_.refs_2_, ...), custom_call_target="tpu_custom_call" | custom-call | flops 30000001024 | bytes 90000000 | tf_op jit(solution)/shard_map/pallas_call | solution.py:226
  280.2 3.4 collective-permute-start.19
  285.4 43.7 %shard_map.151 = (bf16[2048,768]{1,0:T(8,128)(2,1)}, bf16[2048,3072]{1,0:T(8,128)(2,1)}, bf16[2048,768]{1,0:T(8,128)(2,1)}, bf16[2048,768]{1,0:T(8,128)(2,1)}, f...) custom-call(bf16[2048,768]{1,0:T(8,128)(2,1)} %bitcast.196, f32[16,768]{1,0:T(8,128)} %get-tuple-element.310.refs_1_, ...), custom_call_target="tpu_custom_call" | custom-call | flops 44000002048 | bytes 132000000 | tf_op jit(solution)/shard_map/pallas_call | solution.py:226
  333.2 19.2 %shard_map.153 = (bf16[2,2,4,224,128]{4,3,2,1,0:T(8,128)(2,1)}, bf16[2,2,4,224,128]{4,3,2,1,0:T(8,128)(2,1)}, bf16[2,2,4,224,128]{4,3,2,1,0:T(8,128)(2,1)}, bf16...) custom-call(s32[4]{0:T(128)} %pad_add_fusion.refs_0_.refs_1_, ...), custom_call_target="tpu_custom_call" | custom-call | flops 17999998976 | bytes 54000000 | tf_op jit(solution)/shard_map/pallas_call | solution.py:226
  353.0 4.7 convolution_convert_fusion.refs_9_.refs_3_.refs_4_
  360.9 21.9 %shard_map.155 = (bf16[2,2,8,224,128]{4,3,2,1,0:T(8,128)(2,1)}, bf16[2,2,8,224,128]{4,3,2,1,0:T(8,128)(2,1)}, bf16[2,2,8,224,128]{4,3,2,1,0:T(8,128)(2,1)}, bf16[2,2,8,224,128]{4,3,2,1,0:T(8,128)(2,1)}, f32[8,128]{1,0:T(8,128)}) custom-call(s32[4]{0:T(128)} %pad_add_fusion.refs_0_.refs_1_, bf16[2048,768]{1,0:T(8,128)(2,1)} %get-tuple-element.212.refs_1_, ...), custom_call_target="tpu_custom_call" | custom-call | flops 17999998976 | bytes 54000000 | tf_op jit(solution)/shard_map/pallas_call | solution.py:226
  386.7 11.7 %shard_map.156 = (bf16[2048,2304]{1,0:T(8,128)(2,1)}, f32[8,768]{1,0:T(8,128)}, f32[8,128]{1,0:T(8,128)}) custom-call(bf16[2048,2304]{1,0:T(8,128)(2,1)} %get-tuple-element.209.refs_0_, f32[2048,128]{1,0:T(8,128)} %get-tuple-element.210.refs_1_, bf16[2048,768]{1,0:T(8,128)(2,1)} %get-tuple-element.211.refs_2_, f32[8,768]{1,0:T(8,128)} %broadcast_in_dim.47.refs_3_, ...), custom_call_target="tpu_custom_call" | custom-call | flops 10000000000 | bytes 30000000 | tf_op jit(solution)/shard_map/pallas_call | solution.py:226
  400.2 4.6 shard_map.157
  412.2 20.0 %shard_map.158 = (bf16[2048,2304]{1,0:T(8,128)(2,1)}, f32[8,768]{1,0:T(8,128)}, f32[8,128]{1,0:T(8,128)}) custom-call(bf16[2048,2304]{1,0:T(8,128)(2,1)} %get-tuple-element.209.refs_0_, f32[2048,128]{1,0:T(8,128)} %get-tuple-element.210.refs_1_, bf16[2048,768]{1,0:T(8,128)(2,1)} %get-tuple-element.211.refs_2_, ...), custom_call_target="tpu_custom_call", output_to_operand_aliasing={{0}: (4, {})} | custom-call | flops 20000000000 | bytes 60000000 | tf_op jit(solution)/shard_map/pallas_call | solution.py:226
  443.6 11.6 %shard_map.161 = (bf16[2048,2304]{1,0:T(8,128)(2,1)}, f32[8,768]{1,0:T(8,128)}, f32[8,128]{1,0:T(8,128)}) custom-call(bf16[2048,2304]{1,0:T(8,128)(2,1)} %get-tuple-element.209.refs_0_, f32[2048,128]{1,0:T(8,128)} %get-tuple-element.210.refs_1_, bf16[2048,768]{1,0:T(8,128)(2,1)} %get-tuple-element.211.refs_2_, ...), custom_call_target="tpu_custom_call", output_to_operand_aliasing={{0}: (4, {})} | custom-call | flops 10000000000 | bytes 30000000 | tf_op jit(solution)/shard_map/pallas_call | solution.py:226
  459.2 15.7 %shard_map.164 = (bf16[2,2,4,224,128]{4,3,2,1,0:T(8,128)(2,1)}, bf16[2,2,4,224,128]{4,3,2,1,0:T(8,128)(2,1)}, bf16[2,2,4,224,128]{4,3,2,1,0:T(8,128)(2,1)}, bf16[2,2,4,224,128]{4,3,2,1,0:T(8,128)(2,1)}, f32[8,128]{1,0:T(8,128)}) custom-call(s32[4]{0:T(128)} %pad_add_fusion.refs_0_.refs_1_, bf16[2048,768]{1,0:T(8,128)(2,1)} %bitcast.205, ...), custom_call_target="tpu_custom_call" | custom-call | flops 17999998976 | bytes 54000000 | tf_op jit(solution)/shard_map/pallas_call | solution.py:226
  486.1 13.2 %shard_map.166 = (bf16[2048,768]{1,0:T(8,128)(2,1)}, f32[8,128]{1,0:T(8,128)}) custom-call(f32[2048,768]{1,0:T(8,128)} %get-tuple-element.208.refs_0_, bf16[2048,2304]{1,0:T(8,128)(2,1)} %get-tuple-element.257.refs_2_.refs_1_, bf16[768,2304]{1,0:T(8,128)(2,1)} %get-tuple-element.175.refs_1_.refs_2_, f32[8,128]{1,0:T(8,128)} %copy-done.57), custom_call_target="tpu_custom_call" | custom-call | flops 12000000000 | bytes 36000000 | tf_op jit(solution)/shard_map/pallas_call | solution.py:226
  502.0 5.3 collective-permute-done.43.refs_2_
  512.5 3.0 collective-permute-done.45.refs_1_
  519.3 3.6 all-to-all-start.1
  523.7 4.0 broadcast_select_fusion
  527.6 9.2 %all-to-all-done.1 = bf16[8,448,128]{2,1,0:T(8,128)(2,1)S(1)} async-done(((bf16[8,448,128]{2,1,0:T(8,128)(2,1)}), bf16[8,448,128]{2,1,0:T(8,128)(2,1)S(1)}, u32[]{:S(2)}, u32[]{:S(2)}) %all-to-all-start.1) | async-done | bytes 917536 | tf_op jit(solution)/shard_map/all_to_all | solution.py:1752
  539.7 5.3 shard_map.171
  (259 shorter events, 108.8 us)
Async XLA Ops:
  7.2 219.2 %all-gather.2.cloned.1.call-start = ((), (), s32[]{:S(2)}) async-start(), calls=%async_computation.2 | async-start | bytes 15138816 | tf_op jit(solution)/shard_map/all_gather | solution.py:1690
  33.4 17.0 %collective-permute-start.4 = (bf16[1,448,128]{2,1,0:T(8,128)(2,1)S(1)}, bf16[1,448,128]{2,1,0:T(8,128)(2,1)S(1)}, u32[]{:S(2)}, u32[]{:S(2)}) collective-permute-start(bf16[1,448,128]{2,1,0:T(8,128)(2,1)S(1)} %slice.40.refs_1_), channel_id=1, source_target_pairs={{0,2},{1,3},{2,0},{3,1},{4,6},{5,7},{6,4},{7,5},{8,10},{9,11},{10,... | collective-permute-start | bytes 344072 | tf_op jit(solution)/shard_map/ppermute | solution.py:1460
  33.4 17.0 %collective-permute-start.3 = (bf16[1,448,128]{2,1,0:T(8,128)(2,1)S(1)}, bf16[1,448,128]{2,1,0:T(8,128)(2,1)S(1)}, u32[]{:S(2)}, u32[]{:S(2)}) collective-permute-start(bf16[1,448,128]{2,1,0:T(8,128)(2,1)S(1)} %slice.40.refs_1_), channel_id=1, source_target_pairs={{0,1},{1,2},{2,3},{3,0},{4,5},{5,6},{6,7},{7,4},{8,9},{9,10},{10,1... | collective-permute-start | bytes 344072 | tf_op jit(solution)/shard_map/ppermute | solution.py:1460
  34.4 17.5 %collective-permute-start = (bf16[3,448,128]{2,1,0:T(8,128)(2,1)S(1)}, bf16[3,448,128]{2,1,0:T(8,128)(2,1)S(1)}, u32[]{:S(2)}, u32[]{:S(2)}) collective-permute-start(bf16[3,448,128]{2,1,0:T(8,128)(2,1)S(1)} %slice.39.refs_1_), channel_id=1, source_target_pairs={{0,1},{1,2},{2,3},{3,0},{4,5},{5,6},{6,7},{7,4},{8,9},{9,10},{10,1... | collective-permute-start | bytes 1032200 | tf_op jit(solution)/shard_map/ppermute | solution.py:1460
  71.3 13.3 %collective-permute-start.12 = (bf16[2,2,4,224,128]{4,3,2,1,0:T(8,128)(2,1)}, bf16[2,2,4,224,128]{4,3,2,1,0:T(8,128)(2,1)}, u32[]{:S(2)}, u32[]{:S(2)}) collective-permute-start(bf16[2,2,4,224,128]{4,3,2,1,0:T(8,128)(2,1)} %bitcast.23.refs_1_), channel_id=1, source_target_pairs={{0,4},{1,5},{2,6},{3,7},{4,0},{5,1},{6,2},{7,3},{8,12},{9,13},{10,... | collective-permute-start | bytes 2752520 | tf_op jit(solution)/shard_map/ppermute | solution.py:1460
  71.3 13.3 %collective-permute-start.13 = (bf16[2,2,4,224,128]{4,3,2,1,0:T(8,128)(2,1)}, bf16[2,2,4,224,128]{4,3,2,1,0:T(8,128)(2,1)}, u32[]{:S(2)}, u32[]{:S(2)}) collective-permute-start(bf16[2,2,4,224,128]{4,3,2,1,0:T(8,128)(2,1)} %bitcast.24.refs_3_), channel_id=1, source_target_pairs={{0,4},{1,5},{2,6},{3,7},{4,0},{5,1},{6,2},{7,3},{8,12},{9,13},{10,... | collective-permute-start | bytes 2752520 | tf_op jit(solution)/shard_map/ppermute | solution.py:1460
  82.5 16.5 %collective-permute-start.10 = (bf16[12,224,128]{2,1,0:T(8,128)(2,1)S(1)}, bf16[12,224,128]{2,1,0:T(8,128)(2,1)S(1)}, u32[]{:S(2)}, u32[]{:S(2)}) collective-permute-start(bf16[12,224,128]{2,1,0:T(8,128)(2,1)S(1)} %get-tuple-element.165), channel_id=1, source_target_pairs={{0,8},{1,9},{2,10},{3,11},{4,12},{5,13},{6,14},{7,15},{8,0},{9,1},... | collective-permute-start | bytes 2064392 | tf_op jit(solution)/shard_map/ppermute | solution.py:1460
  83.2 16.6 %collective-permute-start.11 = (bf16[12,224,128]{2,1,0:T(8,128)(2,1)S(1)}, bf16[12,224,128]{2,1,0:T(8,128)(2,1)S(1)}, u32[]{:S(2)}, u32[]{:S(2)}) collective-permute-start(bf16[12,224,128]{2,1,0:T(8,128)(2,1)S(1)} %get-tuple-element.166), channel_id=1, source_target_pairs={{0,16},{1,17},{2,18},{3,19},{4,20},{5,21},{6,22},{7,23},{8,24},{9,... | collective-permute-start | bytes 2064392 | tf_op jit(solution)/shard_map/ppermute | solution.py:1460
  107.3 33.9 %collective-permute-start.15 = (bf16[2,12,224,128]{3,2,1,0:T(8,128)(2,1)S(1)}, bf16[2,12,224,128]{3,2,1,0:T(8,128)(2,1)}, u32[]{:S(2)}, u32[]{:S(2)}) collective-permute-start(bf16[2,12,224,128]{3,2,1,0:T(8,128)(2,1)S(1)} %bitcast.155), channel_id=1, source_target_pairs={{0,8},{1,9},{2,10},{3,11},{4,12},{5,13},{6,14},{7,15},{8,0},{9,1},... | collective-permute-start | bytes 4128776 | tf_op jit(solution)/shard_map/ppermute | solution.py:1460
  108.3 35.3 %collective-permute-start.14 = (bf16[2,12,224,128]{3,2,1,0:T(8,128)(2,1)S(1)}, bf16[2,12,224,128]{3,2,1,0:T(8,128)(2,1)}, u32[]{:S(2)}, u32[]{:S(2)}) collective-permute-start(bf16[2,12,224,128]{3,2,1,0:T(8,128)(2,1)S(1)} %bitcast.153), channel_id=1, source_target_pairs={{0,16},{1,17},{2,18},{3,19},{4,20},{5,21},{6,22},{7,23},{8,24},{9,... | collective-permute-start | bytes 4128776 | tf_op jit(solution)/shard_map/ppermute | solution.py:1460
  280.1 50.7 %collective-permute-start.18 = (bf16[4,448,128]{2,1,0:T(8,128)(2,1)S(1)}, bf16[4,448,128]{2,1,0:T(8,128)(2,1)S(1)}, u32[]{:S(2)}, u32[]{:S(2)}) collective-permute-start(bf16[4,448,128]{2,1,0:T(8,128)(2,1)S(1)} %get-tuple-element.219), channel_id=1, source_target_pairs={{0,1},{1,2},{2,3},{3,0},{4,5},{5,6},{6,7},{7,4},{8,9},{9,10},{10,1... | collective-permute-start | bytes 1376264 | tf_op jit(solution)/shard_map/ppermute | solution.py:1460
  280.2 50.7 %collective-permute-start.19 = (bf16[4,448,128]{2,1,0:T(8,128)(2,1)S(1)}, bf16[4,448,128]{2,1,0:T(8,128)(2,1)S(1)}, u32[]{:S(2)}, u32[]{:S(2)}) collective-permute-start(bf16[4,448,128]{2,1,0:T(8,128)(2,1)S(1)} %get-tuple-element.220), channel_id=1, source_target_pairs={{0,2},{1,3},{2,0},{3,1},{4,6},{5,7},{6,4},{7,5},{8,10},{9,11},{10,... | collective-permute-start | bytes 1376264 | tf_op jit(solution)/shard_map/ppermute | solution.py:1460
  283.5 47.3 %collective-permute-start.20 = (bf16[4,448,128]{2,1,0:T(8,128)(2,1)S(1)}, bf16[4,448,128]{2,1,0:T(8,128)(2,1)S(1)}, u32[]{:S(2)}, u32[]{:S(2)}) collective-permute-start(bf16[4,448,128]{2,1,0:T(8,128)(2,1)S(1)} %get-tuple-element.221), channel_id=1, source_target_pairs={{0,3},{1,0},{2,1},{3,2},{4,7},{5,4},{6,5},{7,6},{8,11},{9,8},{10,9... | collective-permute-start | bytes 1376264 | tf_op jit(solution)/shard_map/ppermute | solution.py:1460
  382.9 15.6 %collective-permute-start.25 = (bf16[2,2,8,224,128]{4,3,2,1,0:T(8,128)(2,1)}, bf16[2,2,8,224,128]{4,3,2,1,0:T(8,128)(2,1)}, u32[]{:S(2)}, u32[]{:S(2)}) collective-permute-start(bf16[2,2,8,224,128]{4,3,2,1,0:T(8,128)(2,1)} %get-tuple-element.239), channel_id=1, source_target_pairs={{0,4},{1,5},{2,6},{3,7},{4,0},{5,1},{6,2},{7,3},{8,12},{9,13},{10,... | collective-permute-start | bytes 5505032 | tf_op jit(solution)/shard_map/ppermute | solution.py:1460
  383.3 15.1 %collective-permute-start.26 = (bf16[2,2,8,224,128]{4,3,2,1,0:T(8,128)(2,1)}, bf16[2,2,8,224,128]{4,3,2,1,0:T(8,128)(2,1)}, u32[]{:S(2)}, u32[]{:S(2)}) collective-permute-start(bf16[2,2,8,224,128]{4,3,2,1,0:T(8,128)(2,1)} %get-tuple-element.241), channel_id=1, source_target_pairs={{0,4},{1,5},{2,6},{3,7},{4,0},{5,1},{6,2},{7,3},{8,12},{9,13},{10,... | collective-permute-start | bytes 5505032 | tf_op jit(solution)/shard_map/ppermute | solution.py:1460
  383.4 15.0 %collective-permute-start.23 = (bf16[2,4,224,128]{3,2,1,0:T(8,128)(2,1)}, bf16[2,4,224,128]{3,2,1,0:T(8,128)(2,1)}, u32[]{:S(2)}, u32[]{:S(2)}) collective-permute-start(bf16[2,4,224,128]{3,2,1,0:T(8,128)(2,1)} %bitcast.49), channel_id=1, source_target_pairs={{0,16},{1,17},{2,18},{3,19},{4,20},{5,21},{6,22},{7,23},{8,24},{9,... | collective-permute-start | bytes 1376264 | tf_op jit(solution)/shard_map/ppermute | solution.py:1460
  384.8 13.6 %collective-permute-start.24 = (bf16[2,4,224,128]{3,2,1,0:T(8,128)(2,1)}, bf16[2,4,224,128]{3,2,1,0:T(8,128)(2,1)}, u32[]{:S(2)}, u32[]{:S(2)}) collective-permute-start(bf16[2,4,224,128]{3,2,1,0:T(8,128)(2,1)} %bitcast.52), channel_id=1, source_target_pairs={{0,8},{1,9},{2,10},{3,11},{4,12},{5,13},{6,14},{7,15},{8,0},{9,1},... | collective-permute-start | bytes 1376264 | tf_op jit(solution)/shard_map/ppermute | solution.py:1460
  408.1 24.1 %collective-permute-start.29 = (bf16[4,224,128]{2,1,0:T(8,128)(2,1)}, bf16[4,224,128]{2,1,0:T(8,128)(2,1)}, u32[]{:S(2)}, u32[]{:S(2)}) collective-permute-start(bf16[4,224,128]{2,1,0:T(8,128)(2,1)} %bitcast.65), channel_id=1, source_target_pairs={{0,8},{1,9},{2,10},{3,11},{4,12},{5,13},{6,14},{7,15},{8,0},{9,1},... | collective-permute-start | bytes 688136 | tf_op jit(solution)/shard_map/ppermute | solution.py:1460
  408.8 23.3 %collective-permute-start.30 = (bf16[4,224,128]{2,1,0:T(8,128)(2,1)}, bf16[4,224,128]{2,1,0:T(8,128)(2,1)}, u32[]{:S(2)}, u32[]{:S(2)}) collective-permute-start(bf16[4,224,128]{2,1,0:T(8,128)(2,1)} %bitcast.67), channel_id=1, source_target_pairs={{0,16},{1,17},{2,18},{3,19},{4,20},{5,21},{6,22},{7,23},{8,24},{9,... | collective-permute-start | bytes 688136 | tf_op jit(solution)/shard_map/ppermute | solution.py:1460
  409.5 30.1 %collective-permute-start.27 = (bf16[2,8,224,128]{3,2,1,0:T(8,128)(2,1)}, bf16[2,8,224,128]{3,2,1,0:T(8,128)(2,1)S(1)}, u32[]{:S(2)}, u32[]{:S(2)}) collective-permute-start(bf16[2,8,224,128]{3,2,1,0:T(8,128)(2,1)} %bitcast.59), channel_id=1, source_target_pairs={{0,16},{1,17},{2,18},{3,19},{4,20},{5,21},{6,22},{7,23},{8,24},{9,... | collective-permute-start | bytes 2752520 | tf_op jit(solution)/shard_map/ppermute | solution.py:1460
  410.9 28.7 %collective-permute-start.28 = (bf16[2,8,224,128]{3,2,1,0:T(8,128)(2,1)}, bf16[2,8,224,128]{3,2,1,0:T(8,128)(2,1)S(1)}, u32[]{:S(2)}, u32[]{:S(2)}) collective-permute-start(bf16[2,8,224,128]{3,2,1,0:T(8,128)(2,1)} %bitcast.62), channel_id=1, source_target_pairs={{0,8},{1,9},{2,10},{3,11},{4,12},{5,13},{6,14},{7,15},{8,0},{9,1},... | collective-permute-start | bytes 2752520 | tf_op jit(solution)/shard_map/ppermute | solution.py:1460
  434.7 20.6 %collective-permute-start.33 = (bf16[1,448,128]{2,1,0:T(8,128)(2,1)}, bf16[1,448,128]{2,1,0:T(8,128)(2,1)}, u32[]{:S(2)}, u32[]{:S(2)}) collective-permute-start(bf16[1,448,128]{2,1,0:T(8,128)(2,1)} %get-tuple-element.264), channel_id=1, source_target_pairs={{0,1},{1,2},{2,3},{3,0},{4,5},{5,6},{6,7},{7,4},{8,9},{9,10},{10,1... | collective-permute-start | bytes 344072 | tf_op jit(solution)/shard_map/ppermute | solution.py:1460
  436.2 19.0 %collective-permute-start.34 = (bf16[1,448,128]{2,1,0:T(8,128)(2,1)}, bf16[1,448,128]{2,1,0:T(8,128)(2,1)}, u32[]{:S(2)}, u32[]{:S(2)}) collective-permute-start(bf16[1,448,128]{2,1,0:T(8,128)(2,1)} %get-tuple-element.265), channel_id=1, source_target_pairs={{0,2},{1,3},{2,0},{3,1},{4,6},{5,7},{6,4},{7,5},{8,10},{9,11},{10,... | collective-permute-start | bytes 344072 | tf_op jit(solution)/shard_map/ppermute | solution.py:1460
  436.7 18.5 %collective-permute-start.35 = (bf16[1,448,128]{2,1,0:T(8,128)(2,1)}, bf16[1,448,128]{2,1,0:T(8,128)(2,1)}, u32[]{:S(2)}, u32[]{:S(2)}) collective-permute-start(bf16[1,448,128]{2,1,0:T(8,128)(2,1)} %get-tuple-element.266), channel_id=1, source_target_pairs={{0,3},{1,0},{2,1},{3,2},{4,7},{5,4},{6,5},{7,6},{8,11},{9,8},{10,9... | collective-permute-start | bytes 344072 | tf_op jit(solution)/shard_map/ppermute | solution.py:1460
  442.2 15.4 %collective-permute-start.31 = (bf16[8,224,128]{2,1,0:T(8,128)(2,1)}, bf16[8,224,128]{2,1,0:T(8,128)(2,1)S(1)}, u32[]{:S(2)}, u32[]{:S(2)}) collective-permute-start(bf16[8,224,128]{2,1,0:T(8,128)(2,1)} %bitcast.69), channel_id=1, source_target_pairs={{0,8},{1,9},{2,10},{3,11},{4,12},{5,13},{6,14},{7,15},{8,0},{9,1},... | collective-permute-start | bytes 1376264 | tf_op jit(solution)/shard_map/ppermute | solution.py:1460
  443.0 14.6 %collective-permute-start.32 = (bf16[8,224,128]{2,1,0:T(8,128)(2,1)}, bf16[8,224,128]{2,1,0:T(8,128)(2,1)S(1)}, u32[]{:S(2)}, u32[]{:S(2)}) collective-permute-start(bf16[8,224,128]{2,1,0:T(8,128)(2,1)} %bitcast.71), channel_id=1, source_target_pairs={{0,16},{1,17},{2,18},{3,19},{4,20},{5,21},{6,22},{7,23},{8,24},{9,... | collective-permute-start | bytes 1376264 | tf_op jit(solution)/shard_map/ppermute | solution.py:1460
  475.5 23.8 %collective-permute-start.40 = (bf16[2,448,128]{2,1,0:T(8,128)(2,1)}, bf16[2,448,128]{2,1,0:T(8,128)(2,1)S(1)}, u32[]{:S(2)}, u32[]{:S(2)}) collective-permute-start(bf16[2,448,128]{2,1,0:T(8,128)(2,1)} %get-tuple-element.282), channel_id=1, source_target_pairs={{0,1},{1,2},{2,3},{3,0},{4,5},{5,6},{6,7},{7,4},{8,9},{9,10},{10,1... | collective-permute-start | bytes 688136 | tf_op jit(solution)/shard_map/ppermute | solution.py:1460
  475.5 23.8 %collective-permute-start.41 = (bf16[2,448,128]{2,1,0:T(8,128)(2,1)}, bf16[2,448,128]{2,1,0:T(8,128)(2,1)S(1)}, u32[]{:S(2)}, u32[]{:S(2)}) collective-permute-start(bf16[2,448,128]{2,1,0:T(8,128)(2,1)} %get-tuple-element.283), channel_id=1, source_target_pairs={{0,2},{1,3},{2,0},{3,1},{4,6},{5,7},{6,4},{7,5},{8,10},{9,11},{10,... | collective-permute-start | bytes 688136 | tf_op jit(solution)/shard_map/ppermute | solution.py:1460
  477.1 22.2 %collective-permute-start.42 = (bf16[2,448,128]{2,1,0:T(8,128)(2,1)}, bf16[2,448,128]{2,1,0:T(8,128)(2,1)S(1)}, u32[]{:S(2)}, u32[]{:S(2)}) collective-permute-start(bf16[2,448,128]{2,1,0:T(8,128)(2,1)} %get-tuple-element.284), channel_id=1, source_target_pairs={{0,3},{1,0},{2,1},{3,2},{4,7},{5,4},{6,5},{7,6},{8,11},{9,8},{10,9... | collective-permute-start | bytes 688136 | tf_op jit(solution)/shard_map/ppermute | solution.py:1460
  483.4 16.8 %collective-permute-start.38 = (bf16[2,4,224,128]{3,2,1,0:T(8,128)(2,1)S(1)}, bf16[2,4,224,128]{3,2,1,0:T(8,128)(2,1)S(1)}, u32[]{:S(2)}, u32[]{:S(2)}) collective-permute-start(bf16[2,4,224,128]{3,2,1,0:T(8,128)(2,1)S(1)} %bitcast.191), channel_id=1, source_target_pairs={{0,16},{1,17},{2,18},{3,19},{4,20},{5,21},{6,22},{7,23},{8,24},{9,... | collective-permute-start | bytes 1376264 | tf_op jit(solution)/shard_map/ppermute | solution.py:1460
  484.8 15.4 %collective-permute-start.39 = (bf16[2,4,224,128]{3,2,1,0:T(8,128)(2,1)S(1)}, bf16[2,4,224,128]{3,2,1,0:T(8,128)(2,1)S(1)}, u32[]{:S(2)}, u32[]{:S(2)}) collective-permute-start(bf16[2,4,224,128]{3,2,1,0:T(8,128)(2,1)S(1)} %bitcast.190), channel_id=1, source_target_pairs={{0,8},{1,9},{2,10},{3,11},{4,12},{5,13},{6,14},{7,15},{8,0},{9,1},... | collective-permute-start | bytes 1376264 | tf_op jit(solution)/shard_map/ppermute | solution.py:1460
  519.3 17.5 %all-to-all-start.1 = ((bf16[8,448,128]{2,1,0:T(8,128)(2,1)}), bf16[8,448,128]{2,1,0:T(8,128)(2,1)S(1)}, u32[]{:S(2)}, u32[]{:S(2)}) async-start(bf16[8,448,128]{2,1,0:T(8,128)(2,1)} %get-tuple-element.300), calls=%async_computation.1 | async-start | bytes 1835008 | tf_op jit(solution)/shard_map/all_to_all | solution.py:1752
  (83 other events, 614.2 us)
Sparse Core Ops, SparseCore 0:
  107.5 108.6 all-gather.1

commit v7 on v6

--- a/solution.py
+++ b/solution.py
@@ -784,18 +784,6 @@
                         rows_out(n, lo + shift, lo - g * cols, hi - lo)
 TILE = 512
 PAIRS = HEADS // 2
-TAIL_RATE = 0.3
-TAIL = (
-    0.11962929605681312,
-    0.12075400207853171,
-    0.0999131861559567,
-    0.12856268365589474,
-    -0.05368570534984477,
-    0.20635578836359286,
-    -0.15720441932045734,
-    0.0356750954846771,
-)
-
 
 def dot_nn(left, right):
     return lax.dot_general(left, right, (((1,), (0,)), ((), ())), preferred_element_type=jnp.float32)
@@ -814,14 +802,8 @@
 
 
 def gelu_pair(u):
-    t = 1.0 / (1.0 + TAIL_RATE * jnp.abs(u))
-    poly = TAIL[-1] * t + TAIL[-2]
-    for coef in TAIL[-3::-1]:
-        poly = poly * t + coef
-    bell = jnp.exp(-0.5 * (u * u))
-    tail = bell * (poly * t)
-    spread = jnp.where(u < 0.0, tail, 1.0 - tail)
-    return u * spread, spread + u * bell * (1.0 / math.sqrt(2.0 * math.pi))
+    spread = 0.5 + 0.5 * lax.erf(u * math.sqrt(0.5))
+    return u * spread, spread + u * jnp.exp(-0.5 * (u * u)) * (1.0 / math.sqrt(2.0 * math.pi))
 
 
 def norm_rows(values, gain, shift):
@@ -859,6 +841,18 @@
     return jnp.concatenate([stacked[:half], stacked[half:]], axis=1)
 
 
+def stacked_heads(values):
+    half = values.shape[1] // 2
+    return jnp.concatenate([values[:, :half], values[:, half:]], axis=0)
+
+
+STATS = 16
+
+
+def stat_tiles(first=0):
+    return pl.BlockSpec((TILE // SEG_LEN * STATS, LANES), lambda i: (i + first, 0))
+
+
 def third(part, pair):
     start = part * D + pair * LANES
     return slice(start, start + LANES)
@@ -870,30 +864,25 @@
         cols = slice(j * D, (j + 1) * D)
         part = dot_nn(x, wqkv_ref[:, cols])
         packed_ref[:, cols] = low(part if j == 1 else part + vec_ref[j // 2 : j // 2 + 1, :])
-    lanes = lax.broadcasted_iota(jnp.int32, (SEG_LEN, LANES), 1)
 
     def segment(s, carry):
         rows = pl.ds(pl.multiple_of(s * SEG_LEN, SEG_LEN), SEG_LEN)
-        stat = jnp.zeros((SEG_LEN, LANES), jnp.float32)
         for pair in range(PAIRS):
-            q = packed_ref[rows, third(0, pair)] * jnp.bfloat16(HEAD_DIM**-0.5)
-            k = packed_ref[rows, third(1, pair)]
-            v = packed_ref[rows, third(2, pair)]
-            scores = dot_nt(both_heads(q), k)
-            largest = jnp.max(scores, axis=-1, keepdims=True)
+            queries = both_heads(packed_ref[rows, third(0, pair)] * jnp.bfloat16(HEAD_DIM**-0.5))
+            values = both_heads(packed_ref[rows, third(2, pair)])
+            scores = dot_nt(packed_ref[rows, third(1, pair)], queries)
+            largest = jnp.max(scores, axis=0, keepdims=True)
             raised = jnp.exp(scores - largest)
-            summed = jnp.sum(raised, axis=-1, keepdims=True)
+            summed = jnp.sum(raised, axis=0, keepdims=True)
             weights = low(raised * (1.0 / summed))
-            att_ref[rows, pair * LANES : (pair + 1) * LANES] = low(
-                dot_nn(side_by_side(weights), both_heads(v))
-            )
+            att_ref[rows, pair * LANES : (pair + 1) * LANES] = low(dot_tn(stacked_heads(weights), values))
             log_sum = largest + jnp.log(summed)
-            stat = jnp.where(lanes == 2 * pair, log_sum[:SEG_LEN], stat)
-            stat = jnp.where(lanes == 2 * pair + 1, log_sum[SEG_LEN:], stat)
-        stat_ref[rows, :] = stat
+            for head in range(2):
+                row = pl.ds(s * STATS + 2 * pair + head, 1)
+                stat_ref[row, :] = log_sum[:, head * SEG_LEN : (head + 1) * SEG_LEN]
         return carry
 
-    lax.fori_loop(0, TILE // SEG_LEN, segment, 0)
+    lax.fori_loop(0, TILE // SEG_LEN, segment, 0, unroll=2)
 
 
 def in_parts(kernel, micros, count, inputs, in_specs, outs, out_specs, scratch, previous, mib=60):
@@ -925,7 +914,7 @@
         [x, w_qkv, vecs],
         [rows(D), fixed((D, 3 * D)), fixed((VECTOR_ROWS, D))],
         [jax.ShapeDtypeStruct(v.shape, v.dtype) for v in previous],
-        [rows(3 * D), rows(D), rows(LANES)],
+        [rows(3 * D), rows(D), stat_tiles(first)],
         [],
         previous,
     )
@@ -953,11 +942,11 @@
         kernel,
         grid=(1,),
         in_specs=[spec_smem()] + [spec_hbm()] * count + [tiles(D)],
-        out_specs=[tiles(3 * D), tiles(D), tiles(LANES)] + whole,
+        out_specs=[tiles(3 * D), tiles(D), stat_tiles()] + whole,
         out_shape=[
             jax.ShapeDtypeStruct((n, 3 * D), bf),
             jax.ShapeDtypeStruct((n, D), bf),
-            jax.ShapeDtypeStruct((n, LANES), f32),
+            jax.ShapeDtypeStruct((n // SEG_LEN * STATS, LANES), f32),
             jax.ShapeDtypeStruct((D, 3 * D), bf),
             jax.ShapeDtypeStruct((VECTOR_ROWS, D), f32),
         ],
@@ -1173,36 +1162,33 @@
     def _():
         sums_ref[...] = before_ref[...]
 
-    lanes = lax.broadcasted_iota(jnp.int32, (SEG_LEN, LANES), 1)
     scale = HEAD_DIM**-0.5
 
     def segment(s, carry):
         rows = pl.ds(pl.multiple_of(s * SEG_LEN, SEG_LEN), SEG_LEN)
-        stat = stat_ref[rows, :]
         for pair in range(PAIRS):
-            q = packed_ref[rows, third(0, pair)] * jnp.bfloat16(scale)
+            queries = both_heads(packed_ref[rows, third(0, pair)] * jnp.bfloat16(scale))
             k = packed_ref[rows, third(1, pair)]
-            v = packed_ref[rows, third(2, pair)]
-            da = da_ref[rows, pair * LANES : (pair + 1) * LANES]
-            queries, grads = both_heads(q), both_heads(da)
-            log_sum = jnp.concatenate([stat[:, 2 * pair : 2 * pair + 1], stat[:, 2 * pair + 1 : 2 * pair + 2]], axis=0)
-            weights = jnp.exp(dot_nt(queries, k) - log_sum)
-            grad_weights = dot_nt(grads, v)
-            dv = dot_tn(low(weights), grads)
-            inner = jnp.sum(grad_weights * weights, axis=-1, keepdims=True)
+            grads = both_heads(da_ref[rows, pair * LANES : (pair + 1) * LANES])
+            log_sum = jnp.concatenate(
+                [stat_ref[pl.ds(s * STATS + 2 * pair + head, 1), :] for head in range(2)], axis=1
+            )
+            weights = jnp.exp(dot_nt(k, queries) - log_sum)
+            grad_weights = dot_nt(packed_ref[rows, third(2, pair)], grads)
+            inner = jnp.sum(grad_weights * weights, axis=0, keepdims=True)
             ds = low(weights * (grad_weights - inner))
-            dq = dot_nn(side_by_side(ds), both_heads(k)) * scale
-            dk = dot_tn(ds, queries)
+            dv = dot_nn(low(weights), grads)
+            dk = dot_nn(ds, queries)
+            dq = dot_tn(stacked_heads(ds), both_heads(k)) * scale
             for part, grad in enumerate((dq, dk, dv)):
                 grad = low(grad)
-                cols = third(part, pair)
-                dqkv_ref[rows, cols] = grad
+                dqkv_ref[rows, third(part, pair)] = grad
                 if part != 1:
                     here = (slice(part // 2, part // 2 + 1), third(0, pair))
                     sums_ref[here] += jnp.sum(grad.astype(jnp.float32), axis=0, keepdims=True)
         return carry
 
-    lax.fori_loop(0, TILE // SEG_LEN, segment, 0)
+    lax.fori_loop(0, TILE // SEG_LEN, segment, 0, unroll=2)
 
 
 def attend_back(packed, stat, da, first, count, previous=None):
@@ -1213,7 +1199,7 @@
         10 * count,
         count,
         [packed, stat, da, before],
-        [tiles(3 * D, first), tiles(LANES, first), tiles(D, first), fixed((8, D))],
+        [tiles(3 * D, first), stat_tiles(first), tiles(D, first), fixed((8, D))],
         [jax.ShapeDtypeStruct((n, 3 * D), jnp.bfloat16), jax.ShapeDtypeStruct((8, D), jnp.float32)],
         [tiles(3 * D, first), pl.BlockSpec((8, D), lambda i: (0, 0))],
         [],

time: 562 us -> 542 us (0.964)
  Pallas kernels: 325 us -> 294 us
  waiting for transfers between devices: 77.4 us -> 90.7 us
    pallas_call x36, Pallas kernels: 325 us -> 294 us  [run(): pl.pallas_call(wrapped, out_shape=outs + [jax.ShapeDtypeStruct((8, LANES)...]
    all_gather x1, waiting for transfers between devices: 0.02 us -> 6.68 us  [local(): gathered[2] = [lax.all_gather(gate(parts[2]), AXES)]]
    ppermute x48, waiting for transfers between devices: 68.2 us -> 74.8 us  [send(): return lax.ppermute(value, AXES, geo.shift(axis, step))]
  transfers between devices with their start and end apart: 50 -> 50, of which waited for: 14 -> 18; matrix products, arithmetic and copies ran while one was open for 3% -> 3% of each run, Pallas kernels for 39% -> 34%
where the time goes in v7:
time: 542 us; the launch traced here: 533 us
  Pallas kernels  294 us (54%)
  waiting for transfers between devices  90.7 us (17%)
  starting transfers between devices  52.6 us (10%)
  local copies, waits for them, and re-layouts  38.3 us (7%)
  blocking collectives  28.9 us (5%)
  between operations  15.1 us (3%)
  other arithmetic  7.08 us (1%)
  matrix products  6.37 us (1%)
    pallas_call x36, Pallas kernels, run(): pl.pallas_call(wrapped, out_shape=outs + [jax.ShapeDtypeStruct((8, LANES)...  294 us
    ppermute x48, waiting for transfers between devices, send(): return lax.ppermute(value, AXES, geo.shift(axis, step))  74.8 us
    ppermute x48, starting transfers between devices, send(): return lax.ppermute(value, AXES, geo.shift(axis, step))  49.1 us
    unnamed x130, local copies, waits for them, and re-layouts  33.5 us
    all_to_all x1, blocking collectives, local(): lax.all_to_all(aligned.reshape(geo.n_seg, geo.share, LANES), AXES[0], 0,...  19.2 us
  transfers between devices with their start and end apart: 50, of which 18 were waited for; matrix products, arithmetic and copies ran while one was open for 3% of the time, Pallas kernels for 34%

profile of v7, /device:TPU:0, one launch (start us, length us, event | category | flops | bytes accessed | tf_op | source)
XLA Modules:
  0.0 532.6 jit_solution(17404912015668327190)
XLA Ops:
  10.6 19.2 %all_to_all.10 = bf16[8,448,128]{2,1,0:T(8,128)(2,1)S(1)} all-to-all(bf16[8,448,128]{2,1,0:T(8,128)(2,1)S(1)} %bitcast.157), channel_id=1, replica_groups=mesh['seg'=8,'doc'=4] {'seg'}, dimensions={0} | all-to-all | bytes 1835008 | tf_op jit(solution)/shard_map/all_to_all | solution.py:1648
  29.8 3.6 collective-permute-start.5
  37.0 13.4 %collective-permute-done.4.refs_3_ = bf16[1,448,128]{2,1,0:T(8,128)(2,1)S(1)} collective-permute-done((bf16[1,448,128]{2,1,0:T(8,128)(2,1)S(1)}, bf16[1,448,128]{2,1,0:T(8,128)(2,1)S(1)}, u32[]{:S(2)}, u32[]{:S(2)}) %collective-permute-start.4) | collective-permute-done | bytes 114720 | tf_op jit(solution)/shard_map/ppermute | solution.py:1446
  51.9 5.4 %collective-permute-done.6 = bf16[4,224,128]{2,1,0:T(8,128)(2,1)S(1)} collective-permute-done((bf16[4,224,128]{2,1,0:T(8,128)(2,1)S(1)}, bf16[4,224,128]{2,1,0:T(8,128)(2,1)S(1)}, u32[]{:S(2)}, u32[]{:S(2)}) %collective-permute-start.6) | collective-permute-done | bytes 229408 | tf_op jit(solution)/shard_map/ppermute | solution.py:1446
  59.9 9.0 %collective-permute-done.1.refs_5_.refs_3_ = bf16[3,448,128]{2,1,0:T(8,128)(2,1)S(1)} collective-permute-done((bf16[3,448,128]{2,1,0:T(8,128)(2,1)S(1)}, bf16[3,448,128]{2,1,0:T(8,128)(2,1)S(1)}, u32[]{:S(2)}, u32[]{:S(2)}) %collective-permute-start.1) | collective-permute-done | bytes 344096 | tf_op jit(solution)/shard_map/ppermute | solution.py:1446
  73.5 8.3 %collective-permute-done.2.refs_4_ = bf16[3,448,128]{2,1,0:T(8,128)(2,1)S(1)} collective-permute-done((bf16[3,448,128]{2,1,0:T(8,128)(2,1)S(1)}, bf16[3,448,128]{2,1,0:T(8,128)(2,1)S(1)}, u32[]{:S(2)}, u32[]{:S(2)}) %collective-permute-start.2) | collective-permute-done | bytes 344096 | tf_op jit(solution)/shard_map/ppermute | solution.py:1446
  84.6 10.6 %shard_map.141 = (bf16[2048,2304]{1,0:T(8,128)(2,1)}, bf16[2048,768]{1,0:T(8,128)(2,1)}, f32[256,128]{1,0:T(8,128)}, bf16[768,2304]{1,0:T(8,128)(2,1)}, f32[16,768]{1,0:T(8,128)}, /*index=5*/f32[8,128]{1,0:T(8,128)}) custom-call(s32[4]{0:T(128)} %pad_add_fusion.refs_0_.refs_1_, bf16[2,2,4,224,128]{4,3,2,1,0:T(8,128)(2,1)} %bitcast.23.refs_1_, ...), custom_call_target="tpu_custom_call" | custom-call | flops 12000000000 | bytes 36000000 | tf_op jit(solution)/shard_map/pallas_call | solution.py:226
  95.2 3.8 collective-permute-done.10
  109.5 12.5 %shard_map.144 = (bf16[2048,2304]{1,0:T(8,128)(2,1)}, bf16[2048,768]{1,0:T(8,128)(2,1)}, f32[256,128]{1,0:T(8,128)}, f32[8,128]{1,0:T(8,128)}) custom-call(bf16[2048,768]{1,0:T(8,128)(2,1)} %bitcast.202, bf16[768,2304]{1,0:T(8,128)(2,1)} %get-tuple-element.175.refs_1_.refs_2_, ...), custom_call_target="tpu_custom_call", output_to_operand_aliasing={{0}: (3, {}), {1}: (4, {}), {2}: (5, {})} | custom-call | flops 16000000000 | bytes 48000000 | tf_op jit(solution)/shard_map/pallas_call | solution.py:226
  122.1 19.1 %collective-permute-done.15 = bf16[2,12,224,128]{3,2,1,0:T(8,128)(2,1)} collective-permute-done((bf16[2,12,224,128]{3,2,1,0:T(8,128)(2,1)S(1)}, bf16[2,12,224,128]{3,2,1,0:T(8,128)(2,1)}, u32[]{:S(2)}, u32[]{:S(2)}) %collective-permute-start.15) | collective-permute-done | bytes 1376288 | tf_op jit(solution)/shard_map/ppermute | solution.py:1446
  146.9 4.2 shard_map.145
  153.2 7.4 %shard_map.146 = (bf16[2048,2304]{1,0:T(8,128)(2,1)}, bf16[2048,768]{1,0:T(8,128)(2,1)}, f32[256,128]{1,0:T(8,128)}, f32[8,128]{1,0:T(8,128)}) custom-call(bf16[2048,768]{1,0:T(8,128)(2,1)} %bitcast.203, bf16[768,2304]{1,0:T(8,128)(2,1)} %get-tuple-element.175.refs_1_.refs_2_, ...), custom_call_target="tpu_custom_call", output_to_operand_aliasing={{0}: (3, {}), {1}: (4, {}), {2}: (5, {})} | custom-call | flops 8000000000 | bytes 24000000 | tf_op jit(solution)/shard_map/pallas_call | solution.py:226
  161.1 48.5 %shard_map.147 = (bf16[2048,768]{1,0:T(8,128)(2,1)}, bf16[2048,768]{1,0:T(8,128)(2,1)}, bf16[2048,3072]{1,0:T(8,128)(2,1)}, bf16[2048,3072]{1,0:T(8,128)(2,1)}, ...) custom-call(s32[4]{0:T(128)} %pad_add_fusion.refs_0_.refs_1_, ...), custom_call_target="tpu_custom_call" | custom-call | flops 60000002048 | bytes 180000000 | tf_op jit(solution)/shard_map/pallas_call | solution.py:226
  209.5 6.7 %all-gather.2.cloned.1.call-done.refs_5_.refs_2_ = bf16[32,4,448,128]{3,2,1,0:T(8,128)(2,1)} async-done(((bf16[1,4,448,128]{3,2,1,0:T(8,128)(2,1)}), bf16[32,4,448,128]{3,2,1,0:T(8,128)(2,1)}) %all-gather.2.cloned.1.call-update) | async-done | bytes 14680080 | tf_op jit(solution)/shard_map/all_gather | solution.py:1676
  216.2 3.4 shard_map.148
  219.6 9.7 %all_gather.7 = bf16[128,1664]{1,0:T(8,128)(2,1)S(1)} all-gather(bf16[16,1664]{1,0:T(8,128)(2,1)} %get-tuple-element.192), channel_id=1, replica_groups=mesh['seg'=8,'doc'=4] {'seg'}, dimensions={0}, use_global_device_ids=true | all-gather | bytes 479232 | tf_op jit(solution)/shard_map/all_gather | solution.py:1689
  232.1 31.6 %shard_map.149 = (bf16[128,768]{1,0:T(8,128)(2,1)}, bf16[128,768]{1,0:T(8,128)(2,1)}, bf16[16,448,128]{2,1,0:T(8,128)(2,1)}, f32[8,128]{1,0:T(8,128)}) custom-call(s32[1]{0:T(128)} %bitcast.refs_0_, s32[4]{0:T(128)} %pad_add_fusion.refs_0_.refs_1_, bf16[32,4,448,128]{3,2,1,0:T(8,128)(2,1)} %all-gather.2.cloned.1.call-done.refs_5_.refs_2_, ...), custom_call_target="tpu_custom_call" | custom-call | flops 30000001024 | bytes 90000000 | tf_op jit(solution)/shard_map/pallas_call | solution.py:226
  272.8 43.7 %shard_map.151 = (bf16[2048,768]{1,0:T(8,128)(2,1)}, bf16[2048,3072]{1,0:T(8,128)(2,1)}, bf16[2048,768]{1,0:T(8,128)(2,1)}, bf16[2048,768]{1,0:T(8,128)(2,1)}, f...) custom-call(bf16[2048,768]{1,0:T(8,128)(2,1)} %bitcast.196, f32[16,768]{1,0:T(8,128)} %get-tuple-element.310.refs_1_, ...), custom_call_target="tpu_custom_call" | custom-call | flops 44000002048 | bytes 132000000 | tf_op jit(solution)/shard_map/pallas_call | solution.py:226
  320.6 19.2 %shard_map.153 = (bf16[2,2,4,224,128]{4,3,2,1,0:T(8,128)(2,1)}, bf16[2,2,4,224,128]{4,3,2,1,0:T(8,128)(2,1)}, bf16[2,2,4,224,128]{4,3,2,1,0:T(8,128)(2,1)}, bf16...) custom-call(s32[4]{0:T(128)} %pad_add_fusion.refs_0_.refs_1_, ...), custom_call_target="tpu_custom_call" | custom-call | flops 17999998976 | bytes 54000000 | tf_op jit(solution)/shard_map/pallas_call | solution.py:226
  340.4 4.7 convolution_convert_fusion.refs_9_.refs_3_.refs_4_
  348.4 21.9 %shard_map.155 = (bf16[2,2,8,224,128]{4,3,2,1,0:T(8,128)(2,1)}, bf16[2,2,8,224,128]{4,3,2,1,0:T(8,128)(2,1)}, bf16[2,2,8,224,128]{4,3,2,1,0:T(8,128)(2,1)}, bf16[2,2,8,224,128]{4,3,2,1,0:T(8,128)(2,1)}, f32[8,128]{1,0:T(8,128)}) custom-call(s32[4]{0:T(128)} %pad_add_fusion.refs_0_.refs_1_, bf16[2048,768]{1,0:T(8,128)(2,1)} %get-tuple-element.212.refs_1_, ...), custom_call_target="tpu_custom_call" | custom-call | flops 17999998976 | bytes 54000000 | tf_op jit(solution)/shard_map/pallas_call | solution.py:226
  374.1 9.8 %shard_map.156 = (bf16[2048,2304]{1,0:T(8,128)(2,1)}, f32[8,768]{1,0:T(8,128)}, f32[8,128]{1,0:T(8,128)}) custom-call(bf16[2048,2304]{1,0:T(8,128)(2,1)} %get-tuple-element.209.refs_0_, f32[256,128]{1,0:T(8,128)} %get-tuple-element.210.refs_1_, bf16[2048,768]{1,0:T(8,128)(2,1)} %get-tuple-element.211.refs_2_, f32[8,768]{1,0:T(8,128)} %broadcast_in_dim.47.refs_3_, ...), custom_call_target="tpu_custom_call" | custom-call | flops 10000000000 | bytes 30000000 | tf_op jit(solution)/shard_map/pallas_call | solution.py:226
  386.5 4.6 shard_map.157
  398.4 16.2 %shard_map.158 = (bf16[2048,2304]{1,0:T(8,128)(2,1)}, f32[8,768]{1,0:T(8,128)}, f32[8,128]{1,0:T(8,128)}) custom-call(bf16[2048,2304]{1,0:T(8,128)(2,1)} %get-tuple-element.209.refs_0_, f32[256,128]{1,0:T(8,128)} %get-tuple-element.210.refs_1_, bf16[2048,768]{1,0:T(8,128)(2,1)} %get-tuple-element.211.refs_2_, ...), custom_call_target="tpu_custom_call", output_to_operand_aliasing={{0}: (4, {})} | custom-call | flops 20000000000 | bytes 60000000 | tf_op jit(solution)/shard_map/pallas_call | solution.py:226
  426.2 9.7 %shard_map.161 = (bf16[2048,2304]{1,0:T(8,128)(2,1)}, f32[8,768]{1,0:T(8,128)}, f32[8,128]{1,0:T(8,128)}) custom-call(bf16[2048,2304]{1,0:T(8,128)(2,1)} %get-tuple-element.209.refs_0_, f32[256,128]{1,0:T(8,128)} %get-tuple-element.210.refs_1_, bf16[2048,768]{1,0:T(8,128)(2,1)} %get-tuple-element.211.refs_2_, ...), custom_call_target="tpu_custom_call", output_to_operand_aliasing={{0}: (4, {})} | custom-call | flops 10000000000 | bytes 30000000 | tf_op jit(solution)/shard_map/pallas_call | solution.py:226
  439.9 15.7 %shard_map.164 = (bf16[2,2,4,224,128]{4,3,2,1,0:T(8,128)(2,1)}, bf16[2,2,4,224,128]{4,3,2,1,0:T(8,128)(2,1)}, bf16[2,2,4,224,128]{4,3,2,1,0:T(8,128)(2,1)}, bf16[2,2,4,224,128]{4,3,2,1,0:T(8,128)(2,1)}, f32[8,128]{1,0:T(8,128)}) custom-call(s32[4]{0:T(128)} %pad_add_fusion.refs_0_.refs_1_, bf16[2048,768]{1,0:T(8,128)(2,1)} %bitcast.205, ...), custom_call_target="tpu_custom_call" | custom-call | flops 17999998976 | bytes 54000000 | tf_op jit(solution)/shard_map/pallas_call | solution.py:226
  466.7 13.2 %shard_map.166 = (bf16[2048,768]{1,0:T(8,128)(2,1)}, f32[8,128]{1,0:T(8,128)}) custom-call(f32[2048,768]{1,0:T(8,128)} %get-tuple-element.208.refs_0_, bf16[2048,2304]{1,0:T(8,128)(2,1)} %get-tuple-element.257.refs_2_.refs_1_, bf16[768,2304]{1,0:T(8,128)(2,1)} %get-tuple-element.175.refs_1_.refs_2_, f32[8,128]{1,0:T(8,128)} %copy-done.57), custom_call_target="tpu_custom_call" | custom-call | flops 12000000000 | bytes 36000000 | tf_op jit(solution)/shard_map/pallas_call | solution.py:226
  483.3 4.2 collective-permute-done.43.refs_2_
  499.5 3.6 all-to-all-start.1
  503.9 4.0 broadcast_select_fusion
  507.8 9.2 %all-to-all-done.1 = bf16[8,448,128]{2,1,0:T(8,128)(2,1)S(1)} async-done(((bf16[8,448,128]{2,1,0:T(8,128)(2,1)}), bf16[8,448,128]{2,1,0:T(8,128)(2,1)S(1)}, u32[]{:S(2)}, u32[]{:S(2)}) %all-to-all-start.1) | async-done | bytes 917536 | tf_op jit(solution)/shard_map/all_to_all | solution.py:1738
  519.9 5.3 %shard_map.171 = (f32[3473,128]{1,0:T(8,128)}, f32[3473,128]{1,0:T(8,128)}, f32[3473,128]{1,0:T(8,128)}, bf16[3473,128]{1,0:T(8,128)(2,1)}, f32[8,128]{1,0:T(8,128)}) custom-call(s32[156]{0:T(256)S(1)} %bitcast.189, s32[5]{0:T(128)S(1)} %convert_bitcast_fusion.refs_1_, f32[10]{0:T(128)S(1)} %reshape.366.refs_2_, bf16[3584,128]{1,0:T(8,128)(2,1)S(1)} %bitcast.126, ...), custom_call_target="tpu_custom_call" | custom-call | tf_op jit(solution)/shard_map/pallas_call | solution.py:226
  (259 shorter events, 116.3 us)
Async XLA Ops:
  7.2 209.1 %all-gather.2.cloned.1.call-start = ((), (), s32[]{:S(2)}) async-start(), calls=%async_computation.2 | async-start | bytes 15138816 | tf_op jit(solution)/shard_map/all_gather | solution.py:1676
  33.4 17.0 %collective-permute-start.4 = (bf16[1,448,128]{2,1,0:T(8,128)(2,1)S(1)}, bf16[1,448,128]{2,1,0:T(8,128)(2,1)S(1)}, u32[]{:S(2)}, u32[]{:S(2)}) collective-permute-start(bf16[1,448,128]{2,1,0:T(8,128)(2,1)S(1)} %slice.40.refs_1_), channel_id=1, source_target_pairs={{0,2},{1,3},{2,0},{3,1},{4,6},{5,7},{6,4},{7,5},{8,10},{9,11},{10,... | collective-permute-start | bytes 344072 | tf_op jit(solution)/shard_map/ppermute | solution.py:1446
  33.4 17.0 %collective-permute-start.3 = (bf16[1,448,128]{2,1,0:T(8,128)(2,1)S(1)}, bf16[1,448,128]{2,1,0:T(8,128)(2,1)S(1)}, u32[]{:S(2)}, u32[]{:S(2)}) collective-permute-start(bf16[1,448,128]{2,1,0:T(8,128)(2,1)S(1)} %slice.40.refs_1_), channel_id=1, source_target_pairs={{0,1},{1,2},{2,3},{3,0},{4,5},{5,6},{6,7},{7,4},{8,9},{9,10},{10,1... | collective-permute-start | bytes 344072 | tf_op jit(solution)/shard_map/ppermute | solution.py:1446
  34.3 17.5 %collective-permute-start = (bf16[3,448,128]{2,1,0:T(8,128)(2,1)S(1)}, bf16[3,448,128]{2,1,0:T(8,128)(2,1)S(1)}, u32[]{:S(2)}, u32[]{:S(2)}) collective-permute-start(bf16[3,448,128]{2,1,0:T(8,128)(2,1)S(1)} %slice.39.refs_1_), channel_id=1, source_target_pairs={{0,1},{1,2},{2,3},{3,0},{4,5},{5,6},{6,7},{7,4},{8,9},{9,10},{10,1... | collective-permute-start | bytes 1032200 | tf_op jit(solution)/shard_map/ppermute | solution.py:1446
  71.3 13.3 %collective-permute-start.12 = (bf16[2,2,4,224,128]{4,3,2,1,0:T(8,128)(2,1)}, bf16[2,2,4,224,128]{4,3,2,1,0:T(8,128)(2,1)}, u32[]{:S(2)}, u32[]{:S(2)}) collective-permute-start(bf16[2,2,4,224,128]{4,3,2,1,0:T(8,128)(2,1)} %bitcast.23.refs_1_), channel_id=1, source_target_pairs={{0,4},{1,5},{2,6},{3,7},{4,0},{5,1},{6,2},{7,3},{8,12},{9,13},{10,... | collective-permute-start | bytes 2752520 | tf_op jit(solution)/shard_map/ppermute | solution.py:1446
  71.3 13.3 %collective-permute-start.13 = (bf16[2,2,4,224,128]{4,3,2,1,0:T(8,128)(2,1)}, bf16[2,2,4,224,128]{4,3,2,1,0:T(8,128)(2,1)}, u32[]{:S(2)}, u32[]{:S(2)}) collective-permute-start(bf16[2,2,4,224,128]{4,3,2,1,0:T(8,128)(2,1)} %bitcast.24.refs_3_), channel_id=1, source_target_pairs={{0,4},{1,5},{2,6},{3,7},{4,0},{5,1},{6,2},{7,3},{8,12},{9,13},{10,... | collective-permute-start | bytes 2752520 | tf_op jit(solution)/shard_map/ppermute | solution.py:1446
  82.5 16.5 %collective-permute-start.10 = (bf16[12,224,128]{2,1,0:T(8,128)(2,1)S(1)}, bf16[12,224,128]{2,1,0:T(8,128)(2,1)S(1)}, u32[]{:S(2)}, u32[]{:S(2)}) collective-permute-start(bf16[12,224,128]{2,1,0:T(8,128)(2,1)S(1)} %get-tuple-element.165), channel_id=1, source_target_pairs={{0,8},{1,9},{2,10},{3,11},{4,12},{5,13},{6,14},{7,15},{8,0},{9,1},... | collective-permute-start | bytes 2064392 | tf_op jit(solution)/shard_map/ppermute | solution.py:1446
  83.2 16.6 %collective-permute-start.11 = (bf16[12,224,128]{2,1,0:T(8,128)(2,1)S(1)}, bf16[12,224,128]{2,1,0:T(8,128)(2,1)S(1)}, u32[]{:S(2)}, u32[]{:S(2)}) collective-permute-start(bf16[12,224,128]{2,1,0:T(8,128)(2,1)S(1)} %get-tuple-element.166), channel_id=1, source_target_pairs={{0,16},{1,17},{2,18},{3,19},{4,20},{5,21},{6,22},{7,23},{8,24},{9,... | collective-permute-start | bytes 2064392 | tf_op jit(solution)/shard_map/ppermute | solution.py:1446
  107.3 33.9 %collective-permute-start.15 = (bf16[2,12,224,128]{3,2,1,0:T(8,128)(2,1)S(1)}, bf16[2,12,224,128]{3,2,1,0:T(8,128)(2,1)}, u32[]{:S(2)}, u32[]{:S(2)}) collective-permute-start(bf16[2,12,224,128]{3,2,1,0:T(8,128)(2,1)S(1)} %bitcast.155), channel_id=1, source_target_pairs={{0,8},{1,9},{2,10},{3,11},{4,12},{5,13},{6,14},{7,15},{8,0},{9,1},... | collective-permute-start | bytes 4128776 | tf_op jit(solution)/shard_map/ppermute | solution.py:1446
  108.3 35.3 %collective-permute-start.14 = (bf16[2,12,224,128]{3,2,1,0:T(8,128)(2,1)S(1)}, bf16[2,12,224,128]{3,2,1,0:T(8,128)(2,1)}, u32[]{:S(2)}, u32[]{:S(2)}) collective-permute-start(bf16[2,12,224,128]{3,2,1,0:T(8,128)(2,1)S(1)} %bitcast.153), channel_id=1, source_target_pairs={{0,16},{1,17},{2,18},{3,19},{4,20},{5,21},{6,22},{7,23},{8,24},{9,... | collective-permute-start | bytes 4128776 | tf_op jit(solution)/shard_map/ppermute | solution.py:1446
  266.8 51.4 %collective-permute-start.18 = (bf16[4,448,128]{2,1,0:T(8,128)(2,1)S(1)}, bf16[4,448,128]{2,1,0:T(8,128)(2,1)S(1)}, u32[]{:S(2)}, u32[]{:S(2)}) collective-permute-start(bf16[4,448,128]{2,1,0:T(8,128)(2,1)S(1)} %get-tuple-element.219), channel_id=1, source_target_pairs={{0,1},{1,2},{2,3},{3,0},{4,5},{5,6},{6,7},{7,4},{8,9},{9,10},{10,1... | collective-permute-start | bytes 1376264 | tf_op jit(solution)/shard_map/ppermute | solution.py:1446
  267.6 50.7 %collective-permute-start.19 = (bf16[4,448,128]{2,1,0:T(8,128)(2,1)S(1)}, bf16[4,448,128]{2,1,0:T(8,128)(2,1)S(1)}, u32[]{:S(2)}, u32[]{:S(2)}) collective-permute-start(bf16[4,448,128]{2,1,0:T(8,128)(2,1)S(1)} %get-tuple-element.220), channel_id=1, source_target_pairs={{0,2},{1,3},{2,0},{3,1},{4,6},{5,7},{6,4},{7,5},{8,10},{9,11},{10,... | collective-permute-start | bytes 1376264 | tf_op jit(solution)/shard_map/ppermute | solution.py:1446
  269.0 49.3 %collective-permute-start.20 = (bf16[4,448,128]{2,1,0:T(8,128)(2,1)S(1)}, bf16[4,448,128]{2,1,0:T(8,128)(2,1)S(1)}, u32[]{:S(2)}, u32[]{:S(2)}) collective-permute-start(bf16[4,448,128]{2,1,0:T(8,128)(2,1)S(1)} %get-tuple-element.221), channel_id=1, source_target_pairs={{0,3},{1,0},{2,1},{3,2},{4,7},{5,4},{6,5},{7,6},{8,11},{9,8},{10,9... | collective-permute-start | bytes 1376264 | tf_op jit(solution)/shard_map/ppermute | solution.py:1446
  370.3 14.5 %collective-permute-start.25 = (bf16[2,2,8,224,128]{4,3,2,1,0:T(8,128)(2,1)}, bf16[2,2,8,224,128]{4,3,2,1,0:T(8,128)(2,1)}, u32[]{:S(2)}, u32[]{:S(2)}) collective-permute-start(bf16[2,2,8,224,128]{4,3,2,1,0:T(8,128)(2,1)} %get-tuple-element.239), channel_id=1, source_target_pairs={{0,4},{1,5},{2,6},{3,7},{4,0},{5,1},{6,2},{7,3},{8,12},{9,13},{10,... | collective-permute-start | bytes 5505032 | tf_op jit(solution)/shard_map/ppermute | solution.py:1446
  370.4 14.3 %collective-permute-start.26 = (bf16[2,2,8,224,128]{4,3,2,1,0:T(8,128)(2,1)}, bf16[2,2,8,224,128]{4,3,2,1,0:T(8,128)(2,1)}, u32[]{:S(2)}, u32[]{:S(2)}) collective-permute-start(bf16[2,2,8,224,128]{4,3,2,1,0:T(8,128)(2,1)} %get-tuple-element.241), channel_id=1, source_target_pairs={{0,4},{1,5},{2,6},{3,7},{4,0},{5,1},{6,2},{7,3},{8,12},{9,13},{10,... | collective-permute-start | bytes 5505032 | tf_op jit(solution)/shard_map/ppermute | solution.py:1446
  370.9 13.0 %collective-permute-start.23 = (bf16[2,4,224,128]{3,2,1,0:T(8,128)(2,1)}, bf16[2,4,224,128]{3,2,1,0:T(8,128)(2,1)}, u32[]{:S(2)}, u32[]{:S(2)}) collective-permute-start(bf16[2,4,224,128]{3,2,1,0:T(8,128)(2,1)} %bitcast.49), channel_id=1, source_target_pairs={{0,16},{1,17},{2,18},{3,19},{4,20},{5,21},{6,22},{7,23},{8,24},{9,... | collective-permute-start | bytes 1376264 | tf_op jit(solution)/shard_map/ppermute | solution.py:1446
  372.2 12.5 %collective-permute-start.24 = (bf16[2,4,224,128]{3,2,1,0:T(8,128)(2,1)}, bf16[2,4,224,128]{3,2,1,0:T(8,128)(2,1)}, u32[]{:S(2)}, u32[]{:S(2)}) collective-permute-start(bf16[2,4,224,128]{3,2,1,0:T(8,128)(2,1)} %bitcast.52), channel_id=1, source_target_pairs={{0,8},{1,9},{2,10},{3,11},{4,12},{5,13},{6,14},{7,15},{8,0},{9,1},... | collective-permute-start | bytes 1376264 | tf_op jit(solution)/shard_map/ppermute | solution.py:1446
  394.3 20.3 %collective-permute-start.29 = (bf16[4,224,128]{2,1,0:T(8,128)(2,1)}, bf16[4,224,128]{2,1,0:T(8,128)(2,1)}, u32[]{:S(2)}, u32[]{:S(2)}) collective-permute-start(bf16[4,224,128]{2,1,0:T(8,128)(2,1)} %bitcast.65), channel_id=1, source_target_pairs={{0,8},{1,9},{2,10},{3,11},{4,12},{5,13},{6,14},{7,15},{8,0},{9,1},... | collective-permute-start | bytes 688136 | tf_op jit(solution)/shard_map/ppermute | solution.py:1446
  395.6 19.0 %collective-permute-start.30 = (bf16[4,224,128]{2,1,0:T(8,128)(2,1)}, bf16[4,224,128]{2,1,0:T(8,128)(2,1)}, u32[]{:S(2)}, u32[]{:S(2)}) collective-permute-start(bf16[4,224,128]{2,1,0:T(8,128)(2,1)} %bitcast.67), channel_id=1, source_target_pairs={{0,16},{1,17},{2,18},{3,19},{4,20},{5,21},{6,22},{7,23},{8,24},{9,... | collective-permute-start | bytes 688136 | tf_op jit(solution)/shard_map/ppermute | solution.py:1446
  396.4 25.2 %collective-permute-start.27 = (bf16[2,8,224,128]{3,2,1,0:T(8,128)(2,1)}, bf16[2,8,224,128]{3,2,1,0:T(8,128)(2,1)S(1)}, u32[]{:S(2)}, u32[]{:S(2)}) collective-permute-start(bf16[2,8,224,128]{3,2,1,0:T(8,128)(2,1)} %bitcast.59), channel_id=1, source_target_pairs={{0,16},{1,17},{2,18},{3,19},{4,20},{5,21},{6,22},{7,23},{8,24},{9,... | collective-permute-start | bytes 2752520 | tf_op jit(solution)/shard_map/ppermute | solution.py:1446
  397.7 24.0 %collective-permute-start.28 = (bf16[2,8,224,128]{3,2,1,0:T(8,128)(2,1)}, bf16[2,8,224,128]{3,2,1,0:T(8,128)(2,1)S(1)}, u32[]{:S(2)}, u32[]{:S(2)}) collective-permute-start(bf16[2,8,224,128]{3,2,1,0:T(8,128)(2,1)} %bitcast.62), channel_id=1, source_target_pairs={{0,8},{1,9},{2,10},{3,11},{4,12},{5,13},{6,14},{7,15},{8,0},{9,1},... | collective-permute-start | bytes 2752520 | tf_op jit(solution)/shard_map/ppermute | solution.py:1446
  417.2 18.7 %collective-permute-start.33 = (bf16[1,448,128]{2,1,0:T(8,128)(2,1)}, bf16[1,448,128]{2,1,0:T(8,128)(2,1)}, u32[]{:S(2)}, u32[]{:S(2)}) collective-permute-start(bf16[1,448,128]{2,1,0:T(8,128)(2,1)} %get-tuple-element.264), channel_id=1, source_target_pairs={{0,1},{1,2},{2,3},{3,0},{4,5},{5,6},{6,7},{7,4},{8,9},{9,10},{10,1... | collective-permute-start | bytes 344072 | tf_op jit(solution)/shard_map/ppermute | solution.py:1446
  417.2 18.7 %collective-permute-start.34 = (bf16[1,448,128]{2,1,0:T(8,128)(2,1)}, bf16[1,448,128]{2,1,0:T(8,128)(2,1)}, u32[]{:S(2)}, u32[]{:S(2)}) collective-permute-start(bf16[1,448,128]{2,1,0:T(8,128)(2,1)} %get-tuple-element.265), channel_id=1, source_target_pairs={{0,2},{1,3},{2,0},{3,1},{4,6},{5,7},{6,4},{7,5},{8,10},{9,11},{10,... | collective-permute-start | bytes 344072 | tf_op jit(solution)/shard_map/ppermute | solution.py:1446
  418.6 17.3 %collective-permute-start.35 = (bf16[1,448,128]{2,1,0:T(8,128)(2,1)}, bf16[1,448,128]{2,1,0:T(8,128)(2,1)}, u32[]{:S(2)}, u32[]{:S(2)}) collective-permute-start(bf16[1,448,128]{2,1,0:T(8,128)(2,1)} %get-tuple-element.266), channel_id=1, source_target_pairs={{0,3},{1,0},{2,1},{3,2},{4,7},{5,4},{6,5},{7,6},{8,11},{9,8},{10,9... | collective-permute-start | bytes 344072 | tf_op jit(solution)/shard_map/ppermute | solution.py:1446
  424.3 14.0 %collective-permute-start.31 = (bf16[8,224,128]{2,1,0:T(8,128)(2,1)}, bf16[8,224,128]{2,1,0:T(8,128)(2,1)S(1)}, u32[]{:S(2)}, u32[]{:S(2)}) collective-permute-start(bf16[8,224,128]{2,1,0:T(8,128)(2,1)} %bitcast.69), channel_id=1, source_target_pairs={{0,8},{1,9},{2,10},{3,11},{4,12},{5,13},{6,14},{7,15},{8,0},{9,1},... | collective-permute-start | bytes 1376264 | tf_op jit(solution)/shard_map/ppermute | solution.py:1446
  425.4 12.9 %collective-permute-start.32 = (bf16[8,224,128]{2,1,0:T(8,128)(2,1)}, bf16[8,224,128]{2,1,0:T(8,128)(2,1)S(1)}, u32[]{:S(2)}, u32[]{:S(2)}) collective-permute-start(bf16[8,224,128]{2,1,0:T(8,128)(2,1)} %bitcast.71), channel_id=1, source_target_pairs={{0,16},{1,17},{2,18},{3,19},{4,20},{5,21},{6,22},{7,23},{8,24},{9,... | collective-permute-start | bytes 1376264 | tf_op jit(solution)/shard_map/ppermute | solution.py:1446
  456.2 23.7 %collective-permute-start.40 = (bf16[2,448,128]{2,1,0:T(8,128)(2,1)}, bf16[2,448,128]{2,1,0:T(8,128)(2,1)S(1)}, u32[]{:S(2)}, u32[]{:S(2)}) collective-permute-start(bf16[2,448,128]{2,1,0:T(8,128)(2,1)} %get-tuple-element.282), channel_id=1, source_target_pairs={{0,1},{1,2},{2,3},{3,0},{4,5},{5,6},{6,7},{7,4},{8,9},{9,10},{10,1... | collective-permute-start | bytes 688136 | tf_op jit(solution)/shard_map/ppermute | solution.py:1446
  456.3 23.6 %collective-permute-start.41 = (bf16[2,448,128]{2,1,0:T(8,128)(2,1)}, bf16[2,448,128]{2,1,0:T(8,128)(2,1)S(1)}, u32[]{:S(2)}, u32[]{:S(2)}) collective-permute-start(bf16[2,448,128]{2,1,0:T(8,128)(2,1)} %get-tuple-element.283), channel_id=1, source_target_pairs={{0,2},{1,3},{2,0},{3,1},{4,6},{5,7},{6,4},{7,5},{8,10},{9,11},{10,... | collective-permute-start | bytes 688136 | tf_op jit(solution)/shard_map/ppermute | solution.py:1446
  457.7 22.2 %collective-permute-start.42 = (bf16[2,448,128]{2,1,0:T(8,128)(2,1)}, bf16[2,448,128]{2,1,0:T(8,128)(2,1)S(1)}, u32[]{:S(2)}, u32[]{:S(2)}) collective-permute-start(bf16[2,448,128]{2,1,0:T(8,128)(2,1)} %get-tuple-element.284), channel_id=1, source_target_pairs={{0,3},{1,0},{2,1},{3,2},{4,7},{5,4},{6,5},{7,6},{8,11},{9,8},{10,9... | collective-permute-start | bytes 688136 | tf_op jit(solution)/shard_map/ppermute | solution.py:1446
  464.7 16.1 %collective-permute-start.38 = (bf16[2,4,224,128]{3,2,1,0:T(8,128)(2,1)S(1)}, bf16[2,4,224,128]{3,2,1,0:T(8,128)(2,1)S(1)}, u32[]{:S(2)}, u32[]{:S(2)}) collective-permute-start(bf16[2,4,224,128]{3,2,1,0:T(8,128)(2,1)S(1)} %bitcast.191), channel_id=1, source_target_pairs={{0,16},{1,17},{2,18},{3,19},{4,20},{5,21},{6,22},{7,23},{8,24},{9,... | collective-permute-start | bytes 1376264 | tf_op jit(solution)/shard_map/ppermute | solution.py:1446
  466.0 14.9 %collective-permute-start.39 = (bf16[2,4,224,128]{3,2,1,0:T(8,128)(2,1)S(1)}, bf16[2,4,224,128]{3,2,1,0:T(8,128)(2,1)S(1)}, u32[]{:S(2)}, u32[]{:S(2)}) collective-permute-start(bf16[2,4,224,128]{3,2,1,0:T(8,128)(2,1)S(1)} %bitcast.190), channel_id=1, source_target_pairs={{0,8},{1,9},{2,10},{3,11},{4,12},{5,13},{6,14},{7,15},{8,0},{9,1},... | collective-permute-start | bytes 1376264 | tf_op jit(solution)/shard_map/ppermute | solution.py:1446
  499.5 17.5 %all-to-all-start.1 = ((bf16[8,448,128]{2,1,0:T(8,128)(2,1)}), bf16[8,448,128]{2,1,0:T(8,128)(2,1)S(1)}, u32[]{:S(2)}, u32[]{:S(2)}) async-start(bf16[8,448,128]{2,1,0:T(8,128)(2,1)} %get-tuple-element.300), calls=%async_computation.1 | async-start | bytes 1835008 | tf_op jit(solution)/shard_map/all_to_all | solution.py:1738
  (83 other events, 580.4 us)
Sparse Core Ops, SparseCore 0:
  107.5 108.7 all-gather.1

commit v8 on v7

--- a/solution.py
+++ b/solution.py
@@ -909,7 +909,7 @@
 
     return in_parts(
         kernel,
-        8 * count,
+        0,
         count,
         [x, w_qkv, vecs],
         [rows(D), fixed((D, 3 * D)), fixed((VECTOR_ROWS, D))],
@@ -952,7 +952,7 @@
         ],
         scratch_shapes=weights.scratch,
         compiler_params=kernel_params(60),
-        cost_estimate=cost(12),
+        cost_estimate=cost(0),
     )(coords, *weights.operands, x)
 
 
@@ -978,7 +978,7 @@
         rate_ref[rows, :] = jnp.broadcast_to(rate, (SEG_LEN, LANES))
         return carry
 
-    lax.fori_loop(0, segs, start, 0)
+    lax.fori_loop(0, segs, start, 0, unroll=2)
     h = h1low_ref[...]
     for j in range(FF // FBLOCK):
         cols = slice(j * FBLOCK, (j + 1) * FBLOCK)
@@ -1002,7 +1002,7 @@
         cls_ref[pl.ds(step * segs + s, 1), :] = hidden[0:1, :]
         return carry
 
-    lax.fori_loop(0, segs, finish, 0)
+    lax.fori_loop(0, segs, finish, 0, unroll=2)
 
 
 def feed_layer(x, att, weights, coords):
@@ -1101,7 +1101,7 @@
         add_sum(9, dm.astype(jnp.float32))
         return carry
 
-    lax.fori_loop(0, segs, start, 0)
+    lax.fori_loop(0, segs, start, 0, unroll=2)
     dm = dm_ref[...]
     for j in range(FF // FBLOCK):
         cols = slice(j * FBLOCK, (j + 1) * FBLOCK)
@@ -1123,7 +1123,7 @@
         add_sum(2, dao.astype(jnp.float32))
         return carry
 
-    lax.fori_loop(0, segs, finish, 0)
+    lax.fori_loop(0, segs, finish, 0, unroll=2)
     da_ref[...] = low(dot_nt(dao_ref[...], wout_ref[...]))
 
 
@@ -1188,7 +1188,7 @@
                     sums_ref[here] += jnp.sum(grad.astype(jnp.float32), axis=0, keepdims=True)
         return carry
 
-    lax.fori_loop(0, TILE // SEG_LEN, segment, 0, unroll=2)
+    lax.fori_loop(0, TILE // SEG_LEN, segment, 0, unroll=4)
 
 
 def attend_back(packed, stat, da, first, count, previous=None):
@@ -1599,6 +1599,20 @@
         target[0] = source[...]
 
     return flat_call(kernel, [(value, 1)], [(value.shape, 0)])[0]
+
+
+def turn():
+    def kernel(target):
+        target[...] = jnp.zeros_like(target)
+
+    ordered(
+        kernel,
+        out_shape=jax.ShapeDtypeStruct((8, LANES), jnp.float32),
+        in_specs=[],
+        out_specs=spec_vmem(),
+        compiler_params=kernel_params(),
+        cost_estimate=cost(0),
+    )()
 def row_rates(geo, n_tokens, n_cls):
     runs = []
     cross = list(LAYOUT)[-13:]
@@ -1661,9 +1675,10 @@
     ORDER.wait_for(*parts_b[1:2])
     plane = gather_plane(geo, line, 0)
     ORDER.wait_for(*parts_b[2:3])
+    turn()
+    plane_b = place_line(geo, parts_b, my_doc)
     plane = gather_plane(geo, plane, 1)
     gathered = [gather_cores(geo, plane), None, None]
-    plane_b = place_line(geo, parts_b, my_doc)
 
     def weights(*numbers):
         return Weights(geo, gather, gathered, [item_name(i) for i in numbers])
@@ -1671,9 +1686,9 @@
     def own(values):
         return lax.dynamic_slice_in_dim(values, my_seg * seg_count, seg_count, axis=0)
 
-    *outs, w_qkv, vec_a = attend_first(inputs, weights(0, 1), coords)
     plane_b = gather_plane(geo, plane_b, 0)
     gathered[2] = [lax.all_gather(gate(parts[2]), AXES)]
+    *outs, w_qkv, vec_a = attend_first(inputs, weights(0, 1), coords)
     outs = attend_layer(inputs, w_qkv, vec_a, 1, middle, outs)
     plane_b = gather_plane(geo, plane_b, 1)
     gathered[1] = gather_cores(geo, plane_b)

time: 542 us -> 537 us (level)
  local copies, waits for them, and re-layouts: 38.3 us -> 32.8 us
    all_gather x1, waiting for transfers between devices: 6.68 us -> 18.6 us  [local(): gathered[2] = [lax.all_gather(gate(parts[2]), AXES)]]
    ppermute x48, waiting for transfers between devices: 74.8 us -> 66.1 us  [send(): return lax.ppermute(value, AXES, geo.shift(axis, step))]
    unnamed x130 -> x118, local copies, waits for them, and re-layouts: 33.5 us -> 27.9 us
    pallas_call x36 -> x37, Pallas kernels: 294 us -> 289 us  [run(): pl.pallas_call(wrapped, out_shape=outs + [jax.ShapeDtypeStruct((8, LANES)...]
  transfers between devices with their start and end apart: 50 -> 50, of which waited for: 18 -> 20; matrix products, arithmetic and copies ran while one was open for 3% -> 3% of each run, Pallas kernels for 34% -> 34%
where the time goes in v8:
time: 537 us; the launch traced here: 528 us
  Pallas kernels  289 us (54%)
  waiting for transfers between devices  93.9 us (17%)
  starting transfers between devices  55.5 us (10%)
  local copies, waits for them, and re-layouts  32.8 us (6%)
  blocking collectives  28.9 us (5%)
  between operations  14.8 us (3%)
  other arithmetic  7.06 us (1%)
  matrix products  6.37 us (1%)
    pallas_call x37, Pallas kernels, run(): pl.pallas_call(wrapped, out_shape=outs + [jax.ShapeDtypeStruct((8, LANES)...  289 us
    ppermute x48, waiting for transfers between devices, send(): return lax.ppermute(value, AXES, geo.shift(axis, step))  66.1 us
    ppermute x48, starting transfers between devices, send(): return lax.ppermute(value, AXES, geo.shift(axis, step))  51.9 us
    unnamed x118, local copies, waits for them, and re-layouts  27.9 us
    all_to_all x1, blocking collectives, local(): lax.all_to_all(aligned.reshape(geo.n_seg, geo.share, LANES), AXES[0], 0,...  19.2 us
    all_gather x1, waiting for transfers between devices, local(): gathered[2] = [lax.all_gather(gate(parts[2]), AXES)]  18.6 us
  transfers between devices with their start and end apart: 50, of which 20 were waited for; matrix products, arithmetic and copies ran while one was open for 3% of the time, Pallas kernels for 34%

profile of v8, /device:TPU:0, one launch (start us, length us, event | category | flops | bytes accessed | tf_op | source)
XLA Modules:
  0.0 528.1 jit_solution(4136626374759140563)
XLA Ops:
  10.6 19.2 %all_to_all.10 = bf16[8,448,128]{2,1,0:T(8,128)(2,1)S(1)} all-to-all(bf16[8,448,128]{2,1,0:T(8,128)(2,1)S(1)} %bitcast.163), channel_id=1, replica_groups=mesh['seg'=8,'doc'=4] {'seg'}, dimensions={0} | all-to-all | bytes 1835008 | tf_op jit(solution)/shard_map/all_to_all | solution.py:1662
  29.8 3.6 collective-permute-start.5
  37.9 3.4 collective-permute-start.2
  41.3 17.4 %collective-permute-done.4.refs_3_ = bf16[1,448,128]{2,1,0:T(8,128)(2,1)S(1)} collective-permute-done((bf16[1,448,128]{2,1,0:T(8,128)(2,1)S(1)}, bf16[1,448,128]{2,1,0:T(8,128)(2,1)S(1)}, u32[]{:S(2)}, u32[]{:S(2)}) %collective-permute-start.4) | collective-permute-done | bytes 114720 | tf_op jit(solution)/shard_map/ppermute | solution.py:1446
  60.1 4.7 collective-permute-done.6
  70.9 21.5 %collective-permute-done.11 = bf16[2,4,224,128]{3,2,1,0:T(8,128)(2,1)S(1)} collective-permute-done((bf16[2,4,224,128]{3,2,1,0:T(8,128)(2,1)S(1)}, bf16[2,4,224,128]{3,2,1,0:T(8,128)(2,1)S(1)}, u32[]{:S(2)}, u32[]{:S(2)}) %collective-permute-start.11) | collective-permute-done | bytes 458784 | tf_op jit(solution)/shard_map/ppermute | solution.py:1446
  103.8 10.6 %shard_map.144 = (bf16[2048,2304]{1,0:T(8,128)(2,1)}, bf16[2048,768]{1,0:T(8,128)(2,1)}, f32[256,128]{1,0:T(8,128)}, bf16[768,2304]{1,0:T(8,128)(2,1)}, f32[16,768]{1,0:T(8,128)}, /*index=5*/f32[8,128]{1,0:T(8,128)}) custom-call(s32[4]{0:T(128)} %pad_add_fusion.refs_0_.refs_1_, bf16[2,2,4,224,128]{4,3,2,1,0:T(8,128)(2,1)} %bitcast.158, ...), custom_call_target="tpu_custom_call" | custom-call | tf_op jit(solution)/shard_map/pallas_call | solution.py:226
  114.4 12.6 %shard_map.145 = (bf16[2048,2304]{1,0:T(8,128)(2,1)}, bf16[2048,768]{1,0:T(8,128)(2,1)}, f32[256,128]{1,0:T(8,128)}, f32[8,128]{1,0:T(8,128)}) custom-call(bf16[2048,768]{1,0:T(8,128)(2,1)} %bitcast.201, bf16[768,2304]{1,0:T(8,128)(2,1)} %get-tuple-element.177.refs_1_.refs_2_, ...), custom_call_target="tpu_custom_call", output_to_operand_aliasing={{0}: (3, {}), {1}: (4, {}), {2}: (5, {})} | custom-call | tf_op jit(solution)/shard_map/pallas_call | solution.py:226
  127.0 3.4 collective-permute-done.13
  134.9 4.2 shard_map.146
  141.1 7.4 %shard_map.147 = (bf16[2048,2304]{1,0:T(8,128)(2,1)}, bf16[2048,768]{1,0:T(8,128)(2,1)}, f32[256,128]{1,0:T(8,128)}, f32[8,128]{1,0:T(8,128)}) custom-call(bf16[2048,768]{1,0:T(8,128)(2,1)} %bitcast.202, bf16[768,2304]{1,0:T(8,128)(2,1)} %get-tuple-element.177.refs_1_.refs_2_, ...), custom_call_target="tpu_custom_call", output_to_operand_aliasing={{0}: (3, {}), {1}: (4, {}), {2}: (5, {})} | custom-call | tf_op jit(solution)/shard_map/pallas_call | solution.py:226
  149.0 45.7 %shard_map.148 = (bf16[2048,768]{1,0:T(8,128)(2,1)}, bf16[2048,768]{1,0:T(8,128)(2,1)}, bf16[2048,3072]{1,0:T(8,128)(2,1)}, bf16[2048,3072]{1,0:T(8,128)(2,1)}, ...) custom-call(s32[4]{0:T(128)} %pad_add_fusion.refs_0_.refs_1_, ...), custom_call_target="tpu_custom_call" | custom-call | flops 60000002048 | bytes 180000000 | tf_op jit(solution)/shard_map/pallas_call | solution.py:226
  194.7 18.6 %all-gather.2.cloned.1.call-done.refs_5_.refs_2_ = bf16[32,4,448,128]{3,2,1,0:T(8,128)(2,1)} async-done(((bf16[1,4,448,128]{3,2,1,0:T(8,128)(2,1)}), bf16[32,4,448,128]{3,2,1,0:T(8,128)(2,1)}) %all-gather.2.cloned.1.call-update) | async-done | bytes 14680080 | tf_op jit(solution)/shard_map/all_gather | solution.py:1690
  213.3 3.4 shard_map.149
  216.7 9.7 %all_gather.7 = bf16[128,1664]{1,0:T(8,128)(2,1)S(1)} all-gather(bf16[16,1664]{1,0:T(8,128)(2,1)} %get-tuple-element.194), channel_id=1, replica_groups=mesh['seg'=8,'doc'=4] {'seg'}, dimensions={0}, use_global_device_ids=true | all-gather | bytes 479232 | tf_op jit(solution)/shard_map/all_gather | solution.py:1704
  229.3 31.6 %shard_map.150 = (bf16[128,768]{1,0:T(8,128)(2,1)}, bf16[128,768]{1,0:T(8,128)(2,1)}, bf16[16,448,128]{2,1,0:T(8,128)(2,1)}, f32[8,128]{1,0:T(8,128)}) custom-call(s32[1]{0:T(128)} %bitcast.refs_0_, s32[4]{0:T(128)} %pad_add_fusion.refs_0_.refs_1_, bf16[32,4,448,128]{3,2,1,0:T(8,128)(2,1)} %all-gather.2.cloned.1.call-done.refs_5_.refs_2_, ...), custom_call_target="tpu_custom_call" | custom-call | flops 30000001024 | bytes 90000000 | tf_op jit(solution)/shard_map/pallas_call | solution.py:226
  269.4 43.1 %shard_map.152 = (bf16[2048,768]{1,0:T(8,128)(2,1)}, bf16[2048,3072]{1,0:T(8,128)(2,1)}, bf16[2048,768]{1,0:T(8,128)(2,1)}, bf16[2048,768]{1,0:T(8,128)(2,1)}, f...) custom-call(bf16[2048,768]{1,0:T(8,128)(2,1)} %bitcast.207, f32[16,768]{1,0:T(8,128)} %get-tuple-element.312.refs_1_, ...), custom_call_target="tpu_custom_call" | custom-call | flops 44000002048 | bytes 132000000 | tf_op jit(solution)/shard_map/pallas_call | solution.py:226
  316.5 19.2 %shard_map.154 = (bf16[2,2,4,224,128]{4,3,2,1,0:T(8,128)(2,1)}, bf16[2,2,4,224,128]{4,3,2,1,0:T(8,128)(2,1)}, bf16[2,2,4,224,128]{4,3,2,1,0:T(8,128)(2,1)}, bf16...) custom-call(s32[4]{0:T(128)} %pad_add_fusion.refs_0_.refs_1_, ...), custom_call_target="tpu_custom_call" | custom-call | flops 17999998976 | bytes 54000000 | tf_op jit(solution)/shard_map/pallas_call | solution.py:226
  336.3 4.7 convolution_convert_fusion.refs_9_.refs_3_.refs_4_
  344.3 22.1 %shard_map.156 = (bf16[2,2,8,224,128]{4,3,2,1,0:T(8,128)(2,1)}, bf16[2,2,8,224,128]{4,3,2,1,0:T(8,128)(2,1)}, bf16[2,2,8,224,128]{4,3,2,1,0:T(8,128)(2,1)}, bf16[2,2,8,224,128]{4,3,2,1,0:T(8,128)(2,1)}, f32[8,128]{1,0:T(8,128)}) custom-call(s32[4]{0:T(128)} %pad_add_fusion.refs_0_.refs_1_, bf16[2048,768]{1,0:T(8,128)(2,1)} %get-tuple-element.214.refs_1_, ...), custom_call_target="tpu_custom_call" | custom-call | flops 17999998976 | bytes 54000000 | tf_op jit(solution)/shard_map/pallas_call | solution.py:226
  370.3 9.6 %shard_map.157 = (bf16[2048,2304]{1,0:T(8,128)(2,1)}, f32[8,768]{1,0:T(8,128)}, f32[8,128]{1,0:T(8,128)}) custom-call(bf16[2048,2304]{1,0:T(8,128)(2,1)} %get-tuple-element.211.refs_0_, f32[256,128]{1,0:T(8,128)} %get-tuple-element.212.refs_1_, bf16[2048,768]{1,0:T(8,128)(2,1)} %get-tuple-element.213.refs_2_, f32[8,768]{1,0:T(8,128)} %broadcast_in_dim.47.refs_3_, ...), custom_call_target="tpu_custom_call" | custom-call | flops 10000000000 | bytes 30000000 | tf_op jit(solution)/shard_map/pallas_call | solution.py:226
  382.6 4.6 shard_map.158
  394.6 15.9 %shard_map.159 = (bf16[2048,2304]{1,0:T(8,128)(2,1)}, f32[8,768]{1,0:T(8,128)}, f32[8,128]{1,0:T(8,128)}) custom-call(bf16[2048,2304]{1,0:T(8,128)(2,1)} %get-tuple-element.211.refs_0_, f32[256,128]{1,0:T(8,128)} %get-tuple-element.212.refs_1_, bf16[2048,768]{1,0:T(8,128)(2,1)} %get-tuple-element.213.refs_2_, ...), custom_call_target="tpu_custom_call", output_to_operand_aliasing={{0}: (4, {})} | custom-call | flops 20000000000 | bytes 60000000 | tf_op jit(solution)/shard_map/pallas_call | solution.py:226
  421.9 9.5 %shard_map.162 = (bf16[2048,2304]{1,0:T(8,128)(2,1)}, f32[8,768]{1,0:T(8,128)}, f32[8,128]{1,0:T(8,128)}) custom-call(bf16[2048,2304]{1,0:T(8,128)(2,1)} %get-tuple-element.211.refs_0_, f32[256,128]{1,0:T(8,128)} %get-tuple-element.212.refs_1_, bf16[2048,768]{1,0:T(8,128)(2,1)} %get-tuple-element.213.refs_2_, ...), custom_call_target="tpu_custom_call", output_to_operand_aliasing={{0}: (4, {})} | custom-call | flops 10000000000 | bytes 30000000 | tf_op jit(solution)/shard_map/pallas_call | solution.py:226
  435.4 15.7 %shard_map.165 = (bf16[2,2,4,224,128]{4,3,2,1,0:T(8,128)(2,1)}, bf16[2,2,4,224,128]{4,3,2,1,0:T(8,128)(2,1)}, bf16[2,2,4,224,128]{4,3,2,1,0:T(8,128)(2,1)}, bf16[2,2,4,224,128]{4,3,2,1,0:T(8,128)(2,1)}, f32[8,128]{1,0:T(8,128)}) custom-call(s32[4]{0:T(128)} %pad_add_fusion.refs_0_.refs_1_, bf16[2048,768]{1,0:T(8,128)(2,1)} %bitcast.204, ...), custom_call_target="tpu_custom_call" | custom-call | flops 17999998976 | bytes 54000000 | tf_op jit(solution)/shard_map/pallas_call | solution.py:226
  462.1 13.2 %shard_map.167 = (bf16[2048,768]{1,0:T(8,128)(2,1)}, f32[8,128]{1,0:T(8,128)}) custom-call(f32[2048,768]{1,0:T(8,128)} %get-tuple-element.210.refs_0_, bf16[2048,2304]{1,0:T(8,128)(2,1)} %get-tuple-element.259.refs_2_.refs_1_, bf16[768,2304]{1,0:T(8,128)(2,1)} %get-tuple-element.177.refs_1_.refs_2_, f32[8,128]{1,0:T(8,128)} %copy-done.51), custom_call_target="tpu_custom_call" | custom-call | flops 12000000000 | bytes 36000000 | tf_op jit(solution)/shard_map/pallas_call | solution.py:226
  478.3 4.5 collective-permute-done.43.refs_2_
  490.8 3.4 collective-permute-done.46.refs_2_
  495.2 3.6 all-to-all-start.1
  499.6 4.0 broadcast_select_fusion
  503.6 9.2 %all-to-all-done.1 = bf16[8,448,128]{2,1,0:T(8,128)(2,1)S(1)} async-done(((bf16[8,448,128]{2,1,0:T(8,128)(2,1)}), bf16[8,448,128]{2,1,0:T(8,128)(2,1)S(1)}, u32[]{:S(2)}, u32[]{:S(2)}) %all-to-all-start.1) | async-done | bytes 917536 | tf_op jit(solution)/shard_map/all_to_all | solution.py:1753
  515.7 5.3 %shard_map.172 = (f32[3473,128]{1,0:T(8,128)}, f32[3473,128]{1,0:T(8,128)}, f32[3473,128]{1,0:T(8,128)}, bf16[3473,128]{1,0:T(8,128)(2,1)}, f32[8,128]{1,0:T(8,128)}) custom-call(s32[156]{0:T(256)S(1)} %bitcast.195, s32[5]{0:T(128)S(1)} %convert_bitcast_fusion.refs_1_, f32[10]{0:T(128)S(1)} %reshape.366.refs_2_, bf16[3584,128]{1,0:T(8,128)(2,1)S(1)} %bitcast.126, ...), custom_call_target="tpu_custom_call" | custom-call | tf_op jit(solution)/shard_map/pallas_call | solution.py:226
  (248 shorter events, 108.9 us)
Async XLA Ops:
  7.2 206.2 %all-gather.2.cloned.1.call-start = ((), (), s32[]{:S(2)}) async-start(), calls=%async_computation.2 | async-start | bytes 15138816 | tf_op jit(solution)/shard_map/all_gather | solution.py:1690
  33.4 25.3 %collective-permute-start.4 = (bf16[1,448,128]{2,1,0:T(8,128)(2,1)S(1)}, bf16[1,448,128]{2,1,0:T(8,128)(2,1)S(1)}, u32[]{:S(2)}, u32[]{:S(2)}) collective-permute-start(bf16[1,448,128]{2,1,0:T(8,128)(2,1)S(1)} %slice.40.refs_1_), channel_id=1, source_target_pairs={{0,2},{1,3},{2,0},{3,1},{4,6},{5,7},{6,4},{7,5},{8,10},{9,11},{10,... | collective-permute-start | bytes 344072 | tf_op jit(solution)/shard_map/ppermute | solution.py:1446
  33.4 25.3 %collective-permute-start.3 = (bf16[1,448,128]{2,1,0:T(8,128)(2,1)S(1)}, bf16[1,448,128]{2,1,0:T(8,128)(2,1)S(1)}, u32[]{:S(2)}, u32[]{:S(2)}) collective-permute-start(bf16[1,448,128]{2,1,0:T(8,128)(2,1)S(1)} %slice.40.refs_1_), channel_id=1, source_target_pairs={{0,1},{1,2},{2,3},{3,0},{4,5},{5,6},{6,7},{7,4},{8,9},{9,10},{10,1... | collective-permute-start | bytes 344072 | tf_op jit(solution)/shard_map/ppermute | solution.py:1446
  34.3 25.8 %collective-permute-start = (bf16[3,448,128]{2,1,0:T(8,128)(2,1)S(1)}, bf16[3,448,128]{2,1,0:T(8,128)(2,1)S(1)}, u32[]{:S(2)}, u32[]{:S(2)}) collective-permute-start(bf16[3,448,128]{2,1,0:T(8,128)(2,1)S(1)} %slice.39.refs_1_), channel_id=1, source_target_pairs={{0,1},{1,2},{2,3},{3,0},{4,5},{5,6},{6,7},{7,4},{8,9},{9,10},{10,1... | collective-permute-start | bytes 1032200 | tf_op jit(solution)/shard_map/ppermute | solution.py:1446
  37.0 29.1 %collective-permute-start.1 = (bf16[3,448,128]{2,1,0:T(8,128)(2,1)S(1)}, bf16[3,448,128]{2,1,0:T(8,128)(2,1)S(1)}, u32[]{:S(2)}, u32[]{:S(2)}) collective-permute-start(bf16[3,448,128]{2,1,0:T(8,128)(2,1)S(1)} %slice.39.refs_1_), channel_id=1, source_target_pairs={{0,2},{1,3},{2,0},{3,1},{4,6},{5,7},{6,4},{7,5},{8,10},{9,11},{10,... | collective-permute-start | bytes 1032200 | tf_op jit(solution)/shard_map/ppermute | solution.py:1446
  37.9 28.8 %collective-permute-start.2 = (bf16[3,448,128]{2,1,0:T(8,128)(2,1)S(1)}, bf16[3,448,128]{2,1,0:T(8,128)(2,1)S(1)}, u32[]{:S(2)}, u32[]{:S(2)}) collective-permute-start(bf16[3,448,128]{2,1,0:T(8,128)(2,1)S(1)} %slice.39.refs_1_), channel_id=1, source_target_pairs={{0,3},{1,0},{2,1},{3,2},{4,7},{5,4},{6,5},{7,6},{8,11},{9,8},{10,9... | collective-permute-start | bytes 1032200 | tf_op jit(solution)/shard_map/ppermute | solution.py:1446
  66.7 28.3 %collective-permute-start.8 = (bf16[12,224,128]{2,1,0:T(8,128)(2,1)S(1)}, bf16[12,224,128]{2,1,0:T(8,128)(2,1)S(1)}, u32[]{:S(2)}, u32[]{:S(2)}) collective-permute-start(bf16[12,224,128]{2,1,0:T(8,128)(2,1)S(1)} %get-tuple-element.164), channel_id=1, source_target_pairs={{0,8},{1,9},{2,10},{3,11},{4,12},{5,13},{6,14},{7,15},{8,0},{9,1},... | collective-permute-start | bytes 2064392 | tf_op jit(solution)/shard_map/ppermute | solution.py:1446
  67.8 27.3 %collective-permute-start.9 = (bf16[12,224,128]{2,1,0:T(8,128)(2,1)S(1)}, bf16[12,224,128]{2,1,0:T(8,128)(2,1)S(1)}, u32[]{:S(2)}, u32[]{:S(2)}) collective-permute-start(bf16[12,224,128]{2,1,0:T(8,128)(2,1)S(1)} %get-tuple-element.165), channel_id=1, source_target_pairs={{0,16},{1,17},{2,18},{3,19},{4,20},{5,21},{6,22},{7,23},{8,24},{9,... | collective-permute-start | bytes 2064392 | tf_op jit(solution)/shard_map/ppermute | solution.py:1446
  68.4 24.0 %collective-permute-start.11 = (bf16[2,4,224,128]{3,2,1,0:T(8,128)(2,1)S(1)}, bf16[2,4,224,128]{3,2,1,0:T(8,128)(2,1)S(1)}, u32[]{:S(2)}, u32[]{:S(2)}) collective-permute-start(bf16[2,4,224,128]{3,2,1,0:T(8,128)(2,1)S(1)} %bitcast.170), channel_id=1, source_target_pairs={{0,8},{1,9},{2,10},{3,11},{4,12},{5,13},{6,14},{7,15},{8,0},{9,1},... | collective-permute-start | bytes 1376264 | tf_op jit(solution)/shard_map/ppermute | solution.py:1446
  69.4 23.5 %collective-permute-start.10 = (bf16[2,4,224,128]{3,2,1,0:T(8,128)(2,1)S(1)}, bf16[2,4,224,128]{3,2,1,0:T(8,128)(2,1)S(1)}, u32[]{:S(2)}, u32[]{:S(2)}) collective-permute-start(bf16[2,4,224,128]{3,2,1,0:T(8,128)(2,1)S(1)} %bitcast.168), channel_id=1, source_target_pairs={{0,16},{1,17},{2,18},{3,19},{4,20},{5,21},{6,22},{7,23},{8,24},{9,... | collective-permute-start | bytes 1376264 | tf_op jit(solution)/shard_map/ppermute | solution.py:1446
  97.8 32.6 %collective-permute-start.13 = (bf16[2,12,224,128]{3,2,1,0:T(8,128)(2,1)S(1)}, bf16[2,12,224,128]{3,2,1,0:T(8,128)(2,1)}, u32[]{:S(2)}, u32[]{:S(2)}) collective-permute-start(bf16[2,12,224,128]{3,2,1,0:T(8,128)(2,1)S(1)} %bitcast.155), channel_id=1, source_target_pairs={{0,8},{1,9},{2,10},{3,11},{4,12},{5,13},{6,14},{7,15},{8,0},{9,1},... | collective-permute-start | bytes 4128776 | tf_op jit(solution)/shard_map/ppermute | solution.py:1446
  99.1 32.4 %collective-permute-start.12 = (bf16[2,12,224,128]{3,2,1,0:T(8,128)(2,1)S(1)}, bf16[2,12,224,128]{3,2,1,0:T(8,128)(2,1)}, u32[]{:S(2)}, u32[]{:S(2)}) collective-permute-start(bf16[2,12,224,128]{3,2,1,0:T(8,128)(2,1)S(1)} %bitcast.153), channel_id=1, source_target_pairs={{0,16},{1,17},{2,18},{3,19},{4,20},{5,21},{6,22},{7,23},{8,24},{9,... | collective-permute-start | bytes 4128776 | tf_op jit(solution)/shard_map/ppermute | solution.py:1446
  263.4 50.8 %collective-permute-start.18 = (bf16[4,448,128]{2,1,0:T(8,128)(2,1)S(1)}, bf16[4,448,128]{2,1,0:T(8,128)(2,1)S(1)}, u32[]{:S(2)}, u32[]{:S(2)}) collective-permute-start(bf16[4,448,128]{2,1,0:T(8,128)(2,1)S(1)} %get-tuple-element.221), channel_id=1, source_target_pairs={{0,1},{1,2},{2,3},{3,0},{4,5},{5,6},{6,7},{7,4},{8,9},{9,10},{10,1... | collective-permute-start | bytes 1376264 | tf_op jit(solution)/shard_map/ppermute | solution.py:1446
  264.2 50.0 %collective-permute-start.19 = (bf16[4,448,128]{2,1,0:T(8,128)(2,1)S(1)}, bf16[4,448,128]{2,1,0:T(8,128)(2,1)S(1)}, u32[]{:S(2)}, u32[]{:S(2)}) collective-permute-start(bf16[4,448,128]{2,1,0:T(8,128)(2,1)S(1)} %get-tuple-element.222), channel_id=1, source_target_pairs={{0,2},{1,3},{2,0},{3,1},{4,6},{5,7},{6,4},{7,5},{8,10},{9,11},{10,... | collective-permute-start | bytes 1376264 | tf_op jit(solution)/shard_map/ppermute | solution.py:1446
  265.6 48.6 %collective-permute-start.20 = (bf16[4,448,128]{2,1,0:T(8,128)(2,1)S(1)}, bf16[4,448,128]{2,1,0:T(8,128)(2,1)S(1)}, u32[]{:S(2)}, u32[]{:S(2)}) collective-permute-start(bf16[4,448,128]{2,1,0:T(8,128)(2,1)S(1)} %get-tuple-element.223), channel_id=1, source_target_pairs={{0,3},{1,0},{2,1},{3,2},{4,7},{5,4},{6,5},{7,6},{8,11},{9,8},{10,9... | collective-permute-start | bytes 1376264 | tf_op jit(solution)/shard_map/ppermute | solution.py:1446
  366.4 14.5 %collective-permute-start.25 = (bf16[2,2,8,224,128]{4,3,2,1,0:T(8,128)(2,1)}, bf16[2,2,8,224,128]{4,3,2,1,0:T(8,128)(2,1)}, u32[]{:S(2)}, u32[]{:S(2)}) collective-permute-start(bf16[2,2,8,224,128]{4,3,2,1,0:T(8,128)(2,1)} %get-tuple-element.241), channel_id=1, source_target_pairs={{0,4},{1,5},{2,6},{3,7},{4,0},{5,1},{6,2},{7,3},{8,12},{9,13},{10,... | collective-permute-start | bytes 5505032 | tf_op jit(solution)/shard_map/ppermute | solution.py:1446
  366.6 14.3 %collective-permute-start.26 = (bf16[2,2,8,224,128]{4,3,2,1,0:T(8,128)(2,1)}, bf16[2,2,8,224,128]{4,3,2,1,0:T(8,128)(2,1)}, u32[]{:S(2)}, u32[]{:S(2)}) collective-permute-start(bf16[2,2,8,224,128]{4,3,2,1,0:T(8,128)(2,1)} %get-tuple-element.243), channel_id=1, source_target_pairs={{0,4},{1,5},{2,6},{3,7},{4,0},{5,1},{6,2},{7,3},{8,12},{9,13},{10,... | collective-permute-start | bytes 5505032 | tf_op jit(solution)/shard_map/ppermute | solution.py:1446
  367.0 12.9 %collective-permute-start.23 = (bf16[2,4,224,128]{3,2,1,0:T(8,128)(2,1)}, bf16[2,4,224,128]{3,2,1,0:T(8,128)(2,1)}, u32[]{:S(2)}, u32[]{:S(2)}) collective-permute-start(bf16[2,4,224,128]{3,2,1,0:T(8,128)(2,1)} %bitcast.49), channel_id=1, source_target_pairs={{0,16},{1,17},{2,18},{3,19},{4,20},{5,21},{6,22},{7,23},{8,24},{9,... | collective-permute-start | bytes 1376264 | tf_op jit(solution)/shard_map/ppermute | solution.py:1446
  390.5 19.9 %collective-permute-start.29 = (bf16[4,224,128]{2,1,0:T(8,128)(2,1)}, bf16[4,224,128]{2,1,0:T(8,128)(2,1)}, u32[]{:S(2)}, u32[]{:S(2)}) collective-permute-start(bf16[4,224,128]{2,1,0:T(8,128)(2,1)} %bitcast.65), channel_id=1, source_target_pairs={{0,8},{1,9},{2,10},{3,11},{4,12},{5,13},{6,14},{7,15},{8,0},{9,1},... | collective-permute-start | bytes 688136 | tf_op jit(solution)/shard_map/ppermute | solution.py:1446
  391.8 18.7 %collective-permute-start.30 = (bf16[4,224,128]{2,1,0:T(8,128)(2,1)}, bf16[4,224,128]{2,1,0:T(8,128)(2,1)}, u32[]{:S(2)}, u32[]{:S(2)}) collective-permute-start(bf16[4,224,128]{2,1,0:T(8,128)(2,1)} %bitcast.67), channel_id=1, source_target_pairs={{0,16},{1,17},{2,18},{3,19},{4,20},{5,21},{6,22},{7,23},{8,24},{9,... | collective-permute-start | bytes 688136 | tf_op jit(solution)/shard_map/ppermute | solution.py:1446
  392.6 25.2 %collective-permute-start.27 = (bf16[2,8,224,128]{3,2,1,0:T(8,128)(2,1)}, bf16[2,8,224,128]{3,2,1,0:T(8,128)(2,1)S(1)}, u32[]{:S(2)}, u32[]{:S(2)}) collective-permute-start(bf16[2,8,224,128]{3,2,1,0:T(8,128)(2,1)} %bitcast.59), channel_id=1, source_target_pairs={{0,16},{1,17},{2,18},{3,19},{4,20},{5,21},{6,22},{7,23},{8,24},{9,... | collective-permute-start | bytes 2752520 | tf_op jit(solution)/shard_map/ppermute | solution.py:1446
  393.8 24.0 %collective-permute-start.28 = (bf16[2,8,224,128]{3,2,1,0:T(8,128)(2,1)}, bf16[2,8,224,128]{3,2,1,0:T(8,128)(2,1)S(1)}, u32[]{:S(2)}, u32[]{:S(2)}) collective-permute-start(bf16[2,8,224,128]{3,2,1,0:T(8,128)(2,1)} %bitcast.62), channel_id=1, source_target_pairs={{0,8},{1,9},{2,10},{3,11},{4,12},{5,13},{6,14},{7,15},{8,0},{9,1},... | collective-permute-start | bytes 2752520 | tf_op jit(solution)/shard_map/ppermute | solution.py:1446
  413.0 18.4 %collective-permute-start.33 = (bf16[1,448,128]{2,1,0:T(8,128)(2,1)}, bf16[1,448,128]{2,1,0:T(8,128)(2,1)}, u32[]{:S(2)}, u32[]{:S(2)}) collective-permute-start(bf16[1,448,128]{2,1,0:T(8,128)(2,1)} %get-tuple-element.266), channel_id=1, source_target_pairs={{0,1},{1,2},{2,3},{3,0},{4,5},{5,6},{6,7},{7,4},{8,9},{9,10},{10,1... | collective-permute-start | bytes 344072 | tf_op jit(solution)/shard_map/ppermute | solution.py:1446
  413.0 18.4 %collective-permute-start.34 = (bf16[1,448,128]{2,1,0:T(8,128)(2,1)}, bf16[1,448,128]{2,1,0:T(8,128)(2,1)}, u32[]{:S(2)}, u32[]{:S(2)}) collective-permute-start(bf16[1,448,128]{2,1,0:T(8,128)(2,1)} %get-tuple-element.267), channel_id=1, source_target_pairs={{0,2},{1,3},{2,0},{3,1},{4,6},{5,7},{6,4},{7,5},{8,10},{9,11},{10,... | collective-permute-start | bytes 344072 | tf_op jit(solution)/shard_map/ppermute | solution.py:1446
  414.4 17.0 %collective-permute-start.35 = (bf16[1,448,128]{2,1,0:T(8,128)(2,1)}, bf16[1,448,128]{2,1,0:T(8,128)(2,1)}, u32[]{:S(2)}, u32[]{:S(2)}) collective-permute-start(bf16[1,448,128]{2,1,0:T(8,128)(2,1)} %get-tuple-element.268), channel_id=1, source_target_pairs={{0,3},{1,0},{2,1},{3,2},{4,7},{5,4},{6,5},{7,6},{8,11},{9,8},{10,9... | collective-permute-start | bytes 344072 | tf_op jit(solution)/shard_map/ppermute | solution.py:1446
  420.4 13.5 %collective-permute-start.31 = (bf16[8,224,128]{2,1,0:T(8,128)(2,1)}, bf16[8,224,128]{2,1,0:T(8,128)(2,1)S(1)}, u32[]{:S(2)}, u32[]{:S(2)}) collective-permute-start(bf16[8,224,128]{2,1,0:T(8,128)(2,1)} %bitcast.69), channel_id=1, source_target_pairs={{0,8},{1,9},{2,10},{3,11},{4,12},{5,13},{6,14},{7,15},{8,0},{9,1},... | collective-permute-start | bytes 1376264 | tf_op jit(solution)/shard_map/ppermute | solution.py:1446
  451.7 23.6 %collective-permute-start.40 = (bf16[2,448,128]{2,1,0:T(8,128)(2,1)}, bf16[2,448,128]{2,1,0:T(8,128)(2,1)S(1)}, u32[]{:S(2)}, u32[]{:S(2)}) collective-permute-start(bf16[2,448,128]{2,1,0:T(8,128)(2,1)} %get-tuple-element.284), channel_id=1, source_target_pairs={{0,1},{1,2},{2,3},{3,0},{4,5},{5,6},{6,7},{7,4},{8,9},{9,10},{10,1... | collective-permute-start | bytes 688136 | tf_op jit(solution)/shard_map/ppermute | solution.py:1446
  452.2 23.1 %collective-permute-start.41 = (bf16[2,448,128]{2,1,0:T(8,128)(2,1)}, bf16[2,448,128]{2,1,0:T(8,128)(2,1)S(1)}, u32[]{:S(2)}, u32[]{:S(2)}) collective-permute-start(bf16[2,448,128]{2,1,0:T(8,128)(2,1)} %get-tuple-element.285), channel_id=1, source_target_pairs={{0,2},{1,3},{2,0},{3,1},{4,6},{5,7},{6,4},{7,5},{8,10},{9,11},{10,... | collective-permute-start | bytes 688136 | tf_op jit(solution)/shard_map/ppermute | solution.py:1446
  453.2 22.1 %collective-permute-start.42 = (bf16[2,448,128]{2,1,0:T(8,128)(2,1)}, bf16[2,448,128]{2,1,0:T(8,128)(2,1)S(1)}, u32[]{:S(2)}, u32[]{:S(2)}) collective-permute-start(bf16[2,448,128]{2,1,0:T(8,128)(2,1)} %get-tuple-element.286), channel_id=1, source_target_pairs={{0,3},{1,0},{2,1},{3,2},{4,7},{5,4},{6,5},{7,6},{8,11},{9,8},{10,9... | collective-permute-start | bytes 688136 | tf_op jit(solution)/shard_map/ppermute | solution.py:1446
  459.7 16.6 %collective-permute-start.38 = (bf16[2,4,224,128]{3,2,1,0:T(8,128)(2,1)S(1)}, bf16[2,4,224,128]{3,2,1,0:T(8,128)(2,1)S(1)}, u32[]{:S(2)}, u32[]{:S(2)}) collective-permute-start(bf16[2,4,224,128]{3,2,1,0:T(8,128)(2,1)S(1)} %bitcast.197), channel_id=1, source_target_pairs={{0,16},{1,17},{2,18},{3,19},{4,20},{5,21},{6,22},{7,23},{8,24},{9,... | collective-permute-start | bytes 1376264 | tf_op jit(solution)/shard_map/ppermute | solution.py:1446
  461.0 15.3 %collective-permute-start.39 = (bf16[2,4,224,128]{3,2,1,0:T(8,128)(2,1)S(1)}, bf16[2,4,224,128]{3,2,1,0:T(8,128)(2,1)S(1)}, u32[]{:S(2)}, u32[]{:S(2)}) collective-permute-start(bf16[2,4,224,128]{3,2,1,0:T(8,128)(2,1)S(1)} %bitcast.196), channel_id=1, source_target_pairs={{0,8},{1,9},{2,10},{3,11},{4,12},{5,13},{6,14},{7,15},{8,0},{9,1},... | collective-permute-start | bytes 1376264 | tf_op jit(solution)/shard_map/ppermute | solution.py:1446
  495.2 17.5 %all-to-all-start.1 = ((bf16[8,448,128]{2,1,0:T(8,128)(2,1)}), bf16[8,448,128]{2,1,0:T(8,128)(2,1)S(1)}, u32[]{:S(2)}, u32[]{:S(2)}) async-start(bf16[8,448,128]{2,1,0:T(8,128)(2,1)} %get-tuple-element.302), calls=%async_computation.1 | async-start | bytes 1835008 | tf_op jit(solution)/shard_map/all_to_all | solution.py:1753
  (77 other events, 561.4 us)
Sparse Core Ops, SparseCore 0:
  97.9 115.3 all-gather.1
